TPU v7x, 128 devices: a whole 4x4x4 slice. The times are simulated.
128 devices in a mesh: dp: 16 (over y_hi, x, core), tensor: 8 (over z, y_lo).
Axes of the slice: x: 4, y: 4 (y_hi: 2, y_lo: 2; y = y_hi * 2 + y_lo), z: 4, core: 2. Of those that a mesh axis runs over, the one named last changes fastest.
Arguments:
- kv_pool: bfloat16 [8192, 8, 16, 256], P('dp', 'tensor'), may hold values from -6 to 6
- page_loc: int32 [8, 128, 64], replicated, may hold values from 0 to 8191, as said below
- lengths: int32 [128], replicated, may hold values from 256 to 1024
- placement: int32 [128], replicated, may hold values from 0 to 127, as said below
- queries: bfloat16 [2, 128, 64, 128], P(None, 'dp', 'tensor'), may hold values from -27 to 27
- new_kv: bfloat16 [2, 128, 8, 256], P(None, 'dp', 'tensor'), may hold values from -6 to 6
- resid_in: bfloat16 [2, 128, 8192], P(None, None, 'dp'), may hold values from -1.5 to 1.5
- w_out: bfloat16 [8192, 8192], P('tensor', 'dp'), may hold values from -0.0625 to 0.0625
- ffn_gain: float32 [8192], replicated, may hold values from 0.1 to 1.9
- w_gate: bfloat16 [8192, 28672], P(None, ('dp', 'tensor')), may hold values from -0.0625 to 0.0625
- w_up: bfloat16 [8192, 28672], P(None, ('dp', 'tensor')), may hold values from -0.0625 to 0.0625
- w_down: bfloat16 [28672, 8192], P(('dp', 'tensor')), may hold values from -0.125 to 0.125
Outputs:
- block_out: bfloat16 [2, 128, 8192], P(None, 'dp', 'tensor')
- kv_cache: bfloat16 [8, 128, 1040, 256], P('tensor', 'dp')
Inputs may be any that keep to these rules, and one draw needn't show every extreme that they name: `placement`: A permutation: every decoding slot holds one request; slots d * 8 to (d + 1) * 8 - 1 belong to dp index d. The requests of one dp index, drawn from the seed, all have 1024 tokens. For p < ceil(lengths[r] / 16), page_loc[h, r, p] = device * 512 + row names the pool row holding tokens 16 * p onward of request r for key-value head h; two pages of one head never share a row; of the pages of one head of the requests of one dp index, at most 32 lie on any one dp index of the pool, and this is reached in every draw; entries past a request's pages are 0.
All inputs are finite; a program needn't handle non-finite values.
Results may differ from a plain program's by a relative error of at most 0.034.
Values may be sent and summed in bfloat16 or wider, within the bound.
No kernel may reach another device: no remote copies, remote signals or barrier semaphores. Data moves between devices by JAX's collectives and lax.ppermute only.
A program may use at most 128 MiB of HBM per device.

v0:
```python
import math

import jax
import jax.numpy as jnp
from jax import lax
from jax.sharding import PartitionSpec as P


def per_device(
    kv_pool,
    page_loc,
    lengths,
    placement,
    queries,
    new_kv,
    resid_in,
    w_out,
    ffn_gain,
    w_gate,
    w_up,
    w_down,
):
    n_dp = lax.axis_size("dp")
    n_tensor = lax.axis_size("tensor")
    dev_dp = lax.axis_index("dp")
    dev_tensor = lax.axis_index("tensor")
    pslots, kv_dev, page_size, width_two = kv_pool.shape
    head_dim = width_two // 2
    n_req = lengths.shape[0]
    req_dev = n_req // n_dp
    max_pages = page_loc.shape[2]
    max_len = max_pages * page_size
    cache_len = max_len + page_size
    capacity = pslots // n_dp
    n_steps = queries.shape[0]
    hq_dev = queries.shape[2]
    group_size = hq_dev // kv_dev
    entries = req_dev * max_pages
    slot_order = (
        jnp.zeros((n_req,), jnp.int32).at[placement].set(jnp.arange(n_req, dtype=jnp.int32))
    )
    len_slot = lengths[slot_order]
    pages_slot = (len_slot + page_size - 1) // page_size
    loc_mine = lax.dynamic_slice_in_dim(page_loc, dev_tensor * kv_dev, kv_dev, 0)[:, slot_order, :]
    live_page = jnp.arange(max_pages, dtype=jnp.int32)[None, :] < pages_slot[:, None]
    loc_dev = loc_mine.reshape(kv_dev, n_dp, entries)
    live_dev = live_page.reshape(1, n_dp, entries)
    source = loc_dev // pslots
    one_hot = (
        (source[..., None] == jnp.arange(n_dp, dtype=jnp.int32)) & live_dev[..., None]
    ).astype(jnp.int32)
    rank_pos = jnp.sum((jnp.cumsum(one_hot, axis=2) - 1) * one_hot, axis=3)
    target = jnp.where(live_dev & (source == dev_dp), rank_pos, capacity)
    head_grid = jnp.broadcast_to(jnp.arange(kv_dev, dtype=jnp.int32)[:, None, None], loc_dev.shape)
    dest_grid = jnp.broadcast_to(jnp.arange(n_dp, dtype=jnp.int32)[None, :, None], loc_dev.shape)
    send_rows = (
        jnp.zeros((kv_dev, n_dp, capacity), jnp.int32)
        .at[head_grid, dest_grid, target]
        .set(loc_dev % pslots, mode="drop")
    )
    outgoing = jnp.stack([kv_pool[send_rows[0], 0]])
    received = lax.all_to_all(outgoing, "dp", split_axis=1, concat_axis=1, tiled=True)
    flat_recv = received.reshape(kv_dev, n_dp * capacity, page_size, width_two)
    my_source = lax.dynamic_index_in_dim(source, dev_dp, 1, keepdims=False)
    my_rank = lax.dynamic_index_in_dim(rank_pos, dev_dp, 1, keepdims=False)
    my_live = lax.dynamic_index_in_dim(live_dev, dev_dp, 1, keepdims=False)
    pick_row = jnp.where(my_live, my_source * capacity + my_rank, 0)
    arrived = jnp.stack([flat_recv[0][pick_row[0]]])
    tokens = arrived.reshape(kv_dev, req_dev, max_len, width_two)
    padded = jnp.concatenate(
        [tokens, jnp.zeros((kv_dev, req_dev, page_size, width_two), tokens.dtype)], axis=2
    )
    my_len = lax.dynamic_slice_in_dim(len_slot, dev_dp * req_dev, req_dev)
    positions = jnp.arange(cache_len, dtype=jnp.int32)
    cache = jnp.where(
        positions[None, None, :, None] < my_len[None, :, None, None],
        padded,
        jnp.zeros((), padded.dtype),
    )
    for step_idx in range(n_steps):
        fresh = jnp.transpose(new_kv[step_idx], (1, 0, 2))
        cache = jnp.where(
            positions[None, None, :, None] == (my_len + step_idx)[None, :, None, None],
            fresh[:, :, None, :],
            cache,
        )
    keys_part = cache[..., :head_dim]
    values_part = cache[..., head_dim:]
    scale = 1.0 / math.sqrt(head_dim)
    width_tensor = ffn_gain.shape[0] // n_tensor
    outputs = []
    for step_idx in range(n_steps):
        query = queries[step_idx].reshape(req_dev, kv_dev, group_size, head_dim)
        scores = (
            jnp.einsum("rhgd,hrtd->rhgt", query, keys_part, preferred_element_type=jnp.float32)
            * scale
        )
        visible = positions[None, None, None, :] < (my_len + step_idx + 1)[:, None, None, None]
        scores = jnp.where(visible, scores, -jnp.inf)
        peak = jnp.max(scores, axis=-1, keepdims=True)
        expo = jnp.exp(scores - peak)
        probs = (expo / jnp.sum(expo, axis=-1, keepdims=True)).astype(jnp.bfloat16)
        mixed = jnp.einsum(
            "rhgt,hrtd->rhgd", probs, values_part, preferred_element_type=jnp.float32
        ).astype(jnp.bfloat16)
        mixed = mixed.reshape(req_dev, hq_dev * head_dim)
        partial_out = jnp.dot(
            lax.all_gather(mixed, "dp", axis=0, tiled=True),
            w_out,
            preferred_element_type=jnp.float32,
        )
        resid_cols = resid_in[step_idx]
        summed = lax.psum(partial_out.astype(jnp.bfloat16), "tensor").astype(jnp.float32)
        hidden_cols = (resid_cols.astype(jnp.float32) + summed).astype(jnp.bfloat16)
        hidden_full = lax.all_gather(hidden_cols, "dp", axis=1, tiled=True)
        hid_wide = hidden_full.astype(jnp.float32)
        inverse = lax.rsqrt(jnp.mean(hid_wide * hid_wide, axis=-1, keepdims=True) + 1e-05)
        normed = (hid_wide * inverse * ffn_gain).astype(jnp.bfloat16)
        gate = jnp.dot(normed, w_gate, preferred_element_type=jnp.float32)
        upper = jnp.dot(normed, w_up, preferred_element_type=jnp.float32)
        act = (jax.nn.silu(gate) * upper).astype(jnp.bfloat16)
        partial_ffn = jnp.dot(act, w_down, preferred_element_type=jnp.float32)
        rows_part = lax.psum_scatter(
            partial_ffn.astype(jnp.bfloat16), "dp", scatter_dimension=0, tiled=True
        )
        ffn_part = lax.psum_scatter(rows_part, "tensor", scatter_dimension=1, tiled=True).astype(
            jnp.float32
        )
        own_hidden = lax.dynamic_slice(
            hidden_full, (dev_dp * req_dev, dev_tensor * width_tensor), (req_dev, width_tensor)
        )
        outputs.append((own_hidden.astype(jnp.float32) + ffn_part).astype(jnp.bfloat16))
    return (jnp.stack(outputs), cache)


def solution(mesh):
    placed = (
        P("dp", "tensor", None, None),
        P(),
        P(),
        P(),
        P(None, "dp", "tensor", None),
        P(None, "dp", "tensor", None),
        P(None, None, "dp"),
        P("tensor", "dp"),
        P(),
        P(None, ("dp", "tensor")),
        P(None, ("dp", "tensor")),
        P(("dp", "tensor"), None),
    )
    return jax.shard_map(
        per_device,
        mesh=mesh,
        in_specs=placed,
        out_specs=(P(None, "dp", "tensor"), P("tensor", "dp", None, None)),
        check_vma=False,
    )
```

profile of v0, /device:TPU:0, one launch (start us, length us, event | category | flops | bytes accessed | tf_op | source)
XLA Modules:
  0.0 613.3 jit_solution(1174052508985452109)
XLA Ops:
  7.2 0.9 constant_dynamic-slice_fusion
  8.0 0.1 copy.20
  8.1 0.7 compare_select_fusion.4
  8.8 1.0 scatter_custom_fusion
  9.8 0.6 gather_fusion.1
  10.4 0.1 reshape.792
  10.6 1.6 gather_fusion
  12.1 0.1 sub.52
  12.3 0.1 lt.199
  12.4 0.1 lt.197
  12.5 0.5 fusion.33
  13.1 18.1 %reduce-window.6 = s32[1,16,16,4,128]{4,2,3,1,0:T(8,128)S(1)} reduce-window(s32[1,16,16,4,128]{4,2,3,1,0:T(8,128)S(1)} %copy.21, s32[]{:T(128)} %constant.55.clone.1), window={size=1x1x1x1x128 pad=0_0x0_0x0_0x0_0x127_0}, to_apply=%region_1.2 | reduce-window | flops 16646144 | bytes 1048580 | tf_op jit(solution)/shard_map/reduce-window
  31.3 0.2 slice.48
  31.5 0.2 copy.22
  31.7 0.1 reshape.791
  31.8 0.1 lt.193
  31.8 0.1 reshape.798
  31.9 0.4 copy.23
  32.3 0.1 fusion.54
  32.5 0.2 copy.24
  32.7 0.1 lt.190
  32.7 0.3 broadcast.595
  33.1 1.3 fusion.32
  34.4 0.1 multiply_reduce_fusion
  34.5 0.1 and_reduce_fusion
  34.7 30.4 %scatter_custom_fusion.1 = s32[512]{0:T(512)S(1)} fusion(s32[8192]{0:T(1024)S(1)} %bitcast.123, s32[8192]{0:T(1024)S(1)} %bitcast.124, s32[]{:T(128)} %constant.55.clone.1), kind=kCustom, calls=%fused_computation.143 | custom fusion | bytes 2052
  65.2 0.1 squeeze.15
  65.2 0.1 reshape.835
  65.3 7.3 %gather_fusion.2 = bf16[512,16,256]{2,1,0:T(8,128)(2,1)} fusion(bf16[512,1,16,256]{3,2,1,0:T(8,128)(2,1)} %param.12, s32[512]{0:T(512)S(1)} %reshape.835), kind=kCustom, calls=%fused_computation.2 | custom fusion | bytes 8392704 | tf_op jit(solution)/shard_map/gather | solution.py:61
  72.7 7.3 %all-to-all-start = ((bf16[1,16,32,16,256]{4,3,2,0,1:T(8,128)(2,1)}), bf16[1,16,32,16,256]{4,3,2,0,1:T(8,128)(2,1)}, u32[]{:S(2)}, u32[]{:S(2)}) async-start(bf16[1,16,32,16,256]{4,3,2,0,1:T(8,128)(2,1)} %bitcast.116), calls=%async_computation | async-start | bytes 8388608 | tf_op jit(solution)/shard_map/all_to_all | solution.py:62
  80.0 0.1 lt.206
  80.2 0.1 iota_compare_fusion
  80.3 0.1 iota_compare_fusion.2
  80.4 0.1 iota_compare_fusion.4
  80.5 55.8 %all-to-all-done = bf16[1,16,32,16,256]{4,3,2,0,1:T(8,128)(2,1)} async-done(((bf16[1,16,32,16,256]{4,3,2,0,1:T(8,128)(2,1)}), bf16[1,16,32,16,256]{4,3,2,0,1:T(8,128)(2,1)}, u32[]{:S(2)}, u32[]{:S(2)}) %all-to-all-start) | async-done | bytes 4194336 | tf_op jit(solution)/shard_map/all_to_all | solution.py:62
  136.3 5.1 gather_fusion.3
  141.4 8.2 %select_select_fusion = bf16[1,8,1040,256]{3,2,1,0:T(8,128)(2,1)} fusion(bf16[1,8,1024,256]{3,2,1,0:T(8,128)(2,1)} %bitcast.115, pred[8,1040]{1,0:T(8,128)(4,1)S(1)} %get-tuple-element.17, pred[8,1040]{1,0:T(8,128)(4,1)S(1)} %get-tuple-element.16, pred[8,1040]{1,0:T(8,128)(4,1)S(1)} %get-tuple-element.15, bf16[8,256]{1,0:T(8,128)(2,1)S(1)} %get-tuple-element.13, ...), kind=kLoop, calls=%fused_computation.14 | loop fusion | flops 6389760 | bytes 8487296 | tf_op jit(solution)/shard_map/jit(_where)/select_n | solution.py:82
  149.7 2.4 fusion.77
  152.1 2.0 fusion.23
  154.2 22.5 %all_gather.12 = bf16[128,1024]{1,0:T(8,128)(2,1)S(1)} all-gather(bf16[8,1024]{1,0:T(8,128)(2,1)S(1)} %bitcast.121), channel_id=1, replica_groups=mesh['dp'=16,'tensor'=8] {'dp'}, dimensions={0}, use_global_device_ids=true | all-gather | bytes 278528 | tf_op jit(solution)/shard_map/all_gather | solution.py:108
  176.7 2.4 fusion.76
  179.2 2.1 fusion.22
  181.3 20.0 %all_gather.14 = bf16[128,1024]{1,0:T(8,128)(2,1)S(1)} all-gather(bf16[8,1024]{1,0:T(8,128)(2,1)S(1)} %bitcast.122), channel_id=1, replica_groups=mesh['dp'=16,'tensor'=8] {'dp'}, dimensions={0}, use_global_device_ids=true | all-gather | bytes 278528 | tf_op jit(solution)/shard_map/all_gather | solution.py:108
  201.3 1.0 convolution_convert_fusion.3
  202.3 1.0 convolution_convert_fusion.2
  203.3 74.7 %all-reduce.5.cloned.1.call-done = (bf16[128,512]{1,0:T(8,128)(2,1)}, bf16[128,512]{1,0:T(8,128)(2,1)}) async-done(((bf16[128,512]{1,0:T(8,128)(2,1)}, bf16[128,512]{1,0:T(8,128)(2,1)}), (bf16[128,512]{1,0:T(8,128)(2,1)}, bf16[128,512]{1,0:T(8,128)(2,1)})) %all-reduce.5.cloned.1.call-update) | async-done | bytes 262160 | tf_op jit(solution)/shard_map/psum | solution.py:113
  278.0 1.7 fusion.35
  279.8 0.7 all-gather.5.cloned.1.call-update
  280.5 0.2 reduce-scatter.5.cloned.1.call-start
  280.7 48.5 %all-gather.3.cloned.1.call-done = bf16[128,8192]{1,0:T(8,128)(2,1)} async-done(((bf16[128,512]{1,0:T(8,128)(2,1)}), bf16[128,8192]{1,0:T(8,128)(2,1)}) %all-gather.3.cloned.1.call-update) | async-done | bytes 2097168 | tf_op jit(solution)/shard_map/all_gather | solution.py:115
  329.2 2.1 fusion.2
  331.3 4.0 fusion.30
  335.3 7.4 %convolution_convert_fusion.1 = bf16[128,8192]{1,0:T(8,128)(2,1)} fusion(bf16[224,8192]{1,0:T(8,128)(2,1)} %param.23, bf16[8192,224]{0,1:T(8,128)(2,1)} %param.22, bf16[128,8192]{1,0:T(8,128)(2,1)S(1)} %copy-done.1, f32[8192]{0:T(1024)S(1)} %copy-done.3, f32[128]{0:T(128)S(1)} %add_rsqrt_fusion.1, f32[128,224]{0,1:T(8,128)S(1)} %fusion.30), kind=kOutput, calls=%fused_computation.9 | convolution fusion | flops 944939008 | bytes 11682304 | tf_op jit(solution)/shard_map/dot_general | solution.py:122
  342.8 37.2 %all-gather.5.cloned.1.call-done = bf16[128,8192]{1,0:T(8,128)(2,1)} async-done(((bf16[128,512]{1,0:T(8,128)(2,1)}), bf16[128,8192]{1,0:T(8,128)(2,1)}) %all-gather.5.cloned.1.call-update) | async-done | bytes 2097168 | tf_op jit(solution)/shard_map/all_gather | solution.py:115
  380.0 2.1 fusion.5
  382.1 3.9 fusion.26
  386.0 8.1 %convolution_convert_fusion = bf16[128,8192]{1,0:T(8,128)(2,1)} fusion(bf16[224,8192]{1,0:T(8,128)(2,1)} %param.23, bf16[8192,224]{0,1:T(8,128)(2,1)} %param.22, bf16[128,8192]{1,0:T(8,128)(2,1)} %all-gather.5.cloned.1.call-done, f32[128]{0:T(128)S(1)} %add_rsqrt_fusion, f32[8192]{0:T(1024)S(1)} %copy-done.3, f32[128,224]{0,1:T(8,128)S(1)} %fusion.26), kind=kOutput, calls=%fused_computation.8 | convolution fusion | flops 944939008 | bytes 11682304 | tf_op jit(solution)/shard_map/dot_general | solution.py:122
  394.2 59.8 %reduce-scatter.5.cloned.1.call-done = bf16[8,8192]{1,0:T(8,128)(2,1)} async-done(((bf16[128,8192]{1,0:T(8,128)(2,1)}), bf16[8,8192]{1,0:T(8,128)(2,1)}) %reduce-scatter.5.cloned.1.call-update) | async-done | bytes 131088 | tf_op jit(solution)/shard_map/reduce_scatter | solution.py:123
  454.1 74.2 %reduce-scatter.9.cloned.1.call-done = bf16[8,8192]{1,0:T(8,128)(2,1)} async-done(((bf16[128,8192]{1,0:T(8,128)(2,1)}), bf16[8,8192]{1,0:T(8,128)(2,1)}) %reduce-scatter.9.cloned.1.call-update) | async-done | bytes 131088 | tf_op jit(solution)/shard_map/reduce_scatter | solution.py:123
  528.4 38.7 %reduce-scatter.7.cloned.1.call-done = bf16[8,1024]{1,0:T(8,128)(2,1)} async-done(((bf16[8,8192]{1,0:T(8,128)(2,1)}), bf16[8,1024]{1,0:T(8,128)(2,1)}) %reduce-scatter.7.cloned.1.call-update) | async-done | bytes 16400 | tf_op jit(solution)/shard_map/reduce_scatter | solution.py:126
  567.1 0.7 fusion.59
  567.8 37.3 %reduce-scatter.11.cloned.1.call-done = bf16[8,1024]{1,0:T(8,128)(2,1)} async-done(((bf16[8,8192]{1,0:T(8,128)(2,1)}), bf16[8,1024]{1,0:T(8,128)(2,1)}) %reduce-scatter.11.cloned.1.call-update) | async-done | bytes 16400 | tf_op jit(solution)/shard_map/reduce_scatter | solution.py:126
  605.1 0.7 fusion.60
  605.9 0.6 pad_maximum_fusion
  (58 shorter events, 0.9 us)
Async XLA Ops:
  7.2 194.1 %copy-start = (bf16[1024,512]{1,0:T(8,128)(2,1)S(1)}, bf16[1024,512]{1,0:T(8,128)(2,1)}, u32[]{:S(2)}) copy-start(bf16[1024,512]{1,0:T(8,128)(2,1)} %param.19) | copy-start | bytes 3145732
  13.0 21.4 %copy-start.6 = (s32[3]{0:T(128)S(1)}, s32[3]{0:T(128)}, u32[]{:S(2)}) copy-start(s32[3]{0:T(128)} %constant.128) | copy-start | bytes 40
  13.1 21.5 %copy-start.5 = (s32[3]{0:T(128)S(1)}, s32[3]{0:T(128)}, u32[]{:S(2)}) copy-start(s32[3]{0:T(128)} %constant.131) | copy-start | bytes 40
  72.7 7.6 %copy-start.4 = (bf16[2,8,1,256]{3,1,2,0:T(8,128)(2,1)S(1)}, bf16[2,8,1,256]{3,1,2,0:T(8,128)(2,1)}, u32[]{:S(2)}) copy-start(bf16[2,8,1,256]{3,1,2,0:T(8,128)(2,1)} %param.17) | copy-start | bytes 24580
  72.7 63.7 %all-to-all-start = ((bf16[1,16,32,16,256]{4,3,2,0,1:T(8,128)(2,1)}), bf16[1,16,32,16,256]{4,3,2,0,1:T(8,128)(2,1)}, u32[]{:S(2)}, u32[]{:S(2)}) async-start(bf16[1,16,32,16,256]{4,3,2,0,1:T(8,128)(2,1)} %bitcast.116), calls=%async_computation | async-start | bytes 8388608 | tf_op jit(solution)/shard_map/all_to_all | solution.py:62
  80.0 198.0 %all-reduce.5.cloned.1.call-start = ((), (), s32[]{:S(2)}) async-start(), calls=%async_computation.11 | async-start | bytes 524288 | tf_op jit(solution)/shard_map/psum | solution.py:113
  141.4 8.3 %copy-start.7 = (bf16[2,8,8,128]{3,2,1,0:T(8,128)(2,1)S(1)}, bf16[2,8,8,128]{3,2,1,0:T(8,128)(2,1)}, u32[]{:S(2)}) copy-start(bf16[2,8,8,128]{3,2,1,0:T(8,128)(2,1)} %param.16) | copy-start | bytes 98308
  179.2 98.8 %copy-start.2 = (bf16[2,128,512]{2,1,0:T(8,128)(2,1)S(1)}, bf16[2,128,512]{2,1,0:T(8,128)(2,1)}, u32[]{:S(2)}) copy-start(bf16[2,128,512]{2,1,0:T(8,128)(2,1)} %param.18) | copy-start | bytes 786436
  181.3 150.0 %copy-start.3 = (f32[8192]{0:T(1024)S(1)}, f32[8192]{0:T(1024)}, u32[]{:S(2)}) copy-start(f32[8192]{0:T(1024)} %param.20) | copy-start | bytes 98308
  203.3 125.9 %all-gather.3.cloned.1.call-start = ((), (), s32[]{:S(2)}) async-start(), calls=%async_computation.5 | async-start | bytes 2228224 | tf_op jit(solution)/shard_map/all_gather | solution.py:115
  279.8 100.3 %all-gather.5.cloned.1.call-start = ((), (), s32[]{:S(2)}) async-start(), calls=%async_computation.8 | async-start | bytes 2228224 | tf_op jit(solution)/shard_map/all_gather | solution.py:115
  280.5 173.5 %reduce-scatter.5.cloned.1.call-start = ((), (), s32[]{:S(2)}) async-start(), calls=%async_computation.6 | async-start | bytes 2228224 | tf_op jit(solution)/shard_map/reduce_scatter | solution.py:123
  331.3 4.0 copy-start.1
  342.8 185.5 %reduce-scatter.9.cloned.1.call-start = ((), (), s32[]{:S(2)}) async-start(), calls=%async_computation.9 | async-start | bytes 2228224 | tf_op jit(solution)/shard_map/reduce_scatter | solution.py:123
  394.1 173.0 %reduce-scatter.7.cloned.1.call-start = ((), (), s32[]{:S(2)}) async-start(), calls=%async_computation.7 | async-start | bytes 147456 | tf_op jit(solution)/shard_map/reduce_scatter | solution.py:126
  454.0 151.1 %reduce-scatter.11.cloned.1.call-start = ((), (), s32[]{:S(2)}) async-start(), calls=%async_computation.10 | async-start | bytes 147456 | tf_op jit(solution)/shard_map/reduce_scatter | solution.py:126
Sparse Core Ops, SparseCore 0:
  203.4 74.5 all-reduce.4
  280.5 48.6 all-gather.2
  331.7 48.2 all-gather.4
  384.4 69.6 reduce-scatter.4
  458.3 69.9 reduce-scatter.8
  530.6 36.4 reduce-scatter.6
  569.4 35.6 reduce-scatter.10
where the time goes:
time: 614 us; the launch traced here: 613 us
  waiting for transfers between devices  427 us (70%)
  local copies, waits for them, and re-layouts  49.5 us (8%)
  blocking collectives  42.5 us (7%)
  other arithmetic  37.6 us (6%)
  matrix products  34.4 us (6%)
  between operations  14.5 us (2%)
  starting transfers between devices  7.77 us (1%)
    reduce_scatter x2, waiting for transfers between devices, per_device(): lax.psum_scatter(partial_ffn.astype(jnp.bfloat16), 'dp', scatter_dimensio...  134 us
    all_gather x2, waiting for transfers between devices, per_device(): hidden_full = lax.all_gather(hidden_cols, 'dp', axis=1, tiled=True)  85.7 us
    reduce_scatter x2, waiting for transfers between devices, per_device(): lax.psum_scatter(rows_part, 'tensor', scatter_dimension=1, tiled=True)  76.1 us
    psum x1, waiting for transfers between devices, per_device(): lax.psum(partial_out.astype(jnp.bfloat16), 'tensor').astype(jnp.float32)  74.7 us
    all_to_all x1, waiting for transfers between devices, per_device(): lax.all_to_all(outgoing, 'dp', split_axis=1, concat_axis=1, tiled=True)  55.8 us
    all_gather x2, blocking collectives, per_device(): lax.all_gather(mixed, 'dp', axis=0, tiled=True)  42.5 us
    unnamed x21, local copies, waits for them, and re-layouts  30.5 us
    another operation x3, other arithmetic  18.8 us
  transfers between devices with their start and end apart: 8, of which 8 were waited for; matrix products, arithmetic and copies ran while one was open for 5% of the time, Pallas kernels for 0%

commit v1 on v0

v1 whole, which is shorter than its diff:
```python
import math

import jax
import jax.numpy as jnp
from jax import lax
from jax.sharding import Mesh, PartitionSpec as P

DP = ("yh", "x", "c")
CDP = ("c", "yh", "x")
TENSOR = ("z", "yl")
CHIPS = ("yh", "x", "z", "yl")


def to_all(block, axes, count):
    copies = lax.optimization_barrier(jnp.broadcast_to(block[None], (count,) + block.shape))
    return lax.all_to_all(copies, axes, 0, 0, tiled=True)


def page_plan(page_loc, lengths, placement, dev_dp, dev_tensor, n_dp, pslots, page_size):
    n_req = lengths.shape[0]
    max_pages = page_loc.shape[2]
    req_dev = n_req // n_dp
    entries = req_dev * max_pages
    capacity = pslots // n_dp
    loc_head = lax.dynamic_index_in_dim(page_loc, dev_tensor, 0, keepdims=False)
    slot_hot = placement[None, :] == jnp.arange(n_req, dtype=jnp.int32)[:, None]
    len_slot = jnp.sum(jnp.where(slot_hot, lengths[None, :], 0), axis=1)
    loc_slot = jnp.dot(
        slot_hot.astype(jnp.float32), loc_head.astype(jnp.float32), precision=lax.Precision.HIGHEST
    ).astype(jnp.int32)
    pages_slot = (len_slot + page_size - 1) // page_size
    live = jnp.arange(max_pages, dtype=jnp.int32)[None, :] < pages_slot[:, None]
    source = jnp.where(live, loc_slot // pslots, n_dp).reshape(n_dp, entries)
    row = (loc_slot % pslots).reshape(n_dp, entries)
    before = (
        jnp.arange(entries, dtype=jnp.int32)[:, None] < jnp.arange(entries, dtype=jnp.int32)[None, :]
    ).astype(jnp.bfloat16)
    mine_out = source == dev_dp
    rank_out = jnp.dot(
        mine_out.astype(jnp.bfloat16), before, preferred_element_type=jnp.float32
    ).astype(jnp.int32)
    rank_out = jnp.where(mine_out, rank_out, capacity)
    hit = rank_out[:, None, :] == jnp.arange(capacity, dtype=jnp.int32)[None, :, None]
    send_rows = jnp.sum(jnp.where(hit, row[:, None, :], 0), axis=2)
    my_source = lax.dynamic_index_in_dim(source, dev_dp, 0, keepdims=False)
    source_hot = my_source[None, :] == jnp.arange(n_dp, dtype=jnp.int32)[:, None]
    rank_in = jnp.dot(
        source_hot.astype(jnp.bfloat16), before, preferred_element_type=jnp.float32
    ).astype(jnp.int32)
    my_rank = jnp.sum(jnp.where(source_hot, rank_in, 0), axis=0)
    pick = jnp.where(my_source < n_dp, my_source * capacity + my_rank, 0)
    my_len = lax.dynamic_slice_in_dim(len_slot, dev_dp * req_dev, req_dev)
    return send_rows, pick, my_len


def per_device(
    kv_pool,
    page_loc,
    lengths,
    placement,
    queries,
    new_kv,
    resid_in,
    w_out,
    ffn_gain,
    w_gate,
    w_up,
    w_down,
):
    n_dp = lax.axis_size(DP)
    n_tensor = lax.axis_size(TENSOR)
    dev_dp = lax.axis_index(DP)
    dev_cdp = lax.axis_index(CDP)
    dev_tensor = lax.axis_index(TENSOR)
    core = lax.axis_index("c")
    pslots, _, page_size, width_two = kv_pool.shape
    head_dim = width_two // 2
    n_req = lengths.shape[0]
    req_dev = n_req // n_dp
    max_pages = page_loc.shape[2]
    max_len = max_pages * page_size
    cache_len = max_len + page_size
    n_steps = queries.shape[0]
    hq_dev = queries.shape[2]
    width = ffn_gain.shape[0]
    rows_dev = n_steps * req_dev
    rows_all = n_steps * n_req
    capacity = pslots // n_dp

    send_rows, pick, my_len = page_plan(
        page_loc, lengths, placement, dev_dp, dev_tensor, n_dp, pslots, page_size
    )
    outgoing = kv_pool[send_rows.reshape(-1), 0].reshape(n_dp, capacity, page_size, width_two)
    received = lax.all_to_all(outgoing, DP, 0, 0, tiled=True)
    arrived = received.reshape(pslots, page_size, width_two)[pick]
    tokens = arrived.reshape(req_dev, max_len, width_two)
    padded = jnp.pad(tokens, ((0, 0), (0, page_size), (0, 0)))
    positions = jnp.arange(cache_len, dtype=jnp.int32)
    cache = jnp.where(
        positions[None, :, None] < my_len[:, None, None], padded, jnp.zeros((), padded.dtype)
    )
    for step_idx in range(n_steps):
        cache = jnp.where(
            positions[None, :, None] == (my_len + step_idx)[:, None, None],
            new_kv[step_idx],
            cache,
        )
    query = jnp.transpose(queries, (1, 0, 2, 3)).reshape(req_dev, n_steps * hq_dev, head_dim)
    scores = jnp.einsum(
        "rqd,rtd->rqt", query, cache[..., :head_dim], preferred_element_type=jnp.float32
    ) * (1.0 / math.sqrt(head_dim))
    step_of = jnp.arange(n_steps * hq_dev, dtype=jnp.int32) // hq_dev
    visible = positions[None, None, :] <= my_len[:, None, None] + step_of[None, :, None]
    scores = jnp.where(visible, scores, -jnp.inf)
    peak = jnp.max(scores, axis=-1, keepdims=True)
    expo = jnp.exp(scores - peak)
    probs = (expo / jnp.sum(expo, axis=-1, keepdims=True)).astype(jnp.bfloat16)
    mixed = jnp.einsum(
        "rqt,rtd->rqd", probs, cache[..., head_dim:], preferred_element_type=jnp.float32
    ).astype(jnp.bfloat16)
    mixed = jnp.transpose(
        mixed.reshape(req_dev, n_steps, hq_dev * head_dim), (1, 0, 2)
    ).reshape(rows_dev, hq_dev * head_dim)

    mixed_all = to_all(mixed, CDP, n_dp).reshape(rows_all, hq_dev * head_dim)
    partial_out = jnp.dot(mixed_all, w_out, preferred_element_type=jnp.float32).astype(jnp.bfloat16)
    rows_blk = rows_all // n_tensor
    cols_blk = width // n_dp
    parts = lax.all_to_all(
        partial_out.reshape(n_tensor, rows_blk, cols_blk), TENSOR, 0, 0, tiled=True
    )
    resid_rows = jnp.transpose(
        resid_in.reshape(n_steps, n_dp // 2, 2, req_dev, cols_blk), (2, 1, 0, 3, 4)
    ).reshape(n_tensor, rows_blk, cols_blk)
    resid_blk = lax.dynamic_index_in_dim(resid_rows, dev_tensor, 0, keepdims=False)
    hidden_blk = (
        resid_blk.astype(jnp.float32) + jnp.sum(parts.astype(jnp.float32), axis=0)
    ).astype(jnp.bfloat16)
    chips_dp = n_dp // 2
    own_half = to_all(hidden_blk, CHIPS, chips_dp * n_tensor).reshape(chips_dp, rows_all, cols_blk)
    other_half = lax.ppermute(own_half, "c", [(0, 1), (1, 0)])
    halves = jnp.stack(
        [
            jnp.where(core == 0, own_half, other_half),
            jnp.where(core == 0, other_half, own_half),
        ],
        axis=1,
    )
    hidden = jnp.transpose(halves, (2, 0, 1, 3)).reshape(rows_all, width)
    hid_wide = hidden.astype(jnp.float32)
    inverse = lax.rsqrt(jnp.mean(hid_wide * hid_wide, axis=-1, keepdims=True) + 1e-05)
    normed = (hid_wide * inverse * ffn_gain).astype(jnp.bfloat16)
    gate = jnp.dot(normed, w_gate, preferred_element_type=jnp.float32)
    upper = jnp.dot(normed, w_up, preferred_element_type=jnp.float32)
    act = (jax.nn.silu(gate) * upper).astype(jnp.bfloat16)
    act_cores = act.reshape(2, rows_all // 2, act.shape[1])
    width_out = width // n_tensor

    def down(rows):
        return jnp.dot(rows, w_down, preferred_element_type=jnp.float32)

    theirs = down(lax.dynamic_index_in_dim(act_cores, 1 - core, 0, keepdims=False)).astype(
        jnp.bfloat16
    )
    from_core = lax.ppermute(theirs, "c", [(0, 1), (1, 0)])
    ours = down(lax.dynamic_index_in_dim(act_cores, core, 0, keepdims=False))
    chip_sum = (ours + from_core.astype(jnp.float32)).astype(jnp.bfloat16)
    chip_sum = jnp.transpose(
        chip_sum.reshape(chips_dp, rows_dev, n_tensor, width_out), (0, 2, 1, 3)
    ).reshape(chips_dp * n_tensor, rows_dev, width_out)
    pieces = lax.all_to_all(chip_sum, CHIPS, 0, 0, tiled=True)
    ffn_part = jnp.sum(pieces.astype(jnp.float32), axis=0)
    own_hidden = lax.dynamic_slice(
        hidden, (dev_cdp * rows_dev, dev_tensor * width_out), (rows_dev, width_out)
    )
    block_out = (own_hidden.astype(jnp.float32) + ffn_part).astype(jnp.bfloat16)
    return (block_out.reshape(n_steps, req_dev, width_out), cache[None])


def solution(mesh):
    fine = Mesh(mesh.devices.reshape(2, 4, 2, 4, 2), ("yh", "x", "c", "z", "yl"))
    placed = (
        P(DP, TENSOR, None, None),
        P(),
        P(),
        P(),
        P(None, DP, TENSOR, None),
        P(None, DP, TENSOR, None),
        P(None, None, DP),
        P(TENSOR, DP),
        P(),
        P(None, DP + TENSOR),
        P(None, DP + TENSOR),
        P(DP + TENSOR, None),
    )
    return jax.shard_map(
        per_device,
        mesh=fine,
        in_specs=placed,
        out_specs=(P(None, DP, TENSOR), P(TENSOR, DP, None, None)),
        check_vma=False,
    )
```

time: 614 us -> 231 us (0.38)
  waiting for transfers between devices: 427 us -> 100 us
  local copies, waits for them, and re-layouts: 49.5 us -> 27.8 us
  other arithmetic: 37.6 us -> 16.3 us
  matrix products: 34.4 us -> 15.4 us
  between operations: 14.5 us -> 0.93 us
  starting transfers between devices: 7.77 us -> 19.2 us
  blocking collectives: 42.5 us -> 50 us
    reduce_scatter x4 -> x0, waiting for transfers between devices: 210 us -> none  [the longest x2 134 us: per_device(): lax.psum_scatter(partial_ffn.astype(jnp.bfloat16), 'dp', scatter_dimensio...]
    all_gather x2 -> x0, waiting for transfers between devices: 85.7 us -> none  [per_device(): hidden_full = lax.all_gather(hidden_cols, 'dp', axis=1, tiled=True)]
    psum x1 -> x0, waiting for transfers between devices: 74.7 us -> none  [per_device(): lax.psum(partial_out.astype(jnp.bfloat16), 'tensor').astype(jnp.float32)]
    all_to_all x0 -> x2, blocking collectives: none -> 50 us  [to_all(): return lax.all_to_all(copies, axes, 0, 0, tiled=True)]
    all_gather x2 -> x0, blocking collectives: 42.5 us -> none  [per_device(): lax.all_gather(mixed, 'dp', axis=0, tiled=True)]
    all_to_all x1 -> x3, waiting for transfers between devices: 55.8 us -> 91.9 us  [the longest x1 56 us: per_device(): received = lax.all_to_all(outgoing, DP, 0, 0, tiled=True)]
    unnamed x21 -> x22, local copies, waits for them, and re-layouts: 30.5 us -> 4.22 us
    another operation x6 -> x1, other arithmetic: 20.9 us -> 1.86 us  [per_device(): jnp.stack([jnp.where(core == 0, own_half, other_half), jnp.where(core ==...]
  transfers between devices with their start and end apart: 8 -> 5, of which waited for: 8 -> 5; matrix products, arithmetic and copies ran while one was open for 5% -> 1% of each run, Pallas kernels for 0% -> 0%
where the time goes in v1:
time: 231 us; the launch traced here: 230 us
  waiting for transfers between devices  100 us (43%)
  blocking collectives  50 us (22%)
  local copies, waits for them, and re-layouts  27.8 us (12%)
  starting transfers between devices  19.2 us (8%)
  other arithmetic  16.3 us (7%)
  matrix products  15.4 us (7%)
    all_to_all x1, waiting for transfers between devices, per_device(): received = lax.all_to_all(outgoing, DP, 0, 0, tiled=True)  56 us
    all_to_all x2, blocking collectives, to_all(): return lax.all_to_all(copies, axes, 0, 0, tiled=True)  50 us
    all_to_all x1, waiting for transfers between devices, per_device(): pieces = lax.all_to_all(chip_sum, CHIPS, 0, 0, tiled=True)  28.2 us
    broadcast_in_dim x1, other arithmetic, per_device(): return (block_out.reshape(n_steps, req_dev, width_out), cache[None])  8.23 us
    all_to_all x1, waiting for transfers between devices, per_device(): lax.all_to_all(partial_out.reshape(n_tensor, rows_blk, cols_blk), TENSOR,...  7.7 us
    gather x1, local copies, waits for them, and re-layouts, per_device(): kv_pool[send_rows.reshape(-1), 0]  7.33 us
    all_to_all x1, starting transfers between devices, per_device(): received = lax.all_to_all(outgoing, DP, 0, 0, tiled=True)  7.3 us
    transpose x1, local copies, waits for them, and re-layouts, per_device(): hidden = jnp.transpose(halves, (2, 0, 1, 3)).reshape(rows_all, width)  6.45 us
  transfers between devices with their start and end apart: 5, of which 5 were waited for; matrix products, arithmetic and copies ran while one was open for 1% of the time, Pallas kernels for 0%

profile of v1, /device:TPU:0, one launch (start us, length us, event | category | flops | bytes accessed | tf_op | source)
XLA Modules:
  0.0 229.9 jit_solution(7805974309945214037)
XLA Ops:
  0.6 0.0 copy-start
  0.7 0.9 select_reduce_fusion.1
  1.5 1.0 fusion.21
  2.6 0.1 copy.53
  2.7 0.1 reshape.281
  2.7 0.2 fusion.16
  2.9 0.2 fusion.17
  3.1 0.1 copy.54
  3.2 0.1 broadcast_in_dim.141
  3.3 0.4 select_reduce_fusion
  3.7 0.1 reshape.282
  3.8 7.3 %gather_fusion = bf16[512,16,256]{2,1,0:T(8,128)(2,1)} fusion(bf16[512,1,16,256]{3,2,1,0:T(8,128)(2,1)} %param.12, s32[512]{0:T(512)S(1)} %bitcast.93), kind=kCustom, calls=%fused_computation | custom fusion | bytes 8392704 | tf_op jit(solution)/shard_map/gather | solution.py:93
  11.1 7.3 %all-to-all-start = ((bf16[16,32,16,256]{3,2,1,0:T(8,128)(2,1)}), bf16[16,32,16,256]{3,2,1,0:T(8,128)(2,1)}, u32[]{:S(2)}, u32[]{:S(2)}) async-start(bf16[16,32,16,256]{3,2,1,0:T(8,128)(2,1)} %bitcast.95), calls=%async_computation | async-start | bytes 8388608 | tf_op jit(solution)/shard_map/all_to_all | solution.py:94
  18.4 0.1 broadcast_add_fusion.1
  18.5 0.1 broadcast_add_fusion
  18.6 0.0 copy-done.6
  18.6 0.1 iota_compare_fusion.9
  18.7 0.1 iota_compare_fusion.8
  18.8 56.0 %all-to-all-done = bf16[16,32,16,256]{3,2,1,0:T(8,128)(2,1)} async-done(((bf16[16,32,16,256]{3,2,1,0:T(8,128)(2,1)}), bf16[16,32,16,256]{3,2,1,0:T(8,128)(2,1)}, u32[]{:S(2)}, u32[]{:S(2)}) %all-to-all-start) | async-done | bytes 4194336 | tf_op jit(solution)/shard_map/all_to_all | solution.py:94
  74.8 5.1 %gather_fusion.1 = bf16[512,16,256]{2,1,0:T(8,128)(2,1)} fusion(bf16[512,16,256]{2,1,0:T(8,128)(2,1)} %bitcast.8, s32[1024]{0:T(1024)S(1)} %pad_clamp_fusion), kind=kCustom, calls=%fused_computation.1 | custom fusion | bytes 8390656 | tf_op jit(solution)/shard_map/gather | solution.py:95
  79.9 8.2 %fusion.39 = (bf16[1,8,1040,256]{3,2,1,0:T(8,128)(2,1)}, bf16[8,1040,256]{2,1,0:T(8,128)(2,1)S(1)}) fusion(bf16[8,1024,256]{2,1,0:T(8,128)(2,1)} %bitcast.94, pred[8,1040]{1,0:T(8,128)(4,1)S(1)} %get-tuple-element.17, bf16[8,256]{1,0:T(8,128)(2,1)S(1)} %get-tuple-element.15, pred[8,1040]{1,0:T(8,128)(4,1)S(1)} %get-tuple-element.16, ...), kind=kLoop, calls=%fused_computation.98 | loop fusion | flops 6389760 | bytes 12747136 | tf_op jit(solution)/shard_map/broadcast_in_dim | solution.py:177
  88.2 2.0 copy-done.4
  90.1 0.0 copy-done.8
  90.1 0.7 fusion.4
  90.8 0.2 fusion.40
  91.0 0.0 copy-start.5
  91.0 2.1 fusion.12
  93.2 0.1 broadcast_in_dim.148
  93.3 18.1 %all_to_all.25 = bf16[16,16,1024]{2,1,0:T(8,128)(2,1)S(1)} all-to-all(bf16[16,16,1024]{2,1,0:T(8,128)(2,1)S(1)} %broadcast_in_dim.148), channel_id=1, replica_groups=mesh['yh'=2,'x'=4,'c'=2,'z'=4,'yl'=2] {'c','yh','x'}, dimensions={0} | all-to-all | bytes 1048576 | tf_op jit(solution)/shard_map/all_to_all | solution.py:16
  111.4 0.0 copy-done
  111.4 1.1 convolution_convert_fusion.1
  112.5 5.4 %all-to-all-start.2 = ((bf16[8,32,512]{2,1,0:T(8,128)(2,1)}), bf16[8,32,512]{2,1,0:T(8,128)(2,1)S(1)}, u32[]{:S(2)}, u32[]{:S(2)}) async-start(bf16[8,32,512]{2,1,0:T(8,128)(2,1)} %bitcast.21), calls=%async_computation.2 | async-start | bytes 524288 | tf_op jit(solution)/shard_map/all_to_all | solution.py:129
  118.0 0.0 copy-done.5
  118.0 7.7 %all-to-all-done.2 = bf16[8,32,512]{2,1,0:T(8,128)(2,1)S(1)} async-done(((bf16[8,32,512]{2,1,0:T(8,128)(2,1)}), bf16[8,32,512]{2,1,0:T(8,128)(2,1)S(1)}, u32[]{:S(2)}, u32[]{:S(2)}) %all-to-all-start.2) | async-done | bytes 262176 | tf_op jit(solution)/shard_map/all_to_all | solution.py:129
  125.8 0.2 broadcast_in_dim.150
  126.0 31.9 %all_to_all.26 = bf16[64,32,512]{2,1,0:T(8,128)(2,1)S(1)} all-to-all(bf16[64,32,512]{2,1,0:T(8,128)(2,1)S(1)} %broadcast_in_dim.150), channel_id=1, replica_groups=mesh['yh'=2,'x'=4,'c'=2,'z'=4,'yl'=2] {'yh','x','z','yl'}, dimensions={0} | all-to-all | bytes 4194304 | tf_op jit(solution)/shard_map/all_to_all | solution.py:16
  157.9 0.0 collective-permute-start
  157.9 4.3 %collective-permute-done = bf16[8,256,512]{2,1,0:T(8,128)(2,1)} collective-permute-done((bf16[8,256,512]{2,1,0:T(8,128)(2,1)S(1)}, bf16[8,256,512]{2,1,0:T(8,128)(2,1)}, u32[]{:S(2)}, u32[]{:S(2)}) %collective-permute-start) | collective-permute-done | bytes 2097184 | tf_op jit(solution)/shard_map/ppermute | solution.py:141
  162.2 1.9 select_bitcast_fusion.1
  164.1 1.0 multiply_reduce_fusion
  165.0 2.3 %maximum_bitcast_fusion = bf16[256,8,2,512]{3,0,1,2:T(8,128)(2,1)} fusion(bf16[8,1,256,512]{3,2,0,1:T(8,128)(2,1)S(1)} %get-tuple-element.9, bf16[8,1,256,512]{3,2,0,1:T(8,128)(2,1)S(1)} %get-tuple-element.8), kind=kLoop, calls=%fused_computation.7 | loop fusion | flops 2097152 | bytes 8388608 | tf_op jit(solution)/shard_map/transpose | solution.py:149
  167.4 6.5 %copy.57 = bf16[256,8,2,512]{0,3,2,1:T(8,128)(2,1)} copy(bf16[256,8,2,512]{3,0,1,2:T(8,128)(2,1)} %maximum_bitcast_fusion) | data formatting | bytes 8388608 | tf_op jit(solution)/shard_map/transpose | solution.py:149
  173.8 0.0 copy-done.9
  173.8 4.9 %fusion.8 = f32[256,224]{0,1:T(8,128)S(1)} fusion(bf16[8192,224]{0,1:T(8,128)(2,1)} %param.21, bf16[256,8192]{0,1:T(8,128)(2,1)} %bitcast.101, f32[8192]{0:T(1024)S(1)} %copy-done.9, f32[256]{0:T(256)S(1)} %add_rsqrt_fusion), kind=kOutput, calls=%fused_computation.21 | convolution fusion | flops 947912704 | bytes 8127488 | tf_op jit(solution)/shard_map/dot_general | solution.py:153
  178.8 0.0 copy-done.3
  178.8 0.7 copy-done.7
  179.5 1.5 fusion.11
  181.0 0.0 copy-start.2
  181.0 0.2 constant_dynamic-slice_fusion.2
  181.3 2.9 %convolution_convert_fusion = bf16[128,8192]{1,0:T(8,128)(2,1)S(1)} fusion(bf16[224,8192]{1,0:T(8,128)(2,1)} %param.23, bf16[1,128,224]{1,0,2:T(2,128)(2,1)S(1)} %get-tuple-element.11), kind=kOutput, calls=%fused_computation.3 | convolution fusion | flops 470810624 | bytes 5824512 | tf_op jit(solution)/shard_map/dot_general | solution.py:160
  184.2 0.4 collective-permute-start.1
  184.6 4.0 %collective-permute-done.1 = bf16[128,8192]{1,0:T(8,128)(2,1)S(1)} collective-permute-done((bf16[128,8192]{1,0:T(8,128)(2,1)S(1)}, bf16[128,8192]{1,0:T(8,128)(2,1)S(1)}, u32[]{:S(2)}, u32[]{:S(2)}) %collective-permute-start.1) | collective-permute-done | bytes 2097184 | tf_op jit(solution)/shard_map/ppermute | solution.py:165
  188.7 0.0 copy-done.2
  188.7 0.7 add_convert_fusion
  189.4 1.4 copy.65
  190.8 0.0 copy-start.1
  190.8 2.5 %copy.61 = bf16[8,16,8,1024]{3,1,2,0:T(8,128)(2,1)} copy(bf16[8,16,8,1024]{3,2,1,0:T(8,128)(2,1)S(1)} %bitcast.98) | data formatting | bytes 4194304 | tf_op jit(solution)/shard_map/reshape | solution.py:169
  193.4 6.1 %all-to-all-start.4 = ((bf16[64,16,1024]{2,1,0:T(8,128)(2,1)}), bf16[64,16,1024]{2,1,0:T(8,128)(2,1)S(1)}, u32[]{:S(2)}, u32[]{:S(2)}) async-start(bf16[64,16,1024]{2,1,0:T(8,128)(2,1)} %bitcast.97), calls=%async_computation.4 | async-start | bytes 4194304 | tf_op jit(solution)/shard_map/all_to_all | solution.py:171
  199.5 1.1 dynamic_slice.29
  200.6 0.1 copy.62
  200.7 28.2 %all-to-all-done.4 = bf16[64,16,1024]{2,1,0:T(8,128)(2,1)S(1)} async-done(((bf16[64,16,1024]{2,1,0:T(8,128)(2,1)}), bf16[64,16,1024]{2,1,0:T(8,128)(2,1)S(1)}, u32[]{:S(2)}, u32[]{:S(2)}) %all-to-all-start.4) | async-done | bytes 2097184 | tf_op jit(solution)/shard_map/all_to_all | solution.py:171
  228.9 0.4 convert_reduce_fusion
  229.3 0.6 fusion.22
  229.9 0.0 copy-done.1
  (19 shorter events, 0.2 us)
Async XLA Ops:
  0.6 110.8 %copy-start = (bf16[1024,512]{1,0:T(8,128)(2,1)S(1)}, bf16[1024,512]{1,0:T(8,128)(2,1)}, u32[]{:S(2)}) copy-start(bf16[1024,512]{1,0:T(8,128)(2,1)} %param.19) | copy-start | bytes 3145732
  11.1 7.5 %copy-start.6 = (bf16[2,8,1,256]{3,1,2,0:T(8,128)(2,1)S(1)}, bf16[2,8,1,256]{3,1,2,0:T(8,128)(2,1)}, u32[]{:S(2)}) copy-start(bf16[2,8,1,256]{3,1,2,0:T(8,128)(2,1)} %param.17) | copy-start | bytes 24580
  11.1 63.7 %all-to-all-start = ((bf16[16,32,16,256]{3,2,1,0:T(8,128)(2,1)}), bf16[16,32,16,256]{3,2,1,0:T(8,128)(2,1)}, u32[]{:S(2)}, u32[]{:S(2)}) async-start(bf16[16,32,16,256]{3,2,1,0:T(8,128)(2,1)} %bitcast.95), calls=%async_computation | async-start | bytes 8388608 | tf_op jit(solution)/shard_map/all_to_all | solution.py:94
  79.9 10.2 %copy-start.8 = (bf16[2,8,8,128]{3,2,1,0:T(8,128)(2,1)S(1)}, bf16[2,8,8,128]{3,2,1,0:T(8,128)(2,1)}, u32[]{:S(2)}) copy-start(bf16[2,8,8,128]{3,2,1,0:T(8,128)(2,1)} %param.16) | copy-start | bytes 98308
  88.1 2.0 copy-start.4
  91.0 26.9 %copy-start.5 = (bf16[2,128,512]{2,1,0:T(8,128)(2,1)S(1)}, bf16[2,128,512]{2,1,0:T(8,128)(2,1)}, u32[]{:S(2)}) copy-start(bf16[2,128,512]{2,1,0:T(8,128)(2,1)} %param.18) | copy-start | bytes 786436
  112.5 13.2 %all-to-all-start.2 = ((bf16[8,32,512]{2,1,0:T(8,128)(2,1)}), bf16[8,32,512]{2,1,0:T(8,128)(2,1)S(1)}, u32[]{:S(2)}, u32[]{:S(2)}) async-start(bf16[8,32,512]{2,1,0:T(8,128)(2,1)} %bitcast.21), calls=%async_computation.2 | async-start | bytes 524288 | tf_op jit(solution)/shard_map/all_to_all | solution.py:129
  157.9 4.3 %collective-permute-start = (bf16[8,256,512]{2,1,0:T(8,128)(2,1)S(1)}, bf16[8,256,512]{2,1,0:T(8,128)(2,1)}, u32[]{:S(2)}, u32[]{:S(2)}) collective-permute-start(bf16[8,256,512]{2,1,0:T(8,128)(2,1)S(1)} %bitcast.99), channel_id=1, source_target_pairs={{0,8},{8,0},{1,9},{9,1},{2,10},{10,2},{3,11},{11,3},{4,12},{12,4},... | collective-permute-start | bytes 6291464 | tf_op jit(solution)/shard_map/ppermute | solution.py:141
  167.4 6.5 %copy-start.9 = (f32[8192]{0:T(1024)S(1)}, f32[8192]{0:T(1024)}, u32[]{:S(2)}) copy-start(f32[8192]{0:T(1024)} %param.20) | copy-start | bytes 98308
  173.8 4.9 %copy-start.3 = (bf16[256,8,2,512]{0,3,2,1:T(8,128)(2,1)S(1)}, bf16[256,8,2,512]{0,3,2,1:T(8,128)(2,1)}, u32[]{:S(2)}) copy-start(bf16[256,8,2,512]{0,3,2,1:T(8,128)(2,1)} %copy.57) | copy-start | bytes 12582916
  173.8 5.6 %copy-start.7 = (bf16[8192,224]{0,1:T(8,128)(2,1)S(1)}, bf16[8192,224]{0,1:T(8,128)(2,1)}, u32[]{:S(2)}) copy-start(bf16[8192,224]{0,1:T(8,128)(2,1)} %param.22) | copy-start | bytes 11010052
  181.0 7.6 %copy-start.2 = (bf16[224,8192]{1,0:T(8,128)(2,1)S(1)}, bf16[224,8192]{1,0:T(8,128)(2,1)}, u32[]{:S(2)}) copy-start(bf16[224,8192]{1,0:T(8,128)(2,1)} %param.23) | copy-start | bytes 11010052
  184.2 4.4 %collective-permute-start.1 = (bf16[128,8192]{1,0:T(8,128)(2,1)S(1)}, bf16[128,8192]{1,0:T(8,128)(2,1)S(1)}, u32[]{:S(2)}, u32[]{:S(2)}) collective-permute-start(bf16[128,8192]{1,0:T(8,128)(2,1)S(1)} %convolution_convert_fusion), channel_id=1, source_target_pairs={{0,8},{8,0},{1,9},{9,1},{2,10},{10,2},{3,11},{11,3},{4,12},{12,4},... | collective-permute-start | bytes 6291464 | tf_op jit(solution)/shard_map/ppermute | solution.py:165
  190.8 39.1 %copy-start.1 = (bf16[1024,512]{1,0:T(8,128)(2,1)S(1)}, bf16[1024,512]{1,0:T(8,128)(2,1)}, u32[]{:S(2)}) copy-start(bf16[1024,512]{1,0:T(8,128)(2,1)} %param.19) | copy-start | bytes 3145732
  193.4 35.5 %all-to-all-start.4 = ((bf16[64,16,1024]{2,1,0:T(8,128)(2,1)}), bf16[64,16,1024]{2,1,0:T(8,128)(2,1)S(1)}, u32[]{:S(2)}, u32[]{:S(2)}) async-start(bf16[64,16,1024]{2,1,0:T(8,128)(2,1)} %bitcast.97), calls=%async_computation.4 | async-start | bytes 4194304 | tf_op jit(solution)/shard_map/all_to_all | solution.py:171

commit v2 on v1

--- a/solution.py
+++ b/solution.py
@@ -3,6 +3,8 @@
 import jax
 import jax.numpy as jnp
 from jax import lax
+from jax.experimental import pallas as pl
+from jax.experimental.pallas import tpu as pltpu
 from jax.sharding import Mesh, PartitionSpec as P
 
 DP = ("yh", "x", "c")
@@ -14,6 +16,271 @@
 def to_all(block, axes, count):
     copies = lax.optimization_barrier(jnp.broadcast_to(block[None], (count,) + block.shape))
     return lax.all_to_all(copies, axes, 0, 0, tiled=True)
+
+VMEM_LIMIT = 48 * 1024 * 1024
+
+
+def intake(pick, lens, received, fresh, query, n_copies):
+    req_dev, n_rows, head_dim = query.shape
+    n_steps = fresh.shape[0]
+    _, page_size, width_two = received.shape
+    max_pages = pick.shape[0] // req_dev
+    pages = max_pages + 1
+    group = n_rows // n_steps
+    scale = 1.0 / math.sqrt(head_dim)
+    ahead = 2
+
+    def kernel(pick_ref, len_ref, recv_ref, fresh_ref, q_ref, cache_ref, mixed_ref, buf, heads, in_sems, out_sems):
+        def start(r):
+            def body(p, carry):
+                pltpu.make_async_copy(
+                    recv_ref.at[pick_ref[r * max_pages + p]], buf.at[r, p], in_sems.at[r]
+                ).start()
+                return carry
+
+            lax.fori_loop(0, max_pages, body, 0, unroll=8)
+
+        def copy_out(r):
+            return pltpu.make_async_copy(buf.at[r], cache_ref.at[r], out_sems.at[r])
+
+        for r in range(ahead):
+            start(r)
+        row_at = lax.broadcasted_iota(jnp.int32, (page_size, width_two), 0)
+        for r in range(req_dev):
+            if r + ahead < req_dev:
+                start(r + ahead)
+            pltpu.make_async_copy(
+                recv_ref.at[pl.ds(0, max_pages)], buf.at[r, pl.ds(0, max_pages)], in_sems.at[r]
+            ).wait()
+            length = len_ref[r]
+            full = length // page_size
+
+            def clear(p, carry):
+                buf[r, p] = jnp.zeros((page_size, width_two), buf.dtype)
+                return carry
+
+            lax.fori_loop(full + 1, pages, clear, 0)
+            edge = buf[r, full].astype(jnp.float32)
+            buf[r, full] = jnp.where(row_at < length % page_size, edge, 0.0).astype(buf.dtype)
+            for s in range(n_steps):
+                at = length + s
+                page = buf[r, at // page_size].astype(jnp.float32)
+                token = fresh_ref[s, r : r + 1, :]
+                buf[r, at // page_size] = jnp.where(
+                    row_at == at % page_size, token, page
+                ).astype(buf.dtype)
+            copy_out(r).start()
+            tokens = buf[r].reshape(pages * page_size, width_two)
+            scores = scale * lax.dot_general(
+                q_ref[r],
+                tokens[:, :head_dim],
+                (((1,), (1,)), ((), ())),
+                preferred_element_type=jnp.float32,
+            )
+            last = length + lax.broadcasted_iota(jnp.int32, scores.shape, 0) // group
+            scores = jnp.where(
+                lax.broadcasted_iota(jnp.int32, scores.shape, 1) <= last, scores, -jnp.inf
+            )
+            expo = jnp.exp(scores - jnp.max(scores, axis=1, keepdims=True))
+            total = jnp.sum(expo, axis=1, keepdims=True)
+            probs = (expo / total).astype(jnp.bfloat16)
+            head_out = jnp.dot(probs, tokens[:, head_dim:], preferred_element_type=jnp.float32)
+            for i in range(n_rows):
+                heads[i, r : r + 1, :] = head_out[i : i + 1, :]
+        for g in range(group):
+            block = jnp.concatenate([heads[s * group + g] for s in range(n_steps)], axis=0)
+            block = block.astype(mixed_ref.dtype)
+            for k in range(n_copies):
+                mixed_ref[k, :, g * head_dim : (g + 1) * head_dim] = block
+        for r in range(req_dev):
+            copy_out(r).wait()
+
+    smem = pl.BlockSpec(memory_space=pltpu.SMEM)
+    vmem = pl.BlockSpec(memory_space=pltpu.VMEM)
+    hbm = pl.BlockSpec(memory_space=pl.ANY)
+    return pl.pallas_call(
+        kernel,
+        in_specs=[smem, smem, hbm, vmem, vmem],
+        out_specs=[hbm, vmem],
+        out_shape=[
+            jax.ShapeDtypeStruct((req_dev, pages, page_size, width_two), received.dtype),
+            jax.ShapeDtypeStruct(
+                (n_copies, n_steps * req_dev, group * head_dim), received.dtype
+            ),
+        ],
+        scratch_shapes=[
+            pltpu.VMEM((req_dev, pages, page_size, width_two), received.dtype),
+            pltpu.VMEM((n_rows, req_dev, head_dim), jnp.float32),
+            pltpu.SemaphoreType.DMA((req_dev,)),
+            pltpu.SemaphoreType.DMA((req_dev,)),
+        ],
+        compiler_params=pltpu.CompilerParams(vmem_limit_bytes=VMEM_LIMIT),
+        name="intake",
+    )(pick, lens, received, fresh, query)
+
+
+def expand_step(x_ref, gate_ref, up_ref, gain_ref, gate_sum, up_sum, squares):
+    wide = x_ref[0].astype(jnp.float32)
+    lanes = squares.shape[1]
+    square = wide * wide
+    squares[...] += sum(
+        square[:, k * lanes : (k + 1) * lanes] for k in range(square.shape[1] // lanes)
+    )
+    scaled = (wide * gain_ref[...]).astype(jnp.bfloat16)
+    contract = (((1,), (1,)), ((), ()))
+    gate_sum[...] += lax.dot_general(
+        scaled, gate_ref[...], contract, preferred_element_type=jnp.float32
+    )
+    up_sum[...] += lax.dot_general(
+        scaled, up_ref[...], contract, preferred_element_type=jnp.float32
+    )
+
+
+def expand_own(core_at, own_half, gate_rows, up_rows, gain_row):
+    steps, rows, cols = own_half.shape
+    units = gate_rows.shape[0]
+
+    def kernel(core_ref, x_ref, gate_ref, up_ref, gain_ref, gate_sum, up_sum, squares):
+        @pl.when(pl.program_id(0) == 0)
+        def _():
+            gate_sum[...] = jnp.zeros_like(gate_sum)
+            up_sum[...] = jnp.zeros_like(up_sum)
+            squares[...] = jnp.zeros_like(squares)
+
+        expand_step(x_ref, gate_ref, up_ref, gain_ref, gate_sum, up_sum, squares)
+
+    weight = pl.BlockSpec((units, cols), lambda i, core: (0, 2 * i + core[0]))
+    return pl.pallas_call(
+        kernel,
+        grid_spec=pltpu.PrefetchScalarGridSpec(
+            num_scalar_prefetch=1,
+            grid=(steps,),
+            in_specs=[
+                pl.BlockSpec((1, rows, cols), lambda i, core: (i, 0, 0)),
+                weight,
+                weight,
+                pl.BlockSpec((1, cols), lambda i, core: (0, 2 * i + core[0])),
+            ],
+            out_specs=[
+                pl.BlockSpec((rows, units), lambda i, core: (0, 0)),
+                pl.BlockSpec((rows, units), lambda i, core: (0, 0)),
+                pl.BlockSpec((rows, 128), lambda i, core: (0, 0)),
+            ],
+        ),
+        out_shape=[
+            jax.ShapeDtypeStruct((rows, units), jnp.float32),
+            jax.ShapeDtypeStruct((rows, units), jnp.float32),
+            jax.ShapeDtypeStruct((rows, 128), jnp.float32),
+        ],
+        compiler_params=pltpu.CompilerParams(vmem_limit_bytes=VMEM_LIMIT),
+        name="expand_own",
+    )(core_at, own_half, gate_rows, up_rows, gain_row)
+
+
+def expand_other(core_at, other_half, gate_rows, up_rows, gain_row, sums, w_down, n_tensor, rows_dev):
+    steps, rows, cols = other_half.shape
+    units, width = w_down.shape
+    cols_out = width // n_tensor
+    half_rows = rows // 2
+    chips = half_rows // rows_dev
+
+    def kernel(
+        core_ref, x_ref, gate_ref, up_ref, gain_ref, gate_in, up_in, squares_in, down_ref,
+        act_ref, theirs_ref, gate_sum, up_sum, squares,
+    ):
+        step = pl.program_id(0)
+
+        @pl.when(step == 0)
+        def _():
+            gate_sum[...] = gate_in[...]
+            up_sum[...] = up_in[...]
+            squares[...] = squares_in[...]
+
+        @pl.when(step < steps)
+        def _():
+            expand_step(x_ref, gate_ref, up_ref, gain_ref, gate_sum, up_sum, squares)
+
+        @pl.when(step == steps - 1)
+        def _():
+            mean = jnp.sum(squares[...], axis=1, keepdims=True) * (1.0 / width)
+            inverse = lax.rsqrt(mean + 1e-05)
+            gate = gate_sum[...] * inverse
+            act = gate / (1.0 + jnp.exp(-gate)) * (up_sum[...] * inverse)
+            act_ref[...] = act.astype(act_ref.dtype).reshape(2, half_rows, units)
+
+        @pl.when(step >= steps)
+        def _():
+            out = jnp.dot(
+                act_ref[1 - core_ref[0]], down_ref[...], preferred_element_type=jnp.float32
+            )
+            theirs_ref[...] = out.astype(theirs_ref.dtype).reshape(chips, 1, rows_dev, cols_out)
+
+    def into(i):
+        return jnp.minimum(i, steps - 1)
+
+    def out_of(i):
+        return jnp.maximum(i - steps, 0)
+
+    weight = pl.BlockSpec((units, cols), lambda i, core: (0, 2 * into(i) + 1 - core[0]))
+    whole = pl.BlockSpec((rows, units), lambda i, core: (0, 0))
+    return pl.pallas_call(
+        kernel,
+        grid_spec=pltpu.PrefetchScalarGridSpec(
+            num_scalar_prefetch=1,
+            grid=(steps + n_tensor,),
+            in_specs=[
+                pl.BlockSpec((1, rows, cols), lambda i, core: (into(i), 0, 0)),
+                weight,
+                weight,
+                pl.BlockSpec((1, cols), lambda i, core: (0, 2 * into(i) + 1 - core[0])),
+                whole,
+                whole,
+                pl.BlockSpec((rows, 128), lambda i, core: (0, 0)),
+                pl.BlockSpec((units, cols_out), lambda i, core: (0, out_of(i))),
+            ],
+            out_specs=[
+                pl.BlockSpec((2, half_rows, units), lambda i, core: (0, 0, 0)),
+                pl.BlockSpec((chips, 1, rows_dev, cols_out), lambda i, core: (0, out_of(i), 0, 0)),
+            ],
+            scratch_shapes=[
+                pltpu.VMEM((rows, units), jnp.float32),
+                pltpu.VMEM((rows, units), jnp.float32),
+                pltpu.VMEM((rows, 128), jnp.float32),
+            ],
+        ),
+        out_shape=[
+            jax.ShapeDtypeStruct((2, half_rows, units), jnp.bfloat16),
+            jax.ShapeDtypeStruct((chips, n_tensor, rows_dev, cols_out), jnp.bfloat16),
+        ],
+        compiler_params=pltpu.CompilerParams(vmem_limit_bytes=VMEM_LIMIT),
+        name="expand_other",
+    )(core_at, other_half, gate_rows, up_rows, gain_row, *sums, w_down)
+
+
+def shrink_own(core_at, act, w_down, n_tensor, rows_dev):
+    _, half_rows, units = act.shape
+    cols_out = w_down.shape[1] // n_tensor
+    chips = half_rows // rows_dev
+
+    def kernel(core_ref, act_ref, down_ref, ours_ref):
+        out = jnp.dot(act_ref[0], down_ref[...], preferred_element_type=jnp.float32)
+        ours_ref[...] = out.astype(ours_ref.dtype).reshape(chips, 1, rows_dev, cols_out)
+
+    return pl.pallas_call(
+        kernel,
+        grid_spec=pltpu.PrefetchScalarGridSpec(
+            num_scalar_prefetch=1,
+            grid=(n_tensor,),
+            in_specs=[
+                pl.BlockSpec((1, half_rows, units), lambda i, core: (core[0], 0, 0)),
+                pl.BlockSpec((units, cols_out), lambda i, core: (0, i)),
+            ],
+            out_specs=pl.BlockSpec((chips, 1, rows_dev, cols_out), lambda i, core: (0, i, 0, 0)),
+        ),
+        out_shape=jax.ShapeDtypeStruct((chips, n_tensor, rows_dev, cols_out), jnp.bfloat16),
+        compiler_params=pltpu.CompilerParams(vmem_limit_bytes=VMEM_LIMIT),
+        name="shrink_own",
+    )(core_at, act, w_down)
 
 
 def page_plan(page_loc, lengths, placement, dev_dp, dev_tensor, n_dp, pslots, page_size):
@@ -92,37 +359,19 @@
     )
     outgoing = kv_pool[send_rows.reshape(-1), 0].reshape(n_dp, capacity, page_size, width_two)
     received = lax.all_to_all(outgoing, DP, 0, 0, tiled=True)
-    arrived = received.reshape(pslots, page_size, width_two)[pick]
-    tokens = arrived.reshape(req_dev, max_len, width_two)
-    padded = jnp.pad(tokens, ((0, 0), (0, page_size), (0, 0)))
-    positions = jnp.arange(cache_len, dtype=jnp.int32)
-    cache = jnp.where(
-        positions[None, :, None] < my_len[:, None, None], padded, jnp.zeros((), padded.dtype)
-    )
-    for step_idx in range(n_steps):
-        cache = jnp.where(
-            positions[None, :, None] == (my_len + step_idx)[:, None, None],
-            new_kv[step_idx],
-            cache,
-        )
     query = jnp.transpose(queries, (1, 0, 2, 3)).reshape(req_dev, n_steps * hq_dev, head_dim)
-    scores = jnp.einsum(
-        "rqd,rtd->rqt", query, cache[..., :head_dim], preferred_element_type=jnp.float32
-    ) * (1.0 / math.sqrt(head_dim))
-    step_of = jnp.arange(n_steps * hq_dev, dtype=jnp.int32) // hq_dev
-    visible = positions[None, None, :] <= my_len[:, None, None] + step_of[None, :, None]
-    scores = jnp.where(visible, scores, -jnp.inf)
-    peak = jnp.max(scores, axis=-1, keepdims=True)
-    expo = jnp.exp(scores - peak)
-    probs = (expo / jnp.sum(expo, axis=-1, keepdims=True)).astype(jnp.bfloat16)
-    mixed = jnp.einsum(
-        "rqt,rtd->rqd", probs, cache[..., head_dim:], preferred_element_type=jnp.float32
-    ).astype(jnp.bfloat16)
-    mixed = jnp.transpose(
-        mixed.reshape(req_dev, n_steps, hq_dev * head_dim), (1, 0, 2)
-    ).reshape(rows_dev, hq_dev * head_dim)
-
-    mixed_all = to_all(mixed, CDP, n_dp).reshape(rows_all, hq_dev * head_dim)
+    cache, mixed_copies = intake(
+        pick,
+        my_len,
+        received.reshape(pslots, page_size, width_two),
+        new_kv.reshape(n_steps, req_dev, width_two).astype(jnp.float32),
+        query,
+        n_dp,
+    )
+
+    mixed_all = lax.all_to_all(mixed_copies, CDP, 0, 0, tiled=True).reshape(
+        rows_all, hq_dev * head_dim
+    )
     partial_out = jnp.dot(mixed_all, w_out, preferred_element_type=jnp.float32).astype(jnp.bfloat16)
     rows_blk = rows_all // n_tensor
     cols_blk = width // n_dp
@@ -139,42 +388,36 @@
     chips_dp = n_dp // 2
     own_half = to_all(hidden_blk, CHIPS, chips_dp * n_tensor).reshape(chips_dp, rows_all, cols_blk)
     other_half = lax.ppermute(own_half, "c", [(0, 1), (1, 0)])
-    halves = jnp.stack(
-        [
-            jnp.where(core == 0, own_half, other_half),
-            jnp.where(core == 0, other_half, own_half),
-        ],
-        axis=1,
-    )
-    hidden = jnp.transpose(halves, (2, 0, 1, 3)).reshape(rows_all, width)
-    hid_wide = hidden.astype(jnp.float32)
-    inverse = lax.rsqrt(jnp.mean(hid_wide * hid_wide, axis=-1, keepdims=True) + 1e-05)
-    normed = (hid_wide * inverse * ffn_gain).astype(jnp.bfloat16)
-    gate = jnp.dot(normed, w_gate, preferred_element_type=jnp.float32)
-    upper = jnp.dot(normed, w_up, preferred_element_type=jnp.float32)
-    act = (jax.nn.silu(gate) * upper).astype(jnp.bfloat16)
-    act_cores = act.reshape(2, rows_all // 2, act.shape[1])
+    core_at = core.reshape(1).astype(jnp.int32)
+    gate_rows = jnp.swapaxes(w_gate, 0, 1)
+    up_rows = jnp.swapaxes(w_up, 0, 1)
+    gain_row = ffn_gain.reshape(1, width)
     width_out = width // n_tensor
-
-    def down(rows):
-        return jnp.dot(rows, w_down, preferred_element_type=jnp.float32)
-
-    theirs = down(lax.dynamic_index_in_dim(act_cores, 1 - core, 0, keepdims=False)).astype(
-        jnp.bfloat16
+    sums = expand_own(core_at, own_half, gate_rows, up_rows, gain_row)
+    act, theirs = expand_other(
+        core_at, other_half, gate_rows, up_rows, gain_row, sums, w_down, n_tensor, rows_dev
     )
     from_core = lax.ppermute(theirs, "c", [(0, 1), (1, 0)])
-    ours = down(lax.dynamic_index_in_dim(act_cores, core, 0, keepdims=False))
-    chip_sum = (ours + from_core.astype(jnp.float32)).astype(jnp.bfloat16)
-    chip_sum = jnp.transpose(
-        chip_sum.reshape(chips_dp, rows_dev, n_tensor, width_out), (0, 2, 1, 3)
-    ).reshape(chips_dp * n_tensor, rows_dev, width_out)
+    ours = shrink_own(core_at, act, w_down, n_tensor, rows_dev)
+    chip_sum = (
+        (ours.astype(jnp.float32) + from_core.astype(jnp.float32))
+        .astype(jnp.bfloat16)
+        .reshape(chips_dp * n_tensor, rows_dev, width_out)
+    )
     pieces = lax.all_to_all(chip_sum, CHIPS, 0, 0, tiled=True)
     ffn_part = jnp.sum(pieces.astype(jnp.float32), axis=0)
-    own_hidden = lax.dynamic_slice(
-        hidden, (dev_cdp * rows_dev, dev_tensor * width_out), (rows_dev, width_out)
+
+    def own_cols(half):
+        return lax.dynamic_slice(
+            half, (dev_tensor, dev_cdp * rows_dev, 0), (1, rows_dev, cols_blk)
+        )[0]
+
+    mine, partners = own_cols(own_half), own_cols(other_half)
+    own_hidden = jnp.concatenate(
+        [jnp.where(core == 0, mine, partners), jnp.where(core == 0, partners, mine)], axis=1
     )
     block_out = (own_hidden.astype(jnp.float32) + ffn_part).astype(jnp.bfloat16)
-    return (block_out.reshape(n_steps, req_dev, width_out), cache[None])
+    return (block_out.reshape(n_steps, req_dev, width_out), cache.reshape(1, req_dev, cache_len, width_two))
 
 
 def solution(mesh):

time: 231 us -> 216 us (0.935)
  Pallas kernels: 0 us -> 32.4 us
  local copies, waits for them, and re-layouts: 27.8 us -> 8.13 us
  matrix products: 15.4 us -> 2.55 us
  other arithmetic: 16.3 us -> 7.05 us
  waiting for transfers between devices: 100 us -> 94.1 us
    pallas_call x0 -> x4, Pallas kernels: none -> 32.4 us  [the longest x1 12.7 us: expand_other(): pl.pallas_call(kernel, grid_spec=pltpu.PrefetchScalarGridSpec(num_scalar_...]
    all_to_all x2 -> x1, blocking collectives: 50 us -> 31.9 us  [to_all(): return lax.all_to_all(copies, axes, 0, 0, tiled=True)]
    all_to_all x0 -> x1, blocking collectives: none -> 17.9 us  [per_device(): lax.all_to_all(mixed_copies, CDP, 0, 0, tiled=True)]
    dot_general x6 -> x0, matrix products: 12.9 us -> none  [the longest x1 4.9 us: per_device(): gate = jnp.dot(normed, w_gate, preferred_element_type=jnp.float32)]
    broadcast_in_dim x1 -> x0, other arithmetic: 8.23 us -> none  [per_device(): return (block_out.reshape(n_steps, req_dev, width_out), cache[None])]
    transpose x1 -> x0, local copies, waits for them, and re-layouts: 6.45 us -> none  [per_device(): hidden = jnp.transpose(halves, (2, 0, 1, 3)).reshape(rows_all, width)]
    gather x1 -> x0, local copies, waits for them, and re-layouts: 5.13 us -> none  [per_device(): arrived = received.reshape(pslots, page_size, width_two)[pick]]
    ppermute x1, waiting for transfers between devices: 4.29 us -> 0.01 us  [per_device(): other_half = lax.ppermute(own_half, 'c', [(0, 1), (1, 0)])]
  transfers between devices with their start and end apart: 5 -> 5, of which waited for: 5 -> 4; matrix products, arithmetic and copies ran while one was open for 1% -> 0% of each run, Pallas kernels for 0% -> 4%
where the time goes in v2:
time: 216 us; the launch traced here: 215 us
  waiting for transfers between devices  94.1 us (44%)
  blocking collectives  49.8 us (23%)
  Pallas kernels  32.4 us (15%)
  starting transfers between devices  19.7 us (9%)
  local copies, waits for them, and re-layouts  8.13 us (4%)
  other arithmetic  7.05 us (3%)
  matrix products  2.55 us (1%)
    all_to_all x1, waiting for transfers between devices, per_device(): received = lax.all_to_all(outgoing, DP, 0, 0, tiled=True)  56 us
    all_to_all x1, blocking collectives, to_all(): return lax.all_to_all(copies, axes, 0, 0, tiled=True)  31.9 us
    all_to_all x1, waiting for transfers between devices, per_device(): pieces = lax.all_to_all(chip_sum, CHIPS, 0, 0, tiled=True)  28.9 us
    all_to_all x1, blocking collectives, per_device(): lax.all_to_all(mixed_copies, CDP, 0, 0, tiled=True)  17.9 us
    pallas_call x1, Pallas kernels, expand_other(): pl.pallas_call(kernel, grid_spec=pltpu.PrefetchScalarGridSpec(num_scalar_...  12.7 us
    pallas_call x1, Pallas kernels, intake(): pl.pallas_call(kernel, in_specs=[smem, smem, hbm, vmem, vmem], out_specs=...  11.3 us
    all_to_all x1, waiting for transfers between devices, per_device(): lax.all_to_all(partial_out.reshape(n_tensor, rows_blk, cols_blk), TENSOR,...  7.69 us
    gather x1, local copies, waits for them, and re-layouts, per_device(): kv_pool[send_rows.reshape(-1), 0]  7.33 us
  transfers between devices with their start and end apart: 5, of which 4 were waited for; matrix products, arithmetic and copies ran while one was open for 0% of the time, Pallas kernels for 4%

profile of v2, /device:TPU:0, one launch (start us, length us, event | category | flops | bytes accessed | tf_op | source)
XLA Modules:
  0.0 214.6 jit_solution(1915589908963357110)
XLA Ops:
  0.6 0.0 copy-start
  0.7 0.9 select_reduce_fusion.1
  1.5 1.0 add_select_fusion
  2.6 0.1 copy.26
  2.7 0.1 reshape.115
  2.7 0.1 copy.27
  2.8 0.1 broadcast_in_dim.70
  2.9 0.2 fusion
  3.1 0.4 select_reduce_fusion
  3.5 0.1 reshape.116
  3.6 7.3 %gather_fusion = bf16[512,16,256]{2,1,0:T(8,128)(2,1)} fusion(bf16[512,1,16,256]{3,2,1,0:T(8,128)(2,1)} %param.12, s32[512]{0:T(512)S(1)} %bitcast.55), kind=kCustom, calls=%fused_computation | custom fusion | bytes 8392704 | tf_op jit(solution)/shard_map/gather | solution.py:360
  10.9 0.0 copy-start.6
  10.9 0.0 copy-start.5
  10.9 7.3 %all-to-all-start = ((bf16[16,32,16,256]{3,2,1,0:T(8,128)(2,1)}), bf16[16,32,16,256]{3,2,1,0:T(8,128)(2,1)}, u32[]{:S(2)}, u32[]{:S(2)}) async-start(bf16[16,32,16,256]{3,2,1,0:T(8,128)(2,1)} %bitcast.56), calls=%async_computation | async-start | bytes 8388608 | tf_op jit(solution)/shard_map/all_to_all | solution.py:361
  18.2 0.1 dynamic_slice.24.len_ref
  18.3 0.2 fusion.2
  18.5 0.0 copy-done.6
  18.5 0.0 copy-done.5
  18.6 56.0 %all-to-all-done = bf16[16,32,16,256]{3,2,1,0:T(8,128)(2,1)} async-done(((bf16[16,32,16,256]{3,2,1,0:T(8,128)(2,1)}), bf16[16,32,16,256]{3,2,1,0:T(8,128)(2,1)}, u32[]{:S(2)}, u32[]{:S(2)}) %all-to-all-start) | async-done | bytes 4194336 | tf_op jit(solution)/shard_map/all_to_all | solution.py:361
  74.5 0.0 copy-start.4
  74.5 11.3 %intake.1 = (bf16[8,65,16,256]{3,2,1,0:T(8,128)(2,1)}, bf16[16,16,1024]{2,1,0:T(8,128)(2,1)S(1)}) custom-call(s32[512]{0:T(512)S(1)} %add_select_fusion.2.pick_ref, s32[8]{0:T(128)S(1)} %dynamic_slice.24.len_ref, bf16[512,16,256]{2,1,0:T(8,128)(2,1)} %bitcast.7.recv_ref, f32[2,8,256]{2,1,0:T(8,128)S(1)} %bitcast_convert_fusion.fresh_ref, ...), custom_call_target="tpu_custom_call" | custom-call | tf_op jit(solution)/shard_map/intake/pallas_call | solution.py:101
  85.9 17.9 %all_to_all.25 = bf16[16,16,1024]{2,1,0:T(8,128)(2,1)S(1)} all-to-all(bf16[16,16,1024]{2,1,0:T(8,128)(2,1)S(1)} %get-tuple-element.9), channel_id=1, replica_groups=mesh['yh'=2,'x'=4,'c'=2,'z'=4,'yl'=2] {'c','yh','x'}, dimensions={0} | all-to-all | bytes 1048576 | tf_op jit(solution)/shard_map/all_to_all | solution.py:372
  103.8 0.0 copy-done
  103.8 1.2 convolution_convert_fusion
  104.9 5.4 %all-to-all-start.2 = ((bf16[8,32,512]{2,1,0:T(8,128)(2,1)}), bf16[8,32,512]{2,1,0:T(8,128)(2,1)S(1)}, u32[]{:S(2)}, u32[]{:S(2)}) async-start(bf16[8,32,512]{2,1,0:T(8,128)(2,1)} %bitcast.13), calls=%async_computation.2 | async-start | bytes 524288 | tf_op jit(solution)/shard_map/all_to_all | solution.py:378
  110.4 0.0 copy-start.3
  110.4 0.0 copy-done.4
  110.4 7.7 %all-to-all-done.2 = bf16[8,32,512]{2,1,0:T(8,128)(2,1)S(1)} async-done(((bf16[8,32,512]{2,1,0:T(8,128)(2,1)}), bf16[8,32,512]{2,1,0:T(8,128)(2,1)S(1)}, u32[]{:S(2)}, u32[]{:S(2)}) %all-to-all-start.2) | async-done | bytes 262176 | tf_op jit(solution)/shard_map/all_to_all | solution.py:378
  118.2 0.2 broadcast_in_dim.75
  118.4 31.9 %all_to_all.26 = bf16[64,32,512]{2,1,0:T(8,128)(2,1)S(1)} all-to-all(bf16[64,32,512]{2,1,0:T(8,128)(2,1)S(1)} %broadcast_in_dim.75), channel_id=1, replica_groups=mesh['yh'=2,'x'=4,'c'=2,'z'=4,'yl'=2] {'yh','x','z','yl'}, dimensions={0} | all-to-all | bytes 4194304 | tf_op jit(solution)/shard_map/all_to_all | solution.py:18
  150.3 0.0 collective-permute-start
  150.3 0.0 copy-done.3
  150.3 6.2 %expand_own.1 = (f32[256,224]{1,0:T(8,128)S(1)}, f32[256,224]{1,0:T(8,128)S(1)}, f32[256,128]{1,0:T(8,128)S(1)}) custom-call(s32[1]{0:T(128)} %bitcast.19.core_ref, bf16[8,256,512]{2,1,0:T(8,128)(2,1)S(1)} %bitcast.51, bf16[224,8192]{1,0:T(8,128)(2,1)} %bitcast.57, bf16[224,8192]{1,0:T(8,128)(2,1)} %bitcast.59, f32[1,8192]{1,0:T(1,128)S(1)} %bitcast.53), custom_call_target="tpu_custom_call" | custom-call | tf_op jit(solution)/shard_map/expand_own/pallas_call | solution.py:153
  156.5 0.0 collective-permute-done.x_ref
  156.5 0.0 copy-start.2
  156.5 0.0 copy-start.1
  156.5 12.7 %expand_other.1 = (bf16[2,128,224]{2,1,0:T(8,128)(2,1)S(1)}, bf16[8,8,16,1024]{3,2,1,0:T(8,128)(2,1)S(1)}) custom-call(s32[1]{0:T(128)} %bitcast.19.core_ref, bf16[8,256,512]{2,1,0:T(8,128)(2,1)S(1)} %collective-permute-done.x_ref, bf16[224,8192]{1,0:T(8,128)(2,1)} %bitcast.58, bf16[224,8192]{1,0:T(8,128)(2,1)} %bitcast.60, f32[1,8192]{1,0:T(1,128)S(1)} %bitcast.54, ...), custom_call_target="tpu_custom_call" | custom-call | tf_op jit(solution)/shard_map/expand_other/pallas_call | solution.py:226
  169.2 0.0 copy-done.2
  169.2 0.6 collective-permute-start.1
  169.8 0.0 copy-done.1
  169.8 2.2 %shrink_own.1 = bf16[8,8,16,1024]{3,2,1,0:T(8,128)(2,1)S(1)} custom-call(s32[1]{0:T(128)} %bitcast.19.core_ref, bf16[2,128,224]{2,1,0:T(8,128)(2,1)S(1)} %get-tuple-element.13.act_ref, bf16[224,8192]{1,0:T(8,128)(2,1)S(1)} %copy-done.1), custom_call_target="tpu_custom_call" | custom-call | tf_op jit(solution)/shard_map/shrink_own/pallas_call | solution.py:269
  172.0 1.5 collective-permute-done.1
  173.6 2.4 %add_convert_fusion = bf16[8,8,16,1024]{3,2,1,0:T(8,128)(2,1)} fusion(bf16[8,8,16,1024]{3,2,1,0:T(8,128)(2,1)S(1)} %collective-permute-done.1, bf16[8,8,16,1024]{3,2,1,0:T(8,128)(2,1)S(1)} %shrink_own.1), kind=kLoop, calls=%fused_computation.2 | loop fusion | flops 4194304 | bytes 6291456 | tf_op jit(solution)/shard_map/convert_element_type | solution.py:404
  176.0 6.4 %all-to-all-start.4 = ((bf16[64,16,1024]{2,1,0:T(8,128)(2,1)}), bf16[64,16,1024]{2,1,0:T(8,128)(2,1)}, u32[]{:S(2)}, u32[]{:S(2)}) async-start(bf16[64,16,1024]{2,1,0:T(8,128)(2,1)} %bitcast.61), calls=%async_computation.4 | async-start | bytes 4194304 | tf_op jit(solution)/shard_map/all_to_all | solution.py:407
  182.4 0.7 select_bitcast_fusion.1
  183.1 28.9 %all-to-all-done.4 = bf16[64,16,1024]{2,1,0:T(8,128)(2,1)} async-done(((bf16[64,16,1024]{2,1,0:T(8,128)(2,1)}), bf16[64,16,1024]{2,1,0:T(8,128)(2,1)}, u32[]{:S(2)}, u32[]{:S(2)}) %all-to-all-start.4) | async-done | bytes 2097184 | tf_op jit(solution)/shard_map/all_to_all | solution.py:407
  212.0 2.0 convert_reduce_fusion
  214.0 0.6 fusion.3
  (9 shorter events, 0.1 us)
Async XLA Ops:
  0.6 103.1 %copy-start = (bf16[1024,512]{1,0:T(8,128)(2,1)S(1)}, bf16[1024,512]{1,0:T(8,128)(2,1)}, u32[]{:S(2)}) copy-start(bf16[1024,512]{1,0:T(8,128)(2,1)} %param.19) | copy-start | bytes 3145732
  10.9 7.6 %copy-start.6 = (bf16[2,8,1,256]{3,1,2,0:T(8,128)(2,1)S(1)}, bf16[2,8,1,256]{3,1,2,0:T(8,128)(2,1)}, u32[]{:S(2)}) copy-start(bf16[2,8,1,256]{3,1,2,0:T(8,128)(2,1)} %param.17) | copy-start | bytes 24580
  10.9 7.6 %copy-start.5 = (bf16[2,8,8,128]{3,2,1,0:T(8,128)(2,1)S(1)}, bf16[2,8,8,128]{3,2,1,0:T(8,128)(2,1)}, u32[]{:S(2)}) copy-start(bf16[2,8,8,128]{3,2,1,0:T(8,128)(2,1)} %param.16) | copy-start | bytes 98308
  10.9 63.7 %all-to-all-start = ((bf16[16,32,16,256]{3,2,1,0:T(8,128)(2,1)}), bf16[16,32,16,256]{3,2,1,0:T(8,128)(2,1)}, u32[]{:S(2)}, u32[]{:S(2)}) async-start(bf16[16,32,16,256]{3,2,1,0:T(8,128)(2,1)} %bitcast.56), calls=%async_computation | async-start | bytes 8388608 | tf_op jit(solution)/shard_map/all_to_all | solution.py:361
  74.5 35.8 %copy-start.4 = (bf16[2,128,512]{2,1,0:T(8,128)(2,1)S(1)}, bf16[2,128,512]{2,1,0:T(8,128)(2,1)}, u32[]{:S(2)}) copy-start(bf16[2,128,512]{2,1,0:T(8,128)(2,1)} %param.18) | copy-start | bytes 786436
  104.9 13.2 %all-to-all-start.2 = ((bf16[8,32,512]{2,1,0:T(8,128)(2,1)}), bf16[8,32,512]{2,1,0:T(8,128)(2,1)S(1)}, u32[]{:S(2)}, u32[]{:S(2)}) async-start(bf16[8,32,512]{2,1,0:T(8,128)(2,1)} %bitcast.13), calls=%async_computation.2 | async-start | bytes 524288 | tf_op jit(solution)/shard_map/all_to_all | solution.py:378
  110.4 39.9 %copy-start.3 = (f32[8192]{0:T(1024)S(1)}, f32[8192]{0:T(1024)}, u32[]{:S(2)}) copy-start(f32[8192]{0:T(1024)} %param.20) | copy-start | bytes 98308
  150.3 6.2 %collective-permute-start = (bf16[8,256,512]{2,1,0:T(8,128)(2,1)S(1)}, bf16[8,256,512]{2,1,0:T(8,128)(2,1)S(1)}, u32[]{:S(2)}, u32[]{:S(2)}) collective-permute-start(bf16[8,256,512]{2,1,0:T(8,128)(2,1)S(1)} %bitcast.50), channel_id=1, source_target_pairs={{0,8},{8,0},{1,9},{9,1},{2,10},{10,2},{3,11},{11,3},{4,12},{12,4},... | collective-permute-start | bytes 6291464 | tf_op jit(solution)/shard_map/ppermute | solution.py:390
  156.5 12.7 %copy-start.2 = (bf16[8,256,512]{2,1,0:T(8,128)(2,1)}, bf16[8,256,512]{2,1,0:T(8,128)(2,1)S(1)}, u32[]{:S(2)}) copy-start(bf16[8,256,512]{2,1,0:T(8,128)(2,1)S(1)} %collective-permute-done.x_ref) | copy-start | bytes 6291460
  156.5 13.3 %copy-start.1 = (bf16[224,8192]{1,0:T(8,128)(2,1)S(1)}, bf16[224,8192]{1,0:T(8,128)(2,1)}, u32[]{:S(2)}) copy-start(bf16[224,8192]{1,0:T(8,128)(2,1)} %down_ref.3) | copy-start | bytes 11010052
  169.2 4.4 %collective-permute-start.1 = (bf16[8,8,16,1024]{3,2,1,0:T(8,128)(2,1)S(1)}, bf16[8,8,16,1024]{3,2,1,0:T(8,128)(2,1)S(1)}, u32[]{:S(2)}, u32[]{:S(2)}) collective-permute-start(bf16[8,8,16,1024]{3,2,1,0:T(8,128)(2,1)S(1)} %get-tuple-element.14), channel_id=1, source_target_pairs={{0,8},{8,0},{1,9},{9,1},{2,10},{10,2},{3,11},{11,3},{4,12},{12,4},... | collective-permute-start | bytes 6291464 | tf_op jit(solution)/shard_map/ppermute | solution.py:400
  176.0 36.0 %all-to-all-start.4 = ((bf16[64,16,1024]{2,1,0:T(8,128)(2,1)}), bf16[64,16,1024]{2,1,0:T(8,128)(2,1)}, u32[]{:S(2)}, u32[]{:S(2)}) async-start(bf16[64,16,1024]{2,1,0:T(8,128)(2,1)} %bitcast.61), calls=%async_computation.4 | async-start | bytes 4194304 | tf_op jit(solution)/shard_map/all_to_all | solution.py:407

commit v3 on v2

--- a/solution.py
+++ b/solution.py
@@ -17,7 +17,11 @@
     copies = lax.optimization_barrier(jnp.broadcast_to(block[None], (count,) + block.shape))
     return lax.all_to_all(copies, axes, 0, 0, tiled=True)
 
-VMEM_LIMIT = 48 * 1024 * 1024
+VMEM_LIMIT = 20 * 1024 * 1024
+BLOCK = 512
+SMEM = pl.BlockSpec(memory_space=pltpu.SMEM)
+VMEM = pl.BlockSpec(memory_space=pltpu.VMEM)
+HBM = pl.BlockSpec(memory_space=pltpu.HBM)
 
 
 def intake(pick, lens, received, fresh, query, n_copies):
@@ -95,13 +99,10 @@
         for r in range(req_dev):
             copy_out(r).wait()
 
-    smem = pl.BlockSpec(memory_space=pltpu.SMEM)
-    vmem = pl.BlockSpec(memory_space=pltpu.VMEM)
-    hbm = pl.BlockSpec(memory_space=pl.ANY)
-    return pl.pallas_call(
-        kernel,
-        in_specs=[smem, smem, hbm, vmem, vmem],
-        out_specs=[hbm, vmem],
+    return pl.pallas_call(
+        kernel,
+        in_specs=[SMEM, SMEM, HBM, VMEM, VMEM],
+        out_specs=[HBM, VMEM],
         out_shape=[
             jax.ShapeDtypeStruct((req_dev, pages, page_size, width_two), received.dtype),
             jax.ShapeDtypeStruct(
@@ -119,66 +120,85 @@
     )(pick, lens, received, fresh, query)
 
 
-def expand_step(x_ref, gate_ref, up_ref, gain_ref, gate_sum, up_sum, squares):
-    wide = x_ref[0].astype(jnp.float32)
-    lanes = squares.shape[1]
-    square = wide * wide
-    squares[...] += sum(
-        square[:, k * lanes : (k + 1) * lanes] for k in range(square.shape[1] // lanes)
-    )
-    scaled = (wide * gain_ref[...]).astype(jnp.bfloat16)
-    contract = (((1,), (1,)), ((), ()))
-    gate_sum[...] += lax.dot_general(
-        scaled, gate_ref[...], contract, preferred_element_type=jnp.float32
-    )
-    up_sum[...] += lax.dot_general(
-        scaled, up_ref[...], contract, preferred_element_type=jnp.float32
-    )
+def start_weights(side, sources, buffers, sems):
+    for m, (source, buffer) in enumerate(zip(sources, buffers)):
+        for i in range(buffer.shape[1] // BLOCK):
+            weight_copy(side, source, buffer, sems.at[m, i], i).start()
+
+
+def weight_copy(side, source, buffer, sem, i):
+    at = pl.multiple_of((2 * i + side) * BLOCK, BLOCK)
+    return pltpu.make_async_copy(
+        source.at[:, pl.ds(at, BLOCK)], buffer.at[:, pl.ds(i * BLOCK, BLOCK)], sem
+    )
+
+
+def expand(side, x_ref, gain_ref, sources, buffers, sems, scaled, parts=2):
+    steps = x_ref.shape[0]
+    squares = 0.0
+    for i in range(steps):
+        at = pl.multiple_of((2 * i + side) * BLOCK, BLOCK)
+        wide = x_ref[i].astype(jnp.float32)
+        square = wide * wide
+        squares += sum(square[:, k * 128 : (k + 1) * 128] for k in range(BLOCK // 128))
+        scaled[:, i * BLOCK : (i + 1) * BLOCK] = (wide * gain_ref[:, pl.ds(at, BLOCK)]).astype(
+            scaled.dtype
+        )
+    products = [0.0] * len(sources)
+    for part in range(parts):
+        span = steps // parts
+        cols = slice(part * span * BLOCK, (part + 1) * span * BLOCK)
+        for m, (source, buffer) in enumerate(zip(sources, buffers)):
+            for i in range(part * span, (part + 1) * span):
+                weight_copy(side, source, buffer, sems.at[m, i], i).wait()
+            products[m] += lax.dot_general(
+                scaled[:, cols],
+                buffer[:, cols],
+                (((1,), (1,)), ((), ())),
+                preferred_element_type=jnp.float32,
+            )
+    return products, squares
+
+
+def expand_scratch(steps, rows, units):
+    return [
+        pltpu.VMEM((units, steps * BLOCK), jnp.bfloat16),
+        pltpu.VMEM((units, steps * BLOCK), jnp.bfloat16),
+        pltpu.VMEM((rows, steps * BLOCK), jnp.bfloat16),
+        pltpu.SemaphoreType.DMA((2, steps)),
+    ]
 
 
 def expand_own(core_at, own_half, gate_rows, up_rows, gain_row):
-    steps, rows, cols = own_half.shape
+    steps, rows, _ = own_half.shape
     units = gate_rows.shape[0]
 
-    def kernel(core_ref, x_ref, gate_ref, up_ref, gain_ref, gate_sum, up_sum, squares):
-        @pl.when(pl.program_id(0) == 0)
-        def _():
-            gate_sum[...] = jnp.zeros_like(gate_sum)
-            up_sum[...] = jnp.zeros_like(up_sum)
-            squares[...] = jnp.zeros_like(squares)
-
-        expand_step(x_ref, gate_ref, up_ref, gain_ref, gate_sum, up_sum, squares)
-
-    weight = pl.BlockSpec((units, cols), lambda i, core: (0, 2 * i + core[0]))
-    return pl.pallas_call(
-        kernel,
-        grid_spec=pltpu.PrefetchScalarGridSpec(
-            num_scalar_prefetch=1,
-            grid=(steps,),
-            in_specs=[
-                pl.BlockSpec((1, rows, cols), lambda i, core: (i, 0, 0)),
-                weight,
-                weight,
-                pl.BlockSpec((1, cols), lambda i, core: (0, 2 * i + core[0])),
-            ],
-            out_specs=[
-                pl.BlockSpec((rows, units), lambda i, core: (0, 0)),
-                pl.BlockSpec((rows, units), lambda i, core: (0, 0)),
-                pl.BlockSpec((rows, 128), lambda i, core: (0, 0)),
-            ],
-        ),
+    def kernel(core_ref, x_ref, gate_ref, up_ref, gain_ref, gate_sum, up_sum, squares_sum, gate_buf, up_buf, scaled, sems):
+        side = core_ref[0]
+        sources, buffers = (gate_ref, up_ref), (gate_buf, up_buf)
+        start_weights(side, sources, buffers, sems)
+        (gate, upper), squares = expand(side, x_ref, gain_ref, sources, buffers, sems, scaled)
+        gate_sum[...] = gate
+        up_sum[...] = upper
+        squares_sum[...] = squares
+
+    return pl.pallas_call(
+        kernel,
+        in_specs=[SMEM, VMEM, HBM, HBM, VMEM],
+        out_specs=[VMEM, VMEM, VMEM],
         out_shape=[
             jax.ShapeDtypeStruct((rows, units), jnp.float32),
             jax.ShapeDtypeStruct((rows, units), jnp.float32),
             jax.ShapeDtypeStruct((rows, 128), jnp.float32),
         ],
+        scratch_shapes=expand_scratch(steps, rows, units),
         compiler_params=pltpu.CompilerParams(vmem_limit_bytes=VMEM_LIMIT),
         name="expand_own",
     )(core_at, own_half, gate_rows, up_rows, gain_row)
 
 
 def expand_other(core_at, other_half, gate_rows, up_rows, gain_row, sums, w_down, n_tensor, rows_dev):
-    steps, rows, cols = other_half.shape
+    steps, rows, _ = other_half.shape
     units, width = w_down.shape
     cols_out = width // n_tensor
     half_rows = rows // 2
@@ -186,75 +206,63 @@
 
     def kernel(
         core_ref, x_ref, gate_ref, up_ref, gain_ref, gate_in, up_in, squares_in, down_ref,
-        act_ref, theirs_ref, gate_sum, up_sum, squares,
+        act_ref, theirs_ref, gate_buf, up_buf, scaled, sems, down_buf, down_sem,
     ):
-        step = pl.program_id(0)
-
-        @pl.when(step == 0)
-        def _():
-            gate_sum[...] = gate_in[...]
-            up_sum[...] = up_in[...]
-            squares[...] = squares_in[...]
-
-        @pl.when(step < steps)
-        def _():
-            expand_step(x_ref, gate_ref, up_ref, gain_ref, gate_sum, up_sum, squares)
-
-        @pl.when(step == steps - 1)
-        def _():
-            mean = jnp.sum(squares[...], axis=1, keepdims=True) * (1.0 / width)
-            inverse = lax.rsqrt(mean + 1e-05)
-            gate = gate_sum[...] * inverse
-            act = gate / (1.0 + jnp.exp(-gate)) * (up_sum[...] * inverse)
-            act_ref[...] = act.astype(act_ref.dtype).reshape(2, half_rows, units)
-
-        @pl.when(step >= steps)
-        def _():
+        side = 1 - core_ref[0]
+        sources, buffers = (gate_ref, up_ref), (gate_buf, up_buf)
+        start_weights(side, sources, buffers, sems)
+        down_copy = pltpu.make_async_copy(down_ref, down_buf, down_sem)
+        down_copy.start()
+        (gate, upper), squares = expand(side, x_ref, gain_ref, sources, buffers, sems, scaled)
+        squares += squares_in[...]
+        inverse = lax.rsqrt(jnp.sum(squares, axis=1, keepdims=True) * (1.0 / width) + 1e-05)
+        gate = (gate + gate_in[...]) * inverse
+        act = gate / (1.0 + jnp.exp(-gate)) * ((upper + up_in[...]) * inverse)
+        act_ref[...] = act.astype(act_ref.dtype).reshape(2, half_rows, units)
+        down_copy.wait()
+        picked = act_ref[side]
+        for t in range(n_tensor):
             out = jnp.dot(
-                act_ref[1 - core_ref[0]], down_ref[...], preferred_element_type=jnp.float32
+                picked,
+                down_buf[:, t * cols_out : (t + 1) * cols_out],
+                preferred_element_type=jnp.float32,
             )
-            theirs_ref[...] = out.astype(theirs_ref.dtype).reshape(chips, 1, rows_dev, cols_out)
-
-    def into(i):
-        return jnp.minimum(i, steps - 1)
-
-    def out_of(i):
-        return jnp.maximum(i - steps, 0)
-
-    weight = pl.BlockSpec((units, cols), lambda i, core: (0, 2 * into(i) + 1 - core[0]))
-    whole = pl.BlockSpec((rows, units), lambda i, core: (0, 0))
-    return pl.pallas_call(
-        kernel,
-        grid_spec=pltpu.PrefetchScalarGridSpec(
-            num_scalar_prefetch=1,
-            grid=(steps + n_tensor,),
-            in_specs=[
-                pl.BlockSpec((1, rows, cols), lambda i, core: (into(i), 0, 0)),
-                weight,
-                weight,
-                pl.BlockSpec((1, cols), lambda i, core: (0, 2 * into(i) + 1 - core[0])),
-                whole,
-                whole,
-                pl.BlockSpec((rows, 128), lambda i, core: (0, 0)),
-                pl.BlockSpec((units, cols_out), lambda i, core: (0, out_of(i))),
-            ],
-            out_specs=[
-                pl.BlockSpec((2, half_rows, units), lambda i, core: (0, 0, 0)),
-                pl.BlockSpec((chips, 1, rows_dev, cols_out), lambda i, core: (0, out_of(i), 0, 0)),
-            ],
-            scratch_shapes=[
-                pltpu.VMEM((rows, units), jnp.float32),
-                pltpu.VMEM((rows, units), jnp.float32),
-                pltpu.VMEM((rows, 128), jnp.float32),
-            ],
-        ),
+            theirs_ref[:, t] = out.astype(theirs_ref.dtype).reshape(chips, rows_dev, cols_out)
+
+    return pl.pallas_call(
+        kernel,
+        in_specs=[SMEM, VMEM, HBM, HBM, VMEM, VMEM, VMEM, VMEM, HBM],
+        out_specs=[VMEM, VMEM],
         out_shape=[
             jax.ShapeDtypeStruct((2, half_rows, units), jnp.bfloat16),
             jax.ShapeDtypeStruct((chips, n_tensor, rows_dev, cols_out), jnp.bfloat16),
         ],
+        scratch_shapes=expand_scratch(steps, rows, units)
+        + [pltpu.VMEM((units, width), jnp.bfloat16), pltpu.SemaphoreType.DMA],
         compiler_params=pltpu.CompilerParams(vmem_limit_bytes=VMEM_LIMIT),
         name="expand_other",
     )(core_at, other_half, gate_rows, up_rows, gain_row, *sums, w_down)
+
+
+def gather_pages(rows, pool):
+    count = rows.shape[0]
+
+    def kernel(rows_ref, pool_ref, out_ref, sem):
+        def body(k, carry):
+            pltpu.make_async_copy(pool_ref.at[rows_ref[k]], out_ref.at[k], sem).start()
+            return carry
+
+        lax.fori_loop(0, count, body, 0, unroll=16)
+        pltpu.make_async_copy(pool_ref, out_ref, sem).wait()
+
+    return pl.pallas_call(
+        kernel,
+        in_specs=[SMEM, HBM],
+        out_specs=HBM,
+        out_shape=jax.ShapeDtypeStruct((count,) + pool.shape[1:], pool.dtype),
+        scratch_shapes=[pltpu.SemaphoreType.DMA],
+        name="gather_pages",
+    )(rows, pool)
 
 
 def shrink_own(core_at, act, w_down, n_tensor, rows_dev):
@@ -263,24 +271,47 @@
     chips = half_rows // rows_dev
 
     def kernel(core_ref, act_ref, down_ref, ours_ref):
-        out = jnp.dot(act_ref[0], down_ref[...], preferred_element_type=jnp.float32)
-        ours_ref[...] = out.astype(ours_ref.dtype).reshape(chips, 1, rows_dev, cols_out)
-
-    return pl.pallas_call(
-        kernel,
-        grid_spec=pltpu.PrefetchScalarGridSpec(
-            num_scalar_prefetch=1,
-            grid=(n_tensor,),
-            in_specs=[
-                pl.BlockSpec((1, half_rows, units), lambda i, core: (core[0], 0, 0)),
-                pl.BlockSpec((units, cols_out), lambda i, core: (0, i)),
-            ],
-            out_specs=pl.BlockSpec((chips, 1, rows_dev, cols_out), lambda i, core: (0, i, 0, 0)),
-        ),
+        picked = act_ref[core_ref[0]]
+        for t in range(n_tensor):
+            out = jnp.dot(
+                picked,
+                down_ref[:, t * cols_out : (t + 1) * cols_out],
+                preferred_element_type=jnp.float32,
+            )
+            ours_ref[:, t] = out.astype(ours_ref.dtype).reshape(chips, rows_dev, cols_out)
+
+    return pl.pallas_call(
+        kernel,
+        in_specs=[SMEM, VMEM, VMEM],
+        out_specs=VMEM,
         out_shape=jax.ShapeDtypeStruct((chips, n_tensor, rows_dev, cols_out), jnp.bfloat16),
         compiler_params=pltpu.CompilerParams(vmem_limit_bytes=VMEM_LIMIT),
         name="shrink_own",
     )(core_at, act, w_down)
+
+
+def add_cores(ours, from_core):
+    chips = ours.shape[0]
+
+    def kernel(a_ref, b_ref, out_ref, buf, sems):
+        def copy(i):
+            return pltpu.make_async_copy(buf.at[i], out_ref.at[i], sems.at[i])
+
+        for i in range(chips):
+            buf[i] = (a_ref[i].astype(jnp.float32) + b_ref[i].astype(jnp.float32)).astype(buf.dtype)
+            copy(i).start()
+        for i in range(chips):
+            copy(i).wait()
+
+    return pl.pallas_call(
+        kernel,
+        in_specs=[VMEM, VMEM],
+        out_specs=HBM,
+        out_shape=pltpu.HBM(ours.shape, ours.dtype),
+        scratch_shapes=[pltpu.VMEM(ours.shape, ours.dtype), pltpu.SemaphoreType.DMA((chips,))],
+        compiler_params=pltpu.CompilerParams(vmem_limit_bytes=VMEM_LIMIT),
+        name="add_cores",
+    )(ours, from_core)
 
 
 def page_plan(page_loc, lengths, placement, dev_dp, dev_tensor, n_dp, pslots, page_size):
@@ -357,7 +388,9 @@
     send_rows, pick, my_len = page_plan(
         page_loc, lengths, placement, dev_dp, dev_tensor, n_dp, pslots, page_size
     )
-    outgoing = kv_pool[send_rows.reshape(-1), 0].reshape(n_dp, capacity, page_size, width_two)
+    outgoing = gather_pages(
+        send_rows.reshape(-1), kv_pool.reshape(pslots, page_size, width_two)
+    ).reshape(n_dp, capacity, page_size, width_two)
     received = lax.all_to_all(outgoing, DP, 0, 0, tiled=True)
     query = jnp.transpose(queries, (1, 0, 2, 3)).reshape(req_dev, n_steps * hq_dev, head_dim)
     cache, mixed_copies = intake(
@@ -399,11 +432,7 @@
     )
     from_core = lax.ppermute(theirs, "c", [(0, 1), (1, 0)])
     ours = shrink_own(core_at, act, w_down, n_tensor, rows_dev)
-    chip_sum = (
-        (ours.astype(jnp.float32) + from_core.astype(jnp.float32))
-        .astype(jnp.bfloat16)
-        .reshape(chips_dp * n_tensor, rows_dev, width_out)
-    )
+    chip_sum = add_cores(ours, from_core).reshape(chips_dp * n_tensor, rows_dev, width_out)
     pieces = lax.all_to_all(chip_sum, CHIPS, 0, 0, tiled=True)
     ffn_part = jnp.sum(pieces.astype(jnp.float32), axis=0)
 

time: 216 us -> 331 us (1.53)
  Pallas kernels: 32.4 us -> 152 us
  local copies, waits for them, and re-layouts: 8.13 us -> 3.44 us
    pallas_call x4 -> x6, Pallas kernels: 32.4 us -> 152 us  [the longest x1 129 us: gather_pages(): pl.pallas_call(kernel, in_specs=[SMEM, HBM], out_specs=HBM, out_shape=jax...]
    gather x1 -> x0, local copies, waits for them, and re-layouts: 7.33 us -> none  [per_device(): kv_pool[send_rows.reshape(-1), 0]]
  transfers between devices with their start and end apart: 5 -> 5, of which waited for: 4 -> 4; matrix products, arithmetic and copies ran while one was open for 0% -> 0% of each run, Pallas kernels for 4% -> 2%
where the time goes in v3:
time: 331 us; the launch traced here: 329 us
  Pallas kernels  152 us (46%)
  waiting for transfers between devices  95.6 us (29%)
  blocking collectives  49.7 us (15%)
  starting transfers between devices  19.7 us (6%)
  other arithmetic  4.61 us (1%)
  local copies, waits for them, and re-layouts  3.44 us (1%)
    pallas_call x1, Pallas kernels, gather_pages(): pl.pallas_call(kernel, in_specs=[SMEM, HBM], out_specs=HBM, out_shape=jax...  129 us
    all_to_all x1, waiting for transfers between devices, per_device(): received = lax.all_to_all(outgoing, DP, 0, 0, tiled=True)  56 us
    all_to_all x1, blocking collectives, to_all(): return lax.all_to_all(copies, axes, 0, 0, tiled=True)  32.1 us
    all_to_all x1, waiting for transfers between devices, per_device(): pieces = lax.all_to_all(chip_sum, CHIPS, 0, 0, tiled=True)  28.9 us
    all_to_all x1, blocking collectives, per_device(): lax.all_to_all(mixed_copies, CDP, 0, 0, tiled=True)  17.5 us
    pallas_call x1, Pallas kernels, intake(): pl.pallas_call(kernel, in_specs=[SMEM, SMEM, HBM, VMEM, VMEM], out_specs=...  11.5 us
    all_to_all x1, waiting for transfers between devices, per_device(): lax.all_to_all(partial_out.reshape(n_tensor, rows_blk, cols_blk), TENSOR,...  7.7 us
    all_to_all x1, starting transfers between devices, per_device(): received = lax.all_to_all(outgoing, DP, 0, 0, tiled=True)  7.18 us
  transfers between devices with their start and end apart: 5, of which 4 were waited for; matrix products, arithmetic and copies ran while one was open for 0% of the time, Pallas kernels for 2%

profile of v3, /device:TPU:0, one launch (start us, length us, event | category | flops | bytes accessed | tf_op | source)
XLA Modules:
  0.0 328.9 jit_solution(8594062490112899008)
XLA Ops:
  0.6 0.0 copy-start
  0.7 0.9 select_reduce_fusion.1
  1.5 1.0 add_select_fusion
  2.6 0.1 copy.26
  2.7 0.1 reshape.90
  2.7 0.1 copy.27
  2.8 0.1 broadcast_in_dim.66
  2.9 0.2 fusion
  3.1 0.4 select_reduce_fusion
  3.5 0.7 reshape.91.rows_ref
  4.1 129.0 %gather_pages.1 = bf16[512,16,256]{2,1,0:T(8,128)(2,1)} custom-call(s32[512]{0:T(512)} %reshape.91.rows_ref, bf16[512,16,256]{2,1,0:T(8,128)(2,1)} %bitcast.61), custom_call_target="tpu_custom_call" | custom-call | tf_op jit(solution)/shard_map/gather_pages/pallas_call | solution.py:258
  133.1 0.0 copy-start.9
  133.1 0.0 copy-start.8
  133.2 7.2 %all-to-all-start = ((bf16[16,32,16,256]{3,2,1,0:T(8,128)(2,1)}), bf16[16,32,16,256]{3,2,1,0:T(8,128)(2,1)}, u32[]{:S(2)}, u32[]{:S(2)}) async-start(bf16[16,32,16,256]{3,2,1,0:T(8,128)(2,1)} %bitcast.59), calls=%async_computation | async-start | bytes 8388608 | tf_op jit(solution)/shard_map/all_to_all | solution.py:394
  140.3 0.1 dynamic_slice.24.len_ref
  140.4 0.2 fusion.2
  140.6 0.0 copy-done.9
  140.7 0.0 copy-done.8
  140.7 56.0 %all-to-all-done = bf16[16,32,16,256]{3,2,1,0:T(8,128)(2,1)} async-done(((bf16[16,32,16,256]{3,2,1,0:T(8,128)(2,1)}), bf16[16,32,16,256]{3,2,1,0:T(8,128)(2,1)}, u32[]{:S(2)}, u32[]{:S(2)}) %all-to-all-start) | async-done | bytes 4194336 | tf_op jit(solution)/shard_map/all_to_all | solution.py:394
  196.7 11.5 %intake.1 = (bf16[8,65,16,256]{3,2,1,0:T(8,128)(2,1)}, bf16[16,16,1024]{2,1,0:T(8,128)(2,1)S(1)}) custom-call(s32[512]{0:T(512)S(1)} %add_select_fusion.2.pick_ref, s32[8]{0:T(128)S(1)} %dynamic_slice.24.len_ref, bf16[512,16,256]{2,1,0:T(8,128)(2,1)} %bitcast.7.recv_ref, f32[2,8,256]{2,1,0:T(8,128)S(1)} %bitcast_convert_fusion.fresh_ref, ...), custom_call_target="tpu_custom_call" | custom-call | tf_op jit(solution)/shard_map/intake/pallas_call | solution.py:102
  208.2 0.0 copy-start.7
  208.2 17.5 %all_to_all.25 = bf16[16,16,1024]{2,1,0:T(8,128)(2,1)S(1)} all-to-all(bf16[16,16,1024]{2,1,0:T(8,128)(2,1)S(1)} %get-tuple-element.9), channel_id=1, replica_groups=mesh['yh'=2,'x'=4,'c'=2,'z'=4,'yl'=2] {'c','yh','x'}, dimensions={0} | all-to-all | bytes 1048576 | tf_op jit(solution)/shard_map/all_to_all | solution.py:405
  225.8 0.0 copy-done
  225.8 1.1 convolution_convert_fusion
  226.9 5.4 %all-to-all-start.2 = ((bf16[8,32,512]{2,1,0:T(8,128)(2,1)}), bf16[8,32,512]{2,1,0:T(8,128)(2,1)S(1)}, u32[]{:S(2)}, u32[]{:S(2)}) async-start(bf16[8,32,512]{2,1,0:T(8,128)(2,1)} %bitcast.13), calls=%async_computation.2 | async-start | bytes 524288 | tf_op jit(solution)/shard_map/all_to_all | solution.py:411
  232.3 0.0 copy-done.7
  232.4 7.7 %all-to-all-done.2 = bf16[8,32,512]{2,1,0:T(8,128)(2,1)S(1)} async-done(((bf16[8,32,512]{2,1,0:T(8,128)(2,1)}), bf16[8,32,512]{2,1,0:T(8,128)(2,1)S(1)}, u32[]{:S(2)}, u32[]{:S(2)}) %all-to-all-start.2) | async-done | bytes 262176 | tf_op jit(solution)/shard_map/all_to_all | solution.py:411
  240.1 0.2 broadcast_in_dim.70
  240.4 0.0 copy-start.1
  240.4 0.0 copy-start.6
  240.4 32.1 %all_to_all.26 = bf16[64,32,512]{2,1,0:T(8,128)(2,1)S(1)} all-to-all(bf16[64,32,512]{2,1,0:T(8,128)(2,1)S(1)} %broadcast_in_dim.70), channel_id=1, replica_groups=mesh['yh'=2,'x'=4,'c'=2,'z'=4,'yl'=2] {'yh','x','z','yl'}, dimensions={0} | all-to-all | bytes 4194304 | tf_op jit(solution)/shard_map/all_to_all | solution.py:18
  272.5 0.0 collective-permute-start
  272.5 0.0 copy-done.1
  272.5 0.0 copy-done.6
  272.6 0.0 copy-start.2
  272.6 2.0 copy-done.2
  274.6 0.0 copy-start.3
  274.6 0.0 copy-start.4
  274.6 4.3 %expand_own.1 = (f32[256,224]{1,0:T(8,128)S(1)}, f32[256,224]{1,0:T(8,128)S(1)}, f32[256,128]{1,0:T(8,128)S(1)}) custom-call(s32[1]{0:T(128)} %bitcast.19.core_ref, bf16[8,256,512]{2,1,0:T(8,128)(2,1)S(1)} %bitcast.55, bf16[224,8192]{1,0:T(8,128)(2,1)S(1)} %bitcast.50, bf16[224,8192]{1,0:T(8,128)(2,1)S(1)} %bitcast.52, f32[1,8192]{1,0:T(1,128)S(1)} %bitcast.57), custom_call_target="tpu_custom_call" | custom-call | tf_op jit(solution)/shard_map/expand_own/pallas_call | solution.py:185
  278.9 0.0 collective-permute-done.x_ref
  278.9 0.0 copy-start.5
  278.9 0.0 copy-done.3
  278.9 0.0 copy-done.4
  279.0 5.3 %expand_other.1 = (bf16[2,128,224]{2,1,0:T(8,128)(2,1)S(1)}, bf16[8,8,16,1024]{3,2,1,0:T(8,128)(2,1)S(1)}) custom-call(s32[1]{0:T(128)} %bitcast.19.core_ref, bf16[8,256,512]{2,1,0:T(8,128)(2,1)S(1)} %collective-permute-done.x_ref, bf16[224,8192]{1,0:T(8,128)(2,1)S(1)} %bitcast.51, bf16[224,8192]{1,0:T(8,128)(2,1)S(1)} %bitcast.53, f32[1,8192]{1,0:T(1,128)S(1)} %bitcast.58, ...), custom_call_target="tpu_custom_call" | custom-call | tf_op jit(solution)/shard_map/expand_other/pallas_call | solution.py:232
  284.3 0.0 copy-done.5
  284.3 0.8 collective-permute-start.1
  285.0 0.7 shrink_own.1.a_ref
  285.7 3.1 collective-permute-done.1.b_ref
  288.8 1.4 add_cores.1
  290.3 6.4 %all-to-all-start.4 = ((bf16[64,16,1024]{2,1,0:T(8,128)(2,1)}), bf16[64,16,1024]{2,1,0:T(8,128)(2,1)}, u32[]{:S(2)}, u32[]{:S(2)}) async-start(bf16[64,16,1024]{2,1,0:T(8,128)(2,1)} %bitcast.60), calls=%async_computation.4 | async-start | bytes 4194304 | tf_op jit(solution)/shard_map/all_to_all | solution.py:436
  296.7 0.7 select_bitcast_fusion.1
  297.4 28.9 %all-to-all-done.4 = bf16[64,16,1024]{2,1,0:T(8,128)(2,1)} async-done(((bf16[64,16,1024]{2,1,0:T(8,128)(2,1)}), bf16[64,16,1024]{2,1,0:T(8,128)(2,1)}, u32[]{:S(2)}, u32[]{:S(2)}) %all-to-all-start.4) | async-done | bytes 2097184 | tf_op jit(solution)/shard_map/all_to_all | solution.py:436
  326.3 2.0 convert_reduce_fusion
  328.2 0.6 fusion.3
  (8 shorter events, 0.1 us)
Async XLA Ops:
  0.6 225.2 %copy-start = (bf16[1024,512]{1,0:T(8,128)(2,1)S(1)}, bf16[1024,512]{1,0:T(8,128)(2,1)}, u32[]{:S(2)}) copy-start(bf16[1024,512]{1,0:T(8,128)(2,1)} %param.19) | copy-start | bytes 3145732
  133.1 7.5 %copy-start.9 = (bf16[2,8,1,256]{3,1,2,0:T(8,128)(2,1)S(1)}, bf16[2,8,1,256]{3,1,2,0:T(8,128)(2,1)}, u32[]{:S(2)}) copy-start(bf16[2,8,1,256]{3,1,2,0:T(8,128)(2,1)} %param.17) | copy-start | bytes 24580
  133.1 7.5 %copy-start.8 = (bf16[2,8,8,128]{3,2,1,0:T(8,128)(2,1)S(1)}, bf16[2,8,8,128]{3,2,1,0:T(8,128)(2,1)}, u32[]{:S(2)}) copy-start(bf16[2,8,8,128]{3,2,1,0:T(8,128)(2,1)} %param.16) | copy-start | bytes 98308
  133.2 63.5 %all-to-all-start = ((bf16[16,32,16,256]{3,2,1,0:T(8,128)(2,1)}), bf16[16,32,16,256]{3,2,1,0:T(8,128)(2,1)}, u32[]{:S(2)}, u32[]{:S(2)}) async-start(bf16[16,32,16,256]{3,2,1,0:T(8,128)(2,1)} %bitcast.59), calls=%async_computation | async-start | bytes 8388608 | tf_op jit(solution)/shard_map/all_to_all | solution.py:394
  208.2 24.1 %copy-start.7 = (bf16[2,128,512]{2,1,0:T(8,128)(2,1)S(1)}, bf16[2,128,512]{2,1,0:T(8,128)(2,1)}, u32[]{:S(2)}) copy-start(bf16[2,128,512]{2,1,0:T(8,128)(2,1)} %param.18) | copy-start | bytes 786436
  226.9 13.1 %all-to-all-start.2 = ((bf16[8,32,512]{2,1,0:T(8,128)(2,1)}), bf16[8,32,512]{2,1,0:T(8,128)(2,1)S(1)}, u32[]{:S(2)}, u32[]{:S(2)}) async-start(bf16[8,32,512]{2,1,0:T(8,128)(2,1)} %bitcast.13), calls=%async_computation.2 | async-start | bytes 524288 | tf_op jit(solution)/shard_map/all_to_all | solution.py:411
  240.4 32.2 %copy-start.1 = (bf16[8192,224]{0,1:T(8,128)(2,1)S(1)}, bf16[8192,224]{0,1:T(8,128)(2,1)}, u32[]{:S(2)}) copy-start(bf16[8192,224]{0,1:T(8,128)(2,1)} %param.21) | copy-start | bytes 11010052
  240.4 32.2 %copy-start.6 = (f32[8192]{0:T(1024)S(1)}, f32[8192]{0:T(1024)}, u32[]{:S(2)}) copy-start(f32[8192]{0:T(1024)} %param.20) | copy-start | bytes 98308
  272.5 6.4 %collective-permute-start = (bf16[8,256,512]{2,1,0:T(8,128)(2,1)S(1)}, bf16[8,256,512]{2,1,0:T(8,128)(2,1)S(1)}, u32[]{:S(2)}, u32[]{:S(2)}) collective-permute-start(bf16[8,256,512]{2,1,0:T(8,128)(2,1)S(1)} %bitcast.54), channel_id=1, source_target_pairs={{0,8},{8,0},{1,9},{9,1},{2,10},{10,2},{3,11},{11,3},{4,12},{12,4},... | collective-permute-start | bytes 6291464 | tf_op jit(solution)/shard_map/ppermute | solution.py:423
  272.6 2.0 copy-start.2
  274.6 4.3 %copy-start.3 = (bf16[8192,224]{0,1:T(8,128)(2,1)S(1)}, bf16[8192,224]{0,1:T(8,128)(2,1)}, u32[]{:S(2)}) copy-start(bf16[8192,224]{0,1:T(8,128)(2,1)} %param.22) | copy-start | bytes 11010052
  274.6 4.4 %copy-start.4 = (bf16[224,8192]{1,0:T(8,128)(2,1)S(1)}, bf16[224,8192]{1,0:T(8,128)(2,1)}, u32[]{:S(2)}) copy-start(bf16[224,8192]{1,0:T(8,128)(2,1)} %down_ref.3) | copy-start | bytes 11010052
  278.9 5.3 %copy-start.5 = (bf16[8,256,512]{2,1,0:T(8,128)(2,1)}, bf16[8,256,512]{2,1,0:T(8,128)(2,1)S(1)}, u32[]{:S(2)}) copy-start(bf16[8,256,512]{2,1,0:T(8,128)(2,1)S(1)} %collective-permute-done.x_ref) | copy-start | bytes 6291460
  284.3 4.5 %collective-permute-start.1 = (bf16[8,8,16,1024]{3,2,1,0:T(8,128)(2,1)S(1)}, bf16[8,8,16,1024]{3,2,1,0:T(8,128)(2,1)S(1)}, u32[]{:S(2)}, u32[]{:S(2)}) collective-permute-start(bf16[8,8,16,1024]{3,2,1,0:T(8,128)(2,1)S(1)} %get-tuple-element.14), channel_id=1, source_target_pairs={{0,8},{8,0},{1,9},{9,1},{2,10},{10,2},{3,11},{11,3},{4,12},{12,4},... | collective-permute-start | bytes 6291464 | tf_op jit(solution)/shard_map/ppermute | solution.py:433
  290.3 36.0 %all-to-all-start.4 = ((bf16[64,16,1024]{2,1,0:T(8,128)(2,1)}), bf16[64,16,1024]{2,1,0:T(8,128)(2,1)}, u32[]{:S(2)}, u32[]{:S(2)}) async-start(bf16[64,16,1024]{2,1,0:T(8,128)(2,1)} %bitcast.60), calls=%async_computation.4 | async-start | bytes 4194304 | tf_op jit(solution)/shard_map/all_to_all | solution.py:436

commit v4 on v3

v4 whole, which is shorter than its diff:
```python
import math

import jax
import jax.numpy as jnp
from jax import lax
from jax.experimental import pallas as pl
from jax.experimental.pallas import tpu as pltpu
from jax.sharding import Mesh, PartitionSpec as P

DP = ("yh", "x", "c")
CHIP_DP = ("yh", "x")
TENSOR = ("z", "yl")
CHIPS = ("yh", "x", "z", "yl")


def to_all(block, axes, count):
    copies = lax.optimization_barrier(jnp.broadcast_to(block[None], (count,) + block.shape))
    return lax.all_to_all(copies, axes, 0, 0, tiled=True)

MIB = 1024 * 1024
SMEM = pl.BlockSpec(memory_space=pltpu.SMEM)
VMEM = pl.BlockSpec(memory_space=pltpu.VMEM)
HBM = pl.BlockSpec(memory_space=pltpu.HBM)


def intake(pick, lens, received, fresh, query, n_copies):
    req_dev, n_rows, head_dim = query.shape
    n_steps = fresh.shape[0]
    _, page_size, width_two = received.shape
    max_pages = pick.shape[0] // req_dev
    pages = max_pages + 1
    group = n_rows // n_steps
    scale = 1.0 / math.sqrt(head_dim)
    ahead = 2

    def kernel(pick_ref, len_ref, recv_ref, fresh_ref, q_ref, cache_ref, mixed_ref, buf, heads, in_sems, out_sems):
        def start(r):
            def body(p, carry):
                pltpu.make_async_copy(
                    recv_ref.at[pick_ref[r * max_pages + p]], buf.at[r, p], in_sems.at[r]
                ).start()
                return carry

            lax.fori_loop(0, max_pages, body, 0, unroll=8)

        def copy_out(r):
            return pltpu.make_async_copy(buf.at[r], cache_ref.at[r], out_sems.at[r])

        for r in range(ahead):
            start(r)
        row_at = lax.broadcasted_iota(jnp.int32, (page_size, width_two), 0)
        for r in range(req_dev):
            if r + ahead < req_dev:
                start(r + ahead)
            pltpu.make_async_copy(
                recv_ref.at[pl.ds(0, max_pages)], buf.at[r, pl.ds(0, max_pages)], in_sems.at[r]
            ).wait()
            length = len_ref[r]
            full = length // page_size

            def clear(p, carry):
                buf[r, p] = jnp.zeros((page_size, width_two), buf.dtype)
                return carry

            lax.fori_loop(full + 1, pages, clear, 0)
            edge = buf[r, full].astype(jnp.float32)
            buf[r, full] = jnp.where(row_at < length % page_size, edge, 0.0).astype(buf.dtype)
            for s in range(n_steps):
                at = length + s
                page = buf[r, at // page_size].astype(jnp.float32)
                token = fresh_ref[s, r : r + 1, :]
                buf[r, at // page_size] = jnp.where(
                    row_at == at % page_size, token, page
                ).astype(buf.dtype)
            copy_out(r).start()
            tokens = buf[r].reshape(pages * page_size, width_two)
            scores = scale * lax.dot_general(
                q_ref[r],
                tokens[:, :head_dim],
                (((1,), (1,)), ((), ())),
                preferred_element_type=jnp.float32,
            )
            last = length + lax.broadcasted_iota(jnp.int32, scores.shape, 0) // group
            scores = jnp.where(
                lax.broadcasted_iota(jnp.int32, scores.shape, 1) <= last, scores, -jnp.inf
            )
            expo = jnp.exp(scores - jnp.max(scores, axis=1, keepdims=True))
            total = jnp.sum(expo, axis=1, keepdims=True)
            probs = (expo / total).astype(jnp.bfloat16)
            head_out = jnp.dot(probs, tokens[:, head_dim:], preferred_element_type=jnp.float32)
            for i in range(n_rows):
                heads[i, r : r + 1, :] = head_out[i : i + 1, :]
        for g in range(group):
            block = jnp.concatenate([heads[s * group + g] for s in range(n_steps)], axis=0)
            block = block.astype(mixed_ref.dtype)
            for k in range(n_copies):
                mixed_ref[k, :, g * head_dim : (g + 1) * head_dim] = block
        for r in range(req_dev):
            copy_out(r).wait()

    return pl.pallas_call(
        kernel,
        in_specs=[SMEM, SMEM, HBM, VMEM, VMEM],
        out_specs=[HBM, VMEM],
        out_shape=[
            jax.ShapeDtypeStruct((req_dev, pages, page_size, width_two), received.dtype),
            jax.ShapeDtypeStruct(
                (n_copies, n_steps * req_dev, group * head_dim), received.dtype
            ),
        ],
        scratch_shapes=[
            pltpu.VMEM((req_dev, pages, page_size, width_two), received.dtype),
            pltpu.VMEM((n_rows, req_dev, head_dim), jnp.float32),
            pltpu.SemaphoreType.DMA((req_dev,)),
            pltpu.SemaphoreType.DMA((req_dev,)),
        ],
        compiler_params=pltpu.CompilerParams(vmem_limit_bytes=10 * MIB),
        name="intake",
    )(pick, lens, received, fresh, query)


def feed_forward(hidden, gate_rows, up_rows, gain_row, w_down, n_tensor, rows_dev):
    blocks, rows, cols = hidden.shape
    units, width = w_down.shape
    cols_out = width // n_tensor
    chips = rows // rows_dev
    contract = (((1,), (1,)), ((), ()))

    def kernel(x_ref, gate_ref, up_ref, gain_ref, down_ref, out_ref, scaled):
        squares = 0.0
        for i in range(blocks):
            wide = x_ref[i].astype(jnp.float32)
            square = wide * wide
            squares += sum(square[:, k * 128 : (k + 1) * 128] for k in range(cols // 128))
            scaled[:, i * cols : (i + 1) * cols] = (
                wide * gain_ref[:, i * cols : (i + 1) * cols]
            ).astype(scaled.dtype)
        inverse = lax.rsqrt(jnp.sum(squares, axis=1, keepdims=True) * (1.0 / width) + 1e-05)
        gate = inverse * lax.dot_general(
            scaled[...], gate_ref[...], contract, preferred_element_type=jnp.float32
        )
        upper = inverse * lax.dot_general(
            scaled[...], up_ref[...], contract, preferred_element_type=jnp.float32
        )
        act = (gate / (1.0 + jnp.exp(-gate)) * upper).astype(jnp.bfloat16)
        for t in range(n_tensor):
            out = jnp.dot(
                act,
                down_ref[:, t * cols_out : (t + 1) * cols_out],
                preferred_element_type=jnp.float32,
            )
            out_ref[:, t] = out.astype(out_ref.dtype).reshape(chips, rows_dev, cols_out)

    return pl.pallas_call(
        kernel,
        in_specs=[VMEM] * 5,
        out_specs=VMEM,
        out_shape=jax.ShapeDtypeStruct((chips, n_tensor, rows_dev, cols_out), jnp.bfloat16),
        scratch_shapes=[pltpu.VMEM((rows, width), jnp.bfloat16)],
        compiler_params=pltpu.CompilerParams(vmem_limit_bytes=24 * MIB),
        name="feed_forward",
    )(hidden, gate_rows, up_rows, gain_row, w_down)


def gather_pages(rows, pool, parts):
    count = rows.shape[0]
    span = count // parts
    ahead = 3

    def kernel(rows_ref, pool_ref, out_ref, buf, in_sems, out_sems):
        def start(d):
            def body(k, carry):
                at = d * span + k
                pltpu.make_async_copy(
                    pool_ref.at[rows_ref[at]], buf.at[at], in_sems.at[d]
                ).start()
                return carry

            lax.fori_loop(0, span, body, 0, unroll=8)

        def copy_out(d):
            part = pl.ds(d * span, span)
            return pltpu.make_async_copy(buf.at[part], out_ref.at[part], out_sems.at[d])

        for d in range(ahead):
            start(d)
        for d in range(parts):
            if d + ahead < parts:
                start(d + ahead)
            part = pl.ds(d * span, span)
            pltpu.make_async_copy(pool_ref.at[part], buf.at[part], in_sems.at[d]).wait()
            copy_out(d).start()
        for d in range(parts):
            copy_out(d).wait()

    return pl.pallas_call(
        kernel,
        in_specs=[SMEM, HBM],
        out_specs=HBM,
        out_shape=pltpu.HBM((count,) + pool.shape[1:], pool.dtype),
        scratch_shapes=[
            pltpu.VMEM((count,) + pool.shape[1:], pool.dtype),
            pltpu.SemaphoreType.DMA((parts,)),
            pltpu.SemaphoreType.DMA((parts,)),
        ],
        compiler_params=pltpu.CompilerParams(vmem_limit_bytes=10 * MIB),
        name="gather_pages",
    )(rows, pltpu.with_memory_space_constraint(pool, pltpu.HBM))


def add_cores(ours, from_core):
    chips = ours.shape[0]

    def kernel(a_ref, b_ref, out_ref, buf, sems):
        def copy(i):
            return pltpu.make_async_copy(buf.at[i], out_ref.at[i], sems.at[i])

        for i in range(chips):
            buf[i] = (a_ref[i].astype(jnp.float32) + b_ref[i].astype(jnp.float32)).astype(buf.dtype)
            copy(i).start()
        for i in range(chips):
            copy(i).wait()

    return pl.pallas_call(
        kernel,
        in_specs=[VMEM, VMEM],
        out_specs=HBM,
        out_shape=pltpu.HBM(ours.shape, ours.dtype),
        scratch_shapes=[pltpu.VMEM(ours.shape, ours.dtype), pltpu.SemaphoreType.DMA((chips,))],
        compiler_params=pltpu.CompilerParams(vmem_limit_bytes=12 * MIB),
        name="add_cores",
    )(ours, from_core)


def page_plan(page_loc, lengths, placement, dev_dp, dev_tensor, n_dp, pslots, page_size):
    n_req = lengths.shape[0]
    max_pages = page_loc.shape[2]
    req_dev = n_req // n_dp
    entries = req_dev * max_pages
    capacity = pslots // n_dp
    loc_head = lax.dynamic_index_in_dim(page_loc, dev_tensor, 0, keepdims=False)
    slot_hot = placement[None, :] == jnp.arange(n_req, dtype=jnp.int32)[:, None]
    len_slot = jnp.sum(jnp.where(slot_hot, lengths[None, :], 0), axis=1)
    loc_slot = jnp.dot(
        slot_hot.astype(jnp.float32), loc_head.astype(jnp.float32), precision=lax.Precision.HIGHEST
    ).astype(jnp.int32)
    pages_slot = (len_slot + page_size - 1) // page_size
    live = jnp.arange(max_pages, dtype=jnp.int32)[None, :] < pages_slot[:, None]
    source = jnp.where(live, loc_slot // pslots, n_dp).reshape(n_dp, entries)
    row = (loc_slot % pslots).reshape(n_dp, entries)
    before = (
        jnp.arange(entries, dtype=jnp.int32)[:, None] < jnp.arange(entries, dtype=jnp.int32)[None, :]
    ).astype(jnp.bfloat16)
    mine_out = source == dev_dp
    rank_out = jnp.dot(
        mine_out.astype(jnp.bfloat16), before, preferred_element_type=jnp.float32
    ).astype(jnp.int32)
    rank_out = jnp.where(mine_out, rank_out, capacity)
    hit = rank_out[:, None, :] == jnp.arange(capacity, dtype=jnp.int32)[None, :, None]
    send_rows = jnp.sum(jnp.where(hit, row[:, None, :], 0), axis=2)
    slot = jnp.arange(pslots, dtype=jnp.int32).reshape(n_dp, capacity)
    used = jnp.sum(mine_out.astype(jnp.int32), axis=1, keepdims=True)
    send_rows = jnp.where(slot % capacity < used, send_rows, slot)
    my_source = lax.dynamic_index_in_dim(source, dev_dp, 0, keepdims=False)
    source_hot = my_source[None, :] == jnp.arange(n_dp, dtype=jnp.int32)[:, None]
    rank_in = jnp.dot(
        source_hot.astype(jnp.bfloat16), before, preferred_element_type=jnp.float32
    ).astype(jnp.int32)
    my_rank = jnp.sum(jnp.where(source_hot, rank_in, 0), axis=0)
    pick = jnp.where(
        my_source < n_dp, my_source * capacity + my_rank, jnp.arange(entries, dtype=jnp.int32)
    )
    my_len = lax.dynamic_slice_in_dim(len_slot, dev_dp * req_dev, req_dev)
    return send_rows, pick, my_len


def per_device(
    kv_pool,
    page_loc,
    lengths,
    placement,
    queries,
    new_kv,
    resid_in,
    w_out,
    ffn_gain,
    w_gate,
    w_up,
    w_down,
):
    n_dp = lax.axis_size(DP)
    n_tensor = lax.axis_size(TENSOR)
    dev_dp = lax.axis_index(DP)
    dev_chip = lax.axis_index(CHIP_DP)
    dev_tensor = lax.axis_index(TENSOR)
    core = lax.axis_index("c")
    pslots, _, page_size, width_two = kv_pool.shape
    head_dim = width_two // 2
    n_req = lengths.shape[0]
    req_dev = n_req // n_dp
    max_pages = page_loc.shape[2]
    max_len = max_pages * page_size
    cache_len = max_len + page_size
    n_steps = queries.shape[0]
    hq_dev = queries.shape[2]
    width = ffn_gain.shape[0]
    rows_dev = n_steps * req_dev
    chips_dp = n_dp // 2
    rows_core = n_steps * n_req // 2
    capacity = pslots // n_dp

    send_rows, pick, my_len = page_plan(
        page_loc, lengths, placement, dev_dp, dev_tensor, n_dp, pslots, page_size
    )
    outgoing = gather_pages(
        send_rows.reshape(-1), kv_pool.reshape(pslots, page_size, width_two), n_dp
    ).reshape(n_dp, capacity, page_size, width_two)
    received = lax.all_to_all(outgoing, DP, 0, 0, tiled=True)
    query = jnp.transpose(queries, (1, 0, 2, 3)).reshape(req_dev, n_steps * hq_dev, head_dim)
    cache, mixed_copies = intake(
        pick,
        my_len,
        received.reshape(pslots, page_size, width_two),
        new_kv.reshape(n_steps, req_dev, width_two).astype(jnp.float32),
        query,
        chips_dp,
    )

    cols_dev = width // n_dp
    cols_chip = 2 * cols_dev
    swap = [(0, 1), (1, 0)]

    def both(own, other):
        return jnp.where(
            core == 0,
            jnp.concatenate([own, other], axis=-1),
            jnp.concatenate([other, own], axis=-1),
        )

    w_both = both(w_out, lax.ppermute(w_out, "c", swap))
    resid_rows = jnp.transpose(
        resid_in.reshape(n_steps, chips_dp, 2, req_dev, cols_dev), (2, 1, 0, 3, 4)
    ).reshape(2, n_tensor, rows_core // n_tensor, cols_dev)

    def resid_of(at_core):
        return lax.dynamic_slice(
            resid_rows, (at_core, dev_tensor, 0, 0), (1, 1) + resid_rows.shape[2:]
        )[0, 0]

    resid_blk = both(resid_of(core), lax.ppermute(resid_of(1 - core), "c", swap))
    mixed_rows = lax.all_to_all(mixed_copies, CHIP_DP, 0, 0, tiled=True).reshape(
        rows_core, hq_dev * head_dim
    )
    partial_out = jnp.dot(mixed_rows, w_both, preferred_element_type=jnp.float32).astype(
        jnp.bfloat16
    )
    rows_blk = rows_core // n_tensor
    parts = lax.all_to_all(
        partial_out.reshape(n_tensor, rows_blk, cols_chip), TENSOR, 0, 0, tiled=True
    )
    hidden_blk = (
        resid_blk.astype(jnp.float32) + jnp.sum(parts.astype(jnp.float32), axis=0)
    ).astype(jnp.bfloat16)
    own_rows = to_all(hidden_blk, CHIPS, chips_dp * n_tensor).reshape(
        chips_dp, rows_core, cols_chip
    )
    other_rows = lax.ppermute(own_rows, "c", swap)
    gate_rows = jnp.swapaxes(w_gate, 0, 1)
    up_rows = jnp.swapaxes(w_up, 0, 1)
    gain_row = ffn_gain.reshape(1, width)
    width_out = width // n_tensor

    def block_of(rows):
        return feed_forward(rows, gate_rows, up_rows, gain_row, w_down, n_tensor, rows_dev)

    ours = block_of(own_rows)
    other_rows, ours = lax.optimization_barrier((other_rows, ours))
    theirs = block_of(other_rows)
    from_core = lax.ppermute(theirs, "c", swap)
    chip_sum = add_cores(ours, from_core).reshape(chips_dp * n_tensor, rows_dev, width_out)
    pieces = lax.all_to_all(chip_sum, CHIPS, 0, 0, tiled=True)
    ffn_part = jnp.sum(pieces.astype(jnp.float32), axis=0)
    own_hidden = lax.dynamic_slice(
        own_rows, (dev_tensor, dev_chip * rows_dev, 0), (1, rows_dev, cols_chip)
    )[0]
    block_out = (own_hidden.astype(jnp.float32) + ffn_part).astype(jnp.bfloat16)
    return (block_out.reshape(n_steps, req_dev, width_out), cache.reshape(1, req_dev, cache_len, width_two))


def solution(mesh):
    fine = Mesh(mesh.devices.reshape(2, 4, 2, 4, 2), ("yh", "x", "c", "z", "yl"))
    placed = (
        P(DP, TENSOR, None, None),
        P(),
        P(),
        P(),
        P(None, DP, TENSOR, None),
        P(None, DP, TENSOR, None),
        P(None, None, DP),
        P(TENSOR, DP),
        P(),
        P(None, DP + TENSOR),
        P(None, DP + TENSOR),
        P(DP + TENSOR, None),
    )
    return jax.shard_map(
        per_device,
        mesh=fine,
        in_specs=placed,
        out_specs=(P(None, DP, TENSOR), P(TENSOR, DP, None, None)),
        check_vma=False,
    )
```

time: 331 us -> 200 us (0.60)
  Pallas kernels: 152 us -> 23.8 us
  blocking collectives: 49.7 us -> 30.8 us
  waiting for transfers between devices: 95.6 us -> 105 us
  starting transfers between devices: 19.7 us -> 26.6 us
    pallas_call x4 -> x3, Pallas kernels: 139 us -> 13.5 us  [the longest x1 6.82 us: gather_pages(): pl.pallas_call(kernel, in_specs=[SMEM, HBM], out_specs=HBM, out_shape=plt...]
    all_to_all x1 -> x0, blocking collectives: 17.5 us -> none  [per_device(): lax.all_to_all(mixed_copies, CDP, 0, 0, tiled=True)]
    all_to_all x1 -> x2, waiting for transfers between devices: 7.7 us -> 15.9 us  [the longest x1 8.78 us: per_device(): lax.all_to_all(mixed_copies, CHIP_DP, 0, 0, tiled=True)]
    all_to_all x1 -> x2, starting transfers between devices: 5.39 us -> 11.8 us  [the longest x1 6.38 us: per_device(): lax.all_to_all(mixed_copies, CHIP_DP, 0, 0, tiled=True)]
  transfers between devices with their start and end apart: 5 -> 8, of which waited for: 4 -> 5; matrix products, arithmetic and copies ran while one was open for 0% -> 0% of each run, Pallas kernels for 2% -> 6%
where the time goes in v4:
time: 200 us; the launch traced here: 199 us
  waiting for transfers between devices  105 us (52%)
  blocking collectives  30.8 us (15%)
  starting transfers between devices  26.6 us (13%)
  Pallas kernels  23.8 us (12%)
  local copies, waits for them, and re-layouts  5.23 us (3%)
  other arithmetic  3.93 us (2%)
  matrix products  2.8 us (1%)
    all_to_all x1, waiting for transfers between devices, per_device(): received = lax.all_to_all(outgoing, DP, 0, 0, tiled=True)  55.6 us
    all_to_all x1, blocking collectives, to_all(): return lax.all_to_all(copies, axes, 0, 0, tiled=True)  30.8 us
    all_to_all x1, waiting for transfers between devices, per_device(): pieces = lax.all_to_all(chip_sum, CHIPS, 0, 0, tiled=True)  29.6 us
    pallas_call x1, Pallas kernels, intake(): pl.pallas_call(kernel, in_specs=[SMEM, SMEM, HBM, VMEM, VMEM], out_specs=...  8.92 us
    all_to_all x1, waiting for transfers between devices, per_device(): lax.all_to_all(mixed_copies, CHIP_DP, 0, 0, tiled=True)  8.78 us
    all_to_all x1, starting transfers between devices, per_device(): received = lax.all_to_all(outgoing, DP, 0, 0, tiled=True)  7.35 us
    all_to_all x1, waiting for transfers between devices, per_device(): lax.all_to_all(partial_out.reshape(n_tensor, rows_blk, cols_chip), TENSOR...  7.13 us
    pallas_call x1, Pallas kernels, gather_pages(): pl.pallas_call(kernel, in_specs=[SMEM, HBM], out_specs=HBM, out_shape=plt...  6.82 us
  transfers between devices with their start and end apart: 8, of which 5 were waited for; matrix products, arithmetic and copies ran while one was open for 0% of the time, Pallas kernels for 6%

profile of v4, /device:TPU:0, one launch (start us, length us, event | category | flops | bytes accessed | tf_op | source)
XLA Modules:
  0.0 199.0 jit_solution(14282152866067171397)
XLA Ops:
  0.6 0.0 copy-start
  0.7 0.8 select_reduce_fusion.1
  1.5 0.1 reshape.138
  1.5 1.0 convert_reduce_fusion.2
  2.6 0.1 reduce_sum.68
  2.7 0.1 reduce_sum.69
  2.8 0.1 lt.98
  2.9 0.1 lt.99
  2.9 0.1 copy.26
  3.0 0.1 reshape.135
  3.1 0.2 fusion.8
  3.3 0.1 copy.27
  3.4 0.1 broadcast_in_dim.60
  3.5 0.4 select_reduce_fusion
  3.9 0.1 reduce_sum.71
  4.0 6.8 %gather_pages.1 = bf16[512,16,256]{2,1,0:T(8,128)(2,1)} custom-call(s32[512]{0:T(512)S(1)} %fusion.24.rows_ref, bf16[512,16,256]{2,1,0:T(8,128)(2,1)} %bitcast.54), custom_call_target="tpu_custom_call" | custom-call | tf_op jit(solution)/shard_map/gather_pages/pallas_call | solution.py:196
  10.8 0.0 copy-start.8
  10.8 0.0 copy-start.7
  10.8 7.3 %all-to-all-start = ((bf16[16,32,16,256]{3,2,1,0:T(8,128)(2,1)}), bf16[16,32,16,256]{3,2,1,0:T(8,128)(2,1)}, u32[]{:S(2)}, u32[]{:S(2)}) async-start(bf16[16,32,16,256]{3,2,1,0:T(8,128)(2,1)} %bitcast.52), calls=%async_computation | async-start | bytes 8388608 | tf_op jit(solution)/shard_map/all_to_all | solution.py:318
  18.2 0.0 copy-done.8
  18.2 0.4 collective-permute-start.1
  18.6 0.1 dynamic_slice.24.len_ref
  18.7 0.2 fusion.10
  18.9 0.0 copy-done.7
  18.9 0.0 copy-done
  19.0 55.6 %all-to-all-done = bf16[16,32,16,256]{3,2,1,0:T(8,128)(2,1)} async-done(((bf16[16,32,16,256]{3,2,1,0:T(8,128)(2,1)}), bf16[16,32,16,256]{3,2,1,0:T(8,128)(2,1)}, u32[]{:S(2)}, u32[]{:S(2)}) %all-to-all-start) | async-done | bytes 4194336 | tf_op jit(solution)/shard_map/all_to_all | solution.py:318
  74.5 8.9 %intake.1 = (bf16[8,65,16,256]{3,2,1,0:T(8,128)(2,1)}, bf16[8,16,1024]{2,1,0:T(8,128)(2,1)}) custom-call(s32[512]{0:T(512)S(1)} %iota_select_fusion.pick_ref, s32[8]{0:T(128)S(1)} %dynamic_slice.24.len_ref, bf16[512,16,256]{2,1,0:T(8,128)(2,1)} %bitcast.9.recv_ref, f32[2,8,256]{2,1,0:T(8,128)S(1)} %bitcast_convert_fusion.fresh_ref, ...), custom_call_target="tpu_custom_call" | custom-call | tf_op jit(solution)/shard_map/intake/pallas_call | solution.py:101
  83.4 6.4 %all-to-all-start.1 = ((bf16[8,16,1024]{2,1,0:T(8,128)(2,1)}), bf16[8,16,1024]{2,1,0:T(8,128)(2,1)S(1)}, u32[]{:S(2)}, u32[]{:S(2)}) async-start(bf16[8,16,1024]{2,1,0:T(8,128)(2,1)} %get-tuple-element.6), calls=%async_computation.1 | async-start | bytes 524288 | tf_op jit(solution)/shard_map/all_to_all | solution.py:351
  89.8 0.0 collective-permute-done.1
  89.8 8.8 %all-to-all-done.1 = bf16[8,16,1024]{2,1,0:T(8,128)(2,1)S(1)} async-done(((bf16[8,16,1024]{2,1,0:T(8,128)(2,1)}), bf16[8,16,1024]{2,1,0:T(8,128)(2,1)S(1)}, u32[]{:S(2)}, u32[]{:S(2)}) %all-to-all-start.1) | async-done | bytes 262176 | tf_op jit(solution)/shard_map/all_to_all | solution.py:351
  98.6 0.0 copy-start.6
  98.6 1.4 fusion.7
  100.0 5.4 %all-to-all-start.2 = ((bf16[8,16,1024]{2,1,0:T(8,128)(2,1)}), bf16[8,16,1024]{2,1,0:T(8,128)(2,1)S(1)}, u32[]{:S(2)}, u32[]{:S(2)}) async-start(bf16[8,16,1024]{2,1,0:T(8,128)(2,1)} %bitcast.15), calls=%async_computation.2 | async-start | bytes 524288 | tf_op jit(solution)/shard_map/all_to_all | solution.py:358
  105.4 0.0 copy-done.6
  105.5 0.1 collective-permute-start
  105.6 7.1 %all-to-all-done.2 = bf16[8,16,1024]{2,1,0:T(8,128)(2,1)S(1)} async-done(((bf16[8,16,1024]{2,1,0:T(8,128)(2,1)}), bf16[8,16,1024]{2,1,0:T(8,128)(2,1)S(1)}, u32[]{:S(2)}, u32[]{:S(2)}) %all-to-all-start.2) | async-done | bytes 262176 | tf_op jit(solution)/shard_map/all_to_all | solution.py:358
  112.7 0.0 collective-permute-done
  112.8 0.2 broadcast_in_dim.63
  113.0 0.0 copy-start.1
  113.0 0.0 copy-start.5
  113.1 30.8 %all_to_all.25 = bf16[64,16,1024]{2,1,0:T(8,128)(2,1)S(1)} all-to-all(bf16[64,16,1024]{2,1,0:T(8,128)(2,1)S(1)} %broadcast_in_dim.63), channel_id=1, replica_groups=mesh['yh'=2,'x'=4,'c'=2,'z'=4,'yl'=2] {'yh','x','z','yl'}, dimensions={0} | all-to-all | bytes 4194304 | tf_op jit(solution)/shard_map/all_to_all | solution.py:18
  143.8 0.0 collective-permute-start.2
  143.8 0.0 copy-done.1
  143.8 0.0 copy-done.5
  143.8 0.0 copy-start.2
  143.9 2.0 %copy-done.2 = bf16[8192,224]{0,1:T(8,128)(2,1)S(1)} copy-done((bf16[8192,224]{0,1:T(8,128)(2,1)S(1)}, bf16[8192,224]{0,1:T(8,128)(2,1)}, u32[]{:S(2)}) %copy-start.2) | copy-done | bytes 3670040
  145.9 0.0 copy-start.3
  145.9 2.0 %copy-done.3 = bf16[224,8192]{1,0:T(8,128)(2,1)S(1)} copy-done((bf16[224,8192]{1,0:T(8,128)(2,1)S(1)}, bf16[224,8192]{1,0:T(8,128)(2,1)}, u32[]{:S(2)}) %copy-start.3) | copy-done | bytes 3670040
  147.9 0.0 copy-start.4
  147.9 3.3 %feed_forward.2.a_ref = bf16[8,8,16,1024]{3,2,1,0:T(8,128)(2,1)S(1)} custom-call(bf16[8,128,1024]{2,1,0:T(8,128)(2,1)S(1)} %bitcast.48, bf16[224,8192]{1,0:T(8,128)(2,1)S(1)} %bitcast.43, bf16[224,8192]{1,0:T(8,128)(2,1)S(1)} %bitcast.45, f32[1,8192]{1,0:T(1,128)S(1)} %bitcast.50, bf16[224,8192]{1,0:T(8,128)(2,1)S(1)} %copy-done.3), custom_call_target="tpu_custom_call" | custom-call | tf_op jit(solution)/shard_map/feed_forward/pallas_call | solution.py:154
  151.3 0.0 collective-permute-done.2.x_ref
  151.3 0.0 copy-done.4
  151.3 3.3 %feed_forward.3 = bf16[8,8,16,1024]{3,2,1,0:T(8,128)(2,1)S(1)} custom-call(bf16[8,128,1024]{2,1,0:T(8,128)(2,1)S(1)} %collective-permute-done.2.x_ref, bf16[224,8192]{1,0:T(8,128)(2,1)S(1)} %bitcast.44, bf16[224,8192]{1,0:T(8,128)(2,1)S(1)} %bitcast.46, f32[1,8192]{1,0:T(1,128)S(1)} %bitcast.51, bf16[224,8192]{1,0:T(8,128)(2,1)S(1)} %copy-done.4), custom_call_target="tpu_custom_call" | custom-call | tf_op jit(solution)/shard_map/feed_forward/pallas_call | solution.py:154
  154.6 0.6 collective-permute-start.3
  155.2 3.8 %collective-permute-done.3.b_ref = bf16[8,8,16,1024]{3,2,1,0:T(8,128)(2,1)S(1)} collective-permute-done((bf16[8,8,16,1024]{3,2,1,0:T(8,128)(2,1)S(1)}, bf16[8,8,16,1024]{3,2,1,0:T(8,128)(2,1)S(1)}, u32[]{:S(2)}, u32[]{:S(2)}) %collective-permute-start.3) | collective-permute-done | bytes 2097184 | tf_op jit(solution)/shard_map/ppermute | solution.py:379
  159.0 1.4 add_cores.1
  160.4 6.3 %all-to-all-start.4 = ((bf16[64,16,1024]{2,1,0:T(8,128)(2,1)}), bf16[64,16,1024]{2,1,0:T(8,128)(2,1)}, u32[]{:S(2)}, u32[]{:S(2)}) async-start(bf16[64,16,1024]{2,1,0:T(8,128)(2,1)} %bitcast.53), calls=%async_computation.4 | async-start | bytes 4194304 | tf_op jit(solution)/shard_map/all_to_all | solution.py:381
  166.8 29.6 %all-to-all-done.4 = bf16[64,16,1024]{2,1,0:T(8,128)(2,1)} async-done(((bf16[64,16,1024]{2,1,0:T(8,128)(2,1)}), bf16[64,16,1024]{2,1,0:T(8,128)(2,1)}, u32[]{:S(2)}, u32[]{:S(2)}) %all-to-all-start.4) | async-done | bytes 2097184 | tf_op jit(solution)/shard_map/all_to_all | solution.py:381
  196.4 2.0 convert_reduce_fusion
  198.3 0.6 fusion.11
  (11 shorter events, 0.1 us)
Async XLA Ops:
  0.6 18.3 %copy-start = (bf16[2,8,8,128]{3,2,1,0:T(8,128)(2,1)S(1)}, bf16[2,8,8,128]{3,2,1,0:T(8,128)(2,1)}, u32[]{:S(2)}) copy-start(bf16[2,8,8,128]{3,2,1,0:T(8,128)(2,1)} %param.16) | copy-start | bytes 98308
  10.8 7.4 %copy-start.8 = (bf16[1024,512]{1,0:T(8,128)(2,1)S(1)}, bf16[1024,512]{1,0:T(8,128)(2,1)}, u32[]{:S(2)}) copy-start(bf16[1024,512]{1,0:T(8,128)(2,1)} %param.19) | copy-start | bytes 3145732
  10.8 8.1 %copy-start.7 = (bf16[2,8,1,256]{3,1,2,0:T(8,128)(2,1)S(1)}, bf16[2,8,1,256]{3,1,2,0:T(8,128)(2,1)}, u32[]{:S(2)}) copy-start(bf16[2,8,1,256]{3,1,2,0:T(8,128)(2,1)} %param.17) | copy-start | bytes 24580
  10.8 63.7 %all-to-all-start = ((bf16[16,32,16,256]{3,2,1,0:T(8,128)(2,1)}), bf16[16,32,16,256]{3,2,1,0:T(8,128)(2,1)}, u32[]{:S(2)}, u32[]{:S(2)}) async-start(bf16[16,32,16,256]{3,2,1,0:T(8,128)(2,1)} %bitcast.52), calls=%async_computation | async-start | bytes 8388608 | tf_op jit(solution)/shard_map/all_to_all | solution.py:318
  18.2 71.6 %collective-permute-start.1 = (bf16[1024,512]{1,0:T(8,128)(2,1)S(1)}, bf16[1024,512]{1,0:T(8,128)(2,1)S(1)}, u32[]{:S(2)}, u32[]{:S(2)}) collective-permute-start(bf16[1024,512]{1,0:T(8,128)(2,1)S(1)} %copy-done.8), channel_id=1, source_target_pairs={{0,8},{8,0},{1,9},{9,1},{2,10},{10,2},{3,11},{11,3},{4,12},{12,4},... | collective-permute-start | bytes 3145736 | tf_op jit(solution)/shard_map/ppermute | solution.py:340
  83.4 15.2 %all-to-all-start.1 = ((bf16[8,16,1024]{2,1,0:T(8,128)(2,1)}), bf16[8,16,1024]{2,1,0:T(8,128)(2,1)S(1)}, u32[]{:S(2)}, u32[]{:S(2)}) async-start(bf16[8,16,1024]{2,1,0:T(8,128)(2,1)} %get-tuple-element.6), calls=%async_computation.1 | async-start | bytes 524288 | tf_op jit(solution)/shard_map/all_to_all | solution.py:351
  98.6 6.8 %copy-start.6 = (bf16[2,128,512]{2,1,0:T(8,128)(2,1)S(1)}, bf16[2,128,512]{2,1,0:T(8,128)(2,1)}, u32[]{:S(2)}) copy-start(bf16[2,128,512]{2,1,0:T(8,128)(2,1)} %param.18) | copy-start | bytes 786436
  100.0 12.7 %all-to-all-start.2 = ((bf16[8,16,1024]{2,1,0:T(8,128)(2,1)}), bf16[8,16,1024]{2,1,0:T(8,128)(2,1)S(1)}, u32[]{:S(2)}, u32[]{:S(2)}) async-start(bf16[8,16,1024]{2,1,0:T(8,128)(2,1)} %bitcast.15), calls=%async_computation.2 | async-start | bytes 524288 | tf_op jit(solution)/shard_map/all_to_all | solution.py:358
  105.5 7.3 %collective-permute-start = (bf16[16,512]{1,0:T(8,128)(2,1)S(1)}, bf16[16,512]{1,0:T(8,128)(2,1)S(1)}, u32[]{:S(2)}, u32[]{:S(2)}) collective-permute-start(bf16[16,512]{1,0:T(8,128)(2,1)S(1)} %get-tuple-element.13), channel_id=1, source_target_pairs={{0,8},{8,0},{1,9},{9,1},{2,10},{10,2},{3,11},{11,3},{4,12},{12,4},... | collective-permute-start | bytes 49160 | tf_op jit(solution)/shard_map/ppermute | solution.py:350
  113.0 30.8 %copy-start.1 = (bf16[8192,224]{0,1:T(8,128)(2,1)S(1)}, bf16[8192,224]{0,1:T(8,128)(2,1)}, u32[]{:S(2)}) copy-start(bf16[8192,224]{0,1:T(8,128)(2,1)} %param.21) | copy-start | bytes 11010052
  113.0 30.8 %copy-start.5 = (f32[8192]{0:T(1024)S(1)}, f32[8192]{0:T(1024)}, u32[]{:S(2)}) copy-start(f32[8192]{0:T(1024)} %param.20) | copy-start | bytes 98308
  143.8 7.4 %collective-permute-start.2 = (bf16[8,128,1024]{2,1,0:T(8,128)(2,1)S(1)}, bf16[8,128,1024]{2,1,0:T(8,128)(2,1)S(1)}, u32[]{:S(2)}, u32[]{:S(2)}) collective-permute-start(bf16[8,128,1024]{2,1,0:T(8,128)(2,1)S(1)} %bitcast.47), channel_id=1, source_target_pairs={{0,8},{8,0},{1,9},{9,1},{2,10},{10,2},{3,11},{11,3},{4,12},{12,4},... | collective-permute-start | bytes 6291464 | tf_op jit(solution)/shard_map/ppermute | solution.py:367
  143.8 2.0 %copy-start.2 = (bf16[8192,224]{0,1:T(8,128)(2,1)S(1)}, bf16[8192,224]{0,1:T(8,128)(2,1)}, u32[]{:S(2)}) copy-start(bf16[8192,224]{0,1:T(8,128)(2,1)} %param.22) | copy-start | bytes 11010052
  145.9 2.0 %copy-start.3 = (bf16[224,8192]{1,0:T(8,128)(2,1)S(1)}, bf16[224,8192]{1,0:T(8,128)(2,1)}, u32[]{:S(2)}) copy-start(bf16[224,8192]{1,0:T(8,128)(2,1)} %down_ref.3) | copy-start | bytes 11010052
  147.9 3.3 %copy-start.4 = (bf16[224,8192]{1,0:T(8,128)(2,1)S(1)}, bf16[224,8192]{1,0:T(8,128)(2,1)}, u32[]{:S(2)}) copy-start(bf16[224,8192]{1,0:T(8,128)(2,1)} %down_ref.3) | copy-start | bytes 11010052
  154.6 4.4 %collective-permute-start.3 = (bf16[8,8,16,1024]{3,2,1,0:T(8,128)(2,1)S(1)}, bf16[8,8,16,1024]{3,2,1,0:T(8,128)(2,1)S(1)}, u32[]{:S(2)}, u32[]{:S(2)}) collective-permute-start(bf16[8,8,16,1024]{3,2,1,0:T(8,128)(2,1)S(1)} %feed_forward.3), channel_id=1, source_target_pairs={{0,8},{8,0},{1,9},{9,1},{2,10},{10,2},{3,11},{11,3},{4,12},{12,4},... | collective-permute-start | bytes 6291464 | tf_op jit(solution)/shard_map/ppermute | solution.py:379
  160.4 35.9 %all-to-all-start.4 = ((bf16[64,16,1024]{2,1,0:T(8,128)(2,1)}), bf16[64,16,1024]{2,1,0:T(8,128)(2,1)}, u32[]{:S(2)}, u32[]{:S(2)}) async-start(bf16[64,16,1024]{2,1,0:T(8,128)(2,1)} %bitcast.53), calls=%async_computation.4 | async-start | bytes 4194304 | tf_op jit(solution)/shard_map/all_to_all | solution.py:381

commit v5 on v4

--- a/solution.py
+++ b/solution.py
@@ -31,30 +31,28 @@
     pages = max_pages + 1
     group = n_rows // n_steps
     scale = 1.0 / math.sqrt(head_dim)
-    ahead = 2
-
-    def kernel(pick_ref, len_ref, recv_ref, fresh_ref, q_ref, cache_ref, mixed_ref, buf, heads, in_sems, out_sems):
-        def start(r):
-            def body(p, carry):
-                pltpu.make_async_copy(
-                    recv_ref.at[pick_ref[r * max_pages + p]], buf.at[r, p], in_sems.at[r]
-                ).start()
-                return carry
-
-            lax.fori_loop(0, max_pages, body, 0, unroll=8)
+    parts = 8
+
+    def kernel(pick_ref, len_ref, recv_ref, fresh_ref, q_ref, cache_ref, mixed_ref, recv_buf, buf, heads, in_sems, out_sems):
+        def copy_in(i):
+            part = pl.ds(i * (recv_ref.shape[0] // parts), recv_ref.shape[0] // parts)
+            return pltpu.make_async_copy(recv_ref.at[part], recv_buf.at[part], in_sems.at[i])
 
         def copy_out(r):
             return pltpu.make_async_copy(buf.at[r], cache_ref.at[r], out_sems.at[r])
 
-        for r in range(ahead):
-            start(r)
+        for i in range(parts):
+            copy_in(i).start()
+        for i in range(parts):
+            copy_in(i).wait()
         row_at = lax.broadcasted_iota(jnp.int32, (page_size, width_two), 0)
         for r in range(req_dev):
-            if r + ahead < req_dev:
-                start(r + ahead)
-            pltpu.make_async_copy(
-                recv_ref.at[pl.ds(0, max_pages)], buf.at[r, pl.ds(0, max_pages)], in_sems.at[r]
-            ).wait()
+
+            def move(p, carry):
+                buf[r, p] = recv_buf[pick_ref[r * max_pages + p]]
+                return carry
+
+            lax.fori_loop(0, max_pages, move, 0, unroll=16)
             length = len_ref[r]
             full = length // page_size
 
@@ -73,6 +71,8 @@
                     row_at == at % page_size, token, page
                 ).astype(buf.dtype)
             copy_out(r).start()
+        for r in range(req_dev):
+            length = len_ref[r]
             tokens = buf[r].reshape(pages * page_size, width_two)
             scores = scale * lax.dot_general(
                 q_ref[r],
@@ -109,14 +109,15 @@
             ),
         ],
         scratch_shapes=[
+            pltpu.VMEM(received.shape, received.dtype),
             pltpu.VMEM((req_dev, pages, page_size, width_two), received.dtype),
             pltpu.VMEM((n_rows, req_dev, head_dim), jnp.float32),
-            pltpu.SemaphoreType.DMA((req_dev,)),
+            pltpu.SemaphoreType.DMA((parts,)),
             pltpu.SemaphoreType.DMA((req_dev,)),
         ],
-        compiler_params=pltpu.CompilerParams(vmem_limit_bytes=10 * MIB),
+        compiler_params=pltpu.CompilerParams(vmem_limit_bytes=16 * MIB),
         name="intake",
-    )(pick, lens, received, fresh, query)
+    )(pick, lens, pltpu.with_memory_space_constraint(received, pltpu.HBM), fresh, query)
 
 
 def feed_forward(hidden, gate_rows, up_rows, gain_row, w_down, n_tensor, rows_dev):
@@ -125,9 +126,23 @@
     cols_out = width // n_tensor
     chips = rows // rows_dev
     contract = (((1,), (1,)), ((), ()))
-
-    def kernel(x_ref, gate_ref, up_ref, gain_ref, down_ref, out_ref, scaled):
+    parts = 4
+    span = width // parts
+
+    def kernel(x_ref, gate_hbm, up_hbm, gain_ref, down_hbm, out_ref, scaled, gate_buf, up_buf, down_buf, sems):
+        def copy(m, i):
+            source, buffer = [(gate_hbm, gate_buf), (up_hbm, up_buf), (down_hbm, down_buf)][m]
+            part = pl.ds(i * span, span)
+            return pltpu.make_async_copy(source.at[:, part], buffer.at[:, part], sems.at[m, i])
+
+        for i in range(parts):
+            copy(0, i).start()
+            copy(1, i).start()
+        for i in range(parts):
+            copy(2, i).start()
         squares = 0.0
+        gate = 0.0
+        upper = 0.0
         for i in range(blocks):
             wide = x_ref[i].astype(jnp.float32)
             square = wide * wide
@@ -135,77 +150,190 @@
             scaled[:, i * cols : (i + 1) * cols] = (
                 wide * gain_ref[:, i * cols : (i + 1) * cols]
             ).astype(scaled.dtype)
+        for i in range(parts):
+            part = slice(i * span, (i + 1) * span)
+            copy(0, i).wait()
+            gate += lax.dot_general(
+                scaled[:, part], gate_buf[:, part], contract, preferred_element_type=jnp.float32
+            )
+            copy(1, i).wait()
+            upper += lax.dot_general(
+                scaled[:, part], up_buf[:, part], contract, preferred_element_type=jnp.float32
+            )
         inverse = lax.rsqrt(jnp.sum(squares, axis=1, keepdims=True) * (1.0 / width) + 1e-05)
-        gate = inverse * lax.dot_general(
-            scaled[...], gate_ref[...], contract, preferred_element_type=jnp.float32
-        )
-        upper = inverse * lax.dot_general(
-            scaled[...], up_ref[...], contract, preferred_element_type=jnp.float32
-        )
+        gate = gate * inverse
+        upper = upper * inverse
         act = (gate / (1.0 + jnp.exp(-gate)) * upper).astype(jnp.bfloat16)
         for t in range(n_tensor):
+            if t % (n_tensor // parts) == 0:
+                copy(2, t // (n_tensor // parts)).wait()
             out = jnp.dot(
                 act,
-                down_ref[:, t * cols_out : (t + 1) * cols_out],
+                down_buf[:, t * cols_out : (t + 1) * cols_out],
                 preferred_element_type=jnp.float32,
             )
             out_ref[:, t] = out.astype(out_ref.dtype).reshape(chips, rows_dev, cols_out)
 
     return pl.pallas_call(
         kernel,
-        in_specs=[VMEM] * 5,
+        in_specs=[VMEM, HBM, HBM, VMEM, HBM],
         out_specs=VMEM,
         out_shape=jax.ShapeDtypeStruct((chips, n_tensor, rows_dev, cols_out), jnp.bfloat16),
-        scratch_shapes=[pltpu.VMEM((rows, width), jnp.bfloat16)],
-        compiler_params=pltpu.CompilerParams(vmem_limit_bytes=24 * MIB),
+        scratch_shapes=[
+            pltpu.VMEM((rows, width), jnp.bfloat16),
+            pltpu.VMEM((units, width), jnp.bfloat16),
+            pltpu.VMEM((units, width), jnp.bfloat16),
+            pltpu.VMEM((units, width), jnp.bfloat16),
+            pltpu.SemaphoreType.DMA((3, parts)),
+        ],
+        compiler_params=pltpu.CompilerParams(vmem_limit_bytes=28 * MIB),
         name="feed_forward",
-    )(hidden, gate_rows, up_rows, gain_row, w_down)
-
-
-def gather_pages(rows, pool, parts):
-    count = rows.shape[0]
+    )(
+        hidden,
+        pltpu.with_memory_space_constraint(gate_rows, pltpu.HBM),
+        pltpu.with_memory_space_constraint(up_rows, pltpu.HBM),
+        gain_row,
+        pltpu.with_memory_space_constraint(w_down, pltpu.HBM),
+    )
+
+
+def add_pieces(pieces, hidden, n_steps):
+    count, rows, cols = pieces.shape
+    parts = 8
     span = count // parts
-    ahead = 3
-
-    def kernel(rows_ref, pool_ref, out_ref, buf, in_sems, out_sems):
-        def start(d):
-            def body(k, carry):
-                at = d * span + k
-                pltpu.make_async_copy(
-                    pool_ref.at[rows_ref[at]], buf.at[at], in_sems.at[d]
-                ).start()
-                return carry
-
-            lax.fori_loop(0, span, body, 0, unroll=8)
-
-        def copy_out(d):
-            part = pl.ds(d * span, span)
-            return pltpu.make_async_copy(buf.at[part], out_ref.at[part], out_sems.at[d])
-
-        for d in range(ahead):
-            start(d)
-        for d in range(parts):
-            if d + ahead < parts:
-                start(d + ahead)
-            part = pl.ds(d * span, span)
-            pltpu.make_async_copy(pool_ref.at[part], buf.at[part], in_sems.at[d]).wait()
-            copy_out(d).start()
-        for d in range(parts):
-            copy_out(d).wait()
+
+    def kernel(pieces_hbm, hidden_ref, out_ref, buf, sems):
+        def copy(i):
+            part = pl.ds(i * span, span)
+            return pltpu.make_async_copy(pieces_hbm.at[part], buf.at[part], sems.at[i])
+
+        for i in range(parts):
+            copy(i).start()
+        total = hidden_ref[...].astype(jnp.float32)
+        for i in range(parts):
+            copy(i).wait()
+            total += jnp.sum(buf[i * span : (i + 1) * span].astype(jnp.float32), axis=0)
+        out_ref[...] = total.reshape(n_steps, rows // n_steps, cols).astype(out_ref.dtype)
 
     return pl.pallas_call(
         kernel,
-        in_specs=[SMEM, HBM],
-        out_specs=HBM,
-        out_shape=pltpu.HBM((count,) + pool.shape[1:], pool.dtype),
+        in_specs=[HBM, VMEM],
+        out_specs=VMEM,
+        out_shape=jax.ShapeDtypeStruct((n_steps, rows // n_steps, cols), pieces.dtype),
         scratch_shapes=[
-            pltpu.VMEM((count,) + pool.shape[1:], pool.dtype),
-            pltpu.SemaphoreType.DMA((parts,)),
+            pltpu.VMEM(pieces.shape, pieces.dtype),
             pltpu.SemaphoreType.DMA((parts,)),
         ],
         compiler_params=pltpu.CompilerParams(vmem_limit_bytes=10 * MIB),
-        name="gather_pages",
-    )(rows, pltpu.with_memory_space_constraint(pool, pltpu.HBM))
+        name="add_pieces",
+    )(pieces, hidden)
+
+
+def exact_dot(left, right, contract):
+    return lax.dot_general(
+        left.astype(jnp.bfloat16),
+        right.astype(jnp.bfloat16),
+        (contract, ((), ())),
+        preferred_element_type=jnp.float32,
+    )
+
+
+def pack_pages(place, page_loc, lengths, placement, pool, n_dp):
+    pslots, page_size, width_two = pool.shape
+    _, max_pages, n_req = page_loc.shape
+    req_dev = n_req // n_dp
+    capacity = pslots // n_dp
+    low = 32
+
+    def kernel(place_ref, loc_hbm, len_ref, placement_ref, pool_hbm, out_hbm, loc, pool_buf, out_buf, rows_vec, rows, loc_sem, pool_sem, rows_sem, out_sems):
+        me = place_ref[0]
+        pool_copy = pltpu.make_async_copy(pool_hbm, pool_buf, pool_sem)
+        loc_copy = pltpu.make_async_copy(loc_hbm.at[place_ref[1]], loc, loc_sem)
+        loc_copy.start()
+        pool_copy.start()
+        shape = (n_req, n_req)
+        down = lax.broadcasted_iota(jnp.int32, shape, 0)
+        across = lax.broadcasted_iota(jnp.int32, shape, 1)
+        slot_hot = jnp.where(placement_ref[...] == down, 1.0, 0.0)
+        lens = jnp.broadcast_to(len_ref[...], (8, n_req))
+        loc_copy.wait()
+        at = loc[...]
+        pieces = jnp.concatenate(
+            [at // pslots, at % pslots // low, at % low, lens // low, lens % low], axis=0
+        )
+        by_slot = exact_dot(pieces.astype(jnp.float32), slot_hot, ((1,), (1,)))
+        source = by_slot[:max_pages]
+        row = by_slot[max_pages : 2 * max_pages] * low + by_slot[2 * max_pages : 3 * max_pages]
+        len_row = by_slot[3 * max_pages : 3 * max_pages + 1] * low + by_slot[3 * max_pages + 8 : 3 * max_pages + 9]
+        page_at = lax.broadcasted_iota(jnp.int32, (max_pages, n_req), 0).astype(jnp.float32)
+        mine = (page_at * page_size < len_row) & (source == me.astype(jnp.float32))
+        ones = jnp.where(mine, 1.0, 0.0)
+        earlier = jnp.where(
+            lax.broadcasted_iota(jnp.int32, (max_pages, max_pages), 1)
+            < lax.broadcasted_iota(jnp.int32, (max_pages, max_pages), 0),
+            1.0,
+            0.0,
+        )
+        in_group = jnp.where((down // req_dev == across // req_dev) & (down < across), 1.0, 0.0)
+        count = jnp.broadcast_to(jnp.sum(ones, axis=0, keepdims=True), (8, n_req))
+        rank = exact_dot(earlier, ones, ((1,), (0,))) + exact_dot(count, in_group, ((1,), (0,)))[:1]
+        rank = jnp.where(mine, rank, -1.0)
+        found = jnp.concatenate(
+            [
+                jnp.sum(jnp.where(rank == float(k), row, 0.0), axis=0, keepdims=True)
+                for k in range(capacity)
+            ],
+            axis=0,
+        ).astype(jnp.int32)
+        group = jnp.where(down // req_dev == across, 1.0, 0.0)
+        high_part = exact_dot((found // low).astype(jnp.float32), group, ((1,), (0,)))
+        low_part = exact_dot((found % low).astype(jnp.float32), group, ((1,), (0,)))
+        rows_vec[...] = (high_part * low + low_part).astype(jnp.int32)
+        rows_copy = pltpu.make_async_copy(rows_vec, rows, rows_sem)
+        rows_copy.start()
+        rows_copy.wait()
+        pool_copy.wait()
+
+        def copy_out(d):
+            part = pl.ds(d * capacity, capacity)
+            return pltpu.make_async_copy(out_buf.at[part], out_hbm.at[part], out_sems.at[d])
+
+        for d in range(n_dp):
+
+            def move(k, carry):
+                out_buf[d * capacity + k] = pool_buf[rows[k, d]]
+                return carry
+
+            lax.fori_loop(0, capacity, move, 0, unroll=16)
+            copy_out(d).start()
+        for d in range(n_dp):
+            copy_out(d).wait()
+
+    return pl.pallas_call(
+        kernel,
+        in_specs=[SMEM, HBM, VMEM, VMEM, HBM],
+        out_specs=HBM,
+        out_shape=pltpu.HBM(pool.shape, pool.dtype),
+        scratch_shapes=[
+            pltpu.VMEM((max_pages, n_req), jnp.int32),
+            pltpu.VMEM(pool.shape, pool.dtype),
+            pltpu.VMEM(pool.shape, pool.dtype),
+            pltpu.VMEM((capacity, n_req), jnp.int32),
+            pltpu.SMEM((capacity, n_req), jnp.int32),
+            pltpu.SemaphoreType.DMA,
+            pltpu.SemaphoreType.DMA,
+            pltpu.SemaphoreType.DMA,
+            pltpu.SemaphoreType.DMA((n_dp,)),
+        ],
+        compiler_params=pltpu.CompilerParams(vmem_limit_bytes=16 * MIB),
+        name="pack_pages",
+    )(
+        place,
+        page_loc,
+        lengths,
+        placement,
+        pltpu.with_memory_space_constraint(pool, pltpu.HBM),
+    )
 
 
 def add_cores(ours, from_core):
@@ -232,46 +360,32 @@
     )(ours, from_core)
 
 
-def page_plan(page_loc, lengths, placement, dev_dp, dev_tensor, n_dp, pslots, page_size):
+def page_picks(page_loc, lengths, placement, dev_dp, dev_tensor, n_dp, pslots, page_size):
     n_req = lengths.shape[0]
     max_pages = page_loc.shape[2]
     req_dev = n_req // n_dp
     entries = req_dev * max_pages
     capacity = pslots // n_dp
     loc_head = lax.dynamic_index_in_dim(page_loc, dev_tensor, 0, keepdims=False)
-    slot_hot = placement[None, :] == jnp.arange(n_req, dtype=jnp.int32)[:, None]
-    len_slot = jnp.sum(jnp.where(slot_hot, lengths[None, :], 0), axis=1)
-    loc_slot = jnp.dot(
+    my_slots = dev_dp * req_dev + jnp.arange(req_dev, dtype=jnp.int32)
+    slot_hot = placement[None, :] == my_slots[:, None]
+    my_len = jnp.sum(jnp.where(slot_hot, lengths[None, :], 0), axis=1)
+    my_loc = jnp.dot(
         slot_hot.astype(jnp.float32), loc_head.astype(jnp.float32), precision=lax.Precision.HIGHEST
     ).astype(jnp.int32)
-    pages_slot = (len_slot + page_size - 1) // page_size
+    pages_slot = (my_len + page_size - 1) // page_size
     live = jnp.arange(max_pages, dtype=jnp.int32)[None, :] < pages_slot[:, None]
-    source = jnp.where(live, loc_slot // pslots, n_dp).reshape(n_dp, entries)
-    row = (loc_slot % pslots).reshape(n_dp, entries)
+    my_source = jnp.where(live, my_loc // pslots, n_dp).reshape(entries)
     before = (
         jnp.arange(entries, dtype=jnp.int32)[:, None] < jnp.arange(entries, dtype=jnp.int32)[None, :]
     ).astype(jnp.bfloat16)
-    mine_out = source == dev_dp
-    rank_out = jnp.dot(
-        mine_out.astype(jnp.bfloat16), before, preferred_element_type=jnp.float32
-    ).astype(jnp.int32)
-    rank_out = jnp.where(mine_out, rank_out, capacity)
-    hit = rank_out[:, None, :] == jnp.arange(capacity, dtype=jnp.int32)[None, :, None]
-    send_rows = jnp.sum(jnp.where(hit, row[:, None, :], 0), axis=2)
-    slot = jnp.arange(pslots, dtype=jnp.int32).reshape(n_dp, capacity)
-    used = jnp.sum(mine_out.astype(jnp.int32), axis=1, keepdims=True)
-    send_rows = jnp.where(slot % capacity < used, send_rows, slot)
-    my_source = lax.dynamic_index_in_dim(source, dev_dp, 0, keepdims=False)
     source_hot = my_source[None, :] == jnp.arange(n_dp, dtype=jnp.int32)[:, None]
     rank_in = jnp.dot(
         source_hot.astype(jnp.bfloat16), before, preferred_element_type=jnp.float32
     ).astype(jnp.int32)
     my_rank = jnp.sum(jnp.where(source_hot, rank_in, 0), axis=0)
-    pick = jnp.where(
-        my_source < n_dp, my_source * capacity + my_rank, jnp.arange(entries, dtype=jnp.int32)
-    )
-    my_len = lax.dynamic_slice_in_dim(len_slot, dev_dp * req_dev, req_dev)
-    return send_rows, pick, my_len
+    pick = jnp.where(my_source < n_dp, my_source * capacity + my_rank, 0)
+    return pick, my_len
 
 
 def per_device(
@@ -309,12 +423,21 @@
     rows_core = n_steps * n_req // 2
     capacity = pslots // n_dp
 
-    send_rows, pick, my_len = page_plan(
+    outgoing = pack_pages(
+        jnp.stack([dev_dp, dev_tensor]).astype(jnp.int32),
+        jnp.swapaxes(page_loc, 1, 2),
+        lengths.reshape(1, n_req),
+        placement.reshape(1, n_req),
+        kv_pool.reshape(pslots, page_size, width_two),
+        n_dp,
+    )
+    outgoing, page_loc, lengths, placement = lax.optimization_barrier(
+        (outgoing, page_loc, lengths, placement)
+    )
+    pick, my_len = page_picks(
         page_loc, lengths, placement, dev_dp, dev_tensor, n_dp, pslots, page_size
     )
-    outgoing = gather_pages(
-        send_rows.reshape(-1), kv_pool.reshape(pslots, page_size, width_two), n_dp
-    ).reshape(n_dp, capacity, page_size, width_two)
+    outgoing = outgoing.reshape(n_dp, capacity, page_size, width_two)
     received = lax.all_to_all(outgoing, DP, 0, 0, tiled=True)
     query = jnp.transpose(queries, (1, 0, 2, 3)).reshape(req_dev, n_steps * hq_dev, head_dim)
     cache, mixed_copies = intake(
@@ -379,12 +502,11 @@
     from_core = lax.ppermute(theirs, "c", swap)
     chip_sum = add_cores(ours, from_core).reshape(chips_dp * n_tensor, rows_dev, width_out)
     pieces = lax.all_to_all(chip_sum, CHIPS, 0, 0, tiled=True)
-    ffn_part = jnp.sum(pieces.astype(jnp.float32), axis=0)
     own_hidden = lax.dynamic_slice(
         own_rows, (dev_tensor, dev_chip * rows_dev, 0), (1, rows_dev, cols_chip)
     )[0]
-    block_out = (own_hidden.astype(jnp.float32) + ffn_part).astype(jnp.bfloat16)
-    return (block_out.reshape(n_steps, req_dev, width_out), cache.reshape(1, req_dev, cache_len, width_two))
+    block_out = add_pieces(pieces, own_hidden, n_steps)
+    return (block_out, cache.reshape(1, req_dev, cache_len, width_two))
 
 
 def solution(mesh):

time: 200 us -> 201 us (level)
  Pallas kernels: 23.8 us -> 32.8 us
  other arithmetic: 3.93 us -> 0.34 us
  local copies, waits for them, and re-layouts: 5.23 us -> 2.69 us
    pallas_call x3 -> x4, Pallas kernels: 13.5 us -> 22.1 us  [the longest x2 14.9 us: feed_forward(): pl.pallas_call(kernel, in_specs=[VMEM, HBM, HBM, VMEM, HBM], out_specs=VM...]
    reduce_sum x4 -> x1, other arithmetic: 3.21 us -> 0.18 us  [page_picks(): my_len = jnp.sum(jnp.where(slot_hot, lengths[None, :], 0), axis=1)]
    unnamed x18 -> x20, local copies, waits for them, and re-layouts: 4.11 us -> 2.3 us
  transfers between devices with their start and end apart: 8 -> 8, of which waited for: 5 -> 5; matrix products, arithmetic and copies ran while one was open for 0% -> 1% of each run, Pallas kernels for 6% -> 8%
where the time goes in v5:
time: 201 us; the launch traced here: 200 us
  waiting for transfers between devices  104 us (52%)
  Pallas kernels  32.8 us (16%)
  blocking collectives  31.5 us (16%)
  starting transfers between devices  25.4 us (13%)
  local copies, waits for them, and re-layouts  2.69 us (1%)
  matrix products  2.57 us (1%)
    all_to_all x1, waiting for transfers between devices, per_device(): received = lax.all_to_all(outgoing, DP, 0, 0, tiled=True)  54.4 us
    all_to_all x1, blocking collectives, to_all(): return lax.all_to_all(copies, axes, 0, 0, tiled=True)  31.5 us
    all_to_all x1, waiting for transfers between devices, per_device(): pieces = lax.all_to_all(chip_sum, CHIPS, 0, 0, tiled=True)  29.6 us
    pallas_call x2, Pallas kernels, feed_forward(): pl.pallas_call(kernel, in_specs=[VMEM, HBM, HBM, VMEM, HBM], out_specs=VM...  14.9 us
    pallas_call x1, Pallas kernels, intake(): pl.pallas_call(kernel, in_specs=[SMEM, SMEM, HBM, VMEM, VMEM], out_specs=...  9.29 us
    all_to_all x1, waiting for transfers between devices, per_device(): lax.all_to_all(mixed_copies, CHIP_DP, 0, 0, tiled=True)  9.01 us
    all_to_all x1, starting transfers between devices, per_device(): received = lax.all_to_all(outgoing, DP, 0, 0, tiled=True)  7.31 us
    all_to_all x1, waiting for transfers between devices, per_device(): lax.all_to_all(partial_out.reshape(n_tensor, rows_blk, cols_chip), TENSOR...  7.13 us
  transfers between devices with their start and end apart: 8, of which 5 were waited for; matrix products, arithmetic and copies ran while one was open for 1% of the time, Pallas kernels for 8%

profile of v5, /device:TPU:0, one launch (start us, length us, event | category | flops | bytes accessed | tf_op | source)
XLA Modules:
  0.0 200.3 jit_solution(17201714475859281872)
XLA Ops:
  0.6 0.0 copy-start
  0.7 0.1 pad_add_fusion.place_ref
  0.7 0.0 copy-start.1
  0.7 0.9 copy-done.1
  1.7 0.0 copy-start.3
  1.7 0.7 copy-done.3
  2.3 0.0 copy-start.5
  2.3 0.7 copy-done.5
  3.0 5.0 %pack_pages.1 = bf16[512,16,256]{2,1,0:T(8,128)(2,1)} custom-call(s32[2]{0:T(128)S(1)} %pad_add_fusion.place_ref, s32[8,64,128]{2,1,0:T(8,128)S(1)} %bitcast.47, s32[1,128]{1,0:T(1,128)S(1)} %bitcast.50, s32[1,128]{1,0:T(1,128)S(1)} %bitcast.51, bf16[512,16,256]{2,1,0:T(8,128)(2,1)} %bitcast.58), custom_call_target="tpu_custom_call" | custom-call | tf_op jit(solution)/shard_map/pack_pages/pallas_call | solution.py:312
  8.0 0.0 copy-start.9
  8.0 0.0 copy-start.4
  8.0 0.0 copy-start.6
  8.0 0.0 copy-start.8
  8.0 7.3 %all-to-all-start = ((bf16[16,32,16,256]{3,2,1,0:T(8,128)(2,1)}), bf16[16,32,16,256]{3,2,1,0:T(8,128)(2,1)}, u32[]{:S(2)}, u32[]{:S(2)}) async-start(bf16[16,32,16,256]{3,2,1,0:T(8,128)(2,1)} %bitcast.52), calls=%async_computation | async-start | bytes 8388608 | tf_op jit(solution)/shard_map/all_to_all | solution.py:441
  15.3 0.0 copy-done.9
  15.3 0.4 collective-permute-start.1
  15.8 0.0 copy-done.4
  15.8 0.0 copy-done.6
  15.8 0.2 fusion.15.len_ref
  16.0 1.0 fusion.17
  17.0 0.1 reshape.119
  17.0 0.2 fusion.9
  17.3 0.0 copy-done.8
  17.3 0.0 copy-done
  17.3 54.4 %all-to-all-done = bf16[16,32,16,256]{3,2,1,0:T(8,128)(2,1)} async-done(((bf16[16,32,16,256]{3,2,1,0:T(8,128)(2,1)}), bf16[16,32,16,256]{3,2,1,0:T(8,128)(2,1)}, u32[]{:S(2)}, u32[]{:S(2)}) %all-to-all-start) | async-done | bytes 4194336 | tf_op jit(solution)/shard_map/all_to_all | solution.py:441
  71.7 9.3 %intake.1 = (bf16[8,65,16,256]{3,2,1,0:T(8,128)(2,1)}, bf16[8,16,1024]{2,1,0:T(8,128)(2,1)}) custom-call(s32[512]{0:T(512)S(1)} %add_select_fusion.1.pick_ref, s32[8]{0:T(128)S(1)} %fusion.15.len_ref, bf16[512,16,256]{2,1,0:T(8,128)(2,1)} %bitcast.13.recv_ref, f32[2,8,256]{2,1,0:T(8,128)S(1)} %bitcast_convert_fusion.fresh_ref, ...), custom_call_target="tpu_custom_call" | custom-call | tf_op jit(solution)/shard_map/intake/pallas_call | solution.py:101
  81.0 5.3 %all-to-all-start.1 = ((bf16[8,16,1024]{2,1,0:T(8,128)(2,1)}), bf16[8,16,1024]{2,1,0:T(8,128)(2,1)S(1)}, u32[]{:S(2)}, u32[]{:S(2)}) async-start(bf16[8,16,1024]{2,1,0:T(8,128)(2,1)} %get-tuple-element.14), calls=%async_computation.1 | async-start | bytes 524288 | tf_op jit(solution)/shard_map/all_to_all | solution.py:474
  86.3 0.0 collective-permute-done.1
  86.3 9.0 %all-to-all-done.1 = bf16[8,16,1024]{2,1,0:T(8,128)(2,1)S(1)} async-done(((bf16[8,16,1024]{2,1,0:T(8,128)(2,1)}), bf16[8,16,1024]{2,1,0:T(8,128)(2,1)S(1)}, u32[]{:S(2)}, u32[]{:S(2)}) %all-to-all-start.1) | async-done | bytes 262176 | tf_op jit(solution)/shard_map/all_to_all | solution.py:474
  95.3 0.0 copy-start.7
  95.3 1.4 fusion.7
  96.7 5.4 %all-to-all-start.2 = ((bf16[8,16,1024]{2,1,0:T(8,128)(2,1)}), bf16[8,16,1024]{2,1,0:T(8,128)(2,1)S(1)}, u32[]{:S(2)}, u32[]{:S(2)}) async-start(bf16[8,16,1024]{2,1,0:T(8,128)(2,1)} %bitcast.19), calls=%async_computation.2 | async-start | bytes 524288 | tf_op jit(solution)/shard_map/all_to_all | solution.py:481
  102.1 0.0 copy-done.7
  102.2 0.1 collective-permute-start
  102.3 7.1 %all-to-all-done.2 = bf16[8,16,1024]{2,1,0:T(8,128)(2,1)S(1)} async-done(((bf16[8,16,1024]{2,1,0:T(8,128)(2,1)}), bf16[8,16,1024]{2,1,0:T(8,128)(2,1)S(1)}, u32[]{:S(2)}, u32[]{:S(2)}) %all-to-all-start.2) | async-done | bytes 262176 | tf_op jit(solution)/shard_map/all_to_all | solution.py:481
  109.5 0.0 collective-permute-done
  109.5 0.2 broadcast_in_dim.43
  109.8 0.0 copy-start.2
  109.8 31.5 %all_to_all.25 = bf16[64,16,1024]{2,1,0:T(8,128)(2,1)S(1)} all-to-all(bf16[64,16,1024]{2,1,0:T(8,128)(2,1)S(1)} %broadcast_in_dim.43), channel_id=1, replica_groups=mesh['yh'=2,'x'=4,'c'=2,'z'=4,'yl'=2] {'yh','x','z','yl'}, dimensions={0} | all-to-all | bytes 4194304 | tf_op jit(solution)/shard_map/all_to_all | solution.py:18
  141.3 0.0 collective-permute-start.2
  141.3 0.0 copy-done.2
  141.3 7.4 %feed_forward.2.a_ref = bf16[8,8,16,1024]{3,2,1,0:T(8,128)(2,1)S(1)} custom-call(bf16[8,128,1024]{2,1,0:T(8,128)(2,1)S(1)} %bitcast.45, bf16[224,8192]{1,0:T(8,128)(2,1)} %bitcast.53, bf16[224,8192]{1,0:T(8,128)(2,1)} %bitcast.55, f32[1,8192]{1,0:T(1,128)S(1)} %bitcast.48, bf16[224,8192]{1,0:T(8,128)(2,1)} %down_hbm.3), custom_call_target="tpu_custom_call" | custom-call | tf_op jit(solution)/shard_map/feed_forward/pallas_call | solution.py:177
  148.7 0.0 collective-permute-done.2.x_ref
  148.7 7.4 %feed_forward.3 = bf16[8,8,16,1024]{3,2,1,0:T(8,128)(2,1)S(1)} custom-call(bf16[8,128,1024]{2,1,0:T(8,128)(2,1)S(1)} %collective-permute-done.2.x_ref, bf16[224,8192]{1,0:T(8,128)(2,1)} %bitcast.54, bf16[224,8192]{1,0:T(8,128)(2,1)} %bitcast.56, f32[1,8192]{1,0:T(1,128)S(1)} %bitcast.49, bf16[224,8192]{1,0:T(8,128)(2,1)} %down_hbm.3), custom_call_target="tpu_custom_call" | custom-call | tf_op jit(solution)/shard_map/feed_forward/pallas_call | solution.py:177
  156.1 0.6 collective-permute-start.3
  156.8 3.8 %collective-permute-done.3.b_ref = bf16[8,8,16,1024]{3,2,1,0:T(8,128)(2,1)S(1)} collective-permute-done((bf16[8,8,16,1024]{3,2,1,0:T(8,128)(2,1)S(1)}, bf16[8,8,16,1024]{3,2,1,0:T(8,128)(2,1)S(1)}, u32[]{:S(2)}, u32[]{:S(2)}) %collective-permute-start.3) | collective-permute-done | bytes 2097184 | tf_op jit(solution)/shard_map/ppermute | solution.py:502
  160.5 1.4 add_cores.1
  162.0 6.3 %all-to-all-start.4 = ((bf16[64,16,1024]{2,1,0:T(8,128)(2,1)}), bf16[64,16,1024]{2,1,0:T(8,128)(2,1)}, u32[]{:S(2)}, u32[]{:S(2)}) async-start(bf16[64,16,1024]{2,1,0:T(8,128)(2,1)} %bitcast.57), calls=%async_computation.4 | async-start | bytes 4194304 | tf_op jit(solution)/shard_map/all_to_all | solution.py:504
  168.3 29.6 %all-to-all-done.4.pieces_hbm = bf16[64,16,1024]{2,1,0:T(8,128)(2,1)} async-done(((bf16[64,16,1024]{2,1,0:T(8,128)(2,1)}), bf16[64,16,1024]{2,1,0:T(8,128)(2,1)}, u32[]{:S(2)}, u32[]{:S(2)}) %all-to-all-start.4) | async-done | bytes 2097184 | tf_op jit(solution)/shard_map/all_to_all | solution.py:504
  197.9 2.2 %add_pieces.1 = bf16[2,8,1024]{2,1,0:T(8,128)(2,1)} custom-call(bf16[64,16,1024]{2,1,0:T(8,128)(2,1)} %all-to-all-done.4.pieces_hbm, bf16[16,1024]{1,0:T(8,128)(2,1)S(1)} %dynamic-slice_bitcast_fusion.hidden_ref), custom_call_target="tpu_custom_call" | custom-call | tf_op jit(solution)/shard_map/add_pieces/pallas_call | solution.py:218
  (10 shorter events, 0.1 us)
Async XLA Ops:
  0.6 16.7 %copy-start = (bf16[2,8,8,128]{3,2,1,0:T(8,128)(2,1)S(1)}, bf16[2,8,8,128]{3,2,1,0:T(8,128)(2,1)}, u32[]{:S(2)}) copy-start(bf16[2,8,8,128]{3,2,1,0:T(8,128)(2,1)} %param.16) | copy-start | bytes 98308
  0.7 1.0 copy-start.1
  1.7 0.7 copy-start.3
  2.3 0.7 copy-start.5
  8.0 7.4 %copy-start.9 = (bf16[1024,512]{1,0:T(8,128)(2,1)S(1)}, bf16[1024,512]{1,0:T(8,128)(2,1)}, u32[]{:S(2)}) copy-start(bf16[1024,512]{1,0:T(8,128)(2,1)} %param.19) | copy-start | bytes 3145732
  8.0 7.8 %copy-start.4 = (s32[128]{0:T(128)S(1)}, s32[128]{0:T(128)}, u32[]{:S(2)}) copy-start(s32[128]{0:T(128)} %param.14) | copy-start | bytes 1540
  8.0 7.8 %copy-start.6 = (s32[128]{0:T(128)S(1)}, s32[128]{0:T(128)}, u32[]{:S(2)}) copy-start(s32[128]{0:T(128)} %param.15) | copy-start | bytes 1540
  8.0 9.3 %copy-start.8 = (bf16[2,8,1,256]{3,1,2,0:T(8,128)(2,1)S(1)}, bf16[2,8,1,256]{3,1,2,0:T(8,128)(2,1)}, u32[]{:S(2)}) copy-start(bf16[2,8,1,256]{3,1,2,0:T(8,128)(2,1)} %param.17) | copy-start | bytes 24580
  8.0 63.7 %all-to-all-start = ((bf16[16,32,16,256]{3,2,1,0:T(8,128)(2,1)}), bf16[16,32,16,256]{3,2,1,0:T(8,128)(2,1)}, u32[]{:S(2)}, u32[]{:S(2)}) async-start(bf16[16,32,16,256]{3,2,1,0:T(8,128)(2,1)} %bitcast.52), calls=%async_computation | async-start | bytes 8388608 | tf_op jit(solution)/shard_map/all_to_all | solution.py:441
  15.3 71.0 %collective-permute-start.1 = (bf16[1024,512]{1,0:T(8,128)(2,1)S(1)}, bf16[1024,512]{1,0:T(8,128)(2,1)S(1)}, u32[]{:S(2)}, u32[]{:S(2)}) collective-permute-start(bf16[1024,512]{1,0:T(8,128)(2,1)S(1)} %copy-done.9), channel_id=1, source_target_pairs={{0,8},{8,0},{1,9},{9,1},{2,10},{10,2},{3,11},{11,3},{4,12},{12,4},... | collective-permute-start | bytes 3145736 | tf_op jit(solution)/shard_map/ppermute | solution.py:463
  81.0 14.3 %all-to-all-start.1 = ((bf16[8,16,1024]{2,1,0:T(8,128)(2,1)}), bf16[8,16,1024]{2,1,0:T(8,128)(2,1)S(1)}, u32[]{:S(2)}, u32[]{:S(2)}) async-start(bf16[8,16,1024]{2,1,0:T(8,128)(2,1)} %get-tuple-element.14), calls=%async_computation.1 | async-start | bytes 524288 | tf_op jit(solution)/shard_map/all_to_all | solution.py:474
  95.3 6.8 %copy-start.7 = (bf16[2,128,512]{2,1,0:T(8,128)(2,1)S(1)}, bf16[2,128,512]{2,1,0:T(8,128)(2,1)}, u32[]{:S(2)}) copy-start(bf16[2,128,512]{2,1,0:T(8,128)(2,1)} %param.18) | copy-start | bytes 786436
  96.7 12.7 %all-to-all-start.2 = ((bf16[8,16,1024]{2,1,0:T(8,128)(2,1)}), bf16[8,16,1024]{2,1,0:T(8,128)(2,1)S(1)}, u32[]{:S(2)}, u32[]{:S(2)}) async-start(bf16[8,16,1024]{2,1,0:T(8,128)(2,1)} %bitcast.19), calls=%async_computation.2 | async-start | bytes 524288 | tf_op jit(solution)/shard_map/all_to_all | solution.py:481
  102.2 7.3 %collective-permute-start = (bf16[16,512]{1,0:T(8,128)(2,1)S(1)}, bf16[16,512]{1,0:T(8,128)(2,1)S(1)}, u32[]{:S(2)}, u32[]{:S(2)}) collective-permute-start(bf16[16,512]{1,0:T(8,128)(2,1)S(1)} %get-tuple-element.19), channel_id=1, source_target_pairs={{0,8},{8,0},{1,9},{9,1},{2,10},{10,2},{3,11},{11,3},{4,12},{12,4},... | collective-permute-start | bytes 49160 | tf_op jit(solution)/shard_map/ppermute | solution.py:473
  109.8 31.5 %copy-start.2 = (f32[8192]{0:T(1024)S(1)}, f32[8192]{0:T(1024)}, u32[]{:S(2)}) copy-start(f32[8192]{0:T(1024)} %param.20) | copy-start | bytes 98308
  141.3 7.4 %collective-permute-start.2 = (bf16[8,128,1024]{2,1,0:T(8,128)(2,1)S(1)}, bf16[8,128,1024]{2,1,0:T(8,128)(2,1)S(1)}, u32[]{:S(2)}, u32[]{:S(2)}) collective-permute-start(bf16[8,128,1024]{2,1,0:T(8,128)(2,1)S(1)} %bitcast.44), channel_id=1, source_target_pairs={{0,8},{8,0},{1,9},{9,1},{2,10},{10,2},{3,11},{11,3},{4,12},{12,4},... | collective-permute-start | bytes 6291464 | tf_op jit(solution)/shard_map/ppermute | solution.py:490
  156.1 4.4 %collective-permute-start.3 = (bf16[8,8,16,1024]{3,2,1,0:T(8,128)(2,1)S(1)}, bf16[8,8,16,1024]{3,2,1,0:T(8,128)(2,1)S(1)}, u32[]{:S(2)}, u32[]{:S(2)}) collective-permute-start(bf16[8,8,16,1024]{3,2,1,0:T(8,128)(2,1)S(1)} %feed_forward.3), channel_id=1, source_target_pairs={{0,8},{8,0},{1,9},{9,1},{2,10},{10,2},{3,11},{11,3},{4,12},{12,4},... | collective-permute-start | bytes 6291464 | tf_op jit(solution)/shard_map/ppermute | solution.py:502
  162.0 35.9 %all-to-all-start.4 = ((bf16[64,16,1024]{2,1,0:T(8,128)(2,1)}), bf16[64,16,1024]{2,1,0:T(8,128)(2,1)}, u32[]{:S(2)}, u32[]{:S(2)}) async-start(bf16[64,16,1024]{2,1,0:T(8,128)(2,1)} %bitcast.57), calls=%async_computation.4 | async-start | bytes 4194304 | tf_op jit(solution)/shard_map/all_to_all | solution.py:504

commit v6 on v5

--- a/solution.py
+++ b/solution.py
@@ -31,25 +31,22 @@
     pages = max_pages + 1
     group = n_rows // n_steps
     scale = 1.0 / math.sqrt(head_dim)
-    parts = 8
-
-    def kernel(pick_ref, len_ref, recv_ref, fresh_ref, q_ref, cache_ref, mixed_ref, recv_buf, buf, heads, in_sems, out_sems):
-        def copy_in(i):
-            part = pl.ds(i * (recv_ref.shape[0] // parts), recv_ref.shape[0] // parts)
-            return pltpu.make_async_copy(recv_ref.at[part], recv_buf.at[part], in_sems.at[i])
-
+    parts = 4
+
+    def kernel(pick_ref, len_ref, recv_ref, fresh_ref, q_ref, cache_ref, mixed_ref, recv_buf, buf, scores, probs, heads, in_sems, out_sems):
         def copy_out(r):
             return pltpu.make_async_copy(buf.at[r], cache_ref.at[r], out_sems.at[r])
 
-        for i in range(parts):
-            copy_in(i).start()
-        for i in range(parts):
-            copy_in(i).wait()
-        row_at = lax.broadcasted_iota(jnp.int32, (page_size, width_two), 0)
-        for r in range(req_dev):
+        def copy_in(half, i):
+            span = recv_ref.shape[0] // parts
+            part = (pl.ds(i * span, span), slice(None), pl.ds(half * head_dim, head_dim))
+            return pltpu.make_async_copy(recv_ref.at[part], recv_buf.at[part], in_sems.at[half, i])
+
+        def fill(half, r):
+            lanes = slice(half * head_dim, (half + 1) * head_dim)
 
             def move(p, carry):
-                buf[r, p] = recv_buf[pick_ref[r * max_pages + p]]
+                buf[r, p, :, lanes] = recv_buf[pick_ref[r * max_pages + p], :, lanes]
                 return carry
 
             lax.fori_loop(0, max_pages, move, 0, unroll=16)
@@ -57,37 +54,51 @@
             full = length // page_size
 
             def clear(p, carry):
-                buf[r, p] = jnp.zeros((page_size, width_two), buf.dtype)
+                buf[r, p, :, lanes] = jnp.zeros((page_size, head_dim), buf.dtype)
                 return carry
 
             lax.fori_loop(full + 1, pages, clear, 0)
-            edge = buf[r, full].astype(jnp.float32)
-            buf[r, full] = jnp.where(row_at < length % page_size, edge, 0.0).astype(buf.dtype)
+            edge = buf[r, full, :, lanes].astype(jnp.float32)
+            buf[r, full, :, lanes] = jnp.where(row_at < length % page_size, edge, 0.0).astype(
+                buf.dtype
+            )
             for s in range(n_steps):
                 at = length + s
-                page = buf[r, at // page_size].astype(jnp.float32)
-                token = fresh_ref[s, r : r + 1, :]
-                buf[r, at // page_size] = jnp.where(
+                page = buf[r, at // page_size, :, lanes].astype(jnp.float32)
+                token = fresh_ref[s, r : r + 1, lanes]
+                buf[r, at // page_size, :, lanes] = jnp.where(
                     row_at == at % page_size, token, page
                 ).astype(buf.dtype)
+
+        for half in range(2):
+            for i in range(parts):
+                copy_in(half, i).start()
+        row_at = lax.broadcasted_iota(jnp.int32, (page_size, head_dim), 0)
+        for i in range(parts):
+            copy_in(0, i).wait()
+        for r in range(req_dev):
+            fill(0, r)
+        for r in range(req_dev):
+            keys = buf[r, :, :, :head_dim].reshape(pages * page_size, head_dim)
+            part = scale * lax.dot_general(
+                q_ref[r], keys, (((1,), (1,)), ((), ())), preferred_element_type=jnp.float32
+            )
+            last = len_ref[r] + lax.broadcasted_iota(jnp.int32, part.shape, 0) // group
+            scores[r * n_rows : (r + 1) * n_rows] = jnp.where(
+                lax.broadcasted_iota(jnp.int32, part.shape, 1) <= last, part, -jnp.inf
+            )
+        for i in range(parts):
+            copy_in(1, i).wait()
+        for r in range(req_dev):
+            fill(1, r)
             copy_out(r).start()
+        expo = jnp.exp(scores[...] - jnp.max(scores[...], axis=1, keepdims=True))
+        probs[...] = (expo / jnp.sum(expo, axis=1, keepdims=True)).astype(probs.dtype)
         for r in range(req_dev):
-            length = len_ref[r]
-            tokens = buf[r].reshape(pages * page_size, width_two)
-            scores = scale * lax.dot_general(
-                q_ref[r],
-                tokens[:, :head_dim],
-                (((1,), (1,)), ((), ())),
-                preferred_element_type=jnp.float32,
+            values = buf[r, :, :, head_dim:].reshape(pages * page_size, head_dim)
+            head_out = jnp.dot(
+                probs[r * n_rows : (r + 1) * n_rows], values, preferred_element_type=jnp.float32
             )
-            last = length + lax.broadcasted_iota(jnp.int32, scores.shape, 0) // group
-            scores = jnp.where(
-                lax.broadcasted_iota(jnp.int32, scores.shape, 1) <= last, scores, -jnp.inf
-            )
-            expo = jnp.exp(scores - jnp.max(scores, axis=1, keepdims=True))
-            total = jnp.sum(expo, axis=1, keepdims=True)
-            probs = (expo / total).astype(jnp.bfloat16)
-            head_out = jnp.dot(probs, tokens[:, head_dim:], preferred_element_type=jnp.float32)
             for i in range(n_rows):
                 heads[i, r : r + 1, :] = head_out[i : i + 1, :]
         for g in range(group):
@@ -111,8 +122,10 @@
         scratch_shapes=[
             pltpu.VMEM(received.shape, received.dtype),
             pltpu.VMEM((req_dev, pages, page_size, width_two), received.dtype),
+            pltpu.VMEM((req_dev * n_rows, pages * page_size), jnp.float32),
+            pltpu.VMEM((req_dev * n_rows, pages * page_size), jnp.bfloat16),
             pltpu.VMEM((n_rows, req_dev, head_dim), jnp.float32),
-            pltpu.SemaphoreType.DMA((parts,)),
+            pltpu.SemaphoreType.DMA((2, parts)),
             pltpu.SemaphoreType.DMA((req_dev,)),
         ],
         compiler_params=pltpu.CompilerParams(vmem_limit_bytes=16 * MIB),
@@ -120,7 +133,7 @@
     )(pick, lens, pltpu.with_memory_space_constraint(received, pltpu.HBM), fresh, query)
 
 
-def feed_forward(hidden, gate_rows, up_rows, gain_row, w_down, n_tensor, rows_dev):
+def feed_forward(hidden, gate_rows, up_rows, gain_row, w_down, n_tensor, rows_dev, keep):
     blocks, rows, cols = hidden.shape
     units, width = w_down.shape
     cols_out = width // n_tensor
@@ -129,20 +142,22 @@
     parts = 4
     span = width // parts
 
-    def kernel(x_ref, gate_hbm, up_hbm, gain_ref, down_hbm, out_ref, scaled, gate_buf, up_buf, down_buf, sems):
+    def kernel(x_ref, gate_ref, up_in, gain_ref, down_in, out_ref, *rest):
+        if keep:
+            up_ref, down_ref, scaled, sems = rest
+        else:
+            up_ref, down_ref, scaled = up_in, down_in, rest[0]
+
         def copy(m, i):
-            source, buffer = [(gate_hbm, gate_buf), (up_hbm, up_buf), (down_hbm, down_buf)][m]
+            source, target = [(up_in, up_ref), (down_in, down_ref)][m]
             part = pl.ds(i * span, span)
-            return pltpu.make_async_copy(source.at[:, part], buffer.at[:, part], sems.at[m, i])
-
-        for i in range(parts):
-            copy(0, i).start()
-            copy(1, i).start()
-        for i in range(parts):
-            copy(2, i).start()
+            return pltpu.make_async_copy(source.at[:, part], target.at[:, part], sems.at[m, i])
+
+        if keep:
+            for m in range(2):
+                for i in range(parts):
+                    copy(m, i).start()
         squares = 0.0
-        gate = 0.0
-        upper = 0.0
         for i in range(blocks):
             wide = x_ref[i].astype(jnp.float32)
             square = wide * wide
@@ -150,56 +165,57 @@
             scaled[:, i * cols : (i + 1) * cols] = (
                 wide * gain_ref[:, i * cols : (i + 1) * cols]
             ).astype(scaled.dtype)
-        for i in range(parts):
-            part = slice(i * span, (i + 1) * span)
-            copy(0, i).wait()
-            gate += lax.dot_general(
-                scaled[:, part], gate_buf[:, part], contract, preferred_element_type=jnp.float32
-            )
-            copy(1, i).wait()
-            upper += lax.dot_general(
-                scaled[:, part], up_buf[:, part], contract, preferred_element_type=jnp.float32
+        gate = lax.dot_general(
+            scaled[...], gate_ref[...], contract, preferred_element_type=jnp.float32
+        )
+        if keep:
+            upper = 0.0
+            for i in range(parts):
+                part = slice(i * span, (i + 1) * span)
+                copy(0, i).wait()
+                upper += lax.dot_general(
+                    scaled[:, part], up_ref[:, part], contract, preferred_element_type=jnp.float32
+                )
+        else:
+            upper = lax.dot_general(
+                scaled[...], up_ref[...], contract, preferred_element_type=jnp.float32
             )
         inverse = lax.rsqrt(jnp.sum(squares, axis=1, keepdims=True) * (1.0 / width) + 1e-05)
         gate = gate * inverse
         upper = upper * inverse
         act = (gate / (1.0 + jnp.exp(-gate)) * upper).astype(jnp.bfloat16)
         for t in range(n_tensor):
-            if t % (n_tensor // parts) == 0:
-                copy(2, t // (n_tensor // parts)).wait()
+            if keep and t % (n_tensor // parts) == 0:
+                copy(1, t // (n_tensor // parts)).wait()
             out = jnp.dot(
                 act,
-                down_buf[:, t * cols_out : (t + 1) * cols_out],
+                down_ref[:, t * cols_out : (t + 1) * cols_out],
                 preferred_element_type=jnp.float32,
             )
             out_ref[:, t] = out.astype(out_ref.dtype).reshape(chips, rows_dev, cols_out)
 
+    weights = HBM if keep else VMEM
+    out_shape = [jax.ShapeDtypeStruct((chips, n_tensor, rows_dev, cols_out), jnp.bfloat16)]
+    scratch = [pltpu.VMEM((rows, width), jnp.bfloat16)]
+    if keep:
+        out_shape += [pltpu.VMEM((units, width), jnp.bfloat16)] * 2
+        scratch += [pltpu.SemaphoreType.DMA((2, parts))]
+        up_rows = pltpu.with_memory_space_constraint(up_rows, pltpu.HBM)
+        w_down = pltpu.with_memory_space_constraint(w_down, pltpu.HBM)
     return pl.pallas_call(
         kernel,
-        in_specs=[VMEM, HBM, HBM, VMEM, HBM],
-        out_specs=VMEM,
-        out_shape=jax.ShapeDtypeStruct((chips, n_tensor, rows_dev, cols_out), jnp.bfloat16),
-        scratch_shapes=[
-            pltpu.VMEM((rows, width), jnp.bfloat16),
-            pltpu.VMEM((units, width), jnp.bfloat16),
-            pltpu.VMEM((units, width), jnp.bfloat16),
-            pltpu.VMEM((units, width), jnp.bfloat16),
-            pltpu.SemaphoreType.DMA((3, parts)),
-        ],
+        in_specs=[VMEM, VMEM, weights, VMEM, weights],
+        out_specs=[VMEM] * len(out_shape),
+        out_shape=out_shape,
+        scratch_shapes=scratch,
         compiler_params=pltpu.CompilerParams(vmem_limit_bytes=28 * MIB),
         name="feed_forward",
-    )(
-        hidden,
-        pltpu.with_memory_space_constraint(gate_rows, pltpu.HBM),
-        pltpu.with_memory_space_constraint(up_rows, pltpu.HBM),
-        gain_row,
-        pltpu.with_memory_space_constraint(w_down, pltpu.HBM),
-    )
+    )(hidden, gate_rows, up_rows, gain_row, w_down)
 
 
 def add_pieces(pieces, hidden, n_steps):
     count, rows, cols = pieces.shape
-    parts = 8
+    parts = 4
     span = count // parts
 
     def kernel(pieces_hbm, hidden_ref, out_ref, buf, sems):
@@ -226,7 +242,7 @@
         ],
         compiler_params=pltpu.CompilerParams(vmem_limit_bytes=10 * MIB),
         name="add_pieces",
-    )(pieces, hidden)
+    )(pltpu.with_memory_space_constraint(pieces, pltpu.HBM), hidden)
 
 
 def exact_dot(left, right, contract):
@@ -245,16 +261,22 @@
     capacity = pslots // n_dp
     low = 32
 
-    def kernel(place_ref, loc_hbm, len_ref, placement_ref, pool_hbm, out_hbm, loc, pool_buf, out_buf, rows_vec, rows, loc_sem, pool_sem, rows_sem, out_sems):
+    def kernel(place_ref, loc_hbm, len_hbm, placement_hbm, pool_hbm, out_hbm, loc, len_ref, placement_ref, pool_buf, out_buf, rows_vec, rows, loc_sem, len_sem, placement_sem, pool_sem, rows_sem, out_sems):
         me = place_ref[0]
+        len_copy = pltpu.make_async_copy(len_hbm, len_ref, len_sem)
+        placement_copy = pltpu.make_async_copy(placement_hbm, placement_ref, placement_sem)
         pool_copy = pltpu.make_async_copy(pool_hbm, pool_buf, pool_sem)
         loc_copy = pltpu.make_async_copy(loc_hbm.at[place_ref[1]], loc, loc_sem)
         loc_copy.start()
+        len_copy.start()
+        placement_copy.start()
         pool_copy.start()
         shape = (n_req, n_req)
         down = lax.broadcasted_iota(jnp.int32, shape, 0)
         across = lax.broadcasted_iota(jnp.int32, shape, 1)
+        placement_copy.wait()
         slot_hot = jnp.where(placement_ref[...] == down, 1.0, 0.0)
+        len_copy.wait()
         lens = jnp.broadcast_to(len_ref[...], (8, n_req))
         loc_copy.wait()
         at = loc[...]
@@ -311,15 +333,19 @@
 
     return pl.pallas_call(
         kernel,
-        in_specs=[SMEM, HBM, VMEM, VMEM, HBM],
+        in_specs=[SMEM, HBM, HBM, HBM, HBM],
         out_specs=HBM,
         out_shape=pltpu.HBM(pool.shape, pool.dtype),
         scratch_shapes=[
             pltpu.VMEM((max_pages, n_req), jnp.int32),
+            pltpu.VMEM((1, n_req), jnp.int32),
+            pltpu.VMEM((1, n_req), jnp.int32),
             pltpu.VMEM(pool.shape, pool.dtype),
             pltpu.VMEM(pool.shape, pool.dtype),
             pltpu.VMEM((capacity, n_req), jnp.int32),
             pltpu.SMEM((capacity, n_req), jnp.int32),
+            pltpu.SemaphoreType.DMA,
+            pltpu.SemaphoreType.DMA,
             pltpu.SemaphoreType.DMA,
             pltpu.SemaphoreType.DMA,
             pltpu.SemaphoreType.DMA,
@@ -329,10 +355,10 @@
         name="pack_pages",
     )(
         place,
-        page_loc,
-        lengths,
-        placement,
-        pltpu.with_memory_space_constraint(pool, pltpu.HBM),
+        *[
+            pltpu.with_memory_space_constraint(array, pltpu.HBM)
+            for array in (page_loc, lengths, placement, pool)
+        ],
     )
 
 
@@ -493,12 +519,13 @@
     gain_row = ffn_gain.reshape(1, width)
     width_out = width // n_tensor
 
-    def block_of(rows):
-        return feed_forward(rows, gate_rows, up_rows, gain_row, w_down, n_tensor, rows_dev)
-
-    ours = block_of(own_rows)
+    ours, up_near, down_near = feed_forward(
+        own_rows, gate_rows, up_rows, gain_row, w_down, n_tensor, rows_dev, True
+    )
     other_rows, ours = lax.optimization_barrier((other_rows, ours))
-    theirs = block_of(other_rows)
+    (theirs,) = feed_forward(
+        other_rows, gate_rows, up_near, gain_row, down_near, n_tensor, rows_dev, False
+    )
     from_core = lax.ppermute(theirs, "c", swap)
     chip_sum = add_cores(ours, from_core).reshape(chips_dp * n_tensor, rows_dev, width_out)
     pieces = lax.all_to_all(chip_sum, CHIPS, 0, 0, tiled=True)

time: 201 us -> 192 us (0.955)
  Pallas kernels: 32.8 us -> 26.2 us
  local copies, waits for them, and re-layouts: 2.69 us -> 0.43 us
    pallas_call x3, Pallas kernels: 19.8 us -> 14 us  [the longest x2 9.02 us: feed_forward(): pl.pallas_call(kernel, in_specs=[VMEM, VMEM, weights, VMEM, weights], out...]
    unnamed x20 -> x16, local copies, waits for them, and re-layouts: 2.3 us -> 0.05 us
  transfers between devices with their start and end apart: 8 -> 8, of which waited for: 5 -> 5; matrix products, arithmetic and copies ran while one was open for 1% -> 1% of each run, Pallas kernels for 8% -> 7%
where the time goes in v6:
time: 192 us
  waiting for transfers between devices  104 us (54%)
  blocking collectives  31.3 us (16%)
  Pallas kernels  26.2 us (14%)
  starting transfers between devices  26.2 us (14%)
  matrix products  2.58 us (1%)
    all_to_all x1, waiting for transfers between devices, per_device(): received = lax.all_to_all(outgoing, DP, 0, 0, tiled=True)  54.4 us
    all_to_all x1, blocking collectives, to_all(): return lax.all_to_all(copies, axes, 0, 0, tiled=True)  31.3 us
    all_to_all x1, waiting for transfers between devices, per_device(): pieces = lax.all_to_all(chip_sum, CHIPS, 0, 0, tiled=True)  29.6 us
    pallas_call x2, Pallas kernels, feed_forward(): pl.pallas_call(kernel, in_specs=[VMEM, VMEM, weights, VMEM, weights], out...  9.02 us
    all_to_all x1, waiting for transfers between devices, per_device(): lax.all_to_all(mixed_copies, CHIP_DP, 0, 0, tiled=True)  8.78 us
    pallas_call x1, Pallas kernels, intake(): pl.pallas_call(kernel, in_specs=[SMEM, SMEM, HBM, VMEM, VMEM], out_specs=...  8.5 us
    all_to_all x1, starting transfers between devices, per_device(): received = lax.all_to_all(outgoing, DP, 0, 0, tiled=True)  7.31 us
    all_to_all x1, waiting for transfers between devices, per_device(): lax.all_to_all(partial_out.reshape(n_tensor, rows_blk, cols_chip), TENSOR...  7.13 us
  transfers between devices with their start and end apart: 8, of which 5 were waited for; matrix products, arithmetic and copies ran while one was open for 1% of the time, Pallas kernels for 7%

profile of v6, /device:TPU:0, one launch (start us, length us, event | category | flops | bytes accessed | tf_op | source)
XLA Modules:
  0.0 191.7 jit_solution(529522782065347071)
XLA Ops:
  0.6 0.0 copy-start
  0.7 0.1 pad_add_fusion.place_ref
  0.7 5.0 %pack_pages.1 = bf16[512,16,256]{2,1,0:T(8,128)(2,1)} custom-call(s32[2]{0:T(128)S(1)} %pad_add_fusion.place_ref, s32[8,64,128]{2,1,0:T(8,128)} %bitcast.56, s32[1,128]{1,0:T(1,128)} %bitcast.59, s32[1,128]{1,0:T(1,128)} %bitcast.60, bf16[512,16,256]{2,1,0:T(8,128)(2,1)} %bitcast.53), custom_call_target="tpu_custom_call" | custom-call | tf_op jit(solution)/shard_map/pack_pages/pallas_call | solution.py:334
  5.7 0.0 copy-start.7
  5.7 0.0 copy-start.5
  5.8 0.0 copy-start.6
  5.8 0.0 copy-start.4
  5.8 7.3 %all-to-all-start = ((bf16[16,32,16,256]{3,2,1,0:T(8,128)(2,1)}), bf16[16,32,16,256]{3,2,1,0:T(8,128)(2,1)}, u32[]{:S(2)}, u32[]{:S(2)}) async-start(bf16[16,32,16,256]{3,2,1,0:T(8,128)(2,1)} %bitcast.51), calls=%async_computation | async-start | bytes 8388608 | tf_op jit(solution)/shard_map/all_to_all | solution.py:467
  13.1 0.0 copy-done.7
  13.1 0.4 collective-permute-start.1
  13.5 0.0 copy-done.5
  13.5 0.0 copy-done.6
  13.6 0.2 fusion.15.len_ref
  13.8 1.0 fusion.17
  14.7 0.1 reshape.119
  14.8 0.2 fusion.9
  15.0 0.0 copy-done.4
  15.0 0.0 copy-done
  15.1 54.4 %all-to-all-done = bf16[16,32,16,256]{3,2,1,0:T(8,128)(2,1)} async-done(((bf16[16,32,16,256]{3,2,1,0:T(8,128)(2,1)}), bf16[16,32,16,256]{3,2,1,0:T(8,128)(2,1)}, u32[]{:S(2)}, u32[]{:S(2)}) %all-to-all-start) | async-done | bytes 4194336 | tf_op jit(solution)/shard_map/all_to_all | solution.py:467
  69.4 8.5 %intake.1 = (bf16[8,65,16,256]{3,2,1,0:T(8,128)(2,1)}, bf16[8,16,1024]{2,1,0:T(8,128)(2,1)}) custom-call(s32[512]{0:T(512)S(1)} %add_select_fusion.1.pick_ref, s32[8]{0:T(128)S(1)} %fusion.15.len_ref, bf16[512,16,256]{2,1,0:T(8,128)(2,1)} %bitcast.13.recv_ref, f32[2,8,256]{2,1,0:T(8,128)S(1)} %bitcast_convert_fusion.fresh_ref, ...), custom_call_target="tpu_custom_call" | custom-call | tf_op jit(solution)/shard_map/intake/pallas_call | solution.py:112
  78.0 6.1 %all-to-all-start.1 = ((bf16[8,16,1024]{2,1,0:T(8,128)(2,1)}), bf16[8,16,1024]{2,1,0:T(8,128)(2,1)S(1)}, u32[]{:S(2)}, u32[]{:S(2)}) async-start(bf16[8,16,1024]{2,1,0:T(8,128)(2,1)} %get-tuple-element.17), calls=%async_computation.1 | async-start | bytes 524288 | tf_op jit(solution)/shard_map/all_to_all | solution.py:500
  84.0 0.0 collective-permute-done.1
  84.1 8.8 %all-to-all-done.1 = bf16[8,16,1024]{2,1,0:T(8,128)(2,1)S(1)} async-done(((bf16[8,16,1024]{2,1,0:T(8,128)(2,1)}), bf16[8,16,1024]{2,1,0:T(8,128)(2,1)S(1)}, u32[]{:S(2)}, u32[]{:S(2)}) %all-to-all-start.1) | async-done | bytes 262176 | tf_op jit(solution)/shard_map/all_to_all | solution.py:500
  92.8 0.0 copy-start.3
  92.8 1.4 fusion.7
  94.2 5.4 %all-to-all-start.2 = ((bf16[8,16,1024]{2,1,0:T(8,128)(2,1)}), bf16[8,16,1024]{2,1,0:T(8,128)(2,1)S(1)}, u32[]{:S(2)}, u32[]{:S(2)}) async-start(bf16[8,16,1024]{2,1,0:T(8,128)(2,1)} %bitcast.19), calls=%async_computation.2 | async-start | bytes 524288 | tf_op jit(solution)/shard_map/all_to_all | solution.py:507
  99.7 0.0 copy-done.3
  99.7 0.1 collective-permute-start
  99.8 7.1 %all-to-all-done.2 = bf16[8,16,1024]{2,1,0:T(8,128)(2,1)S(1)} async-done(((bf16[8,16,1024]{2,1,0:T(8,128)(2,1)}), bf16[8,16,1024]{2,1,0:T(8,128)(2,1)S(1)}, u32[]{:S(2)}, u32[]{:S(2)}) %all-to-all-start.2) | async-done | bytes 262176 | tf_op jit(solution)/shard_map/all_to_all | solution.py:507
  107.0 0.0 collective-permute-done
  107.0 0.2 broadcast_in_dim.43
  107.3 0.0 copy-start.1
  107.3 0.0 copy-start.2
  107.3 31.3 %all_to_all.25 = bf16[64,16,1024]{2,1,0:T(8,128)(2,1)S(1)} all-to-all(bf16[64,16,1024]{2,1,0:T(8,128)(2,1)S(1)} %broadcast_in_dim.43), channel_id=1, replica_groups=mesh['yh'=2,'x'=4,'c'=2,'z'=4,'yl'=2] {'yh','x','z','yl'}, dimensions={0} | all-to-all | bytes 4194304 | tf_op jit(solution)/shard_map/all_to_all | solution.py:18
  138.6 0.0 collective-permute-start.2
  138.6 0.0 copy-done.1
  138.6 0.0 copy-done.2
  138.6 5.7 %feed_forward.2 = (bf16[8,8,16,1024]{3,2,1,0:T(8,128)(2,1)S(1)}, bf16[224,8192]{1,0:T(8,128)(2,1)S(1)}, bf16[224,8192]{1,0:T(8,128)(2,1)S(1)}) custom-call(bf16[8,128,1024]{2,1,0:T(8,128)(2,1)S(1)} %bitcast.47, bf16[224,8192]{1,0:T(8,128)(2,1)S(1)} %bitcast.44, bf16[224,8192]{1,0:T(8,128)(2,1)} %bitcast.54, f32[1,8192]{1,0:T(1,128)S(1)} %bitcast.49, ...), custom_call_target="tpu_custom_call" | custom-call | tf_op jit(solution)/shard_map/feed_forward/pallas_call | solution.py:205
  144.3 0.0 collective-permute-done.2.x_ref
  144.3 3.3 %feed_forward.3 = bf16[8,8,16,1024]{3,2,1,0:T(8,128)(2,1)S(1)} custom-call(bf16[8,128,1024]{2,1,0:T(8,128)(2,1)S(1)} %collective-permute-done.2.x_ref, bf16[224,8192]{1,0:T(8,128)(2,1)S(1)} %bitcast.45, bf16[224,8192]{1,0:T(8,128)(2,1)S(1)} %get-tuple-element.21.up_in, f32[1,8192]{1,0:T(1,128)S(1)} %bitcast.50, bf16[224,8192]{1,0:T(8,128)(2,1)S(1)} %get-tuple-element.22.down_in), custom_call_target="tpu_custom_call" | custom-call | tf_op jit(solution)/shard_map/feed_forward/pallas_call | solution.py:205
  147.7 0.6 collective-permute-start.3
  148.2 3.8 %collective-permute-done.3.b_ref = bf16[8,8,16,1024]{3,2,1,0:T(8,128)(2,1)S(1)} collective-permute-done((bf16[8,8,16,1024]{3,2,1,0:T(8,128)(2,1)S(1)}, bf16[8,8,16,1024]{3,2,1,0:T(8,128)(2,1)S(1)}, u32[]{:S(2)}, u32[]{:S(2)}) %collective-permute-start.3) | collective-permute-done | bytes 2097184 | tf_op jit(solution)/shard_map/ppermute | solution.py:529
  152.0 1.5 add_cores.1
  153.5 6.2 %all-to-all-start.4 = ((bf16[64,16,1024]{2,1,0:T(8,128)(2,1)}), bf16[64,16,1024]{2,1,0:T(8,128)(2,1)}, u32[]{:S(2)}, u32[]{:S(2)}) async-start(bf16[64,16,1024]{2,1,0:T(8,128)(2,1)} %bitcast.52), calls=%async_computation.4 | async-start | bytes 4194304 | tf_op jit(solution)/shard_map/all_to_all | solution.py:531
  159.8 29.6 %all-to-all-done.4.pieces_hbm = bf16[64,16,1024]{2,1,0:T(8,128)(2,1)} async-done(((bf16[64,16,1024]{2,1,0:T(8,128)(2,1)}), bf16[64,16,1024]{2,1,0:T(8,128)(2,1)}, u32[]{:S(2)}, u32[]{:S(2)}) %all-to-all-start.4) | async-done | bytes 2097184 | tf_op jit(solution)/shard_map/all_to_all | solution.py:531
  189.3 2.2 %add_pieces.1 = bf16[2,8,1024]{2,1,0:T(8,128)(2,1)} custom-call(bf16[64,16,1024]{2,1,0:T(8,128)(2,1)} %all-to-all-done.4.pieces_hbm, bf16[16,1024]{1,0:T(8,128)(2,1)S(1)} %dynamic-slice_bitcast_fusion.hidden_ref), custom_call_target="tpu_custom_call" | custom-call | tf_op jit(solution)/shard_map/add_pieces/pallas_call | solution.py:234
  (10 shorter events, 0.1 us)
Async XLA Ops:
  0.6 14.4 %copy-start = (bf16[2,8,8,128]{3,2,1,0:T(8,128)(2,1)S(1)}, bf16[2,8,8,128]{3,2,1,0:T(8,128)(2,1)}, u32[]{:S(2)}) copy-start(bf16[2,8,8,128]{3,2,1,0:T(8,128)(2,1)} %param.16) | copy-start | bytes 98308
  5.7 7.4 %copy-start.7 = (bf16[1024,512]{1,0:T(8,128)(2,1)S(1)}, bf16[1024,512]{1,0:T(8,128)(2,1)}, u32[]{:S(2)}) copy-start(bf16[1024,512]{1,0:T(8,128)(2,1)} %param.19) | copy-start | bytes 3145732
  5.7 7.8 %copy-start.5 = (s32[128]{0:T(128)S(1)}, s32[128]{0:T(128)}, u32[]{:S(2)}) copy-start(s32[128]{0:T(128)} %param.14) | copy-start | bytes 1540
  5.8 7.8 %copy-start.6 = (s32[128]{0:T(128)S(1)}, s32[128]{0:T(128)}, u32[]{:S(2)}) copy-start(s32[128]{0:T(128)} %param.15) | copy-start | bytes 1540
  5.8 9.3 %copy-start.4 = (bf16[2,8,1,256]{3,1,2,0:T(8,128)(2,1)S(1)}, bf16[2,8,1,256]{3,1,2,0:T(8,128)(2,1)}, u32[]{:S(2)}) copy-start(bf16[2,8,1,256]{3,1,2,0:T(8,128)(2,1)} %param.17) | copy-start | bytes 24580
  5.8 63.7 %all-to-all-start = ((bf16[16,32,16,256]{3,2,1,0:T(8,128)(2,1)}), bf16[16,32,16,256]{3,2,1,0:T(8,128)(2,1)}, u32[]{:S(2)}, u32[]{:S(2)}) async-start(bf16[16,32,16,256]{3,2,1,0:T(8,128)(2,1)} %bitcast.51), calls=%async_computation | async-start | bytes 8388608 | tf_op jit(solution)/shard_map/all_to_all | solution.py:467
  13.1 70.9 %collective-permute-start.1 = (bf16[1024,512]{1,0:T(8,128)(2,1)S(1)}, bf16[1024,512]{1,0:T(8,128)(2,1)S(1)}, u32[]{:S(2)}, u32[]{:S(2)}) collective-permute-start(bf16[1024,512]{1,0:T(8,128)(2,1)S(1)} %copy-done.7), channel_id=1, source_target_pairs={{0,8},{8,0},{1,9},{9,1},{2,10},{10,2},{3,11},{11,3},{4,12},{12,4},... | collective-permute-start | bytes 3145736 | tf_op jit(solution)/shard_map/ppermute | solution.py:489
  78.0 14.9 %all-to-all-start.1 = ((bf16[8,16,1024]{2,1,0:T(8,128)(2,1)}), bf16[8,16,1024]{2,1,0:T(8,128)(2,1)S(1)}, u32[]{:S(2)}, u32[]{:S(2)}) async-start(bf16[8,16,1024]{2,1,0:T(8,128)(2,1)} %get-tuple-element.17), calls=%async_computation.1 | async-start | bytes 524288 | tf_op jit(solution)/shard_map/all_to_all | solution.py:500
  92.8 6.8 %copy-start.3 = (bf16[2,128,512]{2,1,0:T(8,128)(2,1)S(1)}, bf16[2,128,512]{2,1,0:T(8,128)(2,1)}, u32[]{:S(2)}) copy-start(bf16[2,128,512]{2,1,0:T(8,128)(2,1)} %param.18) | copy-start | bytes 786436
  94.2 12.7 %all-to-all-start.2 = ((bf16[8,16,1024]{2,1,0:T(8,128)(2,1)}), bf16[8,16,1024]{2,1,0:T(8,128)(2,1)S(1)}, u32[]{:S(2)}, u32[]{:S(2)}) async-start(bf16[8,16,1024]{2,1,0:T(8,128)(2,1)} %bitcast.19), calls=%async_computation.2 | async-start | bytes 524288 | tf_op jit(solution)/shard_map/all_to_all | solution.py:507
  99.7 7.3 %collective-permute-start = (bf16[16,512]{1,0:T(8,128)(2,1)S(1)}, bf16[16,512]{1,0:T(8,128)(2,1)S(1)}, u32[]{:S(2)}, u32[]{:S(2)}) collective-permute-start(bf16[16,512]{1,0:T(8,128)(2,1)S(1)} %get-tuple-element.25), channel_id=1, source_target_pairs={{0,8},{8,0},{1,9},{9,1},{2,10},{10,2},{3,11},{11,3},{4,12},{12,4},... | collective-permute-start | bytes 49160 | tf_op jit(solution)/shard_map/ppermute | solution.py:499
  107.3 31.3 %copy-start.1 = (bf16[8192,224]{0,1:T(8,128)(2,1)S(1)}, bf16[8192,224]{0,1:T(8,128)(2,1)}, u32[]{:S(2)}) copy-start(bf16[8192,224]{0,1:T(8,128)(2,1)} %param.21) | copy-start | bytes 11010052
  107.3 31.3 %copy-start.2 = (f32[8192]{0:T(1024)S(1)}, f32[8192]{0:T(1024)}, u32[]{:S(2)}) copy-start(f32[8192]{0:T(1024)} %param.20) | copy-start | bytes 98308
  138.6 5.7 %collective-permute-start.2 = (bf16[8,128,1024]{2,1,0:T(8,128)(2,1)S(1)}, bf16[8,128,1024]{2,1,0:T(8,128)(2,1)S(1)}, u32[]{:S(2)}, u32[]{:S(2)}) collective-permute-start(bf16[8,128,1024]{2,1,0:T(8,128)(2,1)S(1)} %bitcast.46), channel_id=1, source_target_pairs={{0,8},{8,0},{1,9},{9,1},{2,10},{10,2},{3,11},{11,3},{4,12},{12,4},... | collective-permute-start | bytes 6291464 | tf_op jit(solution)/shard_map/ppermute | solution.py:516
  147.7 4.4 %collective-permute-start.3 = (bf16[8,8,16,1024]{3,2,1,0:T(8,128)(2,1)S(1)}, bf16[8,8,16,1024]{3,2,1,0:T(8,128)(2,1)S(1)}, u32[]{:S(2)}, u32[]{:S(2)}) collective-permute-start(bf16[8,8,16,1024]{3,2,1,0:T(8,128)(2,1)S(1)} %feed_forward.3), channel_id=1, source_target_pairs={{0,8},{8,0},{1,9},{9,1},{2,10},{10,2},{3,11},{11,3},{4,12},{12,4},... | collective-permute-start | bytes 6291464 | tf_op jit(solution)/shard_map/ppermute | solution.py:529
  153.5 35.9 %all-to-all-start.4 = ((bf16[64,16,1024]{2,1,0:T(8,128)(2,1)}), bf16[64,16,1024]{2,1,0:T(8,128)(2,1)}, u32[]{:S(2)}, u32[]{:S(2)}) async-start(bf16[64,16,1024]{2,1,0:T(8,128)(2,1)} %bitcast.52), calls=%async_computation.4 | async-start | bytes 4194304 | tf_op jit(solution)/shard_map/all_to_all | solution.py:531

commit v7 on v6

--- a/solution.py
+++ b/solution.py
@@ -23,75 +23,53 @@
 HBM = pl.BlockSpec(memory_space=pltpu.HBM)
 
 
-def intake(pick, lens, received, fresh, query, n_copies):
+def intake(pick, received, fresh, query, n_copies):
     req_dev, n_rows, head_dim = query.shape
     n_steps = fresh.shape[0]
     _, page_size, width_two = received.shape
-    max_pages = pick.shape[0] // req_dev
+    max_pages = pick.shape[0] - 8
     pages = max_pages + 1
     group = n_rows // n_steps
     scale = 1.0 / math.sqrt(head_dim)
-    parts = 4
-
-    def kernel(pick_ref, len_ref, recv_ref, fresh_ref, q_ref, cache_ref, mixed_ref, recv_buf, buf, scores, probs, heads, in_sems, out_sems):
+    def kernel(pick_ref, recv_ref, fresh_ref, q_ref, cache_ref, mixed_ref, buf, scores, probs, heads, out_sems):
         def copy_out(r):
             return pltpu.make_async_copy(buf.at[r], cache_ref.at[r], out_sems.at[r])
 
-        def copy_in(half, i):
-            span = recv_ref.shape[0] // parts
-            part = (pl.ds(i * span, span), slice(None), pl.ds(half * head_dim, head_dim))
-            return pltpu.make_async_copy(recv_ref.at[part], recv_buf.at[part], in_sems.at[half, i])
-
-        def fill(half, r):
-            lanes = slice(half * head_dim, (half + 1) * head_dim)
+        row_at = lax.broadcasted_iota(jnp.int32, (page_size, width_two), 0)
+        for r in range(req_dev):
 
             def move(p, carry):
-                buf[r, p, :, lanes] = recv_buf[pick_ref[r * max_pages + p], :, lanes]
+                buf[r, p] = recv_ref[pick_ref[p, r]]
                 return carry
 
             lax.fori_loop(0, max_pages, move, 0, unroll=16)
-            length = len_ref[r]
+            length = pick_ref[max_pages, r]
             full = length // page_size
 
             def clear(p, carry):
-                buf[r, p, :, lanes] = jnp.zeros((page_size, head_dim), buf.dtype)
+                buf[r, p] = jnp.zeros((page_size, width_two), buf.dtype)
                 return carry
 
             lax.fori_loop(full + 1, pages, clear, 0)
-            edge = buf[r, full, :, lanes].astype(jnp.float32)
-            buf[r, full, :, lanes] = jnp.where(row_at < length % page_size, edge, 0.0).astype(
-                buf.dtype
-            )
+            edge = buf[r, full].astype(jnp.float32)
+            buf[r, full] = jnp.where(row_at < length % page_size, edge, 0.0).astype(buf.dtype)
             for s in range(n_steps):
                 at = length + s
-                page = buf[r, at // page_size, :, lanes].astype(jnp.float32)
-                token = fresh_ref[s, r : r + 1, lanes]
-                buf[r, at // page_size, :, lanes] = jnp.where(
+                page = buf[r, at // page_size].astype(jnp.float32)
+                token = fresh_ref[s, r : r + 1, :]
+                buf[r, at // page_size] = jnp.where(
                     row_at == at % page_size, token, page
                 ).astype(buf.dtype)
-
-        for half in range(2):
-            for i in range(parts):
-                copy_in(half, i).start()
-        row_at = lax.broadcasted_iota(jnp.int32, (page_size, head_dim), 0)
-        for i in range(parts):
-            copy_in(0, i).wait()
-        for r in range(req_dev):
-            fill(0, r)
+            copy_out(r).start()
         for r in range(req_dev):
             keys = buf[r, :, :, :head_dim].reshape(pages * page_size, head_dim)
             part = scale * lax.dot_general(
                 q_ref[r], keys, (((1,), (1,)), ((), ())), preferred_element_type=jnp.float32
             )
-            last = len_ref[r] + lax.broadcasted_iota(jnp.int32, part.shape, 0) // group
+            last = pick_ref[max_pages, r] + lax.broadcasted_iota(jnp.int32, part.shape, 0) // group
             scores[r * n_rows : (r + 1) * n_rows] = jnp.where(
                 lax.broadcasted_iota(jnp.int32, part.shape, 1) <= last, part, -jnp.inf
             )
-        for i in range(parts):
-            copy_in(1, i).wait()
-        for r in range(req_dev):
-            fill(1, r)
-            copy_out(r).start()
         expo = jnp.exp(scores[...] - jnp.max(scores[...], axis=1, keepdims=True))
         probs[...] = (expo / jnp.sum(expo, axis=1, keepdims=True)).astype(probs.dtype)
         for r in range(req_dev):
@@ -111,7 +89,7 @@
 
     return pl.pallas_call(
         kernel,
-        in_specs=[SMEM, SMEM, HBM, VMEM, VMEM],
+        in_specs=[SMEM, VMEM, VMEM, VMEM],
         out_specs=[HBM, VMEM],
         out_shape=[
             jax.ShapeDtypeStruct((req_dev, pages, page_size, width_two), received.dtype),
@@ -120,20 +98,19 @@
             ),
         ],
         scratch_shapes=[
-            pltpu.VMEM(received.shape, received.dtype),
             pltpu.VMEM((req_dev, pages, page_size, width_two), received.dtype),
             pltpu.VMEM((req_dev * n_rows, pages * page_size), jnp.float32),
             pltpu.VMEM((req_dev * n_rows, pages * page_size), jnp.bfloat16),
             pltpu.VMEM((n_rows, req_dev, head_dim), jnp.float32),
-            pltpu.SemaphoreType.DMA((2, parts)),
             pltpu.SemaphoreType.DMA((req_dev,)),
         ],
-        compiler_params=pltpu.CompilerParams(vmem_limit_bytes=16 * MIB),
+        compiler_params=pltpu.CompilerParams(vmem_limit_bytes=20 * MIB),
         name="intake",
-    )(pick, lens, pltpu.with_memory_space_constraint(received, pltpu.HBM), fresh, query)
-
-
-def feed_forward(hidden, gate_rows, up_rows, gain_row, w_down, n_tensor, rows_dev, keep):
+    )(pick, received, fresh, query)
+
+
+def feed_forward(hidden, gate_rows, up_rows, gain_row, w_down, n_tensor, rows_dev, place=None):
+    keep = place is not None
     blocks, rows, cols = hidden.shape
     units, width = w_down.shape
     cols_out = width // n_tensor
@@ -144,7 +121,7 @@
 
     def kernel(x_ref, gate_ref, up_in, gain_ref, down_in, out_ref, *rest):
         if keep:
-            up_ref, down_ref, scaled, sems = rest
+            place_ref, out_ref, up_ref, down_ref, part_ref, scaled, sems = (out_ref,) + rest
         else:
             up_ref, down_ref, scaled = up_in, down_in, rest[0]
 
@@ -157,6 +134,8 @@
             for m in range(2):
                 for i in range(parts):
                     copy(m, i).start()
+            mine = pl.ds(pl.multiple_of(place_ref[2] * rows_dev, rows_dev), rows_dev)
+            part_ref[...] = x_ref[place_ref[1], mine, :]
         squares = 0.0
         for i in range(blocks):
             wide = x_ref[i].astype(jnp.float32)
@@ -199,50 +178,38 @@
     scratch = [pltpu.VMEM((rows, width), jnp.bfloat16)]
     if keep:
         out_shape += [pltpu.VMEM((units, width), jnp.bfloat16)] * 2
+        out_shape += [jax.ShapeDtypeStruct((rows_dev, cols), hidden.dtype)]
         scratch += [pltpu.SemaphoreType.DMA((2, parts))]
         up_rows = pltpu.with_memory_space_constraint(up_rows, pltpu.HBM)
         w_down = pltpu.with_memory_space_constraint(w_down, pltpu.HBM)
     return pl.pallas_call(
         kernel,
-        in_specs=[VMEM, VMEM, weights, VMEM, weights],
+        in_specs=[VMEM, VMEM, weights, VMEM, weights] + [SMEM] * keep,
         out_specs=[VMEM] * len(out_shape),
         out_shape=out_shape,
         scratch_shapes=scratch,
         compiler_params=pltpu.CompilerParams(vmem_limit_bytes=28 * MIB),
         name="feed_forward",
-    )(hidden, gate_rows, up_rows, gain_row, w_down)
+    )(hidden, gate_rows, up_rows, gain_row, w_down, *([place] if keep else []))
 
 
 def add_pieces(pieces, hidden, n_steps):
     count, rows, cols = pieces.shape
-    parts = 4
-    span = count // parts
-
-    def kernel(pieces_hbm, hidden_ref, out_ref, buf, sems):
-        def copy(i):
-            part = pl.ds(i * span, span)
-            return pltpu.make_async_copy(pieces_hbm.at[part], buf.at[part], sems.at[i])
-
-        for i in range(parts):
-            copy(i).start()
+
+    def kernel(pieces_ref, hidden_ref, out_ref):
         total = hidden_ref[...].astype(jnp.float32)
-        for i in range(parts):
-            copy(i).wait()
-            total += jnp.sum(buf[i * span : (i + 1) * span].astype(jnp.float32), axis=0)
+        for i in range(count):
+            total += pieces_ref[i].astype(jnp.float32)
         out_ref[...] = total.reshape(n_steps, rows // n_steps, cols).astype(out_ref.dtype)
 
     return pl.pallas_call(
         kernel,
-        in_specs=[HBM, VMEM],
+        in_specs=[VMEM, VMEM],
         out_specs=VMEM,
         out_shape=jax.ShapeDtypeStruct((n_steps, rows // n_steps, cols), pieces.dtype),
-        scratch_shapes=[
-            pltpu.VMEM(pieces.shape, pieces.dtype),
-            pltpu.SemaphoreType.DMA((parts,)),
-        ],
         compiler_params=pltpu.CompilerParams(vmem_limit_bytes=10 * MIB),
         name="add_pieces",
-    )(pltpu.with_memory_space_constraint(pieces, pltpu.HBM), hidden)
+    )(pieces, hidden)
 
 
 def exact_dot(left, right, contract):
@@ -261,7 +228,7 @@
     capacity = pslots // n_dp
     low = 32
 
-    def kernel(place_ref, loc_hbm, len_hbm, placement_hbm, pool_hbm, out_hbm, loc, len_ref, placement_ref, pool_buf, out_buf, rows_vec, rows, loc_sem, len_sem, placement_sem, pool_sem, rows_sem, out_sems):
+    def kernel(place_ref, loc_hbm, len_hbm, placement_hbm, pool_hbm, out_buf, pick_ref, loc, len_ref, placement_ref, pool_buf, rows_vec, rows, loc_sem, len_sem, placement_sem, pool_sem, rows_sem):
         me = place_ref[0]
         len_copy = pltpu.make_async_copy(len_hbm, len_ref, len_sem)
         placement_copy = pltpu.make_async_copy(placement_hbm, placement_ref, placement_sem)
@@ -288,7 +255,8 @@
         row = by_slot[max_pages : 2 * max_pages] * low + by_slot[2 * max_pages : 3 * max_pages]
         len_row = by_slot[3 * max_pages : 3 * max_pages + 1] * low + by_slot[3 * max_pages + 8 : 3 * max_pages + 9]
         page_at = lax.broadcasted_iota(jnp.int32, (max_pages, n_req), 0).astype(jnp.float32)
-        mine = (page_at * page_size < len_row) & (source == me.astype(jnp.float32))
+        source = jnp.where(page_at * page_size < len_row, source, float(n_dp))
+        mine = source == me.astype(jnp.float32)
         ones = jnp.where(mine, 1.0, 0.0)
         earlier = jnp.where(
             lax.broadcasted_iota(jnp.int32, (max_pages, max_pages), 1)
@@ -313,12 +281,25 @@
         rows_vec[...] = (high_part * low + low_part).astype(jnp.int32)
         rows_copy = pltpu.make_async_copy(rows_vec, rows, rows_sem)
         rows_copy.start()
+        own = jnp.where(down == me * req_dev + across % req_dev, 1.0, 0.0)
+        ahead = jnp.concatenate([source, jnp.floor(len_row * (1.0 / low)), len_row - jnp.floor(len_row * (1.0 / low)) * low], axis=0)
+        ahead = jnp.concatenate([ahead, jnp.zeros((6, n_req), jnp.float32)], axis=0)
+        own_cols = exact_dot(ahead, own, ((1,), (0,)))
+        lane = lax.broadcasted_iota(jnp.int32, (max_pages, n_req), 1)
+        hit = own_cols[:max_pages] == (lane // req_dev).astype(jnp.float32)
+        ones = jnp.where(hit, 1.0, 0.0)
+        count = jnp.broadcast_to(jnp.sum(ones, axis=0, keepdims=True), (8, n_req))
+        rank = exact_dot(earlier, ones, ((1,), (0,))) + exact_dot(count, in_group, ((1,), (0,)))[:1]
+        spot = jnp.where(hit, rank + 1.0, 0.0)
+        requests = jnp.where(down % req_dev == across, 1.0, 0.0)
+        base = jnp.where(hit, (lane // req_dev).astype(jnp.float32), 0.0)
+        pick = exact_dot(base, requests, ((1,), (0,))) * capacity
+        pick += exact_dot(spot, requests, ((1,), (0,))) - 1.0
+        own_len = own_cols[max_pages : max_pages + 1] * low + own_cols[max_pages + 1 : max_pages + 2]
+        pick_ref[:max_pages] = jnp.maximum(pick, 0.0).astype(jnp.int32)
+        pick_ref[max_pages:] = jnp.broadcast_to(own_len, (8, n_req)).astype(jnp.int32)
         rows_copy.wait()
         pool_copy.wait()
-
-        def copy_out(d):
-            part = pl.ds(d * capacity, capacity)
-            return pltpu.make_async_copy(out_buf.at[part], out_hbm.at[part], out_sems.at[d])
 
         for d in range(n_dp):
 
@@ -327,20 +308,19 @@
                 return carry
 
             lax.fori_loop(0, capacity, move, 0, unroll=16)
-            copy_out(d).start()
-        for d in range(n_dp):
-            copy_out(d).wait()
 
     return pl.pallas_call(
         kernel,
         in_specs=[SMEM, HBM, HBM, HBM, HBM],
-        out_specs=HBM,
-        out_shape=pltpu.HBM(pool.shape, pool.dtype),
+        out_specs=[VMEM, VMEM],
+        out_shape=[
+            jax.ShapeDtypeStruct(pool.shape, pool.dtype),
+            jax.ShapeDtypeStruct((max_pages + 8, n_req), jnp.int32),
+        ],
         scratch_shapes=[
             pltpu.VMEM((max_pages, n_req), jnp.int32),
             pltpu.VMEM((1, n_req), jnp.int32),
             pltpu.VMEM((1, n_req), jnp.int32),
-            pltpu.VMEM(pool.shape, pool.dtype),
             pltpu.VMEM(pool.shape, pool.dtype),
             pltpu.VMEM((capacity, n_req), jnp.int32),
             pltpu.SMEM((capacity, n_req), jnp.int32),
@@ -349,9 +329,8 @@
             pltpu.SemaphoreType.DMA,
             pltpu.SemaphoreType.DMA,
             pltpu.SemaphoreType.DMA,
-            pltpu.SemaphoreType.DMA((n_dp,)),
         ],
-        compiler_params=pltpu.CompilerParams(vmem_limit_bytes=16 * MIB),
+        compiler_params=pltpu.CompilerParams(vmem_limit_bytes=20 * MIB),
         name="pack_pages",
     )(
         place,
@@ -363,55 +342,20 @@
 
 
 def add_cores(ours, from_core):
-    chips = ours.shape[0]
-
-    def kernel(a_ref, b_ref, out_ref, buf, sems):
-        def copy(i):
-            return pltpu.make_async_copy(buf.at[i], out_ref.at[i], sems.at[i])
-
-        for i in range(chips):
-            buf[i] = (a_ref[i].astype(jnp.float32) + b_ref[i].astype(jnp.float32)).astype(buf.dtype)
-            copy(i).start()
-        for i in range(chips):
-            copy(i).wait()
+    def kernel(a_ref, b_ref, out_ref):
+        for i in range(ours.shape[0]):
+            out_ref[i] = (a_ref[i].astype(jnp.float32) + b_ref[i].astype(jnp.float32)).astype(
+                out_ref.dtype
+            )
 
     return pl.pallas_call(
         kernel,
         in_specs=[VMEM, VMEM],
-        out_specs=HBM,
-        out_shape=pltpu.HBM(ours.shape, ours.dtype),
-        scratch_shapes=[pltpu.VMEM(ours.shape, ours.dtype), pltpu.SemaphoreType.DMA((chips,))],
+        out_specs=VMEM,
+        out_shape=jax.ShapeDtypeStruct(ours.shape, ours.dtype),
         compiler_params=pltpu.CompilerParams(vmem_limit_bytes=12 * MIB),
         name="add_cores",
     )(ours, from_core)
-
-
-def page_picks(page_loc, lengths, placement, dev_dp, dev_tensor, n_dp, pslots, page_size):
-    n_req = lengths.shape[0]
-    max_pages = page_loc.shape[2]
-    req_dev = n_req // n_dp
-    entries = req_dev * max_pages
-    capacity = pslots // n_dp
-    loc_head = lax.dynamic_index_in_dim(page_loc, dev_tensor, 0, keepdims=False)
-    my_slots = dev_dp * req_dev + jnp.arange(req_dev, dtype=jnp.int32)
-    slot_hot = placement[None, :] == my_slots[:, None]
-    my_len = jnp.sum(jnp.where(slot_hot, lengths[None, :], 0), axis=1)
-    my_loc = jnp.dot(
-        slot_hot.astype(jnp.float32), loc_head.astype(jnp.float32), precision=lax.Precision.HIGHEST
-    ).astype(jnp.int32)
-    pages_slot = (my_len + page_size - 1) // page_size
-    live = jnp.arange(max_pages, dtype=jnp.int32)[None, :] < pages_slot[:, None]
-    my_source = jnp.where(live, my_loc // pslots, n_dp).reshape(entries)
-    before = (
-        jnp.arange(entries, dtype=jnp.int32)[:, None] < jnp.arange(entries, dtype=jnp.int32)[None, :]
-    ).astype(jnp.bfloat16)
-    source_hot = my_source[None, :] == jnp.arange(n_dp, dtype=jnp.int32)[:, None]
-    rank_in = jnp.dot(
-        source_hot.astype(jnp.bfloat16), before, preferred_element_type=jnp.float32
-    ).astype(jnp.int32)
-    my_rank = jnp.sum(jnp.where(source_hot, rank_in, 0), axis=0)
-    pick = jnp.where(my_source < n_dp, my_source * capacity + my_rank, 0)
-    return pick, my_len
 
 
 def per_device(
@@ -449,31 +393,17 @@
     rows_core = n_steps * n_req // 2
     capacity = pslots // n_dp
 
-    outgoing = pack_pages(
-        jnp.stack([dev_dp, dev_tensor]).astype(jnp.int32),
+    place = jnp.stack([dev_dp, dev_tensor, dev_chip]).astype(jnp.int32)
+    outgoing, pick = pack_pages(
+        place,
         jnp.swapaxes(page_loc, 1, 2),
         lengths.reshape(1, n_req),
         placement.reshape(1, n_req),
         kv_pool.reshape(pslots, page_size, width_two),
         n_dp,
     )
-    outgoing, page_loc, lengths, placement = lax.optimization_barrier(
-        (outgoing, page_loc, lengths, placement)
-    )
-    pick, my_len = page_picks(
-        page_loc, lengths, placement, dev_dp, dev_tensor, n_dp, pslots, page_size
-    )
-    outgoing = outgoing.reshape(n_dp, capacity, page_size, width_two)
-    received = lax.all_to_all(outgoing, DP, 0, 0, tiled=True)
     query = jnp.transpose(queries, (1, 0, 2, 3)).reshape(req_dev, n_steps * hq_dev, head_dim)
-    cache, mixed_copies = intake(
-        pick,
-        my_len,
-        received.reshape(pslots, page_size, width_two),
-        new_kv.reshape(n_steps, req_dev, width_two).astype(jnp.float32),
-        query,
-        chips_dp,
-    )
+    fresh = new_kv.reshape(n_steps, req_dev, width_two).astype(jnp.float32)
 
     cols_dev = width // n_dp
     cols_chip = 2 * cols_dev
@@ -486,7 +416,6 @@
             jnp.concatenate([other, own], axis=-1),
         )
 
-    w_both = both(w_out, lax.ppermute(w_out, "c", swap))
     resid_rows = jnp.transpose(
         resid_in.reshape(n_steps, chips_dp, 2, req_dev, cols_dev), (2, 1, 0, 3, 4)
     ).reshape(2, n_tensor, rows_core // n_tensor, cols_dev)
@@ -497,6 +426,18 @@
         )[0, 0]
 
     resid_blk = both(resid_of(core), lax.ppermute(resid_of(1 - core), "c", swap))
+    w_other = lax.ppermute(w_out, "c", swap)
+    outgoing, pick, query, fresh, resid_blk, w_other, place = lax.optimization_barrier(
+        (outgoing, pick, query, fresh, resid_blk, w_other, place)
+    )
+    received = lax.all_to_all(
+        outgoing.reshape(n_dp, capacity, page_size, width_two), DP, 0, 0, tiled=True
+    )
+    cache, mixed_copies = intake(
+        pick, received.reshape(pslots, page_size, width_two), fresh, query, chips_dp
+    )
+
+    w_both = both(w_out, w_other)
     mixed_rows = lax.all_to_all(mixed_copies, CHIP_DP, 0, 0, tiled=True).reshape(
         rows_core, hq_dev * head_dim
     )
@@ -519,19 +460,16 @@
     gain_row = ffn_gain.reshape(1, width)
     width_out = width // n_tensor
 
-    ours, up_near, down_near = feed_forward(
-        own_rows, gate_rows, up_rows, gain_row, w_down, n_tensor, rows_dev, True
+    ours, up_near, down_near, own_hidden = feed_forward(
+        own_rows, gate_rows, up_rows, gain_row, w_down, n_tensor, rows_dev, place
     )
     other_rows, ours = lax.optimization_barrier((other_rows, ours))
     (theirs,) = feed_forward(
-        other_rows, gate_rows, up_near, gain_row, down_near, n_tensor, rows_dev, False
+        other_rows, gate_rows, up_near, gain_row, down_near, n_tensor, rows_dev
     )
     from_core = lax.ppermute(theirs, "c", swap)
     chip_sum = add_cores(ours, from_core).reshape(chips_dp * n_tensor, rows_dev, width_out)
     pieces = lax.all_to_all(chip_sum, CHIPS, 0, 0, tiled=True)
-    own_hidden = lax.dynamic_slice(
-        own_rows, (dev_tensor, dev_chip * rows_dev, 0), (1, rows_dev, cols_chip)
-    )[0]
     block_out = add_pieces(pieces, own_hidden, n_steps)
     return (block_out, cache.reshape(1, req_dev, cache_len, width_two))
 

time: 192 us -> 178 us (0.927)
  blocking collectives: 31.3 us -> 150 us
  waiting for transfers between devices: 104 us -> 3.79 us
  starting transfers between devices: 26.2 us -> 1.23 us
  Pallas kernels: 26.2 us -> 18.8 us
    all_to_all x0 -> x4, blocking collectives: none -> 118 us  [the longest x1 58.6 us: per_device(): lax.all_to_all(outgoing.reshape(n_dp, capacity, page_size, width_two), DP...]
    all_to_all x4 -> x0, waiting for transfers between devices: 99.9 us -> none  [the longest x1 54.4 us: per_device(): received = lax.all_to_all(outgoing, DP, 0, 0, tiled=True)]
    all_to_all x4 -> x0, starting transfers between devices: 25.1 us -> none  [the longest x1 7.31 us: per_device(): received = lax.all_to_all(outgoing, DP, 0, 0, tiled=True)]
    pallas_call x6, Pallas kernels: 26.2 us -> 18.8 us  [the longest x2 9.6 us: feed_forward(): pl.pallas_call(kernel, in_specs=[VMEM, VMEM, weights, VMEM, weights] + [S...]
  transfers between devices with their start and end apart: 8 -> 4, of which waited for: 5 -> 1; matrix products, arithmetic and copies ran while one was open for 1% -> 1% of each run, Pallas kernels for 7% -> 6%
where the time goes in v7:
time: 178 us; the launch traced here: 177 us
  blocking collectives  150 us (84%)
  Pallas kernels  18.8 us (11%)
  waiting for transfers between devices  3.79 us (2%)
    all_to_all x1, blocking collectives, per_device(): lax.all_to_all(outgoing.reshape(n_dp, capacity, page_size, width_two), DP...  58.6 us
    all_to_all x1, blocking collectives, per_device(): pieces = lax.all_to_all(chip_sum, CHIPS, 0, 0, tiled=True)  35.6 us
    all_to_all x1, blocking collectives, to_all(): return lax.all_to_all(copies, axes, 0, 0, tiled=True)  31.7 us
    all_to_all x1, blocking collectives, per_device(): lax.all_to_all(partial_out.reshape(n_tensor, rows_blk, cols_chip), TENSOR...  12.5 us
    all_to_all x1, blocking collectives, per_device(): lax.all_to_all(mixed_copies, CHIP_DP, 0, 0, tiled=True)  11.4 us
    pallas_call x2, Pallas kernels, feed_forward(): pl.pallas_call(kernel, in_specs=[VMEM, VMEM, weights, VMEM, weights] + [S...  9.6 us
    pallas_call x1, Pallas kernels, intake(): pl.pallas_call(kernel, in_specs=[SMEM, VMEM, VMEM, VMEM], out_specs=[HBM,...  4.17 us
    ppermute x1, waiting for transfers between devices, per_device(): from_core = lax.ppermute(theirs, 'c', swap)  3.79 us
  transfers between devices with their start and end apart: 4, of which 1 were waited for; matrix products, arithmetic and copies ran while one was open for 1% of the time, Pallas kernels for 6%

profile of v7, /device:TPU:0, one launch (start us, length us, event | category | flops | bytes accessed | tf_op | source)
XLA Modules:
  0.0 177.3 jit_solution(424209510266787013)
XLA Ops:
  0.6 0.0 copy-start
  0.6 0.1 collective-permute-start.1
  0.7 1.0 copy.23
  1.7 0.6 collective-permute-start
  2.3 0.7 bitcast_convert_fusion.fresh_ref
  3.0 0.0 copy-done
  3.0 0.1 pad_add_fusion.place_ref.out_ref
  3.1 3.6 %pack_pages.1 = (bf16[512,16,256]{2,1,0:T(8,128)(2,1)S(1)}, s32[72,128]{1,0:T(8,128)S(1)}) custom-call(s32[3]{0:T(128)S(1)} %pad_add_fusion.place_ref.out_ref, s32[8,64,128]{2,1,0:T(8,128)} %bitcast.53, s32[1,128]{1,0:T(1,128)} %bitcast.54, s32[1,128]{1,0:T(1,128)} %bitcast.55, bf16[512,16,256]{2,1,0:T(8,128)(2,1)} %bitcast.47), custom_call_target="tpu_custom_call" | custom-call | tf_op jit(solution)/shard_map/pack_pages/pallas_call | solution.py:312
  6.7 0.0 collective-permute-done
  6.8 0.0 collective-permute-done.1
  6.8 58.6 %all_to_all.25 = bf16[16,32,16,256]{3,2,1,0:T(8,128)(2,1)S(1)} all-to-all(bf16[16,32,16,256]{3,2,1,0:T(8,128)(2,1)S(1)} %bitcast.44), channel_id=1, replica_groups=mesh['yh'=2,'x'=4,'c'=2,'z'=4,'yl'=2] {'yh','x','c'}, dimensions={0} | all-to-all | bytes 8388608 | tf_op jit(solution)/shard_map/all_to_all | solution.py:433
  65.4 0.0 copy-start.3
  65.4 4.2 %intake.1 = (bf16[8,65,16,256]{3,2,1,0:T(8,128)(2,1)}, bf16[8,16,1024]{2,1,0:T(8,128)(2,1)S(1)}) custom-call(s32[72,128]{1,0:T(8,128)S(1)} %get-tuple-element.22.pick_ref, bf16[512,16,256]{2,1,0:T(8,128)(2,1)S(1)} %bitcast.38, f32[2,8,256]{2,1,0:T(8,128)S(1)} %bitcast_convert_fusion.fresh_ref, bf16[8,16,128]{2,1,0:T(8,128)(2,1)S(1)} %copy_bitcast_fusion.1.q_ref), custom_call_target="tpu_custom_call" | custom-call | tf_op jit(solution)/shard_map/intake/pallas_call | solution.py:90
  69.6 11.4 %all_to_all.26 = bf16[8,16,1024]{2,1,0:T(8,128)(2,1)S(1)} all-to-all(bf16[8,16,1024]{2,1,0:T(8,128)(2,1)S(1)} %get-tuple-element.26), channel_id=1, replica_groups=mesh['yh'=2,'x'=4,'c'=2,'z'=4,'yl'=2] {'yh','x'}, dimensions={0} | all-to-all | bytes 524288 | tf_op jit(solution)/shard_map/all_to_all | solution.py:441
  81.0 0.0 copy-done.3
  81.0 0.7 fusion.7
  81.8 12.5 %all_to_all.27 = bf16[8,16,1024]{2,1,0:T(8,128)(2,1)S(1)} all-to-all(bf16[8,16,1024]{2,1,0:T(8,128)(2,1)S(1)} %bitcast.52), channel_id=1, replica_groups=mesh['yh'=2,'x'=4,'c'=2,'z'=4,'yl'=2] {'z','yl'}, dimensions={0} | all-to-all | bytes 524288 | tf_op jit(solution)/shard_map/all_to_all | solution.py:448
  94.3 0.2 broadcast_in_dim.2
  94.6 0.0 copy-start.1
  94.6 0.0 copy-start.2
  94.6 31.7 %all_to_all.28 = bf16[64,16,1024]{2,1,0:T(8,128)(2,1)S(1)} all-to-all(bf16[64,16,1024]{2,1,0:T(8,128)(2,1)S(1)} %broadcast_in_dim.2), channel_id=1, replica_groups=mesh['yh'=2,'x'=4,'c'=2,'z'=4,'yl'=2] {'yh','x','z','yl'}, dimensions={0} | all-to-all | bytes 4194304 | tf_op jit(solution)/shard_map/all_to_all | solution.py:18
  126.4 0.0 collective-permute-start.2
  126.4 0.0 copy-done.1
  126.4 0.0 copy-done.2
  126.4 6.3 %feed_forward.2 = (bf16[8,8,16,1024]{3,2,1,0:T(8,128)(2,1)S(1)}, bf16[224,8192]{1,0:T(8,128)(2,1)S(1)}, bf16[224,8192]{1,0:T(8,128)(2,1)S(1)}, bf16[16,1024]{1,0:T(8,128)(2,1)S(1)}) custom-call(bf16[8,128,1024]{2,1,0:T(8,128)(2,1)S(1)} %bitcast.42, bf16[224,8192]{1,0:T(8,128)(2,1)S(1)} %bitcast.39, bf16[224,8192]{1,0:T(8,128)(2,1)} %bitcast.48, ...), custom_call_target="tpu_custom_call" | custom-call | tf_op jit(solution)/shard_map/feed_forward/pallas_call | solution.py:185
  132.6 0.0 collective-permute-done.2.x_ref
  132.6 3.3 %feed_forward.3 = bf16[8,8,16,1024]{3,2,1,0:T(8,128)(2,1)S(1)} custom-call(bf16[8,128,1024]{2,1,0:T(8,128)(2,1)S(1)} %collective-permute-done.2.x_ref, bf16[224,8192]{1,0:T(8,128)(2,1)S(1)} %bitcast.40, bf16[224,8192]{1,0:T(8,128)(2,1)S(1)} %get-tuple-element.32.up_in, f32[1,8192]{1,0:T(1,128)S(1)} %bitcast.46, bf16[224,8192]{1,0:T(8,128)(2,1)S(1)} %get-tuple-element.33.down_in), custom_call_target="tpu_custom_call" | custom-call | tf_op jit(solution)/shard_map/feed_forward/pallas_call | solution.py:185
  136.0 0.6 collective-permute-start.3
  136.6 3.8 %collective-permute-done.3.b_ref = bf16[8,8,16,1024]{3,2,1,0:T(8,128)(2,1)S(1)} collective-permute-done((bf16[8,8,16,1024]{3,2,1,0:T(8,128)(2,1)S(1)}, bf16[8,8,16,1024]{3,2,1,0:T(8,128)(2,1)S(1)}, u32[]{:S(2)}, u32[]{:S(2)}) %collective-permute-start.3) | collective-permute-done | bytes 2097184 | tf_op jit(solution)/shard_map/ppermute | solution.py:470
  140.4 0.5 add_cores.1
  140.8 35.6 %all_to_all.29.pieces_ref = bf16[64,16,1024]{2,1,0:T(8,128)(2,1)S(1)} all-to-all(bf16[64,16,1024]{2,1,0:T(8,128)(2,1)S(1)} %bitcast.43), channel_id=1, replica_groups=mesh['yh'=2,'x'=4,'c'=2,'z'=4,'yl'=2] {'yh','x','z','yl'}, dimensions={0} | all-to-all | bytes 4194304 | tf_op jit(solution)/shard_map/all_to_all | solution.py:472
  176.4 0.9 add_pieces.1
  (5 shorter events, 0.1 us)
Async XLA Ops:
  0.6 2.4 %copy-start = (bf16[2,8,8,128]{3,2,1,0:T(8,128)(2,1)S(1)}, bf16[2,8,8,128]{3,2,1,0:T(8,128)(2,1)}, u32[]{:S(2)}) copy-start(bf16[2,8,8,128]{3,2,1,0:T(8,128)(2,1)} %param.16) | copy-start | bytes 98308
  0.6 6.1 %collective-permute-start.1 = (bf16[1024,512]{1,0:T(8,128)(2,1)}, bf16[1024,512]{1,0:T(8,128)(2,1)S(1)}, u32[]{:S(2)}, u32[]{:S(2)}) collective-permute-start(bf16[1024,512]{1,0:T(8,128)(2,1)} %param.19), channel_id=1, source_target_pairs={{0,8},{8,0},{1,9},{9,1},{2,10},{10,2},{3,11},{11,3},{4,12},{12,4},... | collective-permute-start | bytes 3145736 | tf_op jit(solution)/shard_map/ppermute | solution.py:429
  1.7 5.0 %collective-permute-start = (bf16[16,512]{1,0:T(8,128)(2,1)S(1)}, bf16[16,512]{1,0:T(8,128)(2,1)S(1)}, u32[]{:S(2)}, u32[]{:S(2)}) collective-permute-start(bf16[16,512]{1,0:T(8,128)(2,1)S(1)} %get-tuple-element.37), channel_id=1, source_target_pairs={{0,8},{8,0},{1,9},{9,1},{2,10},{10,2},{3,11},{11,3},{4,12},{12,4},... | collective-permute-start | bytes 49160 | tf_op jit(solution)/shard_map/ppermute | solution.py:428
  65.4 15.6 %copy-start.3 = (bf16[1024,512]{1,0:T(8,128)(2,1)S(1)}, bf16[1024,512]{1,0:T(8,128)(2,1)}, u32[]{:S(2)}) copy-start(bf16[1024,512]{1,0:T(8,128)(2,1)} %param.19) | copy-start | bytes 3145732
  94.6 31.8 %copy-start.1 = (bf16[8192,224]{0,1:T(8,128)(2,1)S(1)}, bf16[8192,224]{0,1:T(8,128)(2,1)}, u32[]{:S(2)}) copy-start(bf16[8192,224]{0,1:T(8,128)(2,1)} %param.21) | copy-start | bytes 11010052
  94.6 31.8 %copy-start.2 = (f32[8192]{0:T(1024)S(1)}, f32[8192]{0:T(1024)}, u32[]{:S(2)}) copy-start(f32[8192]{0:T(1024)} %param.20) | copy-start | bytes 98308
  126.4 6.3 %collective-permute-start.2 = (bf16[8,128,1024]{2,1,0:T(8,128)(2,1)S(1)}, bf16[8,128,1024]{2,1,0:T(8,128)(2,1)S(1)}, u32[]{:S(2)}, u32[]{:S(2)}) collective-permute-start(bf16[8,128,1024]{2,1,0:T(8,128)(2,1)S(1)} %bitcast.41), channel_id=1, source_target_pairs={{0,8},{8,0},{1,9},{9,1},{2,10},{10,2},{3,11},{11,3},{4,12},{12,4},... | collective-permute-start | bytes 6291464 | tf_op jit(solution)/shard_map/ppermute | solution.py:457
  136.0 4.4 %collective-permute-start.3 = (bf16[8,8,16,1024]{3,2,1,0:T(8,128)(2,1)S(1)}, bf16[8,8,16,1024]{3,2,1,0:T(8,128)(2,1)S(1)}, u32[]{:S(2)}, u32[]{:S(2)}) collective-permute-start(bf16[8,8,16,1024]{3,2,1,0:T(8,128)(2,1)S(1)} %feed_forward.3), channel_id=1, source_target_pairs={{0,8},{8,0},{1,9},{9,1},{2,10},{10,2},{3,11},{11,3},{4,12},{12,4},... | collective-permute-start | bytes 6291464 | tf_op jit(solution)/shard_map/ppermute | solution.py:470

commit v8 on v7

--- a/solution.py
+++ b/solution.py
@@ -36,6 +36,7 @@
             return pltpu.make_async_copy(buf.at[r], cache_ref.at[r], out_sems.at[r])
 
         row_at = lax.broadcasted_iota(jnp.int32, (page_size, width_two), 0)
+        tokens_new = [fresh_ref[s].astype(jnp.float32) for s in range(n_steps)]
         for r in range(req_dev):
 
             def move(p, carry):
@@ -56,7 +57,7 @@
             for s in range(n_steps):
                 at = length + s
                 page = buf[r, at // page_size].astype(jnp.float32)
-                token = fresh_ref[s, r : r + 1, :]
+                token = tokens_new[s][r : r + 1]
                 buf[r, at // page_size] = jnp.where(
                     row_at == at % page_size, token, page
                 ).astype(buf.dtype)
@@ -109,88 +110,134 @@
     )(pick, received, fresh, query)
 
 
-def feed_forward(hidden, gate_rows, up_rows, gain_row, w_down, n_tensor, rows_dev, place=None):
-    keep = place is not None
-    blocks, rows, cols = hidden.shape
+PARTS = 4
+NT = (((1,), (1,)), ((), ()))
+
+
+def in_parts(source, target, sems):
+    span = target.shape[1] // PARTS
+    copies = []
+    for i in range(PARTS):
+        part = pl.ds(i * span, span)
+        copies.append(pltpu.make_async_copy(source.at[:, part], target.at[:, part], sems.at[i]))
+        copies[-1].start()
+    return copies
+
+
+def scale_rows(x_ref, gain_ref, scaled):
+    blocks, _, cols = x_ref.shape
+    squares = 0.0
+    for i in range(blocks):
+        wide = x_ref[i].astype(jnp.float32)
+        square = wide * wide
+        squares += sum(square[:, k * 128 : (k + 1) * 128] for k in range(cols // 128))
+        scaled[:, i * cols : (i + 1) * cols] = (
+            wide * gain_ref[:, i * cols : (i + 1) * cols]
+        ).astype(scaled.dtype)
+    mean = jnp.sum(squares, axis=1, keepdims=True) * (1.0 / (blocks * cols))
+    return lax.rsqrt(mean + 1e-05)
+
+
+def activate(gate, upper):
+    return (gate / (1.0 + jnp.exp(-gate)) * upper).astype(jnp.bfloat16)
+
+
+def down_to(out_ref, act, down_ref, waits=()):
+    chips, n_tensor, rows_dev, cols_out = out_ref.shape
+    for t in range(n_tensor):
+        if waits and t % (n_tensor // PARTS) == 0:
+            waits[t // (n_tensor // PARTS)].wait()
+        out = jnp.dot(
+            act,
+            down_ref[:, t * cols_out : (t + 1) * cols_out],
+            preferred_element_type=jnp.float32,
+        )
+        out_ref[:, t] = out.astype(out_ref.dtype).reshape(chips, rows_dev, cols_out)
+
+
+def expand_own(hidden, gate_rows, up_rows, gain_row, place, rows_dev):
+    _, rows, cols = hidden.shape
+    units, width = up_rows.shape
+
+    def kernel(place_ref, x_ref, gate_ref, up_hbm, gain_ref, act_ref, up_ref, part_ref, scaled, sems):
+        copies = in_parts(up_hbm, up_ref, sems)
+        mine = pl.ds(pl.multiple_of(place_ref[2] * rows_dev, rows_dev), rows_dev)
+        part_ref[...] = x_ref[place_ref[1], mine, :]
+        inverse = scale_rows(x_ref, gain_ref, scaled)
+        gate = lax.dot_general(scaled[...], gate_ref[...], NT, preferred_element_type=jnp.float32)
+        upper = 0.0
+        span = width // PARTS
+        for i in range(PARTS):
+            part = slice(i * span, (i + 1) * span)
+            copies[i].wait()
+            upper += lax.dot_general(
+                scaled[:, part], up_ref[:, part], NT, preferred_element_type=jnp.float32
+            )
+        act_ref[...] = activate(gate * inverse, upper * inverse)
+
+    return pl.pallas_call(
+        kernel,
+        in_specs=[SMEM, VMEM, VMEM, HBM, VMEM],
+        out_specs=[VMEM] * 3,
+        out_shape=[
+            pltpu.VMEM((rows, units), jnp.bfloat16),
+            pltpu.VMEM((units, width), jnp.bfloat16),
+            jax.ShapeDtypeStruct((rows_dev, cols), hidden.dtype),
+        ],
+        scratch_shapes=[
+            pltpu.VMEM((rows, width), jnp.bfloat16),
+            pltpu.SemaphoreType.DMA((PARTS,)),
+        ],
+        compiler_params=pltpu.CompilerParams(vmem_limit_bytes=24 * MIB),
+        name="expand_own",
+    )(place, hidden, gate_rows, pltpu.with_memory_space_constraint(up_rows, pltpu.HBM), gain_row)
+
+
+def feed_forward(hidden, gate_rows, up_rows, gain_row, w_down, n_tensor, rows_dev):
+    _, rows, _ = hidden.shape
     units, width = w_down.shape
-    cols_out = width // n_tensor
-    chips = rows // rows_dev
-    contract = (((1,), (1,)), ((), ()))
-    parts = 4
-    span = width // parts
-
-    def kernel(x_ref, gate_ref, up_in, gain_ref, down_in, out_ref, *rest):
-        if keep:
-            place_ref, out_ref, up_ref, down_ref, part_ref, scaled, sems = (out_ref,) + rest
-        else:
-            up_ref, down_ref, scaled = up_in, down_in, rest[0]
-
-        def copy(m, i):
-            source, target = [(up_in, up_ref), (down_in, down_ref)][m]
-            part = pl.ds(i * span, span)
-            return pltpu.make_async_copy(source.at[:, part], target.at[:, part], sems.at[m, i])
-
-        if keep:
-            for m in range(2):
-                for i in range(parts):
-                    copy(m, i).start()
-            mine = pl.ds(pl.multiple_of(place_ref[2] * rows_dev, rows_dev), rows_dev)
-            part_ref[...] = x_ref[place_ref[1], mine, :]
-        squares = 0.0
-        for i in range(blocks):
-            wide = x_ref[i].astype(jnp.float32)
-            square = wide * wide
-            squares += sum(square[:, k * 128 : (k + 1) * 128] for k in range(cols // 128))
-            scaled[:, i * cols : (i + 1) * cols] = (
-                wide * gain_ref[:, i * cols : (i + 1) * cols]
-            ).astype(scaled.dtype)
-        gate = lax.dot_general(
-            scaled[...], gate_ref[...], contract, preferred_element_type=jnp.float32
-        )
-        if keep:
-            upper = 0.0
-            for i in range(parts):
-                part = slice(i * span, (i + 1) * span)
-                copy(0, i).wait()
-                upper += lax.dot_general(
-                    scaled[:, part], up_ref[:, part], contract, preferred_element_type=jnp.float32
-                )
-        else:
-            upper = lax.dot_general(
-                scaled[...], up_ref[...], contract, preferred_element_type=jnp.float32
-            )
-        inverse = lax.rsqrt(jnp.sum(squares, axis=1, keepdims=True) * (1.0 / width) + 1e-05)
-        gate = gate * inverse
-        upper = upper * inverse
-        act = (gate / (1.0 + jnp.exp(-gate)) * upper).astype(jnp.bfloat16)
-        for t in range(n_tensor):
-            if keep and t % (n_tensor // parts) == 0:
-                copy(1, t // (n_tensor // parts)).wait()
-            out = jnp.dot(
-                act,
-                down_ref[:, t * cols_out : (t + 1) * cols_out],
-                preferred_element_type=jnp.float32,
-            )
-            out_ref[:, t] = out.astype(out_ref.dtype).reshape(chips, rows_dev, cols_out)
-
-    weights = HBM if keep else VMEM
-    out_shape = [jax.ShapeDtypeStruct((chips, n_tensor, rows_dev, cols_out), jnp.bfloat16)]
-    scratch = [pltpu.VMEM((rows, width), jnp.bfloat16)]
-    if keep:
-        out_shape += [pltpu.VMEM((units, width), jnp.bfloat16)] * 2
-        out_shape += [jax.ShapeDtypeStruct((rows_dev, cols), hidden.dtype)]
-        scratch += [pltpu.SemaphoreType.DMA((2, parts))]
-        up_rows = pltpu.with_memory_space_constraint(up_rows, pltpu.HBM)
-        w_down = pltpu.with_memory_space_constraint(w_down, pltpu.HBM)
-    return pl.pallas_call(
-        kernel,
-        in_specs=[VMEM, VMEM, weights, VMEM, weights] + [SMEM] * keep,
-        out_specs=[VMEM] * len(out_shape),
-        out_shape=out_shape,
-        scratch_shapes=scratch,
+
+    def kernel(x_ref, gate_ref, up_ref, gain_ref, down_hbm, out_ref, down_ref, scaled, sems):
+        copies = in_parts(down_hbm, down_ref, sems)
+        inverse = scale_rows(x_ref, gain_ref, scaled)
+        gate = lax.dot_general(scaled[...], gate_ref[...], NT, preferred_element_type=jnp.float32)
+        upper = lax.dot_general(scaled[...], up_ref[...], NT, preferred_element_type=jnp.float32)
+        down_to(out_ref, activate(gate * inverse, upper * inverse), down_ref, copies)
+
+    return pl.pallas_call(
+        kernel,
+        in_specs=[VMEM, VMEM, VMEM, VMEM, HBM],
+        out_specs=[VMEM] * 2,
+        out_shape=[
+            jax.ShapeDtypeStruct(
+                (rows // rows_dev, n_tensor, rows_dev, width // n_tensor), jnp.bfloat16
+            ),
+            pltpu.VMEM((units, width), jnp.bfloat16),
+        ],
+        scratch_shapes=[
+            pltpu.VMEM((rows, width), jnp.bfloat16),
+            pltpu.SemaphoreType.DMA((PARTS,)),
+        ],
         compiler_params=pltpu.CompilerParams(vmem_limit_bytes=28 * MIB),
         name="feed_forward",
-    )(hidden, gate_rows, up_rows, gain_row, w_down, *([place] if keep else []))
+    )(hidden, gate_rows, up_rows, gain_row, pltpu.with_memory_space_constraint(w_down, pltpu.HBM))
+
+
+def shrink_own(act, w_down, n_tensor, rows_dev):
+    def kernel(act_ref, down_ref, out_ref):
+        down_to(out_ref, act_ref[...], down_ref)
+
+    return pl.pallas_call(
+        kernel,
+        in_specs=[VMEM, VMEM],
+        out_specs=VMEM,
+        out_shape=jax.ShapeDtypeStruct(
+            (act.shape[0] // rows_dev, n_tensor, rows_dev, w_down.shape[1] // n_tensor),
+            jnp.bfloat16,
+        ),
+        compiler_params=pltpu.CompilerParams(vmem_limit_bytes=16 * MIB),
+        name="shrink_own",
+    )(act, w_down)
 
 
 def add_pieces(pieces, hidden, n_steps):
@@ -403,7 +450,7 @@
         n_dp,
     )
     query = jnp.transpose(queries, (1, 0, 2, 3)).reshape(req_dev, n_steps * hq_dev, head_dim)
-    fresh = new_kv.reshape(n_steps, req_dev, width_two).astype(jnp.float32)
+    fresh = new_kv.reshape(n_steps, req_dev, width_two)
 
     cols_dev = width // n_dp
     cols_chip = 2 * cols_dev
@@ -416,19 +463,17 @@
             jnp.concatenate([other, own], axis=-1),
         )
 
-    resid_rows = jnp.transpose(
-        resid_in.reshape(n_steps, chips_dp, 2, req_dev, cols_dev), (2, 1, 0, 3, 4)
-    ).reshape(2, n_tensor, rows_core // n_tensor, cols_dev)
-
     def resid_of(at_core):
         return lax.dynamic_slice(
-            resid_rows, (at_core, dev_tensor, 0, 0), (1, 1) + resid_rows.shape[2:]
-        )[0, 0]
+            resid_in,
+            (0, (2 * dev_tensor + at_core) * req_dev, 0),
+            (n_steps, req_dev, cols_dev),
+        ).reshape(rows_dev, cols_dev)
 
     resid_blk = both(resid_of(core), lax.ppermute(resid_of(1 - core), "c", swap))
     w_other = lax.ppermute(w_out, "c", swap)
-    outgoing, pick, query, fresh, resid_blk, w_other, place = lax.optimization_barrier(
-        (outgoing, pick, query, fresh, resid_blk, w_other, place)
+    outgoing, pick, query, resid_blk, w_other, place = lax.optimization_barrier(
+        (outgoing, pick, query, resid_blk, w_other, place)
     )
     received = lax.all_to_all(
         outgoing.reshape(n_dp, capacity, page_size, width_two), DP, 0, 0, tiled=True
@@ -460,14 +505,15 @@
     gain_row = ffn_gain.reshape(1, width)
     width_out = width // n_tensor
 
-    ours, up_near, down_near, own_hidden = feed_forward(
-        own_rows, gate_rows, up_rows, gain_row, w_down, n_tensor, rows_dev, place
-    )
-    other_rows, ours = lax.optimization_barrier((other_rows, ours))
-    (theirs,) = feed_forward(
-        other_rows, gate_rows, up_near, gain_row, down_near, n_tensor, rows_dev
+    act_own, up_near, own_hidden = expand_own(
+        own_rows, gate_rows, up_rows, gain_row, place, rows_dev
+    )
+    other_rows, act_own = lax.optimization_barrier((other_rows, act_own))
+    theirs, down_near = feed_forward(
+        other_rows, gate_rows, up_near, gain_row, w_down, n_tensor, rows_dev
     )
     from_core = lax.ppermute(theirs, "c", swap)
+    ours = shrink_own(act_own, down_near, n_tensor, rows_dev)
     chip_sum = add_cores(ours, from_core).reshape(chips_dp * n_tensor, rows_dev, width_out)
     pieces = lax.all_to_all(chip_sum, CHIPS, 0, 0, tiled=True)
     block_out = add_pieces(pieces, own_hidden, n_steps)

time: 178 us -> 178 us (level)
    pallas_call x2 -> x3, Pallas kernels: 9.6 us -> 11.1 us  [the longest x1 6.2 us: expand_own(): pl.pallas_call(kernel, in_specs=[SMEM, VMEM, VMEM, HBM, VMEM], out_specs=...]
  transfers between devices with their start and end apart: 4 -> 4, of which waited for: 1 -> 1; matrix products, arithmetic and copies ran while one was open for 1% -> 0% of each run, Pallas kernels for 6% -> 6%
where the time goes in v8:
time: 178 us
  blocking collectives  151 us (85%)
  Pallas kernels  19.5 us (11%)
  waiting for transfers between devices  3.08 us (2%)
    all_to_all x1, blocking collectives, per_device(): lax.all_to_all(outgoing.reshape(n_dp, capacity, page_size, width_two), DP...  58.6 us
    all_to_all x1, blocking collectives, per_device(): pieces = lax.all_to_all(chip_sum, CHIPS, 0, 0, tiled=True)  35.8 us
    all_to_all x1, blocking collectives, to_all(): return lax.all_to_all(copies, axes, 0, 0, tiled=True)  31.8 us
    all_to_all x1, blocking collectives, per_device(): lax.all_to_all(partial_out.reshape(n_tensor, rows_blk, cols_chip), TENSOR...  12.5 us
    all_to_all x1, blocking collectives, per_device(): lax.all_to_all(mixed_copies, CHIP_DP, 0, 0, tiled=True)  12.4 us
    pallas_call x1, Pallas kernels, expand_own(): pl.pallas_call(kernel, in_specs=[SMEM, VMEM, VMEM, HBM, VMEM], out_specs=...  6.2 us
    pallas_call x1, Pallas kernels, feed_forward(): pl.pallas_call(kernel, in_specs=[VMEM, VMEM, VMEM, VMEM, HBM], out_specs=...  4.24 us
    pallas_call x1, Pallas kernels, pack_pages(): pl.pallas_call(kernel, in_specs=[SMEM, HBM, HBM, HBM, HBM], out_specs=[VM...  3.63 us
  transfers between devices with their start and end apart: 4, of which 1 were waited for; matrix products, arithmetic and copies ran while one was open for 0% of the time, Pallas kernels for 6%

profile of v8, /device:TPU:0, one launch (start us, length us, event | category | flops | bytes accessed | tf_op | source)
XLA Modules:
  0.0 177.7 jit_solution(5699290285740420352)
XLA Ops:
  0.6 0.0 copy-start
  0.6 0.1 collective-permute-start.1
  0.8 0.7 dynamic-slice_bitcast_fusion.1
  1.5 0.5 collective-permute-start
  2.0 0.0 copy-done
  2.0 0.1 pad_add_fusion.place_ref
  2.1 3.6 %pack_pages.1 = (bf16[512,16,256]{2,1,0:T(8,128)(2,1)S(1)}, s32[72,128]{1,0:T(8,128)S(1)}) custom-call(s32[3]{0:T(128)S(1)} %pad_add_fusion.place_ref, s32[8,64,128]{2,1,0:T(8,128)} %bitcast.42, s32[1,128]{1,0:T(1,128)} %bitcast.43, s32[1,128]{1,0:T(1,128)} %bitcast.44, bf16[512,16,256]{2,1,0:T(8,128)(2,1)} %bitcast.38), custom_call_target="tpu_custom_call" | custom-call | tf_op jit(solution)/shard_map/pack_pages/pallas_call | solution.py:359
  5.7 0.0 collective-permute-done
  5.7 0.0 collective-permute-done.1
  5.7 0.0 copy-start.3
  5.8 58.6 %all_to_all.25 = bf16[16,32,16,256]{3,2,1,0:T(8,128)(2,1)S(1)} all-to-all(bf16[16,32,16,256]{3,2,1,0:T(8,128)(2,1)S(1)} %bitcast.34), channel_id=1, replica_groups=mesh['yh'=2,'x'=4,'c'=2,'z'=4,'yl'=2] {'yh','x','c'}, dimensions={0} | all-to-all | bytes 8388608 | tf_op jit(solution)/shard_map/all_to_all | solution.py:478
  64.4 0.0 copy-done.3
  64.4 0.0 copy-start.4
  64.4 3.3 %intake.1 = (bf16[8,65,16,256]{3,2,1,0:T(8,128)(2,1)}, bf16[8,16,1024]{2,1,0:T(8,128)(2,1)S(1)}) custom-call(s32[72,128]{1,0:T(8,128)S(1)} %get-tuple-element.22.pick_ref, bf16[512,16,256]{2,1,0:T(8,128)(2,1)S(1)} %bitcast.28, bf16[2,8,256]{2,1,0:T(8,128)(2,1)S(1)} %bitcast.37, bf16[8,16,128]{2,1,0:T(8,128)(2,1)S(1)} %copy_bitcast_fusion.q_ref), custom_call_target="tpu_custom_call" | custom-call | tf_op jit(solution)/shard_map/intake/pallas_call | solution.py:91
  67.7 12.4 %all_to_all.26 = bf16[8,16,1024]{2,1,0:T(8,128)(2,1)S(1)} all-to-all(bf16[8,16,1024]{2,1,0:T(8,128)(2,1)S(1)} %get-tuple-element.25), channel_id=1, replica_groups=mesh['yh'=2,'x'=4,'c'=2,'z'=4,'yl'=2] {'yh','x'}, dimensions={0} | all-to-all | bytes 524288 | tf_op jit(solution)/shard_map/all_to_all | solution.py:486
  80.1 0.0 copy-done.4
  80.1 0.8 fusion.7
  80.9 12.5 %all_to_all.27 = bf16[8,16,1024]{2,1,0:T(8,128)(2,1)S(1)} all-to-all(bf16[8,16,1024]{2,1,0:T(8,128)(2,1)S(1)} %bitcast.41), channel_id=1, replica_groups=mesh['yh'=2,'x'=4,'c'=2,'z'=4,'yl'=2] {'z','yl'}, dimensions={0} | all-to-all | bytes 524288 | tf_op jit(solution)/shard_map/all_to_all | solution.py:493
  93.4 0.2 broadcast_in_dim.2
  93.7 0.0 copy-start.1
  93.7 0.0 copy-start.2
  93.7 31.8 %all_to_all.28 = bf16[64,16,1024]{2,1,0:T(8,128)(2,1)S(1)} all-to-all(bf16[64,16,1024]{2,1,0:T(8,128)(2,1)S(1)} %broadcast_in_dim.2), channel_id=1, replica_groups=mesh['yh'=2,'x'=4,'c'=2,'z'=4,'yl'=2] {'yh','x','z','yl'}, dimensions={0} | all-to-all | bytes 4194304 | tf_op jit(solution)/shard_map/all_to_all | solution.py:18
  125.5 0.0 collective-permute-start.2
  125.5 0.0 copy-done.1
  125.5 0.0 copy-done.2
  125.5 6.2 %expand_own.1 = (bf16[128,224]{1,0:T(8,128)(2,1)S(1)}, bf16[224,8192]{1,0:T(8,128)(2,1)S(1)}, bf16[16,1024]{1,0:T(8,128)(2,1)S(1)}) custom-call(s32[3]{0:T(128)S(1)} %pad_add_fusion.place_ref, bf16[8,128,1024]{2,1,0:T(8,128)(2,1)S(1)} %bitcast.32, bf16[224,8192]{1,0:T(8,128)(2,1)S(1)} %bitcast.29, bf16[224,8192]{1,0:T(8,128)(2,1)} %bitcast.39, ...), custom_call_target="tpu_custom_call" | custom-call | tf_op jit(solution)/shard_map/expand_own/pallas_call | solution.py:178
  131.7 0.0 collective-permute-done.2.x_ref
  131.7 4.2 %feed_forward.1 = (bf16[8,8,16,1024]{3,2,1,0:T(8,128)(2,1)S(1)}, bf16[224,8192]{1,0:T(8,128)(2,1)S(1)}) custom-call(bf16[8,128,1024]{2,1,0:T(8,128)(2,1)S(1)} %collective-permute-done.2.x_ref, bf16[224,8192]{1,0:T(8,128)(2,1)S(1)} %bitcast.30, bf16[224,8192]{1,0:T(8,128)(2,1)S(1)} %get-tuple-element.31.up_ref, f32[1,8192]{1,0:T(1,128)S(1)} %bitcast.36, ...), custom_call_target="tpu_custom_call" | custom-call | tf_op jit(solution)/shard_map/feed_forward/pallas_call | solution.py:207
  136.0 0.8 collective-permute-start.3
  136.8 0.7 shrink_own.1.a_ref
  137.5 3.1 %collective-permute-done.3.b_ref = bf16[8,8,16,1024]{3,2,1,0:T(8,128)(2,1)S(1)} collective-permute-done((bf16[8,8,16,1024]{3,2,1,0:T(8,128)(2,1)S(1)}, bf16[8,8,16,1024]{3,2,1,0:T(8,128)(2,1)S(1)}, u32[]{:S(2)}, u32[]{:S(2)}) %collective-permute-start.3) | collective-permute-done | bytes 2097184 | tf_op jit(solution)/shard_map/ppermute | solution.py:515
  140.5 0.5 add_cores.1
  141.0 35.8 %all_to_all.29.pieces_ref = bf16[64,16,1024]{2,1,0:T(8,128)(2,1)S(1)} all-to-all(bf16[64,16,1024]{2,1,0:T(8,128)(2,1)S(1)} %bitcast.33), channel_id=1, replica_groups=mesh['yh'=2,'x'=4,'c'=2,'z'=4,'yl'=2] {'yh','x','z','yl'}, dimensions={0} | all-to-all | bytes 4194304 | tf_op jit(solution)/shard_map/all_to_all | solution.py:518
  176.8 0.9 add_pieces.1
  (4 shorter events, 0.1 us)
Async XLA Ops:
  0.6 1.3 copy-start
  0.6 5.1 %collective-permute-start.1 = (bf16[1024,512]{1,0:T(8,128)(2,1)}, bf16[1024,512]{1,0:T(8,128)(2,1)S(1)}, u32[]{:S(2)}, u32[]{:S(2)}) collective-permute-start(bf16[1024,512]{1,0:T(8,128)(2,1)} %param.19), channel_id=1, source_target_pairs={{0,8},{8,0},{1,9},{9,1},{2,10},{10,2},{3,11},{11,3},{4,12},{12,4},... | collective-permute-start | bytes 3145736 | tf_op jit(solution)/shard_map/ppermute | solution.py:474
  1.5 4.2 %collective-permute-start = (bf16[16,512]{1,0:T(8,128)(2,1)S(1)}, bf16[16,512]{1,0:T(8,128)(2,1)S(1)}, u32[]{:S(2)}, u32[]{:S(2)}) collective-permute-start(bf16[16,512]{1,0:T(8,128)(2,1)S(1)} %get-tuple-element.37), channel_id=1, source_target_pairs={{0,8},{8,0},{1,9},{9,1},{2,10},{10,2},{3,11},{11,3},{4,12},{12,4},... | collective-permute-start | bytes 49160 | tf_op jit(solution)/shard_map/ppermute | solution.py:473
  5.7 58.6 %copy-start.3 = (bf16[2,8,1,256]{3,1,2,0:T(8,128)(2,1)S(1)}, bf16[2,8,1,256]{3,1,2,0:T(8,128)(2,1)}, u32[]{:S(2)}) copy-start(bf16[2,8,1,256]{3,1,2,0:T(8,128)(2,1)} %param.17) | copy-start | bytes 24580
  64.4 15.7 %copy-start.4 = (bf16[1024,512]{1,0:T(8,128)(2,1)S(1)}, bf16[1024,512]{1,0:T(8,128)(2,1)}, u32[]{:S(2)}) copy-start(bf16[1024,512]{1,0:T(8,128)(2,1)} %param.19) | copy-start | bytes 3145732
  93.7 31.8 %copy-start.1 = (bf16[8192,224]{0,1:T(8,128)(2,1)S(1)}, bf16[8192,224]{0,1:T(8,128)(2,1)}, u32[]{:S(2)}) copy-start(bf16[8192,224]{0,1:T(8,128)(2,1)} %param.21) | copy-start | bytes 11010052
  93.7 31.8 %copy-start.2 = (f32[8192]{0:T(1024)S(1)}, f32[8192]{0:T(1024)}, u32[]{:S(2)}) copy-start(f32[8192]{0:T(1024)} %param.20) | copy-start | bytes 98308
  125.5 6.2 %collective-permute-start.2 = (bf16[8,128,1024]{2,1,0:T(8,128)(2,1)S(1)}, bf16[8,128,1024]{2,1,0:T(8,128)(2,1)S(1)}, u32[]{:S(2)}, u32[]{:S(2)}) collective-permute-start(bf16[8,128,1024]{2,1,0:T(8,128)(2,1)S(1)} %bitcast.31), channel_id=1, source_target_pairs={{0,8},{8,0},{1,9},{9,1},{2,10},{10,2},{3,11},{11,3},{4,12},{12,4},... | collective-permute-start | bytes 6291464 | tf_op jit(solution)/shard_map/ppermute | solution.py:502
  136.0 4.5 %collective-permute-start.3 = (bf16[8,8,16,1024]{3,2,1,0:T(8,128)(2,1)S(1)}, bf16[8,8,16,1024]{3,2,1,0:T(8,128)(2,1)S(1)}, u32[]{:S(2)}, u32[]{:S(2)}) collective-permute-start(bf16[8,8,16,1024]{3,2,1,0:T(8,128)(2,1)S(1)} %get-tuple-element.33), channel_id=1, source_target_pairs={{0,8},{8,0},{1,9},{9,1},{2,10},{10,2},{3,11},{11,3},{4,12},{12,4},... | collective-permute-start | bytes 6291464 | tf_op jit(solution)/shard_map/ppermute | solution.py:515

commit v9 on v8

--- a/solution.py
+++ b/solution.py
@@ -23,7 +23,7 @@
 HBM = pl.BlockSpec(memory_space=pltpu.HBM)
 
 
-def intake(pick, received, fresh, query, n_copies):
+def intake(pick, received, fresh, query, up_rows, n_copies):
     req_dev, n_rows, head_dim = query.shape
     n_steps = fresh.shape[0]
     _, page_size, width_two = received.shape
@@ -31,7 +31,7 @@
     pages = max_pages + 1
     group = n_rows // n_steps
     scale = 1.0 / math.sqrt(head_dim)
-    def kernel(pick_ref, recv_ref, fresh_ref, q_ref, cache_ref, mixed_ref, buf, scores, probs, heads, out_sems):
+    def kernel(pick_ref, recv_ref, fresh_ref, q_ref, up_hbm, cache_ref, mixed_ref, up_ref, buf, scores, probs, heads, out_sems, up_sem):
         def copy_out(r):
             return pltpu.make_async_copy(buf.at[r], cache_ref.at[r], out_sems.at[r])
 
@@ -62,6 +62,8 @@
                     row_at == at % page_size, token, page
                 ).astype(buf.dtype)
             copy_out(r).start()
+        up_copy = pltpu.make_async_copy(up_hbm, up_ref, up_sem)
+        up_copy.start()
         for r in range(req_dev):
             keys = buf[r, :, :, :head_dim].reshape(pages * page_size, head_dim)
             part = scale * lax.dot_general(
@@ -87,16 +89,18 @@
                 mixed_ref[k, :, g * head_dim : (g + 1) * head_dim] = block
         for r in range(req_dev):
             copy_out(r).wait()
-
-    return pl.pallas_call(
-        kernel,
-        in_specs=[SMEM, VMEM, VMEM, VMEM],
-        out_specs=[HBM, VMEM],
+        up_copy.wait()
+
+    return pl.pallas_call(
+        kernel,
+        in_specs=[SMEM, VMEM, VMEM, VMEM, HBM],
+        out_specs=[HBM, VMEM, VMEM],
         out_shape=[
             jax.ShapeDtypeStruct((req_dev, pages, page_size, width_two), received.dtype),
             jax.ShapeDtypeStruct(
                 (n_copies, n_steps * req_dev, group * head_dim), received.dtype
             ),
+            pltpu.VMEM(up_rows.shape, up_rows.dtype),
         ],
         scratch_shapes=[
             pltpu.VMEM((req_dev, pages, page_size, width_two), received.dtype),
@@ -104,10 +108,11 @@
             pltpu.VMEM((req_dev * n_rows, pages * page_size), jnp.bfloat16),
             pltpu.VMEM((n_rows, req_dev, head_dim), jnp.float32),
             pltpu.SemaphoreType.DMA((req_dev,)),
+            pltpu.SemaphoreType.DMA,
         ],
         compiler_params=pltpu.CompilerParams(vmem_limit_bytes=20 * MIB),
         name="intake",
-    )(pick, received, fresh, query)
+    )(pick, received, fresh, query, pltpu.with_memory_space_constraint(up_rows, pltpu.HBM))
 
 
 PARTS = 4
@@ -159,38 +164,26 @@
     _, rows, cols = hidden.shape
     units, width = up_rows.shape
 
-    def kernel(place_ref, x_ref, gate_ref, up_hbm, gain_ref, act_ref, up_ref, part_ref, scaled, sems):
-        copies = in_parts(up_hbm, up_ref, sems)
+    def kernel(place_ref, x_ref, gate_ref, up_ref, gain_ref, act_ref, part_ref, scaled):
         mine = pl.ds(pl.multiple_of(place_ref[2] * rows_dev, rows_dev), rows_dev)
         part_ref[...] = x_ref[place_ref[1], mine, :]
         inverse = scale_rows(x_ref, gain_ref, scaled)
         gate = lax.dot_general(scaled[...], gate_ref[...], NT, preferred_element_type=jnp.float32)
-        upper = 0.0
-        span = width // PARTS
-        for i in range(PARTS):
-            part = slice(i * span, (i + 1) * span)
-            copies[i].wait()
-            upper += lax.dot_general(
-                scaled[:, part], up_ref[:, part], NT, preferred_element_type=jnp.float32
-            )
+        upper = lax.dot_general(scaled[...], up_ref[...], NT, preferred_element_type=jnp.float32)
         act_ref[...] = activate(gate * inverse, upper * inverse)
 
     return pl.pallas_call(
         kernel,
-        in_specs=[SMEM, VMEM, VMEM, HBM, VMEM],
-        out_specs=[VMEM] * 3,
+        in_specs=[SMEM, VMEM, VMEM, VMEM, VMEM],
+        out_specs=[VMEM] * 2,
         out_shape=[
             pltpu.VMEM((rows, units), jnp.bfloat16),
-            pltpu.VMEM((units, width), jnp.bfloat16),
             jax.ShapeDtypeStruct((rows_dev, cols), hidden.dtype),
         ],
-        scratch_shapes=[
-            pltpu.VMEM((rows, width), jnp.bfloat16),
-            pltpu.SemaphoreType.DMA((PARTS,)),
-        ],
+        scratch_shapes=[pltpu.VMEM((rows, width), jnp.bfloat16)],
         compiler_params=pltpu.CompilerParams(vmem_limit_bytes=24 * MIB),
         name="expand_own",
-    )(place, hidden, gate_rows, pltpu.with_memory_space_constraint(up_rows, pltpu.HBM), gain_row)
+    )(place, hidden, gate_rows, up_rows, gain_row)
 
 
 def feed_forward(hidden, gate_rows, up_rows, gain_row, w_down, n_tensor, rows_dev):
@@ -478,8 +471,13 @@
     received = lax.all_to_all(
         outgoing.reshape(n_dp, capacity, page_size, width_two), DP, 0, 0, tiled=True
     )
-    cache, mixed_copies = intake(
-        pick, received.reshape(pslots, page_size, width_two), fresh, query, chips_dp
+    cache, mixed_copies, up_near = intake(
+        pick,
+        received.reshape(pslots, page_size, width_two),
+        fresh,
+        query,
+        jnp.swapaxes(w_up, 0, 1),
+        chips_dp,
     )
 
     w_both = both(w_out, w_other)
@@ -501,13 +499,10 @@
     )
     other_rows = lax.ppermute(own_rows, "c", swap)
     gate_rows = jnp.swapaxes(w_gate, 0, 1)
-    up_rows = jnp.swapaxes(w_up, 0, 1)
     gain_row = ffn_gain.reshape(1, width)
     width_out = width // n_tensor
 
-    act_own, up_near, own_hidden = expand_own(
-        own_rows, gate_rows, up_rows, gain_row, place, rows_dev
-    )
+    act_own, own_hidden = expand_own(own_rows, gate_rows, up_near, gain_row, place, rows_dev)
     other_rows, act_own = lax.optimization_barrier((other_rows, act_own))
     theirs, down_near = feed_forward(
         other_rows, gate_rows, up_near, gain_row, w_down, n_tensor, rows_dev

time: 178 us -> 176 us (0.989)
  blocking collectives: 151 us -> 149 us
  transfers between devices with their start and end apart: 4 -> 4, of which waited for: 1 -> 2; matrix products, arithmetic and copies ran while one was open for 0% -> 0% of each run, Pallas kernels for 6% -> 4%
where the time goes in v9:
time: 176 us; the launch traced here: 175 us
  blocking collectives  149 us (85%)
  Pallas kernels  18.7 us (11%)
  waiting for transfers between devices  4.23 us (2%)
    all_to_all x1, blocking collectives, per_device(): lax.all_to_all(outgoing.reshape(n_dp, capacity, page_size, width_two), DP...  58.6 us
    all_to_all x1, blocking collectives, per_device(): pieces = lax.all_to_all(chip_sum, CHIPS, 0, 0, tiled=True)  35.1 us
    all_to_all x1, blocking collectives, to_all(): return lax.all_to_all(copies, axes, 0, 0, tiled=True)  31.3 us
    all_to_all x1, blocking collectives, per_device(): lax.all_to_all(partial_out.reshape(n_tensor, rows_blk, cols_chip), TENSOR...  12.5 us
    all_to_all x1, blocking collectives, per_device(): lax.all_to_all(mixed_copies, CHIP_DP, 0, 0, tiled=True)  11.2 us
    pallas_call x1, Pallas kernels, intake(): pl.pallas_call(kernel, in_specs=[SMEM, VMEM, VMEM, VMEM, HBM], out_specs=...  5.48 us
    pallas_call x1, Pallas kernels, feed_forward(): pl.pallas_call(kernel, in_specs=[VMEM, VMEM, VMEM, VMEM, HBM], out_specs=...  4.25 us
    pallas_call x1, Pallas kernels, pack_pages(): pl.pallas_call(kernel, in_specs=[SMEM, HBM, HBM, HBM, HBM], out_specs=[VM...  3.63 us
  transfers between devices with their start and end apart: 4, of which 2 were waited for; matrix products, arithmetic and copies ran while one was open for 0% of the time, Pallas kernels for 4%

profile of v9, /device:TPU:0, one launch (start us, length us, event | category | flops | bytes accessed | tf_op | source)
XLA Modules:
  0.0 175.2 jit_solution(5830455542968518471)
XLA Ops:
  0.6 0.0 copy-start
  0.6 0.1 collective-permute-start.1
  0.8 0.7 dynamic-slice_bitcast_fusion.1
  1.5 0.5 collective-permute-start
  2.0 0.0 copy-done
  2.0 0.1 pad_add_fusion.place_ref
  2.1 3.6 %pack_pages.1 = (bf16[512,16,256]{2,1,0:T(8,128)(2,1)S(1)}, s32[72,128]{1,0:T(8,128)S(1)}) custom-call(s32[3]{0:T(128)S(1)} %pad_add_fusion.place_ref, s32[8,64,128]{2,1,0:T(8,128)} %bitcast.42, s32[1,128]{1,0:T(1,128)} %bitcast.43, s32[1,128]{1,0:T(1,128)} %bitcast.44, bf16[512,16,256]{2,1,0:T(8,128)(2,1)} %bitcast.38), custom_call_target="tpu_custom_call" | custom-call | tf_op jit(solution)/shard_map/pack_pages/pallas_call | solution.py:352
  5.7 0.0 collective-permute-done
  5.7 0.0 collective-permute-done.1
  5.7 0.0 copy-start.3
  5.8 58.6 %all_to_all.25 = bf16[16,32,16,256]{3,2,1,0:T(8,128)(2,1)S(1)} all-to-all(bf16[16,32,16,256]{3,2,1,0:T(8,128)(2,1)S(1)} %bitcast.34), channel_id=1, replica_groups=mesh['yh'=2,'x'=4,'c'=2,'z'=4,'yl'=2] {'yh','x','c'}, dimensions={0} | all-to-all | bytes 8388608 | tf_op jit(solution)/shard_map/all_to_all | solution.py:471
  64.4 0.0 copy-done.3
  64.4 0.0 copy-start.4
  64.4 5.5 %intake.1 = (bf16[8,65,16,256]{3,2,1,0:T(8,128)(2,1)}, bf16[8,16,1024]{2,1,0:T(8,128)(2,1)S(1)}, bf16[224,8192]{1,0:T(8,128)(2,1)S(1)}) custom-call(s32[72,128]{1,0:T(8,128)S(1)} %get-tuple-element.22.pick_ref, bf16[512,16,256]{2,1,0:T(8,128)(2,1)S(1)} %bitcast.28, bf16[2,8,256]{2,1,0:T(8,128)(2,1)S(1)} %bitcast.37, ...), custom_call_target="tpu_custom_call" | custom-call | tf_op jit(solution)/shard_map/intake/pallas_call | solution.py:94
  69.8 11.2 %all_to_all.26 = bf16[8,16,1024]{2,1,0:T(8,128)(2,1)S(1)} all-to-all(bf16[8,16,1024]{2,1,0:T(8,128)(2,1)S(1)} %get-tuple-element.25), channel_id=1, replica_groups=mesh['yh'=2,'x'=4,'c'=2,'z'=4,'yl'=2] {'yh','x'}, dimensions={0} | all-to-all | bytes 524288 | tf_op jit(solution)/shard_map/all_to_all | solution.py:484
  81.1 0.0 copy-done.4
  81.1 0.7 fusion.7
  81.8 12.5 %all_to_all.27 = bf16[8,16,1024]{2,1,0:T(8,128)(2,1)S(1)} all-to-all(bf16[8,16,1024]{2,1,0:T(8,128)(2,1)S(1)} %bitcast.41), channel_id=1, replica_groups=mesh['yh'=2,'x'=4,'c'=2,'z'=4,'yl'=2] {'z','yl'}, dimensions={0} | all-to-all | bytes 524288 | tf_op jit(solution)/shard_map/all_to_all | solution.py:491
  94.4 0.2 broadcast_in_dim.2
  94.6 0.0 copy-start.1
  94.6 0.0 copy-start.2
  94.6 31.3 %all_to_all.28 = bf16[64,16,1024]{2,1,0:T(8,128)(2,1)S(1)} all-to-all(bf16[64,16,1024]{2,1,0:T(8,128)(2,1)S(1)} %broadcast_in_dim.2), channel_id=1, replica_groups=mesh['yh'=2,'x'=4,'c'=2,'z'=4,'yl'=2] {'yh','x','z','yl'}, dimensions={0} | all-to-all | bytes 4194304 | tf_op jit(solution)/shard_map/all_to_all | solution.py:18
  126.0 0.0 collective-permute-start.2
  126.0 0.0 copy-done.1
  126.0 0.0 copy-done.2
  126.0 3.2 %expand_own.1 = (bf16[128,224]{1,0:T(8,128)(2,1)S(1)}, bf16[16,1024]{1,0:T(8,128)(2,1)S(1)}) custom-call(s32[3]{0:T(128)S(1)} %pad_add_fusion.place_ref, bf16[8,128,1024]{2,1,0:T(8,128)(2,1)S(1)} %bitcast.32, bf16[224,8192]{1,0:T(8,128)(2,1)S(1)} %bitcast.29, bf16[224,8192]{1,0:T(8,128)(2,1)S(1)} %get-tuple-element.28.up_ref, f32[1,8192]{1,0:T(1,128)S(1)} %bitcast.35), custom_call_target="tpu_custom_call" | custom-call | tf_op jit(solution)/shard_map/expand_own/pallas_call | solution.py:175
  129.2 0.9 collective-permute-done.2.x_ref
  130.2 4.3 %feed_forward.1 = (bf16[8,8,16,1024]{3,2,1,0:T(8,128)(2,1)S(1)}, bf16[224,8192]{1,0:T(8,128)(2,1)S(1)}) custom-call(bf16[8,128,1024]{2,1,0:T(8,128)(2,1)S(1)} %collective-permute-done.2.x_ref, bf16[224,8192]{1,0:T(8,128)(2,1)S(1)} %bitcast.30, bf16[224,8192]{1,0:T(8,128)(2,1)S(1)} %get-tuple-element.28.up_ref, f32[1,8192]{1,0:T(1,128)S(1)} %bitcast.36, ...), custom_call_target="tpu_custom_call" | custom-call | tf_op jit(solution)/shard_map/feed_forward/pallas_call | solution.py:200
  134.4 0.2 collective-permute-start.3
  134.6 0.7 shrink_own.1.a_ref
  135.3 3.3 %collective-permute-done.3.b_ref = bf16[8,8,16,1024]{3,2,1,0:T(8,128)(2,1)S(1)} collective-permute-done((bf16[8,8,16,1024]{3,2,1,0:T(8,128)(2,1)S(1)}, bf16[8,8,16,1024]{3,2,1,0:T(8,128)(2,1)S(1)}, u32[]{:S(2)}, u32[]{:S(2)}) %collective-permute-start.3) | collective-permute-done | bytes 2097184 | tf_op jit(solution)/shard_map/ppermute | solution.py:510
  138.7 0.5 add_cores.1
  139.1 35.1 %all_to_all.29.pieces_ref = bf16[64,16,1024]{2,1,0:T(8,128)(2,1)S(1)} all-to-all(bf16[64,16,1024]{2,1,0:T(8,128)(2,1)S(1)} %bitcast.33), channel_id=1, replica_groups=mesh['yh'=2,'x'=4,'c'=2,'z'=4,'yl'=2] {'yh','x','z','yl'}, dimensions={0} | all-to-all | bytes 4194304 | tf_op jit(solution)/shard_map/all_to_all | solution.py:513
  174.3 0.9 add_pieces.1
  (4 shorter events, 0.1 us)
Async XLA Ops:
  0.6 1.3 copy-start
  0.6 5.1 %collective-permute-start.1 = (bf16[1024,512]{1,0:T(8,128)(2,1)}, bf16[1024,512]{1,0:T(8,128)(2,1)S(1)}, u32[]{:S(2)}, u32[]{:S(2)}) collective-permute-start(bf16[1024,512]{1,0:T(8,128)(2,1)} %param.19), channel_id=1, source_target_pairs={{0,8},{8,0},{1,9},{9,1},{2,10},{10,2},{3,11},{11,3},{4,12},{12,4},... | collective-permute-start | bytes 3145736 | tf_op jit(solution)/shard_map/ppermute | solution.py:467
  1.5 4.2 %collective-permute-start = (bf16[16,512]{1,0:T(8,128)(2,1)S(1)}, bf16[16,512]{1,0:T(8,128)(2,1)S(1)}, u32[]{:S(2)}, u32[]{:S(2)}) collective-permute-start(bf16[16,512]{1,0:T(8,128)(2,1)S(1)} %get-tuple-element.37), channel_id=1, source_target_pairs={{0,8},{8,0},{1,9},{9,1},{2,10},{10,2},{3,11},{11,3},{4,12},{12,4},... | collective-permute-start | bytes 49160 | tf_op jit(solution)/shard_map/ppermute | solution.py:466
  5.7 58.6 %copy-start.3 = (bf16[2,8,1,256]{3,1,2,0:T(8,128)(2,1)S(1)}, bf16[2,8,1,256]{3,1,2,0:T(8,128)(2,1)}, u32[]{:S(2)}) copy-start(bf16[2,8,1,256]{3,1,2,0:T(8,128)(2,1)} %param.17) | copy-start | bytes 24580
  64.4 16.7 %copy-start.4 = (bf16[1024,512]{1,0:T(8,128)(2,1)S(1)}, bf16[1024,512]{1,0:T(8,128)(2,1)}, u32[]{:S(2)}) copy-start(bf16[1024,512]{1,0:T(8,128)(2,1)} %param.19) | copy-start | bytes 3145732
  94.6 31.4 %copy-start.1 = (bf16[8192,224]{0,1:T(8,128)(2,1)S(1)}, bf16[8192,224]{0,1:T(8,128)(2,1)}, u32[]{:S(2)}) copy-start(bf16[8192,224]{0,1:T(8,128)(2,1)} %param.21) | copy-start | bytes 11010052
  94.6 31.4 %copy-start.2 = (f32[8192]{0:T(1024)S(1)}, f32[8192]{0:T(1024)}, u32[]{:S(2)}) copy-start(f32[8192]{0:T(1024)} %param.20) | copy-start | bytes 98308
  126.0 4.2 %collective-permute-start.2 = (bf16[8,128,1024]{2,1,0:T(8,128)(2,1)S(1)}, bf16[8,128,1024]{2,1,0:T(8,128)(2,1)S(1)}, u32[]{:S(2)}, u32[]{:S(2)}) collective-permute-start(bf16[8,128,1024]{2,1,0:T(8,128)(2,1)S(1)} %bitcast.31), channel_id=1, source_target_pairs={{0,8},{8,0},{1,9},{9,1},{2,10},{10,2},{3,11},{11,3},{4,12},{12,4},... | collective-permute-start | bytes 6291464 | tf_op jit(solution)/shard_map/ppermute | solution.py:500
  134.4 4.2 %collective-permute-start.3 = (bf16[8,8,16,1024]{3,2,1,0:T(8,128)(2,1)S(1)}, bf16[8,8,16,1024]{3,2,1,0:T(8,128)(2,1)S(1)}, u32[]{:S(2)}, u32[]{:S(2)}) collective-permute-start(bf16[8,8,16,1024]{3,2,1,0:T(8,128)(2,1)S(1)} %get-tuple-element.33), channel_id=1, source_target_pairs={{0,8},{8,0},{1,9},{9,1},{2,10},{10,2},{3,11},{11,3},{4,12},{12,4},... | collective-permute-start | bytes 6291464 | tf_op jit(solution)/shard_map/ppermute | solution.py:510

commit v10 on v9

--- a/solution.py
+++ b/solution.py
@@ -35,6 +35,8 @@
         def copy_out(r):
             return pltpu.make_async_copy(buf.at[r], cache_ref.at[r], out_sems.at[r])
 
+        up_copy = pltpu.make_async_copy(up_hbm, up_ref, up_sem)
+        up_copy.start()
         row_at = lax.broadcasted_iota(jnp.int32, (page_size, width_two), 0)
         tokens_new = [fresh_ref[s].astype(jnp.float32) for s in range(n_steps)]
         for r in range(req_dev):
@@ -62,8 +64,6 @@
                     row_at == at % page_size, token, page
                 ).astype(buf.dtype)
             copy_out(r).start()
-        up_copy = pltpu.make_async_copy(up_hbm, up_ref, up_sem)
-        up_copy.start()
         for r in range(req_dev):
             keys = buf[r, :, :, :head_dim].reshape(pages * page_size, head_dim)
             part = scale * lax.dot_general(
@@ -115,18 +115,7 @@
     )(pick, received, fresh, query, pltpu.with_memory_space_constraint(up_rows, pltpu.HBM))
 
 
-PARTS = 4
 NT = (((1,), (1,)), ((), ()))
-
-
-def in_parts(source, target, sems):
-    span = target.shape[1] // PARTS
-    copies = []
-    for i in range(PARTS):
-        part = pl.ds(i * span, span)
-        copies.append(pltpu.make_async_copy(source.at[:, part], target.at[:, part], sems.at[i]))
-        copies[-1].start()
-    return copies
 
 
 def scale_rows(x_ref, gain_ref, scaled):
@@ -147,11 +136,9 @@
     return (gate / (1.0 + jnp.exp(-gate)) * upper).astype(jnp.bfloat16)
 
 
-def down_to(out_ref, act, down_ref, waits=()):
+def down_to(out_ref, act, down_ref):
     chips, n_tensor, rows_dev, cols_out = out_ref.shape
     for t in range(n_tensor):
-        if waits and t % (n_tensor // PARTS) == 0:
-            waits[t // (n_tensor // PARTS)].wait()
         out = jnp.dot(
             act,
             down_ref[:, t * cols_out : (t + 1) * cols_out],
@@ -190,12 +177,15 @@
     _, rows, _ = hidden.shape
     units, width = w_down.shape
 
-    def kernel(x_ref, gate_ref, up_ref, gain_ref, down_hbm, out_ref, down_ref, scaled, sems):
-        copies = in_parts(down_hbm, down_ref, sems)
+    def kernel(x_ref, gate_ref, up_ref, gain_ref, down_hbm, out_ref, down_ref, scaled, sem):
+        down_copy = pltpu.make_async_copy(down_hbm, down_ref, sem)
+        down_copy.start()
         inverse = scale_rows(x_ref, gain_ref, scaled)
         gate = lax.dot_general(scaled[...], gate_ref[...], NT, preferred_element_type=jnp.float32)
         upper = lax.dot_general(scaled[...], up_ref[...], NT, preferred_element_type=jnp.float32)
-        down_to(out_ref, activate(gate * inverse, upper * inverse), down_ref, copies)
+        act = activate(gate * inverse, upper * inverse)
+        down_copy.wait()
+        down_to(out_ref, act, down_ref)
 
     return pl.pallas_call(
         kernel,
@@ -209,7 +199,7 @@
         ],
         scratch_shapes=[
             pltpu.VMEM((rows, width), jnp.bfloat16),
-            pltpu.SemaphoreType.DMA((PARTS,)),
+            pltpu.SemaphoreType.DMA,
         ],
         compiler_params=pltpu.CompilerParams(vmem_limit_bytes=28 * MIB),
         name="feed_forward",

time: 176 us -> 174 us (0.989)
  no operation moved by 1% of the time
where the time goes in v10:
time: 174 us
  blocking collectives  149 us (86%)
  Pallas kernels  17.2 us (10%)
  waiting for transfers between devices  4.21 us (2%)
    all_to_all x1, blocking collectives, per_device(): lax.all_to_all(outgoing.reshape(n_dp, capacity, page_size, width_two), DP...  58.6 us
    all_to_all x1, blocking collectives, per_device(): pieces = lax.all_to_all(chip_sum, CHIPS, 0, 0, tiled=True)  35.2 us
    all_to_all x1, blocking collectives, to_all(): return lax.all_to_all(copies, axes, 0, 0, tiled=True)  31.5 us
    all_to_all x1, blocking collectives, per_device(): lax.all_to_all(partial_out.reshape(n_tensor, rows_blk, cols_chip), TENSOR...  12.5 us
    all_to_all x1, blocking collectives, per_device(): lax.all_to_all(mixed_copies, CHIP_DP, 0, 0, tiled=True)  11.3 us
    pallas_call x1, Pallas kernels, intake(): pl.pallas_call(kernel, in_specs=[SMEM, VMEM, VMEM, VMEM, HBM], out_specs=...  4.79 us
    pallas_call x1, Pallas kernels, pack_pages(): pl.pallas_call(kernel, in_specs=[SMEM, HBM, HBM, HBM, HBM], out_specs=[VM...  3.63 us
  transfers between devices with their start and end apart: 4, of which 2 were waited for; matrix products, arithmetic and copies ran while one was open for 0% of the time, Pallas kernels for 4%

profile of v10, /device:TPU:0, one launch (start us, length us, event | category | flops | bytes accessed | tf_op | source)
XLA Modules:
  0.0 173.9 jit_solution(17726387654093732336)
XLA Ops:
  0.6 0.0 copy-start
  0.6 0.1 collective-permute-start.1
  0.8 0.7 dynamic-slice_bitcast_fusion.1
  1.5 0.5 collective-permute-start
  2.0 0.0 copy-done
  2.0 0.1 pad_add_fusion.place_ref
  2.1 3.6 %pack_pages.1 = (bf16[512,16,256]{2,1,0:T(8,128)(2,1)S(1)}, s32[72,128]{1,0:T(8,128)S(1)}) custom-call(s32[3]{0:T(128)S(1)} %pad_add_fusion.place_ref, s32[8,64,128]{2,1,0:T(8,128)} %bitcast.42, s32[1,128]{1,0:T(1,128)} %bitcast.43, s32[1,128]{1,0:T(1,128)} %bitcast.44, bf16[512,16,256]{2,1,0:T(8,128)(2,1)} %bitcast.38), custom_call_target="tpu_custom_call" | custom-call | tf_op jit(solution)/shard_map/pack_pages/pallas_call | solution.py:342
  5.7 0.0 collective-permute-done
  5.7 0.0 collective-permute-done.1
  5.7 0.0 copy-start.3
  5.8 58.6 %all_to_all.25 = bf16[16,32,16,256]{3,2,1,0:T(8,128)(2,1)S(1)} all-to-all(bf16[16,32,16,256]{3,2,1,0:T(8,128)(2,1)S(1)} %bitcast.34), channel_id=1, replica_groups=mesh['yh'=2,'x'=4,'c'=2,'z'=4,'yl'=2] {'yh','x','c'}, dimensions={0} | all-to-all | bytes 8388608 | tf_op jit(solution)/shard_map/all_to_all | solution.py:461
  64.4 0.0 copy-done.3
  64.4 0.0 copy-start.4
  64.4 4.8 %intake.1 = (bf16[8,65,16,256]{3,2,1,0:T(8,128)(2,1)}, bf16[8,16,1024]{2,1,0:T(8,128)(2,1)S(1)}, bf16[224,8192]{1,0:T(8,128)(2,1)S(1)}) custom-call(s32[72,128]{1,0:T(8,128)S(1)} %get-tuple-element.22.pick_ref, bf16[512,16,256]{2,1,0:T(8,128)(2,1)S(1)} %bitcast.28, bf16[2,8,256]{2,1,0:T(8,128)(2,1)S(1)} %bitcast.37, ...), custom_call_target="tpu_custom_call" | custom-call | tf_op jit(solution)/shard_map/intake/pallas_call | solution.py:94
  69.2 11.3 %all_to_all.26 = bf16[8,16,1024]{2,1,0:T(8,128)(2,1)S(1)} all-to-all(bf16[8,16,1024]{2,1,0:T(8,128)(2,1)S(1)} %get-tuple-element.25), channel_id=1, replica_groups=mesh['yh'=2,'x'=4,'c'=2,'z'=4,'yl'=2] {'yh','x'}, dimensions={0} | all-to-all | bytes 524288 | tf_op jit(solution)/shard_map/all_to_all | solution.py:474
  80.5 0.0 copy-done.4
  80.5 0.7 fusion.7
  81.2 12.5 %all_to_all.27 = bf16[8,16,1024]{2,1,0:T(8,128)(2,1)S(1)} all-to-all(bf16[8,16,1024]{2,1,0:T(8,128)(2,1)S(1)} %bitcast.41), channel_id=1, replica_groups=mesh['yh'=2,'x'=4,'c'=2,'z'=4,'yl'=2] {'z','yl'}, dimensions={0} | all-to-all | bytes 524288 | tf_op jit(solution)/shard_map/all_to_all | solution.py:481
  93.8 0.2 broadcast_in_dim.2
  94.0 0.0 copy-start.1
  94.0 0.0 copy-start.2
  94.1 31.5 %all_to_all.28 = bf16[64,16,1024]{2,1,0:T(8,128)(2,1)S(1)} all-to-all(bf16[64,16,1024]{2,1,0:T(8,128)(2,1)S(1)} %broadcast_in_dim.2), channel_id=1, replica_groups=mesh['yh'=2,'x'=4,'c'=2,'z'=4,'yl'=2] {'yh','x','z','yl'}, dimensions={0} | all-to-all | bytes 4194304 | tf_op jit(solution)/shard_map/all_to_all | solution.py:18
  125.6 0.0 collective-permute-start.2
  125.6 0.0 copy-done.1
  125.6 0.0 copy-done.2
  125.6 3.2 %expand_own.1 = (bf16[128,224]{1,0:T(8,128)(2,1)S(1)}, bf16[16,1024]{1,0:T(8,128)(2,1)S(1)}) custom-call(s32[3]{0:T(128)S(1)} %pad_add_fusion.place_ref, bf16[8,128,1024]{2,1,0:T(8,128)(2,1)S(1)} %bitcast.32, bf16[224,8192]{1,0:T(8,128)(2,1)S(1)} %bitcast.29, bf16[224,8192]{1,0:T(8,128)(2,1)S(1)} %get-tuple-element.28.up_ref, f32[1,8192]{1,0:T(1,128)S(1)} %bitcast.35), custom_call_target="tpu_custom_call" | custom-call | tf_op jit(solution)/shard_map/expand_own/pallas_call | solution.py:162
  128.8 0.9 collective-permute-done.2.x_ref
  129.7 3.4 %feed_forward.1 = (bf16[8,8,16,1024]{3,2,1,0:T(8,128)(2,1)S(1)}, bf16[224,8192]{1,0:T(8,128)(2,1)S(1)}) custom-call(bf16[8,128,1024]{2,1,0:T(8,128)(2,1)S(1)} %collective-permute-done.2.x_ref, bf16[224,8192]{1,0:T(8,128)(2,1)S(1)} %bitcast.30, bf16[224,8192]{1,0:T(8,128)(2,1)S(1)} %get-tuple-element.28.up_ref, f32[1,8192]{1,0:T(1,128)S(1)} %bitcast.36, ...), custom_call_target="tpu_custom_call" | custom-call | tf_op jit(solution)/shard_map/feed_forward/pallas_call | solution.py:190
  133.1 0.2 collective-permute-start.3
  133.3 0.7 shrink_own.1.a_ref
  134.1 3.3 %collective-permute-done.3.b_ref = bf16[8,8,16,1024]{3,2,1,0:T(8,128)(2,1)S(1)} collective-permute-done((bf16[8,8,16,1024]{3,2,1,0:T(8,128)(2,1)S(1)}, bf16[8,8,16,1024]{3,2,1,0:T(8,128)(2,1)S(1)}, u32[]{:S(2)}, u32[]{:S(2)}) %collective-permute-start.3) | collective-permute-done | bytes 2097184 | tf_op jit(solution)/shard_map/ppermute | solution.py:500
  137.4 0.5 add_cores.1
  137.8 35.2 %all_to_all.29.pieces_ref = bf16[64,16,1024]{2,1,0:T(8,128)(2,1)S(1)} all-to-all(bf16[64,16,1024]{2,1,0:T(8,128)(2,1)S(1)} %bitcast.33), channel_id=1, replica_groups=mesh['yh'=2,'x'=4,'c'=2,'z'=4,'yl'=2] {'yh','x','z','yl'}, dimensions={0} | all-to-all | bytes 4194304 | tf_op jit(solution)/shard_map/all_to_all | solution.py:503
  173.0 0.9 add_pieces.1
  (4 shorter events, 0.1 us)
Async XLA Ops:
  0.6 1.3 copy-start
  0.6 5.1 %collective-permute-start.1 = (bf16[1024,512]{1,0:T(8,128)(2,1)}, bf16[1024,512]{1,0:T(8,128)(2,1)S(1)}, u32[]{:S(2)}, u32[]{:S(2)}) collective-permute-start(bf16[1024,512]{1,0:T(8,128)(2,1)} %param.19), channel_id=1, source_target_pairs={{0,8},{8,0},{1,9},{9,1},{2,10},{10,2},{3,11},{11,3},{4,12},{12,4},... | collective-permute-start | bytes 3145736 | tf_op jit(solution)/shard_map/ppermute | solution.py:457
  1.5 4.2 %collective-permute-start = (bf16[16,512]{1,0:T(8,128)(2,1)S(1)}, bf16[16,512]{1,0:T(8,128)(2,1)S(1)}, u32[]{:S(2)}, u32[]{:S(2)}) collective-permute-start(bf16[16,512]{1,0:T(8,128)(2,1)S(1)} %get-tuple-element.37), channel_id=1, source_target_pairs={{0,8},{8,0},{1,9},{9,1},{2,10},{10,2},{3,11},{11,3},{4,12},{12,4},... | collective-permute-start | bytes 49160 | tf_op jit(solution)/shard_map/ppermute | solution.py:456
  5.7 58.6 %copy-start.3 = (bf16[2,8,1,256]{3,1,2,0:T(8,128)(2,1)S(1)}, bf16[2,8,1,256]{3,1,2,0:T(8,128)(2,1)}, u32[]{:S(2)}) copy-start(bf16[2,8,1,256]{3,1,2,0:T(8,128)(2,1)} %param.17) | copy-start | bytes 24580
  64.4 16.1 %copy-start.4 = (bf16[1024,512]{1,0:T(8,128)(2,1)S(1)}, bf16[1024,512]{1,0:T(8,128)(2,1)}, u32[]{:S(2)}) copy-start(bf16[1024,512]{1,0:T(8,128)(2,1)} %param.19) | copy-start | bytes 3145732
  94.0 31.5 %copy-start.1 = (bf16[8192,224]{0,1:T(8,128)(2,1)S(1)}, bf16[8192,224]{0,1:T(8,128)(2,1)}, u32[]{:S(2)}) copy-start(bf16[8192,224]{0,1:T(8,128)(2,1)} %param.21) | copy-start | bytes 11010052
  94.0 31.5 %copy-start.2 = (f32[8192]{0:T(1024)S(1)}, f32[8192]{0:T(1024)}, u32[]{:S(2)}) copy-start(f32[8192]{0:T(1024)} %param.20) | copy-start | bytes 98308
  125.6 4.2 %collective-permute-start.2 = (bf16[8,128,1024]{2,1,0:T(8,128)(2,1)S(1)}, bf16[8,128,1024]{2,1,0:T(8,128)(2,1)S(1)}, u32[]{:S(2)}, u32[]{:S(2)}) collective-permute-start(bf16[8,128,1024]{2,1,0:T(8,128)(2,1)S(1)} %bitcast.31), channel_id=1, source_target_pairs={{0,8},{8,0},{1,9},{9,1},{2,10},{10,2},{3,11},{11,3},{4,12},{12,4},... | collective-permute-start | bytes 6291464 | tf_op jit(solution)/shard_map/ppermute | solution.py:490
  133.1 4.2 %collective-permute-start.3 = (bf16[8,8,16,1024]{3,2,1,0:T(8,128)(2,1)S(1)}, bf16[8,8,16,1024]{3,2,1,0:T(8,128)(2,1)S(1)}, u32[]{:S(2)}, u32[]{:S(2)}) collective-permute-start(bf16[8,8,16,1024]{3,2,1,0:T(8,128)(2,1)S(1)} %get-tuple-element.33), channel_id=1, source_target_pairs={{0,8},{8,0},{1,9},{9,1},{2,10},{10,2},{3,11},{11,3},{4,12},{12,4},... | collective-permute-start | bytes 6291464 | tf_op jit(solution)/shard_map/ppermute | solution.py:500

commit v11 on v10

--- a/solution.py
+++ b/solution.py
@@ -11,19 +11,13 @@
 CHIP_DP = ("yh", "x")
 TENSOR = ("z", "yl")
 CHIPS = ("yh", "x", "z", "yl")
-
-
-def to_all(block, axes, count):
-    copies = lax.optimization_barrier(jnp.broadcast_to(block[None], (count,) + block.shape))
-    return lax.all_to_all(copies, axes, 0, 0, tiled=True)
-
 MIB = 1024 * 1024
 SMEM = pl.BlockSpec(memory_space=pltpu.SMEM)
 VMEM = pl.BlockSpec(memory_space=pltpu.VMEM)
 HBM = pl.BlockSpec(memory_space=pltpu.HBM)
 
 
-def intake(pick, received, fresh, query, up_rows, n_copies):
+def intake(pick, received, fresh, query, up_rows, up_begun, n_copies):
     req_dev, n_rows, head_dim = query.shape
     n_steps = fresh.shape[0]
     _, page_size, width_two = received.shape
@@ -31,11 +25,13 @@
     pages = max_pages + 1
     group = n_rows // n_steps
     scale = 1.0 / math.sqrt(head_dim)
-    def kernel(pick_ref, recv_ref, fresh_ref, q_ref, up_hbm, cache_ref, mixed_ref, up_ref, buf, scores, probs, heads, out_sems, up_sem):
+
+    def kernel(pick_ref, recv_ref, fresh_ref, q_ref, up_hbm, up_in, cache_ref, mixed_ref, up_ref, buf, scores, probs, heads, out_sems, up_sem):
         def copy_out(r):
             return pltpu.make_async_copy(buf.at[r], cache_ref.at[r], out_sems.at[r])
 
-        up_copy = pltpu.make_async_copy(up_hbm, up_ref, up_sem)
+        rest = pl.ds(up_hbm.shape[0] // 2, up_hbm.shape[0] // 2)
+        up_copy = pltpu.make_async_copy(up_hbm.at[rest], up_ref.at[rest], up_sem)
         up_copy.start()
         row_at = lax.broadcasted_iota(jnp.int32, (page_size, width_two), 0)
         tokens_new = [fresh_ref[s].astype(jnp.float32) for s in range(n_steps)]
@@ -93,7 +89,7 @@
 
     return pl.pallas_call(
         kernel,
-        in_specs=[SMEM, VMEM, VMEM, VMEM, HBM],
+        in_specs=[SMEM, VMEM, VMEM, VMEM, HBM, VMEM],
         out_specs=[HBM, VMEM, VMEM],
         out_shape=[
             jax.ShapeDtypeStruct((req_dev, pages, page_size, width_two), received.dtype),
@@ -111,8 +107,9 @@
             pltpu.SemaphoreType.DMA,
         ],
         compiler_params=pltpu.CompilerParams(vmem_limit_bytes=20 * MIB),
+        input_output_aliases={5: 2},
         name="intake",
-    )(pick, received, fresh, query, pltpu.with_memory_space_constraint(up_rows, pltpu.HBM))
+    )(pick, received, fresh, query, pltpu.with_memory_space_constraint(up_rows, pltpu.HBM), up_begun)
 
 
 NT = (((1,), (1,)), ((), ()))
@@ -251,14 +248,14 @@
     )
 
 
-def pack_pages(place, page_loc, lengths, placement, pool, n_dp):
+def pack_pages(place, page_loc, lengths, placement, pool, up_rows, n_dp):
     pslots, page_size, width_two = pool.shape
     _, max_pages, n_req = page_loc.shape
     req_dev = n_req // n_dp
     capacity = pslots // n_dp
     low = 32
 
-    def kernel(place_ref, loc_hbm, len_hbm, placement_hbm, pool_hbm, out_buf, pick_ref, loc, len_ref, placement_ref, pool_buf, rows_vec, rows, loc_sem, len_sem, placement_sem, pool_sem, rows_sem):
+    def kernel(place_ref, loc_hbm, len_hbm, placement_hbm, pool_hbm, up_hbm, out_buf, pick_ref, up_ref, loc, len_ref, placement_ref, pool_buf, rows_vec, rows, loc_sem, len_sem, placement_sem, pool_sem, rows_sem, up_sem):
         me = place_ref[0]
         len_copy = pltpu.make_async_copy(len_hbm, len_ref, len_sem)
         placement_copy = pltpu.make_async_copy(placement_hbm, placement_ref, placement_sem)
@@ -330,6 +327,9 @@
         pick_ref[max_pages:] = jnp.broadcast_to(own_len, (8, n_req)).astype(jnp.int32)
         rows_copy.wait()
         pool_copy.wait()
+        first = pl.ds(0, up_hbm.shape[0] // 2)
+        up_copy = pltpu.make_async_copy(up_hbm.at[first], up_ref.at[first], up_sem)
+        up_copy.start()
 
         for d in range(n_dp):
 
@@ -338,14 +338,16 @@
                 return carry
 
             lax.fori_loop(0, capacity, move, 0, unroll=16)
-
-    return pl.pallas_call(
-        kernel,
-        in_specs=[SMEM, HBM, HBM, HBM, HBM],
-        out_specs=[VMEM, VMEM],
+        up_copy.wait()
+
+    return pl.pallas_call(
+        kernel,
+        in_specs=[SMEM, HBM, HBM, HBM, HBM, HBM],
+        out_specs=[VMEM, VMEM, VMEM],
         out_shape=[
             jax.ShapeDtypeStruct(pool.shape, pool.dtype),
             jax.ShapeDtypeStruct((max_pages + 8, n_req), jnp.int32),
+            pltpu.VMEM(up_rows.shape, up_rows.dtype),
         ],
         scratch_shapes=[
             pltpu.VMEM((max_pages, n_req), jnp.int32),
@@ -359,6 +361,7 @@
             pltpu.SemaphoreType.DMA,
             pltpu.SemaphoreType.DMA,
             pltpu.SemaphoreType.DMA,
+            pltpu.SemaphoreType.DMA,
         ],
         compiler_params=pltpu.CompilerParams(vmem_limit_bytes=20 * MIB),
         name="pack_pages",
@@ -366,9 +369,43 @@
         place,
         *[
             pltpu.with_memory_space_constraint(array, pltpu.HBM)
-            for array in (page_loc, lengths, placement, pool)
-        ],
-    )
+            for array in (page_loc, lengths, placement, pool, up_rows)
+        ],
+    )
+
+
+def settle(parts, resid_own, resid_other, place, n_copies):
+    n_parts, rows, cols = parts.shape
+    n_steps, _, cols_dev = resid_own.shape
+    req_dev = rows // n_steps
+
+    def kernel(place_ref, parts_ref, own_ref, other_ref, out_ref):
+        core = place_ref[3]
+        both_rows = pl.ds(pl.multiple_of(place_ref[1] * 2 * req_dev, 2 * req_dev), 2 * req_dev)
+        total = parts_ref[0].astype(jnp.float32)
+        for i in range(1, n_parts):
+            total += parts_ref[i].astype(jnp.float32)
+        resid = []
+        for ref in (own_ref, other_ref):
+            steps = []
+            for s in range(n_steps):
+                wide = ref[s, both_rows, :].astype(jnp.float32)
+                steps.append(jnp.where(core == 0, wide[:req_dev], wide[req_dev:]))
+            resid.append(jnp.concatenate(steps, axis=0))
+        left = jnp.where(core == 0, resid[0], resid[1])
+        right = jnp.where(core == 0, resid[1], resid[0])
+        hidden = (total + jnp.concatenate([left, right], axis=1)).astype(out_ref.dtype)
+        for i in range(n_copies):
+            out_ref[i] = hidden
+
+    return pl.pallas_call(
+        kernel,
+        in_specs=[SMEM, VMEM, VMEM, VMEM],
+        out_specs=VMEM,
+        out_shape=jax.ShapeDtypeStruct((n_copies, rows, cols), parts.dtype),
+        compiler_params=pltpu.CompilerParams(vmem_limit_bytes=10 * MIB),
+        name="settle",
+    )(place, parts, resid_own, resid_other)
 
 
 def add_cores(ours, from_core):
@@ -423,13 +460,15 @@
     rows_core = n_steps * n_req // 2
     capacity = pslots // n_dp
 
-    place = jnp.stack([dev_dp, dev_tensor, dev_chip]).astype(jnp.int32)
-    outgoing, pick = pack_pages(
+    place = jnp.stack([dev_dp, dev_tensor, dev_chip, core]).astype(jnp.int32)
+    up_rows = jnp.swapaxes(w_up, 0, 1)
+    outgoing, pick, up_begun = pack_pages(
         place,
         jnp.swapaxes(page_loc, 1, 2),
         lengths.reshape(1, n_req),
         placement.reshape(1, n_req),
         kv_pool.reshape(pslots, page_size, width_two),
+        up_rows,
         n_dp,
     )
     query = jnp.transpose(queries, (1, 0, 2, 3)).reshape(req_dev, n_steps * hq_dev, head_dim)
@@ -439,24 +478,10 @@
     cols_chip = 2 * cols_dev
     swap = [(0, 1), (1, 0)]
 
-    def both(own, other):
-        return jnp.where(
-            core == 0,
-            jnp.concatenate([own, other], axis=-1),
-            jnp.concatenate([other, own], axis=-1),
-        )
-
-    def resid_of(at_core):
-        return lax.dynamic_slice(
-            resid_in,
-            (0, (2 * dev_tensor + at_core) * req_dev, 0),
-            (n_steps, req_dev, cols_dev),
-        ).reshape(rows_dev, cols_dev)
-
-    resid_blk = both(resid_of(core), lax.ppermute(resid_of(1 - core), "c", swap))
+    resid_other = lax.ppermute(resid_in, "c", swap)
     w_other = lax.ppermute(w_out, "c", swap)
-    outgoing, pick, query, resid_blk, w_other, place = lax.optimization_barrier(
-        (outgoing, pick, query, resid_blk, w_other, place)
+    outgoing, pick, query, resid_other, w_other, place, first_core = lax.optimization_barrier(
+        (outgoing, pick, query, resid_other, w_other, place, core == 0)
     )
     received = lax.all_to_all(
         outgoing.reshape(n_dp, capacity, page_size, width_two), DP, 0, 0, tiled=True
@@ -466,11 +491,16 @@
         received.reshape(pslots, page_size, width_two),
         fresh,
         query,
-        jnp.swapaxes(w_up, 0, 1),
+        up_rows,
+        up_begun,
         chips_dp,
     )
 
-    w_both = both(w_out, w_other)
+    w_both = jnp.where(
+        first_core,
+        jnp.concatenate([w_out, w_other], axis=-1),
+        jnp.concatenate([w_other, w_out], axis=-1),
+    )
     mixed_rows = lax.all_to_all(mixed_copies, CHIP_DP, 0, 0, tiled=True).reshape(
         rows_core, hq_dev * head_dim
     )
@@ -481,10 +511,8 @@
     parts = lax.all_to_all(
         partial_out.reshape(n_tensor, rows_blk, cols_chip), TENSOR, 0, 0, tiled=True
     )
-    hidden_blk = (
-        resid_blk.astype(jnp.float32) + jnp.sum(parts.astype(jnp.float32), axis=0)
-    ).astype(jnp.bfloat16)
-    own_rows = to_all(hidden_blk, CHIPS, chips_dp * n_tensor).reshape(
+    hidden_copies = settle(parts, resid_in, resid_other, place, chips_dp * n_tensor)
+    own_rows = lax.all_to_all(hidden_copies, CHIPS, 0, 0, tiled=True).reshape(
         chips_dp, rows_core, cols_chip
     )
     other_rows = lax.ppermute(own_rows, "c", swap)

time: 174 us -> 174 us (level)
    pallas_call x2 -> x3, Pallas kernels: 8.42 us -> 8.89 us  [the longest x1 4.33 us: pack_pages(): pl.pallas_call(kernel, in_specs=[SMEM, HBM, HBM, HBM, HBM, HBM], out_spec...]
  transfers between devices with their start and end apart: 4 -> 4, of which waited for: 2 -> 2; matrix products, arithmetic and copies ran while one was open for 0% -> 0% of each run, Pallas kernels for 4% -> 5%
where the time goes in v11:
time: 174 us
  blocking collectives  150 us (86%)
  Pallas kernels  17.6 us (10%)
  waiting for transfers between devices  4.21 us (2%)
    all_to_all x1, blocking collectives, per_device(): lax.all_to_all(outgoing.reshape(n_dp, capacity, page_size, width_two), DP...  58.6 us
    all_to_all x1, blocking collectives, per_device(): pieces = lax.all_to_all(chip_sum, CHIPS, 0, 0, tiled=True)  35.4 us
    all_to_all x1, blocking collectives, per_device(): lax.all_to_all(hidden_copies, CHIPS, 0, 0, tiled=True)  31.7 us
    all_to_all x1, blocking collectives, per_device(): lax.all_to_all(partial_out.reshape(n_tensor, rows_blk, cols_chip), TENSOR...  12.5 us
    all_to_all x1, blocking collectives, per_device(): lax.all_to_all(mixed_copies, CHIP_DP, 0, 0, tiled=True)  11.8 us
    pallas_call x1, Pallas kernels, pack_pages(): pl.pallas_call(kernel, in_specs=[SMEM, HBM, HBM, HBM, HBM, HBM], out_spec...  4.33 us
    pallas_call x1, Pallas kernels, intake(): pl.pallas_call(kernel, in_specs=[SMEM, VMEM, VMEM, VMEM, HBM, VMEM], out_...  3.76 us
  transfers between devices with their start and end apart: 4, of which 2 were waited for; matrix products, arithmetic and copies ran while one was open for 0% of the time, Pallas kernels for 5%

profile of v11, /device:TPU:0, one launch (start us, length us, event | category | flops | bytes accessed | tf_op | source)
XLA Modules:
  0.0 174.2 jit_solution(3480752644446434547)
XLA Ops:
  0.6 0.0 copy-start
  0.6 0.1 collective-permute-start.1
  0.7 0.5 collective-permute-start
  1.2 0.1 pad_add_fusion.place_ref
  1.3 4.3 %pack_pages.1 = (bf16[512,16,256]{2,1,0:T(8,128)(2,1)S(1)}, s32[72,128]{1,0:T(8,128)S(1)}, bf16[224,8192]{1,0:T(8,128)(2,1)S(1)}) custom-call(s32[4]{0:T(128)S(1)} %pad_add_fusion.place_ref, s32[8,64,128]{2,1,0:T(8,128)} %bitcast.38, s32[1,128]{1,0:T(1,128)} %bitcast.41, s32[1,128]{1,0:T(1,128)} %bitcast.42, bf16[512,16,256]{2,1,0:T(8,128)(2,1)} %bitcast.37, ...), custom_call_target="tpu_custom_call" | custom-call | tf_op jit(solution)/shard_map/pack_pages/pallas_call | solution.py:343
  5.7 0.0 copy-done
  5.7 0.0 collective-permute-done.other_ref
  5.7 0.0 collective-permute-done.1
  5.7 0.0 copy-start.4
  5.7 58.6 %all_to_all.25 = bf16[16,32,16,256]{3,2,1,0:T(8,128)(2,1)S(1)} all-to-all(bf16[16,32,16,256]{3,2,1,0:T(8,128)(2,1)S(1)} %bitcast.31), channel_id=1, replica_groups=mesh['yh'=2,'x'=4,'c'=2,'z'=4,'yl'=2] {'yh','x','c'}, dimensions={0} | all-to-all | bytes 8388608 | tf_op jit(solution)/shard_map/all_to_all | solution.py:486
  64.3 0.0 copy-done.4
  64.3 0.0 copy-start.5
  64.3 3.8 %intake.1 = (bf16[8,65,16,256]{3,2,1,0:T(8,128)(2,1)}, bf16[8,16,1024]{2,1,0:T(8,128)(2,1)S(1)}, bf16[224,8192]{1,0:T(8,128)(2,1)S(1)}) custom-call(s32[72,128]{1,0:T(8,128)S(1)} %get-tuple-element.24.pick_ref, bf16[512,16,256]{2,1,0:T(8,128)(2,1)S(1)} %bitcast.25, bf16[2,8,256]{2,1,0:T(8,128)(2,1)S(1)} %bitcast.34, ...), custom_call_target="tpu_custom_call", output_to_operand_aliasing={{2}: (5, {})} | custom-call | tf_op jit(solution)/shard_map/intake/pallas_call | solution.py:90
  68.1 11.8 %all_to_all.26 = bf16[8,16,1024]{2,1,0:T(8,128)(2,1)S(1)} all-to-all(bf16[8,16,1024]{2,1,0:T(8,128)(2,1)S(1)} %get-tuple-element.28), channel_id=1, replica_groups=mesh['yh'=2,'x'=4,'c'=2,'z'=4,'yl'=2] {'yh','x'}, dimensions={0} | all-to-all | bytes 524288 | tf_op jit(solution)/shard_map/all_to_all | solution.py:504
  79.8 0.0 copy-done.5
  79.9 0.0 copy-start.2
  79.9 0.7 fusion.7
  80.6 12.5 %all_to_all.27.parts_ref = bf16[8,16,1024]{2,1,0:T(8,128)(2,1)S(1)} all-to-all(bf16[8,16,1024]{2,1,0:T(8,128)(2,1)S(1)} %bitcast.40), channel_id=1, replica_groups=mesh['yh'=2,'x'=4,'c'=2,'z'=4,'yl'=2] {'z','yl'}, dimensions={0} | all-to-all | bytes 524288 | tf_op jit(solution)/shard_map/all_to_all | solution.py:511
  93.1 0.0 copy-done.2
  93.1 0.0 copy-start.1
  93.1 0.0 copy-start.3
  93.1 0.8 settle.1
  93.9 31.7 %all_to_all.28 = bf16[64,16,1024]{2,1,0:T(8,128)(2,1)S(1)} all-to-all(bf16[64,16,1024]{2,1,0:T(8,128)(2,1)S(1)} %settle.1), channel_id=1, replica_groups=mesh['yh'=2,'x'=4,'c'=2,'z'=4,'yl'=2] {'yh','x','z','yl'}, dimensions={0} | all-to-all | bytes 4194304 | tf_op jit(solution)/shard_map/all_to_all | solution.py:515
  125.6 0.0 collective-permute-start.2
  125.6 0.0 copy-done.1
  125.6 0.0 copy-done.3
  125.6 3.2 %expand_own.1 = (bf16[128,224]{1,0:T(8,128)(2,1)S(1)}, bf16[16,1024]{1,0:T(8,128)(2,1)S(1)}) custom-call(s32[4]{0:T(128)S(1)} %pad_add_fusion.place_ref, bf16[8,128,1024]{2,1,0:T(8,128)(2,1)S(1)} %bitcast.29, bf16[224,8192]{1,0:T(8,128)(2,1)S(1)} %bitcast.26, bf16[224,8192]{1,0:T(8,128)(2,1)S(1)} %get-tuple-element.32.up_ref, f32[1,8192]{1,0:T(1,128)S(1)} %bitcast.32), custom_call_target="tpu_custom_call" | custom-call | tf_op jit(solution)/shard_map/expand_own/pallas_call | solution.py:159
  128.8 0.9 collective-permute-done.2.x_ref
  129.7 3.4 %feed_forward.1 = (bf16[8,8,16,1024]{3,2,1,0:T(8,128)(2,1)S(1)}, bf16[224,8192]{1,0:T(8,128)(2,1)S(1)}) custom-call(bf16[8,128,1024]{2,1,0:T(8,128)(2,1)S(1)} %collective-permute-done.2.x_ref, bf16[224,8192]{1,0:T(8,128)(2,1)S(1)} %bitcast.27, bf16[224,8192]{1,0:T(8,128)(2,1)S(1)} %get-tuple-element.32.up_ref, f32[1,8192]{1,0:T(1,128)S(1)} %bitcast.33, ...), custom_call_target="tpu_custom_call" | custom-call | tf_op jit(solution)/shard_map/feed_forward/pallas_call | solution.py:187
  133.1 0.2 collective-permute-start.3
  133.4 0.7 shrink_own.1.a_ref
  134.1 3.3 %collective-permute-done.3.b_ref = bf16[8,8,16,1024]{3,2,1,0:T(8,128)(2,1)S(1)} collective-permute-done((bf16[8,8,16,1024]{3,2,1,0:T(8,128)(2,1)S(1)}, bf16[8,8,16,1024]{3,2,1,0:T(8,128)(2,1)S(1)}, u32[]{:S(2)}, u32[]{:S(2)}) %collective-permute-start.3) | collective-permute-done | bytes 2097184 | tf_op jit(solution)/shard_map/ppermute | solution.py:528
  137.4 0.5 add_cores.1
  137.9 35.4 %all_to_all.29.pieces_ref = bf16[64,16,1024]{2,1,0:T(8,128)(2,1)S(1)} all-to-all(bf16[64,16,1024]{2,1,0:T(8,128)(2,1)S(1)} %bitcast.30), channel_id=1, replica_groups=mesh['yh'=2,'x'=4,'c'=2,'z'=4,'yl'=2] {'yh','x','z','yl'}, dimensions={0} | all-to-all | bytes 4194304 | tf_op jit(solution)/shard_map/all_to_all | solution.py:531
  173.3 0.9 add_pieces.1
  (1 shorter events, 0.0 us)
Async XLA Ops:
  0.6 5.0 %copy-start = (bf16[2,8,8,128]{3,2,1,0:T(8,128)(2,1)S(1)}, bf16[2,8,8,128]{3,2,1,0:T(8,128)(2,1)}, u32[]{:S(2)}) copy-start(bf16[2,8,8,128]{3,2,1,0:T(8,128)(2,1)} %param.16) | copy-start | bytes 98308
  0.6 5.0 %collective-permute-start.1 = (bf16[1024,512]{1,0:T(8,128)(2,1)}, bf16[1024,512]{1,0:T(8,128)(2,1)S(1)}, u32[]{:S(2)}, u32[]{:S(2)}) collective-permute-start(bf16[1024,512]{1,0:T(8,128)(2,1)} %param.19), channel_id=1, source_target_pairs={{0,8},{8,0},{1,9},{9,1},{2,10},{10,2},{3,11},{11,3},{4,12},{12,4},... | collective-permute-start | bytes 3145736 | tf_op jit(solution)/shard_map/ppermute | solution.py:482
  0.7 4.9 %collective-permute-start = (bf16[2,128,512]{2,1,0:T(8,128)(2,1)}, bf16[2,128,512]{2,1,0:T(8,128)(2,1)S(1)}, u32[]{:S(2)}, u32[]{:S(2)}) collective-permute-start(bf16[2,128,512]{2,1,0:T(8,128)(2,1)} %own_ref.1), channel_id=1, source_target_pairs={{0,8},{8,0},{1,9},{9,1},{2,10},{10,2},{3,11},{11,3},{4,12},{12,4},... | collective-permute-start | bytes 786440 | tf_op jit(solution)/shard_map/ppermute | solution.py:481
  5.7 58.6 %copy-start.4 = (bf16[2,8,1,256]{3,1,2,0:T(8,128)(2,1)S(1)}, bf16[2,8,1,256]{3,1,2,0:T(8,128)(2,1)}, u32[]{:S(2)}) copy-start(bf16[2,8,1,256]{3,1,2,0:T(8,128)(2,1)} %param.17) | copy-start | bytes 24580
  64.3 15.5 %copy-start.5 = (bf16[1024,512]{1,0:T(8,128)(2,1)S(1)}, bf16[1024,512]{1,0:T(8,128)(2,1)}, u32[]{:S(2)}) copy-start(bf16[1024,512]{1,0:T(8,128)(2,1)} %param.19) | copy-start | bytes 3145732
  79.9 13.3 %copy-start.2 = (bf16[2,128,512]{2,1,0:T(8,128)(2,1)S(1)}, bf16[2,128,512]{2,1,0:T(8,128)(2,1)}, u32[]{:S(2)}) copy-start(bf16[2,128,512]{2,1,0:T(8,128)(2,1)} %own_ref.1) | copy-start | bytes 786436
  93.1 32.5 %copy-start.1 = (bf16[8192,224]{0,1:T(8,128)(2,1)S(1)}, bf16[8192,224]{0,1:T(8,128)(2,1)}, u32[]{:S(2)}) copy-start(bf16[8192,224]{0,1:T(8,128)(2,1)} %param.21) | copy-start | bytes 11010052
  93.1 32.5 %copy-start.3 = (f32[8192]{0:T(1024)S(1)}, f32[8192]{0:T(1024)}, u32[]{:S(2)}) copy-start(f32[8192]{0:T(1024)} %param.20) | copy-start | bytes 98308
  125.6 4.2 %collective-permute-start.2 = (bf16[8,128,1024]{2,1,0:T(8,128)(2,1)S(1)}, bf16[8,128,1024]{2,1,0:T(8,128)(2,1)S(1)}, u32[]{:S(2)}, u32[]{:S(2)}) collective-permute-start(bf16[8,128,1024]{2,1,0:T(8,128)(2,1)S(1)} %bitcast.28), channel_id=1, source_target_pairs={{0,8},{8,0},{1,9},{9,1},{2,10},{10,2},{3,11},{11,3},{4,12},{12,4},... | collective-permute-start | bytes 6291464 | tf_op jit(solution)/shard_map/ppermute | solution.py:518
  133.1 4.2 %collective-permute-start.3 = (bf16[8,8,16,1024]{3,2,1,0:T(8,128)(2,1)S(1)}, bf16[8,8,16,1024]{3,2,1,0:T(8,128)(2,1)S(1)}, u32[]{:S(2)}, u32[]{:S(2)}) collective-permute-start(bf16[8,8,16,1024]{3,2,1,0:T(8,128)(2,1)S(1)} %get-tuple-element.37), channel_id=1, source_target_pairs={{0,8},{8,0},{1,9},{9,1},{2,10},{10,2},{3,11},{11,3},{4,12},{12,4},... | collective-permute-start | bytes 6291464 | tf_op jit(solution)/shard_map/ppermute | solution.py:528

commit v12 on v11

--- a/solution.py
+++ b/solution.py
@@ -134,14 +134,14 @@
 
 
 def down_to(out_ref, act, down_ref):
-    chips, n_tensor, rows_dev, cols_out = out_ref.shape
+    n_tensor, chips, rows_dev, cols_out = out_ref.shape
     for t in range(n_tensor):
         out = jnp.dot(
             act,
             down_ref[:, t * cols_out : (t + 1) * cols_out],
             preferred_element_type=jnp.float32,
         )
-        out_ref[:, t] = out.astype(out_ref.dtype).reshape(chips, rows_dev, cols_out)
+        out_ref[t] = out.astype(out_ref.dtype).reshape(chips, rows_dev, cols_out)
 
 
 def expand_own(hidden, gate_rows, up_rows, gain_row, place, rows_dev):
@@ -190,7 +190,7 @@
         out_specs=[VMEM] * 2,
         out_shape=[
             jax.ShapeDtypeStruct(
-                (rows // rows_dev, n_tensor, rows_dev, width // n_tensor), jnp.bfloat16
+                (n_tensor, rows // rows_dev, rows_dev, width // n_tensor), jnp.bfloat16
             ),
             pltpu.VMEM((units, width), jnp.bfloat16),
         ],
@@ -212,7 +212,7 @@
         in_specs=[VMEM, VMEM],
         out_specs=VMEM,
         out_shape=jax.ShapeDtypeStruct(
-            (act.shape[0] // rows_dev, n_tensor, rows_dev, w_down.shape[1] // n_tensor),
+            (n_tensor, act.shape[0] // rows_dev, rows_dev, w_down.shape[1] // n_tensor),
             jnp.bfloat16,
         ),
         compiler_params=pltpu.CompilerParams(vmem_limit_bytes=16 * MIB),
@@ -528,7 +528,7 @@
     from_core = lax.ppermute(theirs, "c", swap)
     ours = shrink_own(act_own, down_near, n_tensor, rows_dev)
     chip_sum = add_cores(ours, from_core).reshape(chips_dp * n_tensor, rows_dev, width_out)
-    pieces = lax.all_to_all(chip_sum, CHIPS, 0, 0, tiled=True)
+    pieces = lax.all_to_all(chip_sum, TENSOR + CHIP_DP, 0, 0, tiled=True)
     block_out = add_pieces(pieces, own_hidden, n_steps)
     return (block_out, cache.reshape(1, req_dev, cache_len, width_two))
 

time: 174 us -> 176 us (1.011)
  no operation moved by 1% of the time
where the time goes in v12:
time: 176 us
  blocking collectives  151 us (86%)
  Pallas kernels  17.6 us (10%)
  waiting for transfers between devices  4.22 us (2%)
    all_to_all x1, blocking collectives, per_device(): lax.all_to_all(outgoing.reshape(n_dp, capacity, page_size, width_two), DP...  58.6 us
    all_to_all x1, blocking collectives, per_device(): pieces = lax.all_to_all(chip_sum, TENSOR + CHIP_DP, 0, 0, tiled=True)  36.1 us
    all_to_all x1, blocking collectives, per_device(): lax.all_to_all(hidden_copies, CHIPS, 0, 0, tiled=True)  32.1 us
    all_to_all x1, blocking collectives, per_device(): lax.all_to_all(partial_out.reshape(n_tensor, rows_blk, cols_chip), TENSOR...  12.5 us
    all_to_all x1, blocking collectives, per_device(): lax.all_to_all(mixed_copies, CHIP_DP, 0, 0, tiled=True)  12.2 us
    pallas_call x1, Pallas kernels, pack_pages(): pl.pallas_call(kernel, in_specs=[SMEM, HBM, HBM, HBM, HBM, HBM], out_spec...  4.33 us
    pallas_call x1, Pallas kernels, intake(): pl.pallas_call(kernel, in_specs=[SMEM, VMEM, VMEM, VMEM, HBM, VMEM], out_...  3.76 us
  transfers between devices with their start and end apart: 4, of which 2 were waited for; matrix products, arithmetic and copies ran while one was open for 0% of the time, Pallas kernels for 5%

profile of v12, /device:TPU:0, one launch (start us, length us, event | category | flops | bytes accessed | tf_op | source)
XLA Modules:
  0.0 175.7 jit_solution(15231594363140581210)
XLA Ops:
  0.6 0.0 copy-start
  0.6 0.1 collective-permute-start.1
  0.7 0.5 collective-permute-start
  1.2 0.1 pad_add_fusion.place_ref
  1.3 4.3 %pack_pages.1 = (bf16[512,16,256]{2,1,0:T(8,128)(2,1)S(1)}, s32[72,128]{1,0:T(8,128)S(1)}, bf16[224,8192]{1,0:T(8,128)(2,1)S(1)}) custom-call(s32[4]{0:T(128)S(1)} %pad_add_fusion.place_ref, s32[8,64,128]{2,1,0:T(8,128)} %bitcast.38, s32[1,128]{1,0:T(1,128)} %bitcast.41, s32[1,128]{1,0:T(1,128)} %bitcast.42, bf16[512,16,256]{2,1,0:T(8,128)(2,1)} %bitcast.37, ...), custom_call_target="tpu_custom_call" | custom-call | tf_op jit(solution)/shard_map/pack_pages/pallas_call | solution.py:343
  5.7 0.0 copy-done
  5.7 0.0 collective-permute-done.other_ref
  5.7 0.0 collective-permute-done.1
  5.7 0.0 copy-start.4
  5.7 58.6 %all_to_all.25 = bf16[16,32,16,256]{3,2,1,0:T(8,128)(2,1)S(1)} all-to-all(bf16[16,32,16,256]{3,2,1,0:T(8,128)(2,1)S(1)} %bitcast.31), channel_id=1, replica_groups=mesh['yh'=2,'x'=4,'c'=2,'z'=4,'yl'=2] {'yh','x','c'}, dimensions={0} | all-to-all | bytes 8388608 | tf_op jit(solution)/shard_map/all_to_all | solution.py:486
  64.3 0.0 copy-done.4
  64.3 0.0 copy-start.5
  64.3 3.8 %intake.1 = (bf16[8,65,16,256]{3,2,1,0:T(8,128)(2,1)}, bf16[8,16,1024]{2,1,0:T(8,128)(2,1)S(1)}, bf16[224,8192]{1,0:T(8,128)(2,1)S(1)}) custom-call(s32[72,128]{1,0:T(8,128)S(1)} %get-tuple-element.24.pick_ref, bf16[512,16,256]{2,1,0:T(8,128)(2,1)S(1)} %bitcast.25, bf16[2,8,256]{2,1,0:T(8,128)(2,1)S(1)} %bitcast.34, ...), custom_call_target="tpu_custom_call", output_to_operand_aliasing={{2}: (5, {})} | custom-call | tf_op jit(solution)/shard_map/intake/pallas_call | solution.py:90
  68.1 12.2 %all_to_all.26 = bf16[8,16,1024]{2,1,0:T(8,128)(2,1)S(1)} all-to-all(bf16[8,16,1024]{2,1,0:T(8,128)(2,1)S(1)} %get-tuple-element.28), channel_id=1, replica_groups=mesh['yh'=2,'x'=4,'c'=2,'z'=4,'yl'=2] {'yh','x'}, dimensions={0} | all-to-all | bytes 524288 | tf_op jit(solution)/shard_map/all_to_all | solution.py:504
  80.2 0.0 copy-done.5
  80.3 0.0 copy-start.2
  80.3 0.7 fusion.7
  81.0 12.5 %all_to_all.27.parts_ref = bf16[8,16,1024]{2,1,0:T(8,128)(2,1)S(1)} all-to-all(bf16[8,16,1024]{2,1,0:T(8,128)(2,1)S(1)} %bitcast.40), channel_id=1, replica_groups=mesh['yh'=2,'x'=4,'c'=2,'z'=4,'yl'=2] {'z','yl'}, dimensions={0} | all-to-all | bytes 524288 | tf_op jit(solution)/shard_map/all_to_all | solution.py:511
  93.5 0.0 copy-done.2
  93.5 0.0 copy-start.1
  93.5 0.0 copy-start.3
  93.5 0.8 settle.1
  94.3 32.1 %all_to_all.28 = bf16[64,16,1024]{2,1,0:T(8,128)(2,1)S(1)} all-to-all(bf16[64,16,1024]{2,1,0:T(8,128)(2,1)S(1)} %settle.1), channel_id=1, replica_groups=mesh['yh'=2,'x'=4,'c'=2,'z'=4,'yl'=2] {'yh','x','z','yl'}, dimensions={0} | all-to-all | bytes 4194304 | tf_op jit(solution)/shard_map/all_to_all | solution.py:515
  126.4 0.0 collective-permute-start.2
  126.4 0.0 copy-done.1
  126.4 0.0 copy-done.3
  126.4 3.2 %expand_own.1 = (bf16[128,224]{1,0:T(8,128)(2,1)S(1)}, bf16[16,1024]{1,0:T(8,128)(2,1)S(1)}) custom-call(s32[4]{0:T(128)S(1)} %pad_add_fusion.place_ref, bf16[8,128,1024]{2,1,0:T(8,128)(2,1)S(1)} %bitcast.29, bf16[224,8192]{1,0:T(8,128)(2,1)S(1)} %bitcast.26, bf16[224,8192]{1,0:T(8,128)(2,1)S(1)} %get-tuple-element.32.up_ref, f32[1,8192]{1,0:T(1,128)S(1)} %bitcast.32), custom_call_target="tpu_custom_call" | custom-call | tf_op jit(solution)/shard_map/expand_own/pallas_call | solution.py:159
  129.7 0.9 collective-permute-done.2.x_ref
  130.6 3.4 %feed_forward.1 = (bf16[8,8,16,1024]{3,2,1,0:T(8,128)(2,1)S(1)}, bf16[224,8192]{1,0:T(8,128)(2,1)S(1)}) custom-call(bf16[8,128,1024]{2,1,0:T(8,128)(2,1)S(1)} %collective-permute-done.2.x_ref, bf16[224,8192]{1,0:T(8,128)(2,1)S(1)} %bitcast.27, bf16[224,8192]{1,0:T(8,128)(2,1)S(1)} %get-tuple-element.32.up_ref, f32[1,8192]{1,0:T(1,128)S(1)} %bitcast.33, ...), custom_call_target="tpu_custom_call" | custom-call | tf_op jit(solution)/shard_map/feed_forward/pallas_call | solution.py:187
  134.0 0.2 collective-permute-start.3
  134.2 0.7 shrink_own.1.a_ref
  134.9 3.3 %collective-permute-done.3.b_ref = bf16[8,8,16,1024]{3,2,1,0:T(8,128)(2,1)S(1)} collective-permute-done((bf16[8,8,16,1024]{3,2,1,0:T(8,128)(2,1)S(1)}, bf16[8,8,16,1024]{3,2,1,0:T(8,128)(2,1)S(1)}, u32[]{:S(2)}, u32[]{:S(2)}) %collective-permute-start.3) | collective-permute-done | bytes 2097184 | tf_op jit(solution)/shard_map/ppermute | solution.py:528
  138.2 0.5 add_cores.1
  138.7 36.1 %all_to_all.29.pieces_ref = bf16[64,16,1024]{2,1,0:T(8,128)(2,1)S(1)} all-to-all(bf16[64,16,1024]{2,1,0:T(8,128)(2,1)S(1)} %bitcast.30), channel_id=1, replica_groups=mesh['yh'=2,'x'=4,'c'=2,'z'=4,'yl'=2] {'z','yl','yh','x'}, dimensions={0} | all-to-all | bytes 4194304 | tf_op jit(solution)/shard_map/all_to_all | solution.py:531
  174.8 0.9 add_pieces.1
  (1 shorter events, 0.0 us)
Async XLA Ops:
  0.6 5.0 %copy-start = (bf16[2,8,8,128]{3,2,1,0:T(8,128)(2,1)S(1)}, bf16[2,8,8,128]{3,2,1,0:T(8,128)(2,1)}, u32[]{:S(2)}) copy-start(bf16[2,8,8,128]{3,2,1,0:T(8,128)(2,1)} %param.16) | copy-start | bytes 98308
  0.6 5.0 %collective-permute-start.1 = (bf16[1024,512]{1,0:T(8,128)(2,1)}, bf16[1024,512]{1,0:T(8,128)(2,1)S(1)}, u32[]{:S(2)}, u32[]{:S(2)}) collective-permute-start(bf16[1024,512]{1,0:T(8,128)(2,1)} %param.19), channel_id=1, source_target_pairs={{0,8},{8,0},{1,9},{9,1},{2,10},{10,2},{3,11},{11,3},{4,12},{12,4},... | collective-permute-start | bytes 3145736 | tf_op jit(solution)/shard_map/ppermute | solution.py:482
  0.7 4.9 %collective-permute-start = (bf16[2,128,512]{2,1,0:T(8,128)(2,1)}, bf16[2,128,512]{2,1,0:T(8,128)(2,1)S(1)}, u32[]{:S(2)}, u32[]{:S(2)}) collective-permute-start(bf16[2,128,512]{2,1,0:T(8,128)(2,1)} %own_ref.1), channel_id=1, source_target_pairs={{0,8},{8,0},{1,9},{9,1},{2,10},{10,2},{3,11},{11,3},{4,12},{12,4},... | collective-permute-start | bytes 786440 | tf_op jit(solution)/shard_map/ppermute | solution.py:481
  5.7 58.6 %copy-start.4 = (bf16[2,8,1,256]{3,1,2,0:T(8,128)(2,1)S(1)}, bf16[2,8,1,256]{3,1,2,0:T(8,128)(2,1)}, u32[]{:S(2)}) copy-start(bf16[2,8,1,256]{3,1,2,0:T(8,128)(2,1)} %param.17) | copy-start | bytes 24580
  64.3 15.9 %copy-start.5 = (bf16[1024,512]{1,0:T(8,128)(2,1)S(1)}, bf16[1024,512]{1,0:T(8,128)(2,1)}, u32[]{:S(2)}) copy-start(bf16[1024,512]{1,0:T(8,128)(2,1)} %param.19) | copy-start | bytes 3145732
  80.3 13.3 %copy-start.2 = (bf16[2,128,512]{2,1,0:T(8,128)(2,1)S(1)}, bf16[2,128,512]{2,1,0:T(8,128)(2,1)}, u32[]{:S(2)}) copy-start(bf16[2,128,512]{2,1,0:T(8,128)(2,1)} %own_ref.1) | copy-start | bytes 786436
  93.5 32.9 %copy-start.1 = (bf16[8192,224]{0,1:T(8,128)(2,1)S(1)}, bf16[8192,224]{0,1:T(8,128)(2,1)}, u32[]{:S(2)}) copy-start(bf16[8192,224]{0,1:T(8,128)(2,1)} %param.21) | copy-start | bytes 11010052
  93.5 32.9 %copy-start.3 = (f32[8192]{0:T(1024)S(1)}, f32[8192]{0:T(1024)}, u32[]{:S(2)}) copy-start(f32[8192]{0:T(1024)} %param.20) | copy-start | bytes 98308
  126.4 4.2 %collective-permute-start.2 = (bf16[8,128,1024]{2,1,0:T(8,128)(2,1)S(1)}, bf16[8,128,1024]{2,1,0:T(8,128)(2,1)S(1)}, u32[]{:S(2)}, u32[]{:S(2)}) collective-permute-start(bf16[8,128,1024]{2,1,0:T(8,128)(2,1)S(1)} %bitcast.28), channel_id=1, source_target_pairs={{0,8},{8,0},{1,9},{9,1},{2,10},{10,2},{3,11},{11,3},{4,12},{12,4},... | collective-permute-start | bytes 6291464 | tf_op jit(solution)/shard_map/ppermute | solution.py:518
  134.0 4.2 %collective-permute-start.3 = (bf16[8,8,16,1024]{3,2,1,0:T(8,128)(2,1)S(1)}, bf16[8,8,16,1024]{3,2,1,0:T(8,128)(2,1)S(1)}, u32[]{:S(2)}, u32[]{:S(2)}) collective-permute-start(bf16[8,8,16,1024]{3,2,1,0:T(8,128)(2,1)S(1)} %get-tuple-element.37), channel_id=1, source_target_pairs={{0,8},{8,0},{1,9},{9,1},{2,10},{10,2},{3,11},{11,3},{4,12},{12,4},... | collective-permute-start | bytes 6291464 | tf_op jit(solution)/shard_map/ppermute | solution.py:528

commit v13 on v11

--- a/solution.py
+++ b/solution.py
@@ -17,7 +17,7 @@
 HBM = pl.BlockSpec(memory_space=pltpu.HBM)
 
 
-def intake(pick, received, fresh, query, up_rows, up_begun, n_copies):
+def intake(pick, received, fresh, query, up_rows, n_copies):
     req_dev, n_rows, head_dim = query.shape
     n_steps = fresh.shape[0]
     _, page_size, width_two = received.shape
@@ -26,12 +26,11 @@
     group = n_rows // n_steps
     scale = 1.0 / math.sqrt(head_dim)
 
-    def kernel(pick_ref, recv_ref, fresh_ref, q_ref, up_hbm, up_in, cache_ref, mixed_ref, up_ref, buf, scores, probs, heads, out_sems, up_sem):
+    def kernel(pick_ref, recv_ref, fresh_ref, q_ref, up_hbm, cache_ref, mixed_ref, up_ref, buf, scores, probs, heads, out_sems, up_sem):
         def copy_out(r):
             return pltpu.make_async_copy(buf.at[r], cache_ref.at[r], out_sems.at[r])
 
-        rest = pl.ds(up_hbm.shape[0] // 2, up_hbm.shape[0] // 2)
-        up_copy = pltpu.make_async_copy(up_hbm.at[rest], up_ref.at[rest], up_sem)
+        up_copy = pltpu.make_async_copy(up_hbm, up_ref, up_sem)
         up_copy.start()
         row_at = lax.broadcasted_iota(jnp.int32, (page_size, width_two), 0)
         tokens_new = [fresh_ref[s].astype(jnp.float32) for s in range(n_steps)]
@@ -89,7 +88,7 @@
 
     return pl.pallas_call(
         kernel,
-        in_specs=[SMEM, VMEM, VMEM, VMEM, HBM, VMEM],
+        in_specs=[SMEM, VMEM, VMEM, VMEM, HBM],
         out_specs=[HBM, VMEM, VMEM],
         out_shape=[
             jax.ShapeDtypeStruct((req_dev, pages, page_size, width_two), received.dtype),
@@ -107,9 +106,8 @@
             pltpu.SemaphoreType.DMA,
         ],
         compiler_params=pltpu.CompilerParams(vmem_limit_bytes=20 * MIB),
-        input_output_aliases={5: 2},
         name="intake",
-    )(pick, received, fresh, query, pltpu.with_memory_space_constraint(up_rows, pltpu.HBM), up_begun)
+    )(pick, received, fresh, query, pltpu.with_memory_space_constraint(up_rows, pltpu.HBM))
 
 
 NT = (((1,), (1,)), ((), ()))
@@ -248,14 +246,14 @@
     )
 
 
-def pack_pages(place, page_loc, lengths, placement, pool, up_rows, n_dp):
+def pack_pages(place, page_loc, lengths, placement, pool, n_dp):
     pslots, page_size, width_two = pool.shape
     _, max_pages, n_req = page_loc.shape
     req_dev = n_req // n_dp
     capacity = pslots // n_dp
     low = 32
 
-    def kernel(place_ref, loc_hbm, len_hbm, placement_hbm, pool_hbm, up_hbm, out_buf, pick_ref, up_ref, loc, len_ref, placement_ref, pool_buf, rows_vec, rows, loc_sem, len_sem, placement_sem, pool_sem, rows_sem, up_sem):
+    def kernel(place_ref, loc_hbm, len_hbm, placement_hbm, pool_hbm, out_buf, pick_ref, loc, len_ref, placement_ref, pool_buf, rows_vec, rows, loc_sem, len_sem, placement_sem, pool_sem, rows_sem):
         me = place_ref[0]
         len_copy = pltpu.make_async_copy(len_hbm, len_ref, len_sem)
         placement_copy = pltpu.make_async_copy(placement_hbm, placement_ref, placement_sem)
@@ -327,9 +325,6 @@
         pick_ref[max_pages:] = jnp.broadcast_to(own_len, (8, n_req)).astype(jnp.int32)
         rows_copy.wait()
         pool_copy.wait()
-        first = pl.ds(0, up_hbm.shape[0] // 2)
-        up_copy = pltpu.make_async_copy(up_hbm.at[first], up_ref.at[first], up_sem)
-        up_copy.start()
 
         for d in range(n_dp):
 
@@ -338,16 +333,14 @@
                 return carry
 
             lax.fori_loop(0, capacity, move, 0, unroll=16)
-        up_copy.wait()
-
-    return pl.pallas_call(
-        kernel,
-        in_specs=[SMEM, HBM, HBM, HBM, HBM, HBM],
-        out_specs=[VMEM, VMEM, VMEM],
+
+    return pl.pallas_call(
+        kernel,
+        in_specs=[SMEM, HBM, HBM, HBM, HBM],
+        out_specs=[VMEM, VMEM],
         out_shape=[
             jax.ShapeDtypeStruct(pool.shape, pool.dtype),
             jax.ShapeDtypeStruct((max_pages + 8, n_req), jnp.int32),
-            pltpu.VMEM(up_rows.shape, up_rows.dtype),
         ],
         scratch_shapes=[
             pltpu.VMEM((max_pages, n_req), jnp.int32),
@@ -361,7 +354,6 @@
             pltpu.SemaphoreType.DMA,
             pltpu.SemaphoreType.DMA,
             pltpu.SemaphoreType.DMA,
-            pltpu.SemaphoreType.DMA,
         ],
         compiler_params=pltpu.CompilerParams(vmem_limit_bytes=20 * MIB),
         name="pack_pages",
@@ -369,7 +361,7 @@
         place,
         *[
             pltpu.with_memory_space_constraint(array, pltpu.HBM)
-            for array in (page_loc, lengths, placement, pool, up_rows)
+            for array in (page_loc, lengths, placement, pool)
         ],
     )
 
@@ -461,14 +453,12 @@
     capacity = pslots // n_dp
 
     place = jnp.stack([dev_dp, dev_tensor, dev_chip, core]).astype(jnp.int32)
-    up_rows = jnp.swapaxes(w_up, 0, 1)
-    outgoing, pick, up_begun = pack_pages(
+    outgoing, pick = pack_pages(
         place,
         jnp.swapaxes(page_loc, 1, 2),
         lengths.reshape(1, n_req),
         placement.reshape(1, n_req),
         kv_pool.reshape(pslots, page_size, width_two),
-        up_rows,
         n_dp,
     )
     query = jnp.transpose(queries, (1, 0, 2, 3)).reshape(req_dev, n_steps * hq_dev, head_dim)
@@ -491,8 +481,7 @@
         received.reshape(pslots, page_size, width_two),
         fresh,
         query,
-        up_rows,
-        up_begun,
+        jnp.swapaxes(w_up, 0, 1),
         chips_dp,
     )
 

time: 174 us -> 174 us (level)
  transfers between devices with their start and end apart: 4 -> 4, of which waited for: 2 -> 2; matrix products, arithmetic and copies ran while one was open for 0% -> 0% of each run, Pallas kernels for 5% -> 4%
where the time goes in v13:
time: 174 us
  blocking collectives  149 us (86%)
  Pallas kernels  18 us (10%)
  waiting for transfers between devices  4.22 us (2%)
    all_to_all x1, blocking collectives, per_device(): lax.all_to_all(outgoing.reshape(n_dp, capacity, page_size, width_two), DP...  58.6 us
    all_to_all x1, blocking collectives, per_device(): pieces = lax.all_to_all(chip_sum, CHIPS, 0, 0, tiled=True)  35.2 us
    all_to_all x1, blocking collectives, per_device(): lax.all_to_all(hidden_copies, CHIPS, 0, 0, tiled=True)  31.5 us
    all_to_all x1, blocking collectives, per_device(): lax.all_to_all(partial_out.reshape(n_tensor, rows_blk, cols_chip), TENSOR...  12.5 us
    all_to_all x1, blocking collectives, per_device(): lax.all_to_all(mixed_copies, CHIP_DP, 0, 0, tiled=True)  11.3 us
    pallas_call x1, Pallas kernels, intake(): pl.pallas_call(kernel, in_specs=[SMEM, VMEM, VMEM, VMEM, HBM], out_specs=...  4.79 us
    pallas_call x1, Pallas kernels, pack_pages(): pl.pallas_call(kernel, in_specs=[SMEM, HBM, HBM, HBM, HBM], out_specs=[VM...  3.63 us
  transfers between devices with their start and end apart: 4, of which 2 were waited for; matrix products, arithmetic and copies ran while one was open for 0% of the time, Pallas kernels for 4%

profile of v13, /device:TPU:0, one launch (start us, length us, event | category | flops | bytes accessed | tf_op | source)
XLA Modules:
  0.0 173.7 jit_solution(303488260768412677)
XLA Ops:
  0.6 0.0 copy-start
  0.6 0.1 collective-permute-start.1
  0.7 0.5 collective-permute-start
  1.2 0.1 pad_add_fusion.place_ref
  1.3 3.6 %pack_pages.1 = (bf16[512,16,256]{2,1,0:T(8,128)(2,1)S(1)}, s32[72,128]{1,0:T(8,128)S(1)}) custom-call(s32[4]{0:T(128)S(1)} %pad_add_fusion.place_ref, s32[8,64,128]{2,1,0:T(8,128)} %bitcast.39, s32[1,128]{1,0:T(1,128)} %bitcast.40, s32[1,128]{1,0:T(1,128)} %bitcast.41, bf16[512,16,256]{2,1,0:T(8,128)(2,1)} %bitcast.35), custom_call_target="tpu_custom_call" | custom-call | tf_op jit(solution)/shard_map/pack_pages/pallas_call | solution.py:337
  4.9 0.0 copy-done
  5.0 0.0 collective-permute-done.other_ref
  5.0 0.0 collective-permute-done.1
  5.0 0.0 copy-start.4
  5.0 58.6 %all_to_all.25 = bf16[16,32,16,256]{3,2,1,0:T(8,128)(2,1)S(1)} all-to-all(bf16[16,32,16,256]{3,2,1,0:T(8,128)(2,1)S(1)} %bitcast.31), channel_id=1, replica_groups=mesh['yh'=2,'x'=4,'c'=2,'z'=4,'yl'=2] {'yh','x','c'}, dimensions={0} | all-to-all | bytes 8388608 | tf_op jit(solution)/shard_map/all_to_all | solution.py:476
  63.6 0.0 copy-done.4
  63.6 0.0 copy-start.5
  63.6 4.8 %intake.1 = (bf16[8,65,16,256]{3,2,1,0:T(8,128)(2,1)}, bf16[8,16,1024]{2,1,0:T(8,128)(2,1)S(1)}, bf16[224,8192]{1,0:T(8,128)(2,1)S(1)}) custom-call(s32[72,128]{1,0:T(8,128)S(1)} %get-tuple-element.23.pick_ref, bf16[512,16,256]{2,1,0:T(8,128)(2,1)S(1)} %bitcast.25, bf16[2,8,256]{2,1,0:T(8,128)(2,1)S(1)} %bitcast.34, ...), custom_call_target="tpu_custom_call" | custom-call | tf_op jit(solution)/shard_map/intake/pallas_call | solution.py:89
  68.4 11.3 %all_to_all.26 = bf16[8,16,1024]{2,1,0:T(8,128)(2,1)S(1)} all-to-all(bf16[8,16,1024]{2,1,0:T(8,128)(2,1)S(1)} %get-tuple-element.26), channel_id=1, replica_groups=mesh['yh'=2,'x'=4,'c'=2,'z'=4,'yl'=2] {'yh','x'}, dimensions={0} | all-to-all | bytes 524288 | tf_op jit(solution)/shard_map/all_to_all | solution.py:493
  79.7 0.0 copy-done.5
  79.7 0.0 copy-start.2
  79.7 0.7 fusion.7
  80.5 12.5 %all_to_all.27.parts_ref = bf16[8,16,1024]{2,1,0:T(8,128)(2,1)S(1)} all-to-all(bf16[8,16,1024]{2,1,0:T(8,128)(2,1)S(1)} %bitcast.38), channel_id=1, replica_groups=mesh['yh'=2,'x'=4,'c'=2,'z'=4,'yl'=2] {'z','yl'}, dimensions={0} | all-to-all | bytes 524288 | tf_op jit(solution)/shard_map/all_to_all | solution.py:500
  93.0 0.0 copy-done.2
  93.0 0.8 settle.1
  93.8 0.0 copy-start.1
  93.8 0.0 copy-start.3
  93.8 31.5 %all_to_all.28 = bf16[64,16,1024]{2,1,0:T(8,128)(2,1)S(1)} all-to-all(bf16[64,16,1024]{2,1,0:T(8,128)(2,1)S(1)} %settle.1), channel_id=1, replica_groups=mesh['yh'=2,'x'=4,'c'=2,'z'=4,'yl'=2] {'yh','x','z','yl'}, dimensions={0} | all-to-all | bytes 4194304 | tf_op jit(solution)/shard_map/all_to_all | solution.py:504
  125.3 0.0 collective-permute-start.2
  125.3 0.0 copy-done.1
  125.3 0.0 copy-done.3
  125.3 3.2 %expand_own.1 = (bf16[128,224]{1,0:T(8,128)(2,1)S(1)}, bf16[16,1024]{1,0:T(8,128)(2,1)S(1)}) custom-call(s32[4]{0:T(128)S(1)} %pad_add_fusion.place_ref, bf16[8,128,1024]{2,1,0:T(8,128)(2,1)S(1)} %bitcast.29, bf16[224,8192]{1,0:T(8,128)(2,1)S(1)} %bitcast.26, bf16[224,8192]{1,0:T(8,128)(2,1)S(1)} %get-tuple-element.30.up_ref, f32[1,8192]{1,0:T(1,128)S(1)} %bitcast.32), custom_call_target="tpu_custom_call" | custom-call | tf_op jit(solution)/shard_map/expand_own/pallas_call | solution.py:157
  128.5 0.9 collective-permute-done.2.x_ref
  129.5 3.4 %feed_forward.1 = (bf16[8,8,16,1024]{3,2,1,0:T(8,128)(2,1)S(1)}, bf16[224,8192]{1,0:T(8,128)(2,1)S(1)}) custom-call(bf16[8,128,1024]{2,1,0:T(8,128)(2,1)S(1)} %collective-permute-done.2.x_ref, bf16[224,8192]{1,0:T(8,128)(2,1)S(1)} %bitcast.27, bf16[224,8192]{1,0:T(8,128)(2,1)S(1)} %get-tuple-element.30.up_ref, f32[1,8192]{1,0:T(1,128)S(1)} %bitcast.33, ...), custom_call_target="tpu_custom_call" | custom-call | tf_op jit(solution)/shard_map/feed_forward/pallas_call | solution.py:185
  132.9 0.2 collective-permute-start.3
  133.1 0.7 shrink_own.1.a_ref
  133.8 3.3 %collective-permute-done.3.b_ref = bf16[8,8,16,1024]{3,2,1,0:T(8,128)(2,1)S(1)} collective-permute-done((bf16[8,8,16,1024]{3,2,1,0:T(8,128)(2,1)S(1)}, bf16[8,8,16,1024]{3,2,1,0:T(8,128)(2,1)S(1)}, u32[]{:S(2)}, u32[]{:S(2)}) %collective-permute-start.3) | collective-permute-done | bytes 2097184 | tf_op jit(solution)/shard_map/ppermute | solution.py:517
  137.1 0.5 add_cores.1
  137.6 35.2 %all_to_all.29.pieces_ref = bf16[64,16,1024]{2,1,0:T(8,128)(2,1)S(1)} all-to-all(bf16[64,16,1024]{2,1,0:T(8,128)(2,1)S(1)} %bitcast.30), channel_id=1, replica_groups=mesh['yh'=2,'x'=4,'c'=2,'z'=4,'yl'=2] {'yh','x','z','yl'}, dimensions={0} | all-to-all | bytes 4194304 | tf_op jit(solution)/shard_map/all_to_all | solution.py:520
  172.7 0.9 add_pieces.1
  (1 shorter events, 0.0 us)
Async XLA Ops:
  0.6 4.3 %copy-start = (bf16[2,8,8,128]{3,2,1,0:T(8,128)(2,1)S(1)}, bf16[2,8,8,128]{3,2,1,0:T(8,128)(2,1)}, u32[]{:S(2)}) copy-start(bf16[2,8,8,128]{3,2,1,0:T(8,128)(2,1)} %param.16) | copy-start | bytes 98308
  0.6 4.3 %collective-permute-start.1 = (bf16[1024,512]{1,0:T(8,128)(2,1)}, bf16[1024,512]{1,0:T(8,128)(2,1)S(1)}, u32[]{:S(2)}, u32[]{:S(2)}) collective-permute-start(bf16[1024,512]{1,0:T(8,128)(2,1)} %param.19), channel_id=1, source_target_pairs={{0,8},{8,0},{1,9},{9,1},{2,10},{10,2},{3,11},{11,3},{4,12},{12,4},... | collective-permute-start | bytes 3145736 | tf_op jit(solution)/shard_map/ppermute | solution.py:472
  0.7 4.2 %collective-permute-start = (bf16[2,128,512]{2,1,0:T(8,128)(2,1)}, bf16[2,128,512]{2,1,0:T(8,128)(2,1)S(1)}, u32[]{:S(2)}, u32[]{:S(2)}) collective-permute-start(bf16[2,128,512]{2,1,0:T(8,128)(2,1)} %own_ref.1), channel_id=1, source_target_pairs={{0,8},{8,0},{1,9},{9,1},{2,10},{10,2},{3,11},{11,3},{4,12},{12,4},... | collective-permute-start | bytes 786440 | tf_op jit(solution)/shard_map/ppermute | solution.py:471
  5.0 58.6 %copy-start.4 = (bf16[2,8,1,256]{3,1,2,0:T(8,128)(2,1)S(1)}, bf16[2,8,1,256]{3,1,2,0:T(8,128)(2,1)}, u32[]{:S(2)}) copy-start(bf16[2,8,1,256]{3,1,2,0:T(8,128)(2,1)} %param.17) | copy-start | bytes 24580
  63.6 16.1 %copy-start.5 = (bf16[1024,512]{1,0:T(8,128)(2,1)S(1)}, bf16[1024,512]{1,0:T(8,128)(2,1)}, u32[]{:S(2)}) copy-start(bf16[1024,512]{1,0:T(8,128)(2,1)} %param.19) | copy-start | bytes 3145732
  79.7 13.3 %copy-start.2 = (bf16[2,128,512]{2,1,0:T(8,128)(2,1)S(1)}, bf16[2,128,512]{2,1,0:T(8,128)(2,1)}, u32[]{:S(2)}) copy-start(bf16[2,128,512]{2,1,0:T(8,128)(2,1)} %own_ref.1) | copy-start | bytes 786436
  93.8 31.5 %copy-start.1 = (bf16[8192,224]{0,1:T(8,128)(2,1)S(1)}, bf16[8192,224]{0,1:T(8,128)(2,1)}, u32[]{:S(2)}) copy-start(bf16[8192,224]{0,1:T(8,128)(2,1)} %param.21) | copy-start | bytes 11010052
  93.8 31.5 %copy-start.3 = (f32[8192]{0:T(1024)S(1)}, f32[8192]{0:T(1024)}, u32[]{:S(2)}) copy-start(f32[8192]{0:T(1024)} %param.20) | copy-start | bytes 98308
  125.3 4.2 %collective-permute-start.2 = (bf16[8,128,1024]{2,1,0:T(8,128)(2,1)S(1)}, bf16[8,128,1024]{2,1,0:T(8,128)(2,1)S(1)}, u32[]{:S(2)}, u32[]{:S(2)}) collective-permute-start(bf16[8,128,1024]{2,1,0:T(8,128)(2,1)S(1)} %bitcast.28), channel_id=1, source_target_pairs={{0,8},{8,0},{1,9},{9,1},{2,10},{10,2},{3,11},{11,3},{4,12},{12,4},... | collective-permute-start | bytes 6291464 | tf_op jit(solution)/shard_map/ppermute | solution.py:507
  132.9 4.2 %collective-permute-start.3 = (bf16[8,8,16,1024]{3,2,1,0:T(8,128)(2,1)S(1)}, bf16[8,8,16,1024]{3,2,1,0:T(8,128)(2,1)S(1)}, u32[]{:S(2)}, u32[]{:S(2)}) collective-permute-start(bf16[8,8,16,1024]{3,2,1,0:T(8,128)(2,1)S(1)} %get-tuple-element.35), channel_id=1, source_target_pairs={{0,8},{8,0},{1,9},{9,1},{2,10},{10,2},{3,11},{11,3},{4,12},{12,4},... | collective-permute-start | bytes 6291464 | tf_op jit(solution)/shard_map/ppermute | solution.py:517
